TPU v7x, 32 devices: a whole 2x2x4 slice. The times are simulated.
32 devices in a mesh: ep: 8 (over y, x, core), tp: 4 (over z).
Axes of the slice: x: 2, y: 2, z: 4, core: 2. Of those that a mesh axis runs over, the one named last changes fastest.
Arguments:
- tokens: bfloat16 [2048, 2048], P('ep'), may hold values from -6 to 6
- segments: int32 [2048], replicated, may hold values from 0 to 3, never falling along the last dimension, each value on 1 to 1024 neighbouring positions
- routes: int32 [2048, 8], P('ep'), may hold values from 0 to 63, all different within a row; in each aligned block of 256 rows (0 to 255, 256 to 511, ...) at most 64 rows name the same one
- cotangent: bfloat16 [2048, 2048], P('ep'), may hold values from -6 to 6
- norm1_gain: float32 [2048], replicated, may hold values from 0.25 to 1.75
- query_weight: bfloat16 [2048, 2048], P(None, 'tp'), may hold values from -0.125 to 0.125
- key_weight: bfloat16 [2048, 2048], P(None, 'tp'), may hold values from -0.125 to 0.125
- value_weight: bfloat16 [2048, 2048], P(None, 'tp'), may hold values from -0.125 to 0.125
- query_gain: float32 [2048], P('tp'), may hold values from 0.25 to 1.75
- key_gain: float32 [2048], P('tp'), may hold values from 0.25 to 1.75
- output_weight: bfloat16 [2048, 2048], P('tp'), may hold values from -0.75 to 0.75
- norm2_gain: float32 [2048], replicated, may hold values from 0.25 to 1.75
- router_weight: bfloat16 [2048, 64], replicated, may hold values from -0.0625 to 0.0625
- gate_weight: bfloat16 [64, 2048, 1024], P('ep', None, 'tp'), may hold values from -0.125 to 0.125
- up_weight: bfloat16 [64, 2048, 1024], P('ep', None, 'tp'), may hold values from -0.125 to 0.125
- down_weight: bfloat16 [64, 1024, 2048], P('ep', 'tp'), may hold values from -0.5 to 0.5
Outputs:
- mixed: bfloat16 [2048, 2048], P('ep')
- grad_tokens: float32 [2048, 2048], P('ep')
- grad_norm1: float32 [2048], replicated
- grad_query: float32 [2048, 2048], P(None, 'tp')
- grad_key: float32 [2048, 2048], P(None, 'tp')
- grad_value: float32 [2048, 2048], P(None, 'tp')
- grad_qgain: float32 [2048], P('tp')
- grad_kgain: float32 [2048], P('tp')
- grad_output: float32 [2048, 2048], P('tp')
- grad_norm2: float32 [2048], replicated
- grad_router: float32 [2048, 64], replicated
- grad_gate: float32 [64, 2048, 1024], P('ep', None, 'tp')
- grad_up: float32 [64, 2048, 1024], P('ep', None, 'tp')
- grad_down: float32 [64, 1024, 2048], P('ep', 'tp')
Inputs may be any that keep to these rules, and one draw needn't show every extreme that they name: `routes`: each row names 8 different experts; among the 256 rows of one index of ep no expert is named by more than 64 rows, a bound that some block reaches. `segments`: never falling along the positions; each document covers at most half of 2048 positions, and one exactly that many.
All inputs are finite; a program needn't handle non-finite values.
Results may differ from a plain program's by a relative error of at most 0.028.
Values may be sent and summed in bfloat16 or wider, within the bound.
No kernel may reach another device: no remote copies, remote signals or barrier semaphores. Data moves between devices by JAX's collectives and lax.ppermute only.
A program may use at most 320 MiB of HBM per device.

v0:
```python
import math

import jax
import jax.numpy as jnp
from jax import lax
from jax.sharding import PartitionSpec as P

D = 2048
HEADS = 16
HEAD_DIM = 128
EXPERTS = 64
TOP = 8
SEQ_MAX = 4096
WINDOW = 1024
CAP = 64


EPSILON = 1e-05
MASKED = 1e30


def from_behind(value, axis, steps):
    count = lax.axis_size(axis)
    initial, last = (max(0, -steps), min(count, count - steps))
    return lax.ppermute(value, axis, [(source, source + steps) for source in range(initial, last)])


def inverse_rms(values_in):
    return lax.rsqrt(jnp.mean(values_in * values_in, axis=-1, keepdims=True) + EPSILON)


def rotary(row_count, first_row, seq_len, half_width):
    places = ((first_row + jnp.arange(row_count, dtype=jnp.int32)) % seq_len).astype(jnp.float32)
    freqs = jnp.exp(
        jnp.arange(half_width, dtype=jnp.float32) * (-2.0 * math.log(10000.0) / (2 * half_width))
    )
    angles = places[:, None] * freqs[None, :]
    return (jnp.cos(angles), jnp.sin(angles))


def rotate(values_in, cosine_table, sine_table, direction):
    half_width = values_in.shape[-1] // 2
    first_half = values_in[..., :half_width]
    second_half = values_in[..., half_width:]
    cos_part = cosine_table[:, None, :]
    sin_part = sine_table[:, None, :] * direction
    return jnp.concatenate(
        [
            first_half * cos_part - second_half * sin_part,
            second_half * cos_part + first_half * sin_part,
        ],
        axis=-1,
    )


def on_device(
    tokens,
    segments,
    routes,
    cotangent,
    norm1_gain,
    query_weight,
    key_weight,
    value_weight,
    query_gain,
    key_gain,
    output_weight,
    norm2_gain,
    router_weight,
    gate_weight,
    up_weight,
    down_weight,
):
    local_rows = tokens.shape[0]
    ep_count = lax.axis_size("ep")
    first_row = lax.axis_index("ep") * local_rows
    seq_len = min(SEQ_MAX, local_rows * ep_count)
    all_width = HEADS * HEAD_DIM
    head_width = query_weight.shape[1]
    local_heads = head_width // HEAD_DIM
    local_experts = gate_weight.shape[0]
    inner_width = gate_weight.shape[2]
    block_rows = min(512, local_rows)
    block_count = local_rows // block_rows
    reach_rows = min(WINDOW, local_rows)
    hop_count = max(1, WINDOW // local_rows)
    score_scale = HEAD_DIM ** (-0.5)
    inputs = tokens.astype(jnp.float32)
    scale_one = inverse_rms(inputs)
    normal_one = inputs * scale_one
    hidden_one = (normal_one * norm1_gain).astype(jnp.bfloat16)
    query_raw = jnp.dot(hidden_one, query_weight, preferred_element_type=jnp.float32)
    key_raw = jnp.dot(hidden_one, key_weight, preferred_element_type=jnp.float32)
    value_raw = jnp.dot(hidden_one, value_weight, preferred_element_type=jnp.float32)
    query_sum, key_sum = lax.psum(
        (jnp.sum(query_raw * query_raw, axis=1), jnp.sum(key_raw * key_raw, axis=1)), "tp"
    )
    query_scale = lax.rsqrt(query_sum / all_width + EPSILON)[:, None]
    key_scale = lax.rsqrt(key_sum / all_width + EPSILON)[:, None]
    query_normed = query_raw * query_scale * query_gain
    key_normed = key_raw * key_scale * key_gain
    cosine_table, sine_table = rotary(local_rows, first_row, seq_len, HEAD_DIM // 2)
    query_low = (
        rotate(
            query_normed.reshape(local_rows, local_heads, HEAD_DIM), cosine_table, sine_table, 1.0
        )
        .reshape(local_rows, head_width)
        .astype(jnp.bfloat16)
    )
    key_low = (
        rotate(key_normed.reshape(local_rows, local_heads, HEAD_DIM), cosine_table, sine_table, 1.0)
        .reshape(local_rows, head_width)
        .astype(jnp.bfloat16)
    )
    pair_low = jnp.concatenate([key_low, value_raw.astype(jnp.bfloat16)], axis=1)
    earlier = []
    for stride in range(hop_count, 0, -1):
        earlier.append(from_behind(pair_low, "ep", stride))
    key_buffer = jnp.concatenate(earlier + [pair_low], axis=0)
    segment_pad = jnp.concatenate([jnp.full((WINDOW,), -1, jnp.int32), segments], axis=0)

    def block_scores(number):
        offset = number * block_rows
        query_block = query_low.reshape(block_rows, local_heads, HEAD_DIM)
        key_block = key_buffer[:, :head_width].reshape(block_rows + WINDOW, local_heads, HEAD_DIM)
        value_block = key_buffer[:, head_width:].reshape(block_rows + WINDOW, local_heads, HEAD_DIM)
        query_at = first_row + offset + jnp.arange(block_rows, dtype=jnp.int32)
        key_at = first_row + offset - WINDOW + jnp.arange(block_rows + WINDOW, dtype=jnp.int32)
        distance = query_at[:, None] - key_at[None, :]
        same_doc = (
            lax.dynamic_slice_in_dim(segments, first_row + offset, block_rows, 0)[:, None]
            == lax.dynamic_slice_in_dim(segment_pad, first_row + offset, block_rows + WINDOW, 0)[
                None, :
            ]
        )
        allowed = (
            (distance >= 0)
            & (distance < WINDOW)
            & same_doc
            & (query_at[:, None] // seq_len == key_at[None, :] // seq_len)
        )
        scores = (
            jnp.einsum("qhd,khd->hqk", query_block, key_block, preferred_element_type=jnp.float32)
            * score_scale
        )
        return (query_block, key_block, value_block, jnp.where(allowed[None], scores, -MASKED))

    def forward_block(number):
        query_block, key_block, value_block, scores = block_scores(number)
        highest = jnp.max(scores, axis=-1, keepdims=True)
        exponents = jnp.exp(scores - highest)
        totals = jnp.sum(exponents, axis=-1, keepdims=True)
        weights = (exponents / totals).astype(jnp.bfloat16)
        result = jnp.einsum(
            "hqk,khd->qhd", weights, value_block, preferred_element_type=jnp.float32
        )
        return (result.reshape(block_rows, head_width), (highest + jnp.log(totals))[:, :, 0])

    attended, log_totals = lax.map(forward_block, jnp.arange(block_count, dtype=jnp.int32))
    attended_low = attended.reshape(local_rows, head_width).astype(jnp.bfloat16)
    branch = lax.psum(
        jnp.dot(attended_low, output_weight, preferred_element_type=jnp.float32).astype(
            jnp.bfloat16
        ),
        "tp",
    ).astype(jnp.float32)
    middle = inputs + branch
    scale_two = inverse_rms(middle)
    normal_two = middle * scale_two
    hidden_two = (normal_two * norm2_gain).astype(jnp.bfloat16)
    logits = jnp.dot(hidden_two, router_weight, preferred_element_type=jnp.float32)
    picker = (routes[:, :, None] == jnp.arange(EXPERTS, dtype=jnp.int32)[None, None, :]).astype(
        jnp.float32
    )
    chosen = jnp.sum(logits[:, None, :] * picker, axis=2)
    gate_probs = jax.nn.softmax(chosen, axis=1)
    flat_routes = routes.reshape(local_rows * TOP)
    onehot = (flat_routes[:, None] == jnp.arange(EXPERTS, dtype=jnp.int32)[None, :]).astype(
        jnp.int32
    )
    before = jnp.sum((jnp.cumsum(onehot, axis=0) - onehot) * onehot, axis=1)
    slot_index = flat_routes * CAP + before
    pair_of = (
        jnp.full((EXPERTS * CAP,), local_rows * TOP, jnp.int32)
        .at[slot_index]
        .set(jnp.arange(local_rows * TOP, dtype=jnp.int32))
    )
    token_of = pair_of // TOP
    hidden_pad = jnp.concatenate([hidden_two, jnp.zeros((1, D), jnp.bfloat16)], axis=0)
    payload = hidden_pad[token_of]
    arrived = lax.all_to_all(
        payload.reshape(ep_count, local_experts * CAP, payload.shape[1]),
        "ep",
        split_axis=0,
        concat_axis=0,
        tiled=True,
    )
    received = arrived.reshape(ep_count, local_experts, CAP, D)
    paired_weight = jnp.concatenate([gate_weight, up_weight], axis=2)
    gate_up = jnp.einsum(
        "secd,edf->secf", received, paired_weight, preferred_element_type=jnp.float32
    )
    gate_val = gate_up[..., :inner_width]
    up_val = gate_up[..., inner_width:]
    activated = jax.nn.silu(gate_val)
    hidden_mid = (activated * up_val).astype(jnp.bfloat16)
    partial_out = lax.map(
        lambda source_piece: jnp.einsum(
            "ecf,efd->ecd", source_piece, down_weight, preferred_element_type=jnp.float32
        ).astype(jnp.bfloat16),
        hidden_mid,
    )
    upstream = cotangent.astype(jnp.float32)
    returned = lax.all_to_all(
        partial_out.reshape(ep_count, local_experts * CAP, D),
        "ep",
        split_axis=0,
        concat_axis=0,
        tiled=True,
    )
    per_token = returned.reshape(EXPERTS * CAP, D)[slot_index].reshape(local_rows, TOP, D)
    moe_part = jnp.sum(gate_probs[:, :, None] * per_token, axis=1)
    gate_part = jnp.sum(upstream[:, None, :] * per_token, axis=2)
    moe_out, gate_grad = (
        lax.psum(moe_part.astype(jnp.bfloat16), "tp").astype(jnp.float32),
        lax.psum(gate_part.astype(jnp.bfloat16), "tp").astype(jnp.float32),
    )
    mixed_out = (middle + moe_out).astype(jnp.bfloat16)
    gate_pad = jnp.concatenate(
        [gate_probs.reshape(local_rows * TOP), jnp.zeros((1,), jnp.float32)], axis=0
    )
    cotangent_pad = jnp.concatenate([cotangent, jnp.zeros((1, D), jnp.bfloat16)], axis=0)
    grad_send = (gate_pad[pair_of][:, None] * cotangent_pad[token_of]).astype(jnp.bfloat16)
    grad_arrived = lax.all_to_all(
        grad_send.reshape(ep_count, local_experts * CAP, grad_send.shape[1]),
        "ep",
        split_axis=0,
        concat_axis=0,
        tiled=True,
    )
    grad_arrived = grad_arrived.reshape(ep_count, local_experts, CAP, D)
    grad_hidden = jnp.einsum(
        "secd,efd->secf", grad_arrived, down_weight, preferred_element_type=jnp.float32
    )
    grad_down = jnp.einsum(
        "secf,secd->efd", hidden_mid, grad_arrived, preferred_element_type=jnp.float32
    )
    sigmoid_val = jax.nn.sigmoid(gate_val)
    grad_pair = jnp.concatenate(
        [
            grad_hidden * up_val * sigmoid_val * (1.0 + gate_val * (1.0 - sigmoid_val)),
            grad_hidden * activated,
        ],
        axis=3,
    ).astype(jnp.bfloat16)
    grad_paired = jnp.einsum(
        "secd,secf->edf", received, grad_pair, preferred_element_type=jnp.float32
    )
    grad_inputs = lax.map(
        lambda grad_piece: jnp.einsum(
            "ecf,edf->ecd", grad_piece, paired_weight, preferred_element_type=jnp.float32
        ).astype(jnp.bfloat16),
        grad_pair,
    )
    grad_back = lax.all_to_all(
        grad_inputs.reshape(ep_count, local_experts * CAP, D),
        "ep",
        split_axis=0,
        concat_axis=0,
        tiled=True,
    )
    moe_grad_rows = jnp.sum(
        grad_back.reshape(EXPERTS * CAP, D)[slot_index].reshape(local_rows, TOP, D),
        axis=1,
        dtype=jnp.float32,
    )
    grad_two = lax.psum(moe_grad_rows.astype(jnp.bfloat16), "tp").astype(jnp.float32)
    chosen_grad = gate_probs * (gate_grad - jnp.sum(gate_probs * gate_grad, axis=1, keepdims=True))
    logit_grad = jnp.sum(chosen_grad[:, :, None] * picker, axis=1).astype(jnp.bfloat16)
    grad_router = jnp.dot(hidden_two.T, logit_grad, preferred_element_type=jnp.float32)
    grad_two = grad_two + jnp.dot(logit_grad, router_weight.T, preferred_element_type=jnp.float32)
    grad_norm2 = jnp.sum(grad_two * normal_two, axis=0)
    scaled_two = grad_two * norm2_gain
    grad_middle = upstream + scale_two * (
        scaled_two - normal_two * jnp.mean(scaled_two * normal_two, axis=1, keepdims=True)
    )
    middle_low = grad_middle.astype(jnp.bfloat16)
    grad_output = jnp.dot(attended_low.T, middle_low, preferred_element_type=jnp.float32)
    grad_attended = jnp.dot(middle_low, output_weight.T, preferred_element_type=jnp.float32).astype(
        jnp.bfloat16
    )
    grad_att_blocks = grad_attended.reshape(block_count, block_rows, local_heads, HEAD_DIM)

    def backward_block(carried, number):
        query_block, key_block, value_block, scores = block_scores(number)
        weights = jnp.exp(scores - log_totals[number][:, :, None])
        out_grad = grad_att_blocks[number]
        weight_grad = jnp.einsum(
            "qhd,khd->hqk", out_grad, value_block, preferred_element_type=jnp.float32
        )
        inner_sum = jnp.sum(weights * weight_grad, axis=-1, keepdims=True)
        score_grad = (weights * (weight_grad - inner_sum)).astype(jnp.bfloat16)
        query_grad = (
            jnp.einsum("hqk,khd->qhd", score_grad, key_block, preferred_element_type=jnp.float32)
            * score_scale
        )
        key_grad = (
            jnp.einsum("hqk,qhd->khd", score_grad, query_block, preferred_element_type=jnp.float32)
            * score_scale
        )
        value_grad = jnp.einsum(
            "hqk,qhd->khd",
            weights.astype(jnp.bfloat16),
            out_grad,
            preferred_element_type=jnp.float32,
        )
        pair_grad = jnp.concatenate(
            [
                key_grad.reshape(block_rows + WINDOW, head_width),
                value_grad.reshape(block_rows + WINDOW, head_width),
            ],
            axis=1,
        )
        offset = number * block_rows
        current = carried
        carried = current + pair_grad
        return (carried, query_grad.reshape(block_rows, head_width))

    buffer_grad, query_blocks = lax.scan(
        backward_block,
        jnp.zeros((WINDOW + local_rows, 2 * head_width), jnp.float32),
        jnp.arange(block_count, dtype=jnp.int32),
    )
    from_later = jnp.zeros((reach_rows, 2 * head_width), jnp.float32)
    for stride in range(hop_count, 0, -1):
        lower_row = (hop_count - stride) * reach_rows
        from_later = from_later + from_behind(
            buffer_grad[lower_row : lower_row + reach_rows].astype(jnp.bfloat16), "ep", -stride
        ).astype(jnp.float32)
    own_grad = buffer_grad[WINDOW:].at[local_rows - reach_rows :].add(from_later)
    key_back = rotate(
        own_grad[:, :head_width].reshape(local_rows, local_heads, HEAD_DIM),
        cosine_table,
        sine_table,
        -1.0,
    ).reshape(local_rows, head_width)
    query_back = rotate(
        query_blocks.reshape(local_rows, local_heads, HEAD_DIM), cosine_table, sine_table, -1.0
    ).reshape(local_rows, head_width)
    query_dot, key_dot = lax.psum(
        (
            jnp.sum(query_back * query_gain * query_raw, axis=1),
            jnp.sum(key_back * key_gain * key_raw, axis=1),
        ),
        "tp",
    )
    query_cube = query_scale * query_scale * query_scale
    key_cube = key_scale * key_scale * key_scale
    query_grad_low = (
        query_scale * query_gain * query_back
        - query_raw * query_cube * (query_dot[:, None] / all_width)
    ).astype(jnp.bfloat16)
    key_grad_low = (
        key_scale * key_gain * key_back - key_raw * key_cube * (key_dot[:, None] / all_width)
    ).astype(jnp.bfloat16)
    value_grad_low = own_grad[:, head_width:].astype(jnp.bfloat16)
    grad_qgain = jnp.sum(query_back * query_raw * query_scale, axis=0)
    grad_kgain = jnp.sum(key_back * key_raw * key_scale, axis=0)
    grad_query = jnp.dot(hidden_one.T, query_grad_low, preferred_element_type=jnp.float32)
    grad_key = jnp.dot(hidden_one.T, key_grad_low, preferred_element_type=jnp.float32)
    grad_value = jnp.dot(hidden_one.T, value_grad_low, preferred_element_type=jnp.float32)
    one_terms = (
        jnp.dot(query_grad_low, query_weight.T, preferred_element_type=jnp.float32)
        + jnp.dot(key_grad_low, key_weight.T, preferred_element_type=jnp.float32)
        + jnp.dot(value_grad_low, value_weight.T, preferred_element_type=jnp.float32)
    )
    grad_one = lax.psum(one_terms.astype(jnp.bfloat16), "tp").astype(jnp.float32)
    grad_norm1 = jnp.sum(grad_one * normal_one, axis=0)
    scaled_one = grad_one * norm1_gain
    grad_input = grad_middle + scale_one * (
        scaled_one - normal_one * jnp.mean(scaled_one * normal_one, axis=1, keepdims=True)
    )
    summed = (
        lax.psum(grad_norm1.astype(jnp.bfloat16), "ep").astype(jnp.float32),
        lax.psum(grad_query.astype(jnp.bfloat16), "ep").astype(jnp.float32),
        lax.psum(grad_key.astype(jnp.bfloat16), "ep").astype(jnp.float32),
        lax.psum(grad_value.astype(jnp.bfloat16), "ep").astype(jnp.float32),
        lax.psum(grad_qgain.astype(jnp.bfloat16), "ep").astype(jnp.float32),
        lax.psum(grad_kgain.astype(jnp.bfloat16), "ep").astype(jnp.float32),
        lax.psum(grad_output.astype(jnp.bfloat16), "ep").astype(jnp.float32),
        lax.psum(grad_norm2.astype(jnp.bfloat16), "ep").astype(jnp.float32),
        lax.psum(grad_router.astype(jnp.bfloat16), "ep").astype(jnp.float32),
    )
    return (
        mixed_out,
        grad_input,
        summed[0],
        summed[1],
        summed[2],
        summed[3],
        summed[4],
        summed[5],
        summed[6],
        summed[7],
        summed[8],
        grad_paired[:, :, :inner_width],
        grad_paired[:, :, inner_width:],
        grad_down,
    )


def solution(mesh):
    return jax.shard_map(
        on_device,
        mesh=mesh,
        in_specs=(
            P("ep", None),
            P(),
            P("ep", None),
            P("ep", None),
            P(),
            P(None, "tp"),
            P(None, "tp"),
            P(None, "tp"),
            P("tp"),
            P("tp"),
            P("tp", None),
            P(),
            P(),
            P("ep", None, "tp"),
            P("ep", None, "tp"),
            P("ep", "tp", None),
        ),
        out_specs=(
            P("ep", None),
            P("ep", None),
            P(),
            P(None, "tp"),
            P(None, "tp"),
            P(None, "tp"),
            P("tp"),
            P("tp"),
            P("tp", None),
            P(),
            P(),
            P("ep", None, "tp"),
            P("ep", None, "tp"),
            P("ep", "tp", None),
        ),
        check_vma=False,
    )
```

profile of v0, /device:TPU:0, one launch (start us, length us, event | category | flops | bytes accessed | tf_op | source)
XLA Modules:
  0.0 1440.6 jit_solution(9769945327637415525)
XLA Ops:
  15.5 13.6 all-reduce.4
  65.1 34.6 %reduce-window.6 = s32[64,16,128]{2,1,0:T(8,128)} reduce-window(s32[64,16,128]{2,1,0:T(8,128)} %fusion.85, s32[]{:T(128)} %copy.230), window={size=1x1x128 pad=0_0x0_0x127_0}, to_apply=%region_12.13 | reduce-window | flops 16646144 | bytes 1048580 | tf_op jit(solution)/shard_map/reduce-window
  131.6 37.6 %all-reduce.13.cloned.1.call-done = bf16[256,2048]{1,0:T(8,128)(2,1)} async-done(((bf16[256,2048]{1,0:T(8,128)(2,1)}), bf16[256,2048]{1,0:T(8,128)(2,1)}) %all-reduce.13.cloned.1.call-update) | async-done | bytes 1048592 | tf_op jit(solution)/shard_map/psum | solution.py:161
  172.5 20.6 %gather_fusion = bf16[4096,2048]{1,0:T(8,128)(2,1)} fusion(bf16[257,2048]{1,0:T(8,128)(2,1)S(1)} %concatenate.52, s32[4096]{0:T(1024)S(1)} %get-tuple-element.239), kind=kCustom, calls=%fused_computation | custom fusion | bytes 33570816 | tf_op jit(solution)/shard_map/gather | solution.py:190
  200.2 20.6 %gather_fusion.3 = bf16[4096,2048]{1,0:T(8,128)(2,1)} fusion(bf16[257,2048]{1,0:T(8,128)(2,1)S(1)} %concatenate.54, s32[4096]{0:T(1024)S(1)} %get-tuple-element.239), kind=kCustom, calls=%fused_computation.3 | custom fusion | bytes 33570816 | tf_op jit(solution)/shard_map/gather | solution.py:233
  224.7 23.0 %gather_fusion.2 = f32[4096]{0:T(1024)S(1)} fusion(f32[2049]{0:T(1024)S(1)} %pad_maximum_fusion.6, s32[4096]{0:T(1024)S(1)} %get-tuple-element.238), kind=kCustom, calls=%fused_computation.2 | custom fusion | bytes 49152 | tf_op jit(solution)/shard_map/gather | solution.py:233
  247.8 14.8 %fusion.10 = bf16[8,512,2048]{2,1,0:T(8,128)(2,1)} fusion(bf16[8,512,2048]{2,1,0:T(8,128)(2,1)} %bitcast.200, f32[8,512]{1,0:T(8,128)S(1)} %mul.556), kind=kLoop, calls=%fused_computation.19 | loop fusion | flops 25165824 | bytes 33570816 | tf_op jit(solution)/shard_map/convert_element_type | solution.py:233
  262.5 120.3 %all-to-all-done = bf16[8,512,2048]{2,1,0:T(8,128)(2,1)} async-done(((bf16[8,512,2048]{2,1,0:T(8,128)(2,1)}), bf16[8,512,2048]{2,1,0:T(8,128)(2,1)}, u32[]{:S(2)}, u32[]{:S(2)}) %all-to-all-start) | async-done | bytes 16777248 | tf_op jit(solution)/shard_map/all_to_all | solution.py:191
  403.6 19.0 %fusion.32 = f32[8,8,64,512]{3,2,0,1:T(8,128)} fusion(bf16[8,8,64,2048]{3,2,1,0:T(8,128)(2,1)} %bitcast.14, bf16[8,2048,512]{2,1,0:T(8,128)(2,1)} %constant_dynamic-update-slice_fusion.5), kind=kOutput, calls=%fused_computation.58 | convolution fusion | flops 8589934592 | bytes 41943040 | tf_op jit(solution)/shard_map/secd,edf->secf/dot_general | solution.py:200
  422.6 150.3 %all-to-all-done.2 = bf16[8,512,2048]{2,1,0:T(8,128)(2,1)} async-done(((bf16[8,512,2048]{2,1,0:T(8,128)(2,1)}), bf16[8,512,2048]{2,1,0:T(8,128)(2,1)}, u32[]{:S(2)}, u32[]{:S(2)}) %all-to-all-start.2) | async-done | bytes 16777248 | tf_op jit(solution)/shard_map/all_to_all | solution.py:234
  572.9 16.5 %fusion.28 = (bf16[8,8,64,256]{3,2,0,1:T(8,128)(2,1)}, bf16[8,8,64,256]{3,2,0,1:T(8,128)(2,1)}, bf16[8,8,64,256]{3,2,0,1:T(8,128)(2,1)}) fusion(f32[8,8,64,512]{3,2,0,1:T(8,128)} %fusion.32, bf16[8,256,2048]{2,1,0:T(8,128)(2,1)} %param.39, bf16[8,8,64,2048]{3,2,1,0:T(8,128)(2,1)} %bitcast.20), kind=kOutput, calls=%fused_computation.51 | convolution fusion | flops 4310695936 | bytes 39845888 | tf_op jit(solution)/shard_map/secd,efd->secf/dot_general | solution.py:242
  595.5 51.0 %while.6 = (s32[]{:T(128)}, bf16[8,8,64,2048]{3,2,1,0:T(8,128)(2,1)}, bf16[8,8,64,256]{3,2,0,1:T(8,128)(2,1)}, bf16[8,256,2048]{2,1,0:T(8,128)(2,1)}, s32[]{:T(128)}) while((s32[]{:T(128)}, bf16[8,8,64,2048]{3,2,1,0:T(8,128)(2,1)}, bf16[8,8,64,256]{3,2,0,1:T(8,128)(2,1)}, bf16[8,256,2048]{2,1,0:T(8,128)(2,1)}, s32[]{:T(128)}) %tuple.92), condition=%wide.region_17.18_spmd, body=%wide.region_16.17_spmd.sunk | while | flops 537919488 | bytes 10748997 | solution.py:207
  663.6 99.2 %while.7 = (s32[]{:T(128)}, bf16[8,8,64,2048]{3,2,1,0:T(8,128)(2,1)}, bf16[8,8,64,512]{3,2,1,0:T(8,128)(2,1)}, bf16[8,2048,512]{2,1,0:T(8,128)(2,1)}, s32[]{:T(128)}) while((s32[]{:T(128)}, bf16[8,8,64,2048]{3,2,1,0:T(8,128)(2,1)}, bf16[8,8,64,512]{3,2,1,0:T(8,128)(2,1)}, bf16[8,2048,512]{2,1,0:T(8,128)(2,1)}, s32[]{:T(128)}) %tuple.95), condition=%wide.region_21.22_spmd, body=%wide.region_20.21_spmd.sunk | while | flops 1074790400 | bytes 19399748 | solution.py:259
  663.6 12.4 fusion.163
  676.0 12.4 fusion.163
  688.4 12.4 fusion.163
  700.8 12.4 fusion.163
  713.2 12.4 fusion.163
  725.6 12.4 fusion.163
  738.0 12.4 fusion.163
  762.8 73.4 %all-to-all-done.1 = bf16[8,512,2048]{2,1,0:T(8,128)(2,1)} async-done(((bf16[8,512,2048]{2,1,0:T(8,128)(2,1)}), bf16[8,512,2048]{2,1,0:T(8,128)(2,1)}, u32[]{:S(2)}, u32[]{:S(2)}) %all-to-all-start.1) | async-done | bytes 16777248 | tf_op jit(solution)/shard_map/all_to_all | solution.py:214
  844.0 24.2 %gather_fusion.1 = bf16[2048,2048]{1,0:T(8,128)(2,1)} fusion(bf16[4096,2048]{1,0:T(8,128)(2,1)} %bitcast.17, s32[2048]{0:T(1024)S(1)} %broadcast_clamp_fusion), kind=kCustom, calls=%fused_computation.1 | custom fusion | bytes 16785408 | tf_op jit(solution)/shard_map/gather | solution.py:221
  868.2 157.8 %all-to-all-done.3 = bf16[8,512,2048]{2,1,0:T(8,128)(2,1)} async-done(((bf16[8,512,2048]{2,1,0:T(8,128)(2,1)}), bf16[8,512,2048]{2,1,0:T(8,128)(2,1)}, u32[]{:S(2)}, u32[]{:S(2)}) %all-to-all-start.3) | async-done | bytes 16777248 | tf_op jit(solution)/shard_map/all_to_all | solution.py:265
  1026.1 24.2 %gather_fusion.4 = bf16[2048,2048]{1,0:T(8,128)(2,1)} fusion(bf16[4096,2048]{1,0:T(8,128)(2,1)} %bitcast.25, s32[2048]{0:T(1024)S(1)} %broadcast_clamp_fusion), kind=kCustom, calls=%fused_computation.4 | custom fusion | bytes 16785408 | tf_op jit(solution)/shard_map/gather | solution.py:273
  1082.6 28.6 %all-reduce.15.cloned.1.call-done = bf16[256,2048]{1,0:T(8,128)(2,1)} async-done(((bf16[256,2048]{1,0:T(8,128)(2,1)}), bf16[256,2048]{1,0:T(8,128)(2,1)}) %all-reduce.15.cloned.1.call-update) | async-done | bytes 1048592 | tf_op jit(solution)/shard_map/psum | solution.py:277
  1136.5 18.9 %collective-permute-done.6 = bf16[256,1024]{0,1:T(8,128)(2,1)S(1)} collective-permute-done((bf16[256,1024]{0,1:T(8,128)(2,1)S(1)}, bf16[256,1024]{0,1:T(8,128)(2,1)S(1)}, u32[]{:S(2)}, u32[]{:S(2)}) %collective-permute-start.6) | collective-permute-done | bytes 524320 | tf_op jit(solution)/shard_map/ppermute | solution.py:25
  1183.1 21.6 %convolution_bitcast_fusion = f32[8,2048,512]{2,1,0:T(8,128)} fusion(bf16[8,8,64,2048]{3,2,1,0:T(8,128)(2,1)} %bitcast.14, bf16[8,8,64,256]{3,2,0,1:T(8,128)(2,1)} %get-tuple-element.210, bf16[8,8,64,256]{3,2,0,1:T(8,128)(2,1)} %get-tuple-element.209), kind=kOutput, calls=%fused_computation.22 | convolution fusion | flops 8598323200 | bytes 54525952 | tf_op jit(solution)/shard_map/secd,secf->edf/dot_general | solution.py:256
  1214.4 22.3 %fusion.114 = (f32[8,2048,256]{2,1,0:T(8,128)}, f32[8,2048,256]{2,1,0:T(8,128)}) fusion(f32[8,2048,512]{2,1,0:T(8,128)} %convolution_bitcast_fusion), kind=kLoop, calls=%fused_computation.234 | loop fusion | bytes 67108864 | tf_op jit(solution)/shard_map/slice | solution.py:407
  1236.7 17.2 %fusion.21 = f32[8,256,2048]{2,1,0:T(8,128)} fusion(bf16[8,8,64,256]{3,2,0,1:T(8,128)(2,1)} %get-tuple-element.388, bf16[8,8,64,2048]{3,2,1,0:T(8,128)(2,1)} %bitcast.20), kind=kOutput, calls=%fused_computation.34 | convolution fusion | flops 4294967296 | bytes 35651584 | tf_op jit(solution)/shard_map/secf,secd->efd/dot_general | solution.py:245
  1253.9 31.5 %all-reduce.19.cloned.1.call-done = (bf16[256,2048]{1,0:T(8,128)(2,1)}, bf16[256,2048]{1,0:T(8,128)(2,1)}) async-done(((bf16[256,2048]{1,0:T(8,128)(2,1)}, bf16[256,2048]{1,0:T(8,128)(2,1)}), (bf16[256,2048]{1,0:T(8,128)(2,1)}, bf16[256,2048]{1,0:T(8,128)(2,1)})) %all-reduce.19.cloned.1.call-update) | async-done | bytes 2097168 | tf_op jit(solution)/shard_map/psum | solution.py:225
  1287.4 25.6 %all-reduce.5 = (bf16[2048]{0:T(1024)(128)(2,1)S(1)}, bf16[512]{0:T(512)(128)(2,1)S(1)}, bf16[512]{0:T(512)(128)(2,1)S(1)}, bf16[2048]{0:T(1024)(128)(2,1)S(1)}) all-reduce(bf16[2048]{0:T(1024)(128)(2,1)S(1)} %get-tuple-element.170, bf16[512]{0:T(512)(128)(2,1)S(1)} %get-tuple-element.174, ...), channel_id=1, replica_groups=mesh['ep'=8,'tp'=4] {'ep'}, use_global_device_ids=true, to_apply=%region_37.38 | all-reduce | flops 5120 | bytes 20480 | tf_op jit(solution)/shard_map/psum | solution.py:384
  1321.1 99.7 %all-reduce.17.cloned.1.call-done = (bf16[2048,512]{1,0:T(8,128)(2,1)}, bf16[2048,512]{1,0:T(8,128)(2,1)}, bf16[2048,512]{1,0:T(8,128)(2,1)}, bf16[512,2048]{1,0:T(8,128)(2,1)}, bf16[2048,64]{0,1:T(8,128)(2,1)}) async-done(((bf16[2048,512]{1,0:T(8,128)(2,1)}, bf16[2048,512]{1,0:T(8,128)(2,1)}, bf16[2048,512]{1,0:T(8,128)(2,1)}, bf16[512,2048]{1,0:T(8,128)(2,1)}, bf16[2048,64]{0,1:T(8,128)(2,1)}), ...) | async-done | bytes 8650768 | tf_op jit(solution)/shard_map/psum | solution.py:385
  (344 shorter events, 322.5 us)
Async XLA Ops:
  7.2 162.0 %all-reduce.13.cloned.1.call-start = ((), (), s32[]{:S(2)}) async-start(), calls=%async_computation.4 | async-start | bytes 2097152 | tf_op jit(solution)/shard_map/psum | solution.py:161
  15.5 21.1 %copy-start.72 = (f32[512]{0:T(512)S(1)}, f32[512]{0:T(512)}, u32[]{:S(2)}) copy-start(f32[512]{0:T(512)} %param.33) | copy-start | bytes 6148
  44.4 67.7 %copy-start.28 = (bf16[256,4,64]{2,0,1:T(8,128)(2,1)}, bf16[256,4,64]{2,0,1:T(8,128)(2,1)S(1)}, u32[]{:S(2)}) copy-start(bf16[256,4,64]{2,0,1:T(8,128)(2,1)S(1)} %get-tuple-element.220) | copy-start | bytes 393220
  46.1 57.3 %collective-permute-start = (bf16[256,1024]{1,0:T(8,128)(2,1)}, bf16[256,1024]{1,0:T(8,128)(2,1)}, u32[]{:S(2)}, u32[]{:S(2)}) collective-permute-start(bf16[256,1024]{1,0:T(8,128)(2,1)} %pad_maximum_fusion.2), channel_id=1, source_target_pairs={{0,16},{4,20},{8,24},{12,28},{1,17},{5,21},{9,25},{13,29},{2,18},{... | collective-permute-start | bytes 1572872 | tf_op jit(solution)/shard_map/ppermute | solution.py:25
  50.4 54.2 %collective-permute-start.1 = (bf16[256,1024]{1,0:T(8,128)(2,1)}, bf16[256,1024]{1,0:T(8,128)(2,1)}, u32[]{:S(2)}, u32[]{:S(2)}) collective-permute-start(bf16[256,1024]{1,0:T(8,128)(2,1)} %pad_maximum_fusion.2), channel_id=1, source_target_pairs={{0,12},{4,16},{8,20},{12,24},{16,28},{1,13},{5,17},{9,21},{13,25},... | collective-permute-start | bytes 1572872 | tf_op jit(solution)/shard_map/ppermute | solution.py:25
  52.5 53.2 %collective-permute-start.2 = (bf16[256,1024]{1,0:T(8,128)(2,1)}, bf16[256,1024]{1,0:T(8,128)(2,1)}, u32[]{:S(2)}, u32[]{:S(2)}) collective-permute-start(bf16[256,1024]{1,0:T(8,128)(2,1)} %pad_maximum_fusion.2), channel_id=1, source_target_pairs={{0,8},{4,12},{8,16},{12,20},{16,24},{20,28},{1,9},{5,13},{9,17},{1... | collective-permute-start | bytes 1572872 | tf_op jit(solution)/shard_map/ppermute | solution.py:25
  56.7 50.0 %collective-permute-start.3 = (bf16[256,1024]{1,0:T(8,128)(2,1)}, bf16[256,1024]{1,0:T(8,128)(2,1)}, u32[]{:S(2)}, u32[]{:S(2)}) collective-permute-start(bf16[256,1024]{1,0:T(8,128)(2,1)} %pad_maximum_fusion.2), channel_id=1, source_target_pairs={{0,4},{4,8},{8,12},{12,16},{16,20},{20,24},{24,28},{1,5},{5,9},{9,... | collective-permute-start | bytes 1572872 | tf_op jit(solution)/shard_map/ppermute | solution.py:25
  121.3 49.6 %copy-start.63 = (f32[2048]{0:T(1024)S(1)}, f32[2048]{0:T(1024)}, u32[]{:S(2)}) copy-start(f32[2048]{0:T(1024)} %param.35) | copy-start | bytes 24580
  193.2 189.7 %all-to-all-start = ((bf16[8,512,2048]{2,1,0:T(8,128)(2,1)}), bf16[8,512,2048]{2,1,0:T(8,128)(2,1)}, u32[]{:S(2)}, u32[]{:S(2)}) async-start(bf16[8,512,2048]{2,1,0:T(8,128)(2,1)} %bitcast.199), calls=%async_computation | async-start | bytes 33554432 | tf_op jit(solution)/shard_map/all_to_all | solution.py:191
  200.2 20.7 %copy-start.54 = (bf16[2048,64]{0,1:T(8,128)(2,1)S(1)}, bf16[2048,64]{0,1:T(8,128)(2,1)}, u32[]{:S(2)}) copy-start(bf16[2048,64]{0,1:T(8,128)(2,1)} %param.36) | copy-start | bytes 786436
  382.8 190.1 %all-to-all-start.2 = ((bf16[8,512,2048]{2,1,0:T(8,128)(2,1)}), bf16[8,512,2048]{2,1,0:T(8,128)(2,1)}, u32[]{:S(2)}, u32[]{:S(2)}) async-start(bf16[8,512,2048]{2,1,0:T(8,128)(2,1)} %fusion.10), calls=%async_computation.2 | async-start | bytes 33554432 | tf_op jit(solution)/shard_map/all_to_all | solution.py:234
  646.5 189.7 %all-to-all-start.1 = ((bf16[8,512,2048]{2,1,0:T(8,128)(2,1)}), bf16[8,512,2048]{2,1,0:T(8,128)(2,1)}, u32[]{:S(2)}, u32[]{:S(2)}) async-start(bf16[8,512,2048]{2,1,0:T(8,128)(2,1)} %bitcast.202), calls=%async_computation.1 | async-start | bytes 33554432 | tf_op jit(solution)/shard_map/all_to_all | solution.py:214
  836.2 189.8 %all-to-all-start.3 = ((bf16[8,512,2048]{2,1,0:T(8,128)(2,1)}), bf16[8,512,2048]{2,1,0:T(8,128)(2,1)}, u32[]{:S(2)}, u32[]{:S(2)}) async-start(bf16[8,512,2048]{2,1,0:T(8,128)(2,1)} %bitcast.201), calls=%async_computation.3 | async-start | bytes 33554432 | tf_op jit(solution)/shard_map/all_to_all | solution.py:265
  842.1 269.1 %all-reduce.15.cloned.1.call-start = ((), (), s32[]{:S(2)}) async-start(), calls=%async_computation.5 | async-start | bytes 2097152 | tf_op jit(solution)/shard_map/psum | solution.py:277
  1061.4 21.1 %copy-start.52 = (f32[256,8]{0,1:T(8,128)S(1)}, f32[256,8]{0,1:T(8,128)}, u32[]{:S(2)}) copy-start(f32[256,8]{0,1:T(8,128)} %copy-done.51) | copy-start | bytes 24580
  1061.4 21.1 %copy-start.69 = (f32[256]{0:T(256)S(1)}, f32[256]{0:T(256)}, u32[]{:S(2)}) copy-start(f32[256]{0:T(256)} %copy-done.68) | copy-start | bytes 3076
  1061.4 21.1 %copy-start.77 = (f32[256]{0:T(256)S(1)}, f32[256]{0:T(256)}, u32[]{:S(2)}) copy-start(f32[256]{0:T(256)} %copy-done.76) | copy-start | bytes 3076
  1061.4 21.1 %copy-start.56 = (s32[256,8]{0,1:T(8,128)S(1)}, s32[256,8]{0,1:T(8,128)}, u32[]{:S(2)}) copy-start(s32[256,8]{0,1:T(8,128)} %param.26) | copy-start | bytes 24580
  1061.4 49.8 %copy-start.3 = (bf16[256,2048]{1,0:T(8,128)(2,1)S(1)}, bf16[256,2048]{1,0:T(8,128)(2,1)}, u32[]{:S(2)}) copy-start(bf16[256,2048]{1,0:T(8,128)(2,1)} %param.24) | copy-start | bytes 3145732
  1061.4 49.8 %copy-start.64 = (f32[2048]{0:T(1024)S(1)}, f32[2048]{0:T(1024)}, u32[]{:S(2)}) copy-start(f32[2048]{0:T(1024)} %param.35) | copy-start | bytes 24580
  1061.5 49.8 %copy-start.86 = (f32[256]{0:T(256)S(1)}, f32[256]{0:T(256)}, u32[]{:S(2)}) copy-start(f32[256]{0:T(256)} %copy-done.85) | copy-start | bytes 3076
  1061.5 223.9 %all-reduce.19.cloned.1.call-start = ((), (), s32[]{:S(2)}) async-start(), calls=%async_computation.7 | async-start | bytes 4194304 | tf_op jit(solution)/shard_map/psum | solution.py:225
  1082.6 31.4 %copy-start.57 = (bf16[256,64]{0,1:T(8,128)(2,1)}, bf16[256,64]{0,1:T(8,128)(2,1)S(1)}, u32[]{:S(2)}) copy-start(bf16[256,64]{0,1:T(8,128)(2,1)S(1)} %select_reduce_fusion) | copy-start | bytes 98308
  1129.5 7.0 collective-permute-start.7
  1130.9 24.4 %collective-permute-start.6 = (bf16[256,1024]{0,1:T(8,128)(2,1)S(1)}, bf16[256,1024]{0,1:T(8,128)(2,1)S(1)}, u32[]{:S(2)}, u32[]{:S(2)}) collective-permute-start(bf16[256,1024]{0,1:T(8,128)(2,1)S(1)} %get-tuple-element.214), channel_id=1, source_target_pairs={{8,0},{12,4},{16,8},{20,12},{24,16},{28,20},{9,1},{13,5},{17,9},{2... | collective-permute-start | bytes 1572872 | tf_op jit(solution)/shard_map/ppermute | solution.py:25
  1132.2 25.0 %collective-permute-start.5 = (bf16[256,1024]{0,1:T(8,128)(2,1)S(1)}, bf16[256,1024]{0,1:T(8,128)(2,1)S(1)}, u32[]{:S(2)}, u32[]{:S(2)}) collective-permute-start(bf16[256,1024]{0,1:T(8,128)(2,1)S(1)} %get-tuple-element.215), channel_id=1, source_target_pairs={{12,0},{16,4},{20,8},{24,12},{28,16},{13,1},{17,5},{21,9},{25,13},... | collective-permute-start | bytes 1572872 | tf_op jit(solution)/shard_map/ppermute | solution.py:25
  1133.5 23.7 %collective-permute-start.4 = (bf16[256,1024]{0,1:T(8,128)(2,1)S(1)}, bf16[256,1024]{0,1:T(8,128)(2,1)S(1)}, u32[]{:S(2)}, u32[]{:S(2)}) collective-permute-start(bf16[256,1024]{0,1:T(8,128)(2,1)S(1)} %get-tuple-element.212), channel_id=1, source_target_pairs={{16,0},{20,4},{24,8},{28,12},{17,1},{21,5},{25,9},{29,13},{18,2},{... | collective-permute-start | bytes 1572872 | tf_op jit(solution)/shard_map/ppermute | solution.py:25
  1183.0 21.7 %copy-start.58 = (bf16[256,64]{0,1:T(8,128)(2,1)S(1)}, bf16[256,64]{0,1:T(8,128)(2,1)}, u32[]{:S(2)}) copy-start(bf16[256,64]{0,1:T(8,128)(2,1)} %copy-done.57) | copy-start | bytes 98308
  1183.1 237.8 %all-reduce.17.cloned.1.call-start = ((), (), s32[]{:S(2)}) async-start(), calls=%async_computation.6 | async-start | bytes 17301504 | tf_op jit(solution)/shard_map/psum | solution.py:385
  1183.1 21.6 %copy-start.9 = (bf16[256,2048]{1,0:T(8,128)(2,1)S(1)}, bf16[256,2048]{1,0:T(8,128)(2,1)}, u32[]{:S(2)}) copy-start(bf16[256,2048]{1,0:T(8,128)(2,1)} %copy-done.8) | copy-start | bytes 3145732
  1183.1 22.6 %copy-start.5 = (f32[256,2048]{1,0:T(8,128)S(1)}, f32[256,2048]{1,0:T(8,128)}, u32[]{:S(2)}) copy-start(f32[256,2048]{1,0:T(8,128)} %copy-done.4) | copy-start | bytes 6291460
  1183.1 22.6 %copy-start.48 = (bf16[4,128,256]{2,1,0:T(8,128)(2,1)S(1)}, bf16[4,128,256]{2,1,0:T(8,128)(2,1)}, u32[]{:S(2)}) copy-start(bf16[4,128,256]{2,1,0:T(8,128)(2,1)} %copy-done.47) | copy-start | bytes 786436
  (75 other events, 250.8 us)
Sparse Core Ops, SparseCore 0:
  121.5 47.6 all-reduce.12
  1061.5 49.6 all-reduce.14
  1183.2 102.1 all-reduce.18
  1290.8 130.0 all-reduce.16
where the time goes:
time: 1450 us; the launch traced here: 1440 us
  waiting for transfers between devices  720 us (50%)
  matrix products  266 us (18%)
  local copies, waits for them, and re-layouts  214 us (15%)
  other arithmetic  123 us (8%)
  blocking collectives  60.1 us (4%)
  starting transfers between devices  41.9 us (3%)
  between operations  15.2 us (1%)
    all_to_all x1, waiting for transfers between devices, on_device(): lax.all_to_all(grad_inputs.reshape(ep_count, local_experts * CAP, D), 'ep...  158 us
    all_to_all x1, waiting for transfers between devices, on_device(): lax.all_to_all(grad_send.reshape(ep_count, local_experts * CAP, grad_send...  150 us
    all_to_all x1, waiting for transfers between devices, on_device(): lax.all_to_all(payload.reshape(ep_count, local_experts * CAP, payload.sha...  120 us
    psum x1, waiting for transfers between devices, on_device(): lax.psum(grad_query.astype(jnp.bfloat16), 'ep').astype(jnp.float32)  99.7 us
    dot_general x8, matrix products, on_device(): jnp.einsum('ecf,edf->ecd', grad_piece, paired_weight, preferred_element_t...  99.2 us
    all_to_all x1, waiting for transfers between devices, on_device(): lax.all_to_all(partial_out.reshape(ep_count, local_experts * CAP, D), 'ep...  73.4 us
    dot_general x8, matrix products, on_device(): jnp.einsum('ecf,efd->ecd', source_piece, down_weight, preferred_element_t...  51 us
    psum x1, waiting for transfers between devices, on_device(): lax.psum(jnp.dot(attended_low, output_weight, preferred_element_type=jnp....  37.6 us
  transfers between devices with their start and end apart: 16, of which 10 were waited for; matrix products, arithmetic and copies ran while one was open for 26% of the time, Pallas kernels for 0%

commit v1 on v0

v1 whole, which is shorter than its diff:
```python
import math
from functools import partial

import jax
import jax.numpy as jnp
from jax import lax
from jax.experimental import pallas as pl
from jax.experimental.pallas import tpu as pltpu
from jax.sharding import PartitionSpec as P

D = 2048
HEADS = 16
HEAD_DIM = 128
EXPERTS = 64
TOP = 8
SEQ_MAX = 4096
WINDOW = 1024
CAP = 64

EPSILON = 1e-05
MASKED = 1e30
VMEM_BYTES = 58 * 1024 * 1024
BF = jnp.bfloat16
F32 = jnp.float32


def from_behind(value, axis, steps):
    count = lax.axis_size(axis)
    initial, last = (max(0, -steps), min(count, count - steps))
    return lax.ppermute(value, axis, [(source, source + steps) for source in range(initial, last)])


def inverse_rms(values_in):
    return lax.rsqrt(jnp.mean(values_in * values_in, axis=-1, keepdims=True) + EPSILON)


def rotary(row_count, first_row, seq_len, half_width):
    places = ((first_row + jnp.arange(row_count, dtype=jnp.int32)) % seq_len).astype(F32)
    freqs = jnp.exp(
        jnp.arange(half_width, dtype=F32) * (-2.0 * math.log(10000.0) / (2 * half_width))
    )
    angles = places[:, None] * freqs[None, :]
    return (jnp.cos(angles), jnp.sin(angles))


def rotate(values_in, cosine_table, sine_table, direction):
    half_width = values_in.shape[-1] // 2
    first_half = values_in[..., :half_width]
    second_half = values_in[..., half_width:]
    cos_part = cosine_table[:, None, :]
    sin_part = sine_table[:, None, :] * direction
    return jnp.concatenate(
        [
            first_half * cos_part - second_half * sin_part,
            second_half * cos_part + first_half * sin_part,
        ],
        axis=-1,
    )


def sum_scatter(value, axis):
    count = lax.axis_size(axis)
    rows, width = value.shape
    pieces = lax.all_to_all(
        value.reshape(count, rows // count, width), axis, split_axis=0, concat_axis=0, tiled=True
    )
    return jnp.sum(pieces.astype(F32), axis=0)


def dot(left, right):
    return jnp.dot(left, right, preferred_element_type=F32)


def dot_last(left, right):
    return lax.dot_general(left, right, (((1,), (1,)), ((), ())), preferred_element_type=F32)


def dot_first(left, right):
    return lax.dot_general(left, right, (((0,), (0,)), ((), ())), preferred_element_type=F32)


def picks_of(slots, cap):
    return slots == lax.broadcasted_iota(jnp.int32, (cap, slots.shape[1]), 0)


def cotangent_kernel(sources, experts, slot_ref, cot_ref, down_ref, rows_ref, back_ref, held):
    step = pl.program_id(0)

    @pl.when(step < sources)
    def _():
        slots = slot_ref[0]
        picks = jnp.concatenate(
            [picks_of(slots[e : e + 1], CAP) for e in range(experts)], axis=0
        ).astype(F32).astype(BF)
        found = dot(picks, cot_ref[...]).astype(BF).reshape(experts, CAP, D)
        held[:, pl.ds(pl.multiple_of(step * CAP, CAP), CAP), :] = found

    @pl.when(step >= sources)
    def _():
        rows = held[step - sources]
        rows_ref[0] = rows
        back_ref[0] = dot_last(rows, down_ref[0])


def cotangent_rows(slots, cot_all, down_weight):
    sources, experts, rows = slots.shape
    inner = down_weight.shape[1]
    span = sources * CAP
    return pl.pallas_call(
        partial(cotangent_kernel, sources, experts),
        grid=(sources + experts,),
        in_specs=[
            pl.BlockSpec((1, experts, rows), lambda i: (jnp.minimum(i, sources - 1), 0, 0)),
            pl.BlockSpec((rows, D), lambda i: (jnp.minimum(i, sources - 1), 0)),
            pl.BlockSpec((1, inner, D), lambda i: (jnp.maximum(i - sources, 0), 0, 0)),
        ],
        out_specs=[
            pl.BlockSpec((1, span, D), lambda i: (jnp.maximum(i - sources, 0), 0, 0)),
            pl.BlockSpec((1, span, inner), lambda i: (jnp.maximum(i - sources, 0), 0, 0)),
        ],
        out_shape=[
            jax.ShapeDtypeStruct((experts, span, D), BF),
            jax.ShapeDtypeStruct((experts, span, inner), F32),
        ],
        scratch_shapes=[pltpu.VMEM((experts, span, D), BF)],
        compiler_params=pltpu.CompilerParams(vmem_limit_bytes=VMEM_BYTES),
        cost_estimate=pl.CostEstimate(
            flops=2 * experts * span * D * (rows + inner),
            bytes_accessed=2 * experts * span * D + 10 * sources * rows * D,
            transcendentals=0,
        ),
        name="cotangent_rows",
    )(slots, cot_all, down_weight)


def expert_kernel(
    sources,
    experts,
    slot_ref,
    route_ref,
    x_ref,
    router_ref,
    gate_ref,
    up_ref,
    back_ref,
    rows_ref,
    mid_ref,
    pair_ref,
    scale_ref,
    inner_ref,
    sum_ref,
    held,
    picked,
    scales,
):
    step = pl.program_id(0)
    inner = gate_ref.shape[2]

    @pl.when(step < sources)
    def _():
        x = x_ref[...]
        logits = dot_last(router_ref[...], x)
        routes = route_ref[0]
        names = lax.broadcasted_iota(jnp.int32, logits.shape, 0)
        chosen = routes[0:1] == names
        for k in range(1, TOP):
            chosen = chosen | (routes[k : k + 1] == names)
        masked = jnp.where(chosen, logits, -MASKED)
        top = jnp.max(masked, axis=0, keepdims=True)
        weights = jnp.where(chosen, jnp.exp(masked - top), 0.0)
        gates = weights / jnp.sum(weights, axis=0, keepdims=True)
        slots = slot_ref[0]
        parts = []
        at = pl.ds(pl.multiple_of(step * CAP, CAP), CAP)
        for e in range(experts):
            pick = picks_of(slots[e : e + 1], CAP).astype(F32)
            scales[e, at, :] = jnp.sum(pick * gates[e : e + 1], axis=1, keepdims=True)
            parts.append(pick)
        picks = jnp.concatenate(parts, axis=0).astype(BF)
        picked[step] = picks
        held[:, at, :] = dot(picks, x).astype(BF).reshape(experts, CAP, D)

    @pl.when((step >= sources) & (step < sources + experts))
    def _():
        e = step - sources
        rows = held[e]
        rows_ref[0] = rows
        gate_val = dot(rows, gate_ref[0])
        up_val = dot(rows, up_ref[0])
        sig = jax.nn.sigmoid(gate_val)
        act = gate_val * sig
        mid = (act * up_val).astype(BF)
        mid_ref[0] = mid
        back = back_ref[0]
        inner_ref[0] = jnp.sum(back * mid.astype(F32), axis=1, keepdims=True)
        scale = scales[e]
        scale_ref[0] = scale
        hidden_grad = back * scale
        gate_back = (hidden_grad * up_val * sig * (1.0 + gate_val * (1.0 - sig))).astype(BF)
        up_back = (hidden_grad * act).astype(BF)
        pair_ref[0, :, :inner] = gate_back
        pair_ref[0, :, inner:] = up_back
        held[e] = (dot_last(gate_back, gate_ref[0]) + dot_last(up_back, up_ref[0])).astype(BF)

    @pl.when(step >= sources + experts)
    def _():
        s = step - sources - experts
        found = held[:, pl.ds(pl.multiple_of(s * CAP, CAP), CAP), :].reshape(experts * CAP, D)
        sum_ref[...] = dot_first(picked[s], found).astype(BF)


def expert_pass(slots, routes, x_all, router_rows, gate_weight, up_weight, back):
    sources, experts, rows = slots.shape
    inner = gate_weight.shape[2]
    span = sources * CAP

    def by_source(i):
        return jnp.minimum(i, sources - 1)

    def by_expert(i):
        return jnp.clip(i - sources, 0, experts - 1)

    def by_target(i):
        return jnp.maximum(i - sources - experts, 0)

    per_expert = lambda *shape: pl.BlockSpec((1,) + shape, lambda i: (by_expert(i), 0, 0))
    return pl.pallas_call(
        partial(expert_kernel, sources, experts),
        grid=(2 * sources + experts,),
        in_specs=[
            pl.BlockSpec((1, experts, rows), lambda i: (by_source(i), 0, 0)),
            pl.BlockSpec((1, TOP, rows), lambda i: (by_source(i), 0, 0)),
            pl.BlockSpec((rows, D), lambda i: (by_source(i), 0)),
            pl.BlockSpec((EXPERTS, D), lambda i: (0, 0)),
            per_expert(D, inner),
            per_expert(D, inner),
            per_expert(span, inner),
        ],
        out_specs=[
            per_expert(span, D),
            per_expert(span, inner),
            per_expert(span, 2 * inner),
            per_expert(span, 1),
            per_expert(span, 1),
            pl.BlockSpec((rows, D), lambda i: (by_target(i), 0)),
        ],
        out_shape=[
            jax.ShapeDtypeStruct((experts, span, D), BF),
            jax.ShapeDtypeStruct((experts, span, inner), BF),
            jax.ShapeDtypeStruct((experts, span, 2 * inner), BF),
            jax.ShapeDtypeStruct((experts, span, 1), F32),
            jax.ShapeDtypeStruct((experts, span, 1), F32),
            jax.ShapeDtypeStruct((sources * rows, D), BF),
        ],
        scratch_shapes=[
            pltpu.VMEM((experts, span, D), BF),
            pltpu.VMEM((sources, experts * CAP, rows), BF),
            pltpu.VMEM((experts, span, 1), F32),
        ],
        compiler_params=pltpu.CompilerParams(vmem_limit_bytes=VMEM_BYTES),
        cost_estimate=pl.CostEstimate(
            flops=2 * experts * span * D * (2 * rows + 4 * inner),
            bytes_accessed=2 * experts * span * D + 8 * sources * rows * D,
            transcendentals=0,
        ),
        name="expert_pass",
    )(slots, routes, x_all, router_rows, gate_weight, up_weight, back)


def output_kernel(sources, experts, slot_ref, mid_ref, scale_ref, down_ref, sum_ref, held):
    step = pl.program_id(0)

    @pl.when(step < experts)
    def _():
        held[step] = (dot(mid_ref[0], down_ref[0]) * scale_ref[0]).astype(BF)

    @pl.when(step >= experts)
    def _():
        s = step - experts
        slots = slot_ref[0]
        picks = jnp.concatenate(
            [picks_of(slots[e : e + 1], CAP) for e in range(experts)], axis=0
        ).astype(F32).astype(BF)
        found = held[:, pl.ds(pl.multiple_of(s * CAP, CAP), CAP), :].reshape(experts * CAP, D)
        sum_ref[...] = dot_first(picks, found).astype(BF)


def output_pass(slots, mid, scale, down_weight):
    sources, experts, rows = slots.shape
    inner = down_weight.shape[1]
    span = sources * CAP

    def by_expert(i):
        return jnp.minimum(i, experts - 1)

    def by_target(i):
        return jnp.maximum(i - experts, 0)

    return pl.pallas_call(
        partial(output_kernel, sources, experts),
        grid=(sources + experts,),
        in_specs=[
            pl.BlockSpec((1, experts, rows), lambda i: (by_target(i), 0, 0)),
            pl.BlockSpec((1, span, inner), lambda i: (by_expert(i), 0, 0)),
            pl.BlockSpec((1, span, 1), lambda i: (by_expert(i), 0, 0)),
            pl.BlockSpec((1, inner, D), lambda i: (by_expert(i), 0, 0)),
        ],
        out_specs=pl.BlockSpec((rows, D), lambda i: (by_target(i), 0)),
        out_shape=jax.ShapeDtypeStruct((sources * rows, D), BF),
        scratch_shapes=[pltpu.VMEM((experts, span, D), BF)],
        compiler_params=pltpu.CompilerParams(vmem_limit_bytes=VMEM_BYTES),
        cost_estimate=pl.CostEstimate(
            flops=2 * experts * span * D * (rows + inner),
            bytes_accessed=8 * sources * rows * D,
            transcendentals=0,
        ),
        name="output_pass",
    )(slots, mid, scale, down_weight)


def on_device(
    tokens,
    segments,
    routes,
    cotangent,
    norm1_gain,
    query_weight,
    key_weight,
    value_weight,
    query_gain,
    key_gain,
    output_weight,
    norm2_gain,
    router_weight,
    gate_weight,
    up_weight,
    down_weight,
):
    local_rows = tokens.shape[0]
    ep_count = lax.axis_size("ep")
    tp_count = lax.axis_size("tp")
    ep_at = lax.axis_index("ep")
    tp_at = lax.axis_index("tp")
    all_rows = local_rows * ep_count
    own_rows = local_rows // tp_count
    first_row = ep_at * local_rows
    seq_len = min(SEQ_MAX, all_rows)
    all_width = HEADS * HEAD_DIM
    head_width = query_weight.shape[1]
    local_heads = head_width // HEAD_DIM
    local_experts = gate_weight.shape[0]
    inner_width = gate_weight.shape[2]
    reach_rows = min(WINDOW, local_rows)
    hop_count = max(1, WINDOW // local_rows)
    score_scale = HEAD_DIM ** (-0.5)

    def own(value):
        return lax.dynamic_slice_in_dim(value, tp_at * own_rows, own_rows, 0)

    routes_all = lax.all_gather(routes, "ep", tiled=True)
    cot_all = lax.all_gather(cotangent, "ep", tiled=True)

    first_expert = ep_at * local_experts
    routes_rel = jnp.swapaxes(
        ((routes_all - first_expert) % EXPERTS).reshape(ep_count, local_rows, TOP), 1, 2
    )
    named = jnp.any(
        routes_rel[:, None, :, :]
        == jnp.arange(local_experts, dtype=jnp.int32)[None, :, None, None],
        axis=2,
    )
    ahead = jnp.arange(local_rows)[:, None] < jnp.arange(local_rows)[None, :]
    ranks = lax.dot_general(
        named.astype(BF), ahead.astype(BF), (((2,), (0,)), ((), ())), preferred_element_type=F32
    ).astype(jnp.int32)
    slots = jnp.where(named, ranks, -1)
    router_rows = jnp.roll(router_weight.T, -first_expert, axis=0)

    inputs = tokens.astype(F32)
    scale_one = inverse_rms(inputs)
    hidden_one = (inputs * scale_one * norm1_gain).astype(BF)
    key_raw = dot(hidden_one, key_weight)
    value_raw = dot(hidden_one, value_weight)
    query_raw = dot(hidden_one, query_weight)
    cosine_table, sine_table = rotary(local_rows, first_row, seq_len, HEAD_DIM // 2)

    def turned(values, direction):
        return rotate(
            values.reshape(local_rows, local_heads, HEAD_DIM), cosine_table, sine_table, direction
        ).reshape(local_rows, head_width)

    key_plain = turned(key_raw * key_gain, 1.0).astype(BF)
    pair_low = jnp.concatenate([key_plain, value_raw.astype(BF)], axis=1)
    earlier = []
    for stride in range(hop_count, 0, -1):
        earlier.append(from_behind(pair_low, "ep", stride))
    placed = lax.dynamic_update_slice(
        jnp.zeros((2, all_rows), F32),
        jnp.stack([jnp.sum(query_raw * query_raw, axis=1), jnp.sum(key_raw * key_raw, axis=1)]),
        (0, first_row),
    )
    square_sums = lax.psum(placed, ("ep", "tp"))
    scales_all = lax.rsqrt(square_sums / all_width + EPSILON)
    query_scale = lax.dynamic_slice_in_dim(scales_all[0], first_row, local_rows)[:, None]
    key_scale = lax.dynamic_slice_in_dim(scales_all[1], first_row, local_rows)[:, None]
    key_scale_pad = jnp.concatenate([jnp.ones((WINDOW,), F32), scales_all[1]])
    window_scale = lax.dynamic_slice_in_dim(key_scale_pad, first_row, WINDOW + local_rows)
    query_low = turned(query_raw * query_scale * query_gain, 1.0).astype(BF)
    pair_window = jnp.concatenate(earlier + [pair_low], axis=0)
    window_rows = local_rows + WINDOW
    key_window = (pair_window[:, :head_width].astype(F32) * window_scale[:, None]).astype(BF)
    key_heads = key_window.reshape(window_rows, local_heads, HEAD_DIM)
    value_heads = pair_window[:, head_width:].reshape(window_rows, local_heads, HEAD_DIM)
    query_heads = query_low.reshape(local_rows, local_heads, HEAD_DIM)

    segment_pad = jnp.concatenate([jnp.full((WINDOW,), -1, jnp.int32), segments], axis=0)
    query_at = first_row + jnp.arange(local_rows, dtype=jnp.int32)
    key_at = first_row - WINDOW + jnp.arange(window_rows, dtype=jnp.int32)
    distance = query_at[:, None] - key_at[None, :]
    same_doc = (
        lax.dynamic_slice_in_dim(segments, first_row, local_rows, 0)[:, None]
        == lax.dynamic_slice_in_dim(segment_pad, first_row, window_rows, 0)[None, :]
    )
    allowed = (
        (distance >= 0)
        & (distance < WINDOW)
        & same_doc
        & (query_at[:, None] // seq_len == key_at[None, :] // seq_len)
    )

    def masked_scores():
        scores = (
            jnp.einsum("qhd,khd->hqk", query_heads, key_heads, preferred_element_type=F32)
            * score_scale
        )
        return jnp.where(allowed[None], scores, -MASKED)

    scores = masked_scores()
    highest = jnp.max(scores, axis=-1, keepdims=True)
    exponents = jnp.exp(scores - highest)
    totals = jnp.sum(exponents, axis=-1, keepdims=True)
    probs = (exponents / totals).astype(BF)
    log_totals = highest + jnp.log(totals)
    attended_low = (
        jnp.einsum("hqk,khd->qhd", probs, value_heads, preferred_element_type=F32)
        .reshape(local_rows, head_width)
        .astype(BF)
    )
    branch_part = dot(attended_low, output_weight).astype(BF)

    branch = sum_scatter(branch_part, "tp")
    middle = own(inputs) + branch
    scale_two = inverse_rms(middle)
    normal_two = middle * scale_two
    hidden_two = (normal_two * norm2_gain).astype(BF)
    hidden_all = lax.all_gather(hidden_two, ("ep", "tp"), tiled=True)
    routes_own = own(routes)
    logits = dot(hidden_two, router_weight)
    chosen = jnp.any(
        routes_own[:, :, None] == jnp.arange(EXPERTS, dtype=jnp.int32)[None, None, :], axis=1
    )
    gates = jax.nn.softmax(jnp.where(chosen, logits, -MASKED), axis=1)
    gates = jnp.where(chosen, gates, 0.0)

    cot_rows, back = cotangent_rows(slots, cot_all, down_weight)
    x_rows, mid, pair_back, scale, inner, grad_part = expert_pass(
        slots, routes_rel, hidden_all, router_rows, gate_weight, up_weight, back
    )
    expert_grad = sum_scatter(lax.psum_scatter(grad_part, "ep", tiled=True), "tp")

    inner_slots = jnp.swapaxes(inner.reshape(local_experts, ep_count, CAP), 0, 1)
    inner_dense = jnp.sum(
        jnp.where(
            slots[:, :, :, None] == jnp.arange(CAP, dtype=jnp.int32), inner_slots[:, :, None, :], 0.0
        ),
        axis=3,
    )
    inner_send = jnp.swapaxes(inner_dense, 1, 2).reshape(
        ep_count * tp_count, own_rows, local_experts
    )
    inner_got = lax.all_to_all(
        inner_send, ("ep", "tp"), split_axis=0, concat_axis=0, tiled=True
    ).reshape(ep_count, tp_count, own_rows, local_experts)
    gate_grad = jnp.swapaxes(jnp.sum(inner_got, axis=1), 0, 1).reshape(own_rows, EXPERTS)
    logit_grad = (
        gates * (gate_grad - jnp.sum(gates * gate_grad, axis=1, keepdims=True))
    ).astype(BF)
    grad_router_part = dot_first(hidden_two, logit_grad)
    router_term = dot_last(logit_grad, router_weight)

    mix_part = output_pass(slots, mid, scale, down_weight)
    moe_out = sum_scatter(lax.psum_scatter(mix_part, "ep", tiled=True), "tp")
    mixed_out = lax.all_gather((middle + moe_out).astype(BF), "tp", tiled=True)

    out_grad = (cot_rows.astype(F32) * scale).astype(BF)
    grad_down = jnp.einsum("ecf,ecd->efd", mid, out_grad, preferred_element_type=F32)
    grad_gate = jnp.einsum(
        "ecd,ecf->edf", x_rows, pair_back[:, :, :inner_width], preferred_element_type=F32
    )
    grad_up = jnp.einsum(
        "ecd,ecf->edf", x_rows, pair_back[:, :, inner_width:], preferred_element_type=F32
    )

    upstream = own(cotangent).astype(F32)
    grad_two = expert_grad + router_term
    grad_norm2 = jnp.sum(grad_two * normal_two, axis=0)
    scaled_two = grad_two * norm2_gain
    grad_middle = upstream + scale_two * (
        scaled_two - normal_two * jnp.mean(scaled_two * normal_two, axis=1, keepdims=True)
    )
    middle_low = lax.all_gather(grad_middle.astype(BF), "tp", tiled=True)
    grad_attended = dot_last(middle_low, output_weight).astype(BF)
    grad_output = dot_first(attended_low, middle_low)

    out_heads = grad_attended.reshape(local_rows, local_heads, HEAD_DIM)
    weights = jnp.exp(masked_scores() - log_totals)
    weight_grad = jnp.einsum(
        "qhd,khd->hqk", out_heads, value_heads, preferred_element_type=F32
    )
    inner_sum = jnp.sum(weights * weight_grad, axis=-1, keepdims=True)
    score_grad = (weights * (weight_grad - inner_sum)).astype(BF)
    query_turned = (
        jnp.einsum("hqk,khd->qhd", score_grad, key_heads, preferred_element_type=F32) * score_scale
    ).reshape(local_rows, head_width)
    key_turned = (
        jnp.einsum("hqk,qhd->khd", score_grad, query_heads, preferred_element_type=F32)
        * score_scale
    ).reshape(window_rows, head_width)
    value_turned = jnp.einsum(
        "hqk,qhd->khd", weights.astype(BF), out_heads, preferred_element_type=F32
    ).reshape(window_rows, head_width)
    buffer_grad = jnp.concatenate([key_turned, value_turned], axis=1)
    own_grad = buffer_grad[WINDOW:]
    from_later = jnp.zeros((reach_rows, 2 * head_width), F32)
    for stride in range(hop_count, 0, -1):
        lower_row = (hop_count - stride) * reach_rows
        from_later = from_later + from_behind(
            buffer_grad[lower_row : lower_row + reach_rows].astype(BF), "ep", -stride
        ).astype(F32)
    own_grad = own_grad.at[local_rows - reach_rows :].add(from_later)
    query_back = turned(query_turned, -1.0)
    key_back = turned(own_grad[:, :head_width], -1.0)
    query_dot, key_dot = lax.psum(
        (
            jnp.sum(query_back * query_gain * query_raw, axis=1),
            jnp.sum(key_back * key_gain * key_raw, axis=1),
        ),
        "tp",
    )
    query_cube = query_scale * query_scale * query_scale
    key_cube = key_scale * key_scale * key_scale
    query_grad_low = (
        query_scale * query_gain * query_back
        - query_raw * query_cube * (query_dot[:, None] / all_width)
    ).astype(BF)
    key_grad_low = (
        key_scale * key_gain * key_back - key_raw * key_cube * (key_dot[:, None] / all_width)
    ).astype(BF)
    value_grad_low = own_grad[:, head_width:].astype(BF)
    grad_qgain = jnp.sum(query_back * query_raw * query_scale, axis=0)
    grad_kgain = jnp.sum(key_back * key_raw * key_scale, axis=0)

    one_part = (
        dot_last(query_grad_low, query_weight)
        + dot_last(key_grad_low, key_weight)
        + dot_last(value_grad_low, value_weight)
    ).astype(BF)
    grad_one = sum_scatter(one_part, "tp")
    normal_one = own(inputs * scale_one)
    grad_norm1 = jnp.sum(grad_one * normal_one, axis=0)
    scaled_one = grad_one * norm1_gain
    grad_input_own = grad_middle + own(scale_one) * (
        scaled_one - normal_one * jnp.mean(scaled_one * normal_one, axis=1, keepdims=True)
    )
    grad_input = lax.all_gather(grad_input_own.astype(BF), "tp", tiled=True).astype(F32)

    hidden_one_all = lax.all_gather(hidden_one, "ep", tiled=True)
    grads_all = lax.all_gather(
        jnp.concatenate([query_grad_low, key_grad_low, value_grad_low], axis=1), "ep", tiled=True
    )
    grad_query = dot_first(hidden_one_all, grads_all[:, :head_width])
    grad_key = dot_first(hidden_one_all, grads_all[:, head_width : 2 * head_width])
    grad_value = dot_first(hidden_one_all, grads_all[:, 2 * head_width :])
    grad_output = lax.psum(grad_output.astype(BF), "ep").astype(F32)
    grad_router = lax.psum(grad_router_part.astype(BF), ("ep", "tp")).astype(F32)
    grad_norm1, grad_norm2 = lax.psum((grad_norm1, grad_norm2), ("ep", "tp"))
    grad_qgain, grad_kgain = lax.psum((grad_qgain, grad_kgain), "ep")
    return (
        mixed_out,
        grad_input,
        grad_norm1,
        grad_query,
        grad_key,
        grad_value,
        grad_qgain,
        grad_kgain,
        grad_output,
        grad_norm2,
        grad_router,
        grad_gate,
        grad_up,
        grad_down,
    )


def solution(mesh):
    return jax.shard_map(
        on_device,
        mesh=mesh,
        in_specs=(
            P("ep", None),
            P(),
            P("ep", None),
            P("ep", None),
            P(),
            P(None, "tp"),
            P(None, "tp"),
            P(None, "tp"),
            P("tp"),
            P("tp"),
            P("tp", None),
            P(),
            P(),
            P("ep", None, "tp"),
            P("ep", None, "tp"),
            P("ep", "tp", None),
        ),
        out_specs=(
            P("ep", None),
            P("ep", None),
            P(),
            P(None, "tp"),
            P(None, "tp"),
            P(None, "tp"),
            P("tp"),
            P("tp"),
            P("tp", None),
            P(),
            P(),
            P("ep", None, "tp"),
            P("ep", None, "tp"),
            P("ep", "tp", None),
        ),
        check_vma=False,
    )
```

time: 1450 us -> 978 us (0.67)
  waiting for transfers between devices: 720 us -> 506 us
  local copies, waits for them, and re-layouts: 214 us -> 35.7 us
  matrix products: 266 us -> 101 us
  Pallas kernels: 0 us -> 81.2 us
  blocking collectives: 60.1 us -> 130 us
  other arithmetic: 123 us -> 59.4 us
    all_to_all x4, waiting for transfers between devices: 502 us -> 66.8 us  [sum_scatter(): lax.all_to_all(value.reshape(count, rows // count, width), axis, split_ax...]
    all_gather x0 -> x7, waiting for transfers between devices: none -> 167 us  [the longest x1 53.4 us: on_device(): hidden_one_all = lax.all_gather(hidden_one, 'ep', tiled=True)]
    dot_general x41 -> x25, matrix products: 266 us -> 101 us  [the longest x5 26.3 us: dot_first(): lax.dot_general(left, right, (((0,), (0,)), ((), ())), preferred_element_...]
    reduce_scatter x0 -> x2, waiting for transfers between devices: none -> 135 us  [the longest x1 79.2 us: on_device(): moe_out = sum_scatter(lax.psum_scatter(mix_part, 'ep', tiled=True), 'tp')]
    gather x5 -> x0, local copies, waits for them, and re-layouts: 113 us -> none  [the longest x1 24.2 us: on_device(): returned.reshape(EXPERTS * CAP, D)[slot_index].reshape(local_rows, TOP, D)]
    psum x4 -> x2, waiting for transfers between devices: 197 us -> 111 us  [the longest x1 60.9 us: on_device(): lax.psum(grad_router_part.astype(BF), ('ep', 'tp')).astype(F32)]
    pallas_call x0 -> x3, Pallas kernels: none -> 81.2 us  [the longest x1 42.3 us: expert_pass(): pl.pallas_call(partial(expert_kernel, sources, experts), grid=(2 * source...]
    psum x3, blocking collectives: 50.2 us -> 95.8 us  [the longest x1 42.5 us: on_device(): square_sums = lax.psum(placed, ('ep', 'tp'))]
  transfers between devices with their start and end apart: 16 -> 23, of which waited for: 10 -> 13; matrix products, arithmetic and copies ran while one was open for 26% -> 16% of each run, Pallas kernels for 0% -> 4%
where the time goes in v1:
time: 978 us; the launch traced here: 967 us
  waiting for transfers between devices  506 us (52%)
  blocking collectives  130 us (13%)
  matrix products  101 us (10%)
  Pallas kernels  81.2 us (8%)
  other arithmetic  59.4 us (6%)
  starting transfers between devices  38.5 us (4%)
  local copies, waits for them, and re-layouts  35.7 us (4%)
  between operations  15.6 us (2%)
    reduce_scatter x1, waiting for transfers between devices, on_device(): moe_out = sum_scatter(lax.psum_scatter(mix_part, 'ep', tiled=True), 'tp')  79.2 us
    all_to_all x4, waiting for transfers between devices, sum_scatter(): lax.all_to_all(value.reshape(count, rows // count, width), axis, split_ax...  66.8 us
    psum x1, waiting for transfers between devices, on_device(): lax.psum(grad_router_part.astype(BF), ('ep', 'tp')).astype(F32)  60.9 us
    reduce_scatter x1, waiting for transfers between devices, on_device(): lax.psum_scatter(grad_part, 'ep', tiled=True)  55.4 us
    all_gather x1, waiting for transfers between devices, on_device(): hidden_one_all = lax.all_gather(hidden_one, 'ep', tiled=True)  53.4 us
    psum x1, waiting for transfers between devices, on_device(): grad_output = lax.psum(grad_output.astype(BF), 'ep').astype(F32)  49.8 us
    all_gather x1, waiting for transfers between devices, on_device(): lax.all_gather(jnp.concatenate([query_grad_low, key_grad_low, value_grad_...  48 us
    all_gather x1, waiting for transfers between devices, on_device(): hidden_all = lax.all_gather(hidden_two, ('ep', 'tp'), tiled=True)  43.7 us
  transfers between devices with their start and end apart: 23, of which 13 were waited for; matrix products, arithmetic and copies ran while one was open for 16% of the time, Pallas kernels for 4%

profile of v1, /device:TPU:0, one launch (start us, length us, event | category | flops | bytes accessed | tf_op | source)
XLA Modules:
  0.0 966.8 jit_solution(1909551429359531575)
XLA Ops:
  17.4 42.5 %psum.63 = f32[2,2048]{1,0:T(2,128)S(1)} all-reduce(f32[2,2048]{1,0:T(2,128)S(1)} %constant_dynamic-update-slice_fusion.5), channel_id=1, replica_groups=mesh['ep'=8,'tp'=4] {'ep','tp'}, use_global_device_ids=true, to_apply=%region_3.4 | all-reduce | flops 4096 | bytes 32768 | tf_op jit(solution)/shard_map/psum | solution.py:402
  76.1 5.2 collective-permute-start.2
  89.2 24.8 %collective-permute-done = bf16[256,1024]{1,0:T(8,128)(2,1)} collective-permute-done((bf16[256,1024]{1,0:T(8,128)(2,1)}, bf16[256,1024]{1,0:T(8,128)(2,1)}, u32[]{:S(2)}, u32[]{:S(2)}) %collective-permute-start) | collective-permute-done | bytes 524320 | tf_op jit(solution)/shard_map/ppermute | solution.py:30
  137.8 23.6 %all-to-all-done = bf16[4,64,2048]{2,1,0:T(8,128)(2,1)} async-done(((bf16[4,64,2048]{2,1,0:T(8,128)(2,1)}), bf16[4,64,2048]{2,1,0:T(8,128)(2,1)}, u32[]{:S(2)}, u32[]{:S(2)}) %all-to-all-start) | async-done | bytes 1048608 | tf_op jit(solution)/shard_map/all_to_all | solution.py:64
  165.1 10.9 %all_gather.24 = s32[2048,8]{0,1:T(8,128)S(1)} all-gather(s32[256,8]{0,1:T(8,128)S(1)} %copy-done.65), channel_id=1, replica_groups=mesh['ep'=8,'tp'=4] {'ep'}, dimensions={0}, use_global_device_ids=true | all-gather | bytes 73728 | tf_op jit(solution)/shard_map/all_gather | solution.py:360
  177.9 21.6 %cotangent_rows.1 = (bf16[8,512,2048]{2,1,0:T(8,128)(2,1)}, f32[8,512,256]{2,1,0:T(8,128)}) custom-call(s32[8,8,256]{2,1,0:T(8,128)} %fusion.32.slot_ref, bf16[2048,2048]{1,0:T(8,128)(2,1)} %all-gather.10.cloned.1.call-done.cot_ref, bf16[8,256,2048]{2,1,0:T(8,128)(2,1)} %down_ref.3), custom_call_target="tpu_custom_call" | custom-call | flops 8589934592 | bytes 58720256 | tf_op jit(solution)/shard_map/cotangent_rows/pallas_call | solution.py:109
  199.5 43.7 %all-gather.8.cloned.1.call-done.x_ref = bf16[2048,2048]{1,0:T(8,128)(2,1)} async-done(((bf16[64,2048]{1,0:T(8,128)(2,1)}), bf16[2048,2048]{1,0:T(8,128)(2,1)}) %all-gather.8.cloned.1.call-update) | async-done | bytes 8388624 | tf_op jit(solution)/shard_map/all_gather | solution.py:456
  243.1 42.3 %expert_pass.1 = (bf16[8,512,2048]{2,1,0:T(8,128)(2,1)}, bf16[8,512,256]{2,1,0:T(8,128)(2,1)}, bf16[8,512,512]{2,1,0:T(8,128)(2,1)}, f32[8,512,1]{2,1,0:T(8,128)...) custom-call(s32[8,8,256]{2,1,0:T(8,128)} %fusion.32.slot_ref, s32[8,8,256]{2,1,0:T(8,128)} %bitcast.164, ...), custom_call_target="tpu_custom_call" | custom-call | flops 25769803776 | bytes 50331648 | tf_op jit(solution)/shard_map/expert_pass/pallas_call | solution.py:227
  289.5 10.5 %all_to_all.25 = f32[32,1,512]{2,1,0:T(1,128)S(1)} all-to-all(f32[32,1,512]{2,1,0:T(1,128)S(1)} %reshape.492), channel_id=1, replica_groups=mesh['ep'=8,'tp'=4] {'ep','tp'}, dimensions={0} | all-to-all | bytes 131072 | tf_op jit(solution)/shard_map/all_to_all | solution.py:481
  300.0 55.4 %reduce-scatter.5.cloned.1.call-done = bf16[256,2048]{1,0:T(8,128)(2,1)} async-done(((bf16[2048,2048]{1,0:T(8,128)(2,1)}), bf16[256,2048]{1,0:T(8,128)(2,1)}) %reduce-scatter.5.cloned.1.call-update) | async-done | bytes 1048592 | tf_op jit(solution)/shard_map/reduce_scatter | solution.py:469
  362.3 23.6 %all-to-all-done.2 = bf16[4,64,2048]{2,1,0:T(8,128)(2,1)} async-done(((bf16[4,64,2048]{2,1,0:T(8,128)(2,1)}), bf16[4,64,2048]{2,1,0:T(8,128)(2,1)}, u32[]{:S(2)}, u32[]{:S(2)}) %all-to-all-start.2) | async-done | bytes 1048608 | tf_op jit(solution)/shard_map/all_to_all | solution.py:64
  391.1 17.4 %output_pass.1 = bf16[2048,2048]{1,0:T(8,128)(2,1)} custom-call(s32[8,8,256]{2,1,0:T(8,128)} %fusion.32.slot_ref, bf16[8,512,256]{2,1,0:T(8,128)(2,1)} %get-tuple-element.43.mid_ref, f32[8,512,1]{2,1,0:T(8,128)} %get-tuple-element.44.scale_ref, bf16[8,256,2048]{2,1,0:T(8,128)(2,1)} %down_ref.3), custom_call_target="tpu_custom_call" | custom-call | flops 8589934592 | bytes 33554432 | tf_op jit(solution)/shard_map/output_pass/pallas_call | solution.py:299
  409.8 7.3 all-gather.14.cloned.1.call-done
  419.9 5.1 fusion.5
  428.8 5.7 multiply_reduce_fusion
  451.8 79.2 %reduce-scatter.3.cloned.1.call-done = bf16[256,2048]{1,0:T(8,128)(2,1)} async-done(((bf16[2048,2048]{1,0:T(8,128)(2,1)}), bf16[256,2048]{1,0:T(8,128)(2,1)}) %reduce-scatter.3.cloned.1.call-update) | async-done | bytes 1048592 | tf_op jit(solution)/shard_map/reduce_scatter | solution.py:492
  547.5 12.6 %all-reduce.4 = (f32[256]{0:T(256)S(1)}, f32[256]{0:T(256)S(1)}) all-reduce(f32[256]{0:T(256)S(1)} %get-tuple-element.57, f32[256]{0:T(256)S(1)} %get-tuple-element.55), channel_id=1, replica_groups=mesh['ep'=8,'tp'=4] {'tp'}, use_global_device_ids=true, to_apply=%region_22.23 | all-reduce | flops 512 | bytes 4096 | tf_op jit(solution)/shard_map/psum | solution.py:543
  567.7 6.5 all-to-all-start.4
  579.8 19.5 %all-to-all-done.4 = bf16[4,64,2048]{2,1,0:T(8,128)(2,1)} async-done(((bf16[4,64,2048]{2,1,0:T(8,128)(2,1)}), bf16[4,64,2048]{2,1,0:T(8,128)(2,1)}, u32[]{:S(2)}, u32[]{:S(2)}) %all-to-all-start.4) | async-done | bytes 1048608 | tf_op jit(solution)/shard_map/all_to_all | solution.py:64
  609.0 12.9 %fusion.16 = f32[8,2048,256]{2,1,0:T(8,128)} fusion(bf16[8,512,2048]{2,1,0:T(8,128)(2,1)} %get-tuple-element.47, bf16[8,512,512]{2,1,0:T(8,128)(2,1)} %get-tuple-element.48), kind=kOutput, calls=%fused_computation.35 | convolution fusion | flops 4294967296 | bytes 35651584 | tf_op jit(solution)/shard_map/ecd,ecf->edf/dot_general | solution.py:500
  621.9 13.0 %fusion.18 = f32[8,2048,256]{2,1,0:T(8,128)} fusion(bf16[8,512,2048]{2,1,0:T(8,128)(2,1)} %get-tuple-element.47, bf16[8,512,512]{2,1,0:T(8,128)(2,1)} %get-tuple-element.48), kind=kOutput, calls=%fused_computation.37 | convolution fusion | flops 4294967296 | bytes 35651584 | tf_op jit(solution)/shard_map/ecd,ecf->edf/dot_general | solution.py:497
  634.9 12.1 %fusion = f32[8,256,2048]{2,1,0:T(8,128)} fusion(bf16[8,512,256]{2,1,0:T(8,128)(2,1)S(1)} %copy-done.26, bf16[8,512,2048]{2,1,0:T(8,128)(2,1)} %get-tuple-element.49, f32[8,512]{1,0:T(8,128)S(1)} %reduce.4), kind=kOutput, calls=%fused_computation.1 | convolution fusion | flops 4320133120 | bytes 35667968 | tf_op jit(solution)/shard_map/ecf,ecd->efd/dot_general | solution.py:496
  647.0 60.9 %all-reduce.10.cloned.1.call-done = bf16[2048,64]{0,1:T(8,128)(2,1)} async-done(((bf16[2048,64]{0,1:T(8,128)(2,1)}), bf16[2048,64]{0,1:T(8,128)(2,1)}) %all-reduce.10.cloned.1.call-update) | async-done | bytes 262160 | tf_op jit(solution)/shard_map/psum | solution.py:585
  709.6 12.7 %all-reduce.3 = (f32[512]{0:T(512)}, f32[512]{0:T(512)}) all-reduce(f32[512]{0:T(512)S(1)} %get-tuple-element.56, f32[512]{0:T(512)S(1)} %get-tuple-element.54), channel_id=1, replica_groups=mesh['ep'=8,'tp'=4] {'ep'}, use_global_device_ids=true, to_apply=%region_30.31 | all-reduce | flops 1024 | bytes 8192 | tf_op jit(solution)/shard_map/psum | solution.py:587
  722.3 49.8 %all-reduce.8.cloned.1.call-done = bf16[512,2048]{1,0:T(8,128)(2,1)} async-done(((bf16[512,2048]{1,0:T(8,128)(2,1)}), bf16[512,2048]{1,0:T(8,128)(2,1)}) %all-reduce.8.cloned.1.call-update) | async-done | bytes 2097168 | tf_op jit(solution)/shard_map/psum | solution.py:584
  776.3 40.6 %all-reduce.2 = (f32[2048]{0:T(1024)}, f32[2048]{0:T(1024)}) all-reduce(f32[2048]{0:T(1024)S(1)} %get-tuple-element.50, f32[2048]{0:T(1024)S(1)} %copy-done.54), channel_id=1, replica_groups=mesh['ep'=8,'tp'=4] {'ep','tp'}, use_global_device_ids=true, to_apply=%region_28.29 | all-reduce | flops 4096 | bytes 32768 | tf_op jit(solution)/shard_map/psum | solution.py:586
  816.9 14.4 %all-gather.16.cloned.1.call-done = bf16[256,2048]{1,0:T(8,128)(2,1)} async-done(((bf16[64,2048]{1,0:T(8,128)(2,1)}), bf16[256,2048]{1,0:T(8,128)(2,1)}) %all-gather.16.cloned.1.call-update) | async-done | bytes 1048592 | tf_op jit(solution)/shard_map/all_gather | solution.py:575
  834.1 53.4 %all-gather.18.cloned.1.call-done = bf16[2048,2048]{1,0:T(8,128)(2,1)} async-done(((bf16[256,2048]{1,0:T(8,128)(2,1)}), bf16[2048,2048]{1,0:T(8,128)(2,1)}) %all-gather.18.cloned.1.call-update) | async-done | bytes 8388624 | tf_op jit(solution)/shard_map/all_gather | solution.py:577
  887.5 48.0 %all-gather.20.cloned.1.call-done = bf16[2048,1536]{1,0:T(8,128)(2,1)} async-done(((bf16[256,1536]{1,0:T(8,128)(2,1)}), bf16[2048,1536]{1,0:T(8,128)(2,1)}) %all-gather.20.cloned.1.call-update) | async-done | bytes 6291472 | tf_op jit(solution)/shard_map/all_gather | solution.py:578
  935.6 10.7 %fusion.10 = f32[2048,512]{1,0:T(8,128)} fusion(bf16[2048,2048]{1,0:T(8,128)(2,1)} %all-gather.18.cloned.1.call-done, bf16[2048,1536]{1,0:T(8,128)(2,1)} %all-gather.20.cloned.1.call-done), kind=kOutput, calls=%fused_computation.29 | convolution fusion | flops 4294967296 | bytes 14680064 | tf_op jit(solution)/shard_map/dot_general | solution.py:79
  946.3 6.3 fusion.12
  952.6 6.3 fusion.14
  (326 shorter events, 152.7 us)
Async XLA Ops:
  7.2 170.7 %all-gather.10.cloned.1.call-start = ((), (), s32[]{:S(2)}) async-start(), calls=%async_computation.8 | async-start | bytes 9437184 | tf_op jit(solution)/shard_map/all_gather | solution.py:361
  15.7 44.8 %copy-start.62 = (f32[512]{0:T(512)S(1)}, f32[512]{0:T(512)}, u32[]{:S(2)}) copy-start(f32[512]{0:T(512)} %param.28) | copy-start | bytes 6148
  74.2 43.2 %copy-start.40 = (bf16[256,512]{1,0:T(8,128)(2,1)S(1)}, bf16[256,512]{1,0:T(8,128)(2,1)}, u32[]{:S(2)}) copy-start(bf16[256,512]{1,0:T(8,128)(2,1)} %copy-done.39) | copy-start | bytes 786436
  74.2 43.1 %collective-permute-start.3 = (bf16[256,1024]{1,0:T(8,128)(2,1)}, bf16[256,1024]{1,0:T(8,128)(2,1)S(1)}, u32[]{:S(2)}, u32[]{:S(2)}) collective-permute-start(bf16[256,1024]{1,0:T(8,128)(2,1)} %pad_maximum_fusion.2), channel_id=1, source_target_pairs={{0,4},{4,8},{8,12},{12,16},{16,20},{20,24},{24,28},{1,5},{5,9},{9,... | collective-permute-start | bytes 1572872 | tf_op jit(solution)/shard_map/ppermute | solution.py:30
  76.1 40.1 %collective-permute-start.2 = (bf16[256,1024]{1,0:T(8,128)(2,1)}, bf16[256,1024]{1,0:T(8,128)(2,1)}, u32[]{:S(2)}, u32[]{:S(2)}) collective-permute-start(bf16[256,1024]{1,0:T(8,128)(2,1)} %pad_maximum_fusion.2), channel_id=1, source_target_pairs={{0,8},{4,12},{8,16},{12,20},{16,24},{20,28},{1,9},{5,13},{9,17},{1... | collective-permute-start | bytes 1572872 | tf_op jit(solution)/shard_map/ppermute | solution.py:30
  81.3 33.8 %collective-permute-start.1 = (bf16[256,1024]{1,0:T(8,128)(2,1)}, bf16[256,1024]{1,0:T(8,128)(2,1)}, u32[]{:S(2)}, u32[]{:S(2)}) collective-permute-start(bf16[256,1024]{1,0:T(8,128)(2,1)} %pad_maximum_fusion.2), channel_id=1, source_target_pairs={{0,12},{4,16},{8,20},{12,24},{16,28},{1,13},{5,17},{9,21},{13,25},... | collective-permute-start | bytes 1572872 | tf_op jit(solution)/shard_map/ppermute | solution.py:30
  84.9 29.2 %collective-permute-start = (bf16[256,1024]{1,0:T(8,128)(2,1)}, bf16[256,1024]{1,0:T(8,128)(2,1)}, u32[]{:S(2)}, u32[]{:S(2)}) collective-permute-start(bf16[256,1024]{1,0:T(8,128)(2,1)} %pad_maximum_fusion.2), channel_id=1, source_target_pairs={{0,16},{4,20},{8,24},{12,28},{1,17},{5,21},{9,25},{13,29},{2,18},{... | collective-permute-start | bytes 1572872 | tf_op jit(solution)/shard_map/ppermute | solution.py:30
  131.9 29.5 %all-to-all-start = ((bf16[4,64,2048]{2,1,0:T(8,128)(2,1)}), bf16[4,64,2048]{2,1,0:T(8,128)(2,1)}, u32[]{:S(2)}, u32[]{:S(2)}) async-start(bf16[4,64,2048]{2,1,0:T(8,128)(2,1)} %bitcast.154), calls=%async_computation | async-start | bytes 2097152 | tf_op jit(solution)/shard_map/all_to_all | solution.py:64
  136.2 107.0 %all-gather.8.cloned.1.call-start = ((), (), s32[]{:S(2)}) async-start(), calls=%async_computation.7 | async-start | bytes 8650752 | tf_op jit(solution)/shard_map/all_gather | solution.py:456
  137.8 39.2 %copy-start.27 = (bf16[2048,64]{0,1:T(8,128)(2,1)S(1)}, bf16[2048,64]{0,1:T(8,128)(2,1)}, u32[]{:S(2)}) copy-start(bf16[2048,64]{0,1:T(8,128)(2,1)} %param.32) | copy-start | bytes 786436
  164.1 224.2 %copy-start.5 = (f32[64,2048]{1,0:T(8,128)}, f32[64,2048]{1,0:T(8,128)S(1)}, u32[]{:S(2)}) copy-start(f32[64,2048]{1,0:T(8,128)S(1)} %get-tuple-element.65) | copy-start | bytes 1572868
  165.0 190.4 %reduce-scatter.5.cloned.1.call-start = ((), (), s32[]{:S(2)}) async-start(), calls=%async_computation.11 | async-start | bytes 9437184 | tf_op jit(solution)/shard_map/reduce_scatter | solution.py:469
  285.4 75.1 %copy-start.22 = (bf16[64,2048]{1,0:T(8,128)(2,1)S(1)}, bf16[64,2048]{1,0:T(8,128)(2,1)}, u32[]{:S(2)}) copy-start(bf16[64,2048]{1,0:T(8,128)(2,1)} %multiply_convert_fusion.5) | copy-start | bytes 786436
  289.5 97.8 %copy-start.46 = (f32[2048]{0:T(1024)S(1)}, f32[2048]{0:T(1024)}, u32[]{:S(2)}) copy-start(f32[2048]{0:T(1024)} %param.31) | copy-start | bytes 24580
  289.5 97.8 %copy-start.73 = (f32[64]{0:T(128)S(1)}, f32[64]{0:T(128)}, u32[]{:S(2)}) copy-start(f32[64]{0:T(128)} %copy-done.72) | copy-start | bytes 772
  355.5 30.4 %all-to-all-start.2 = ((bf16[4,64,2048]{2,1,0:T(8,128)(2,1)}), bf16[4,64,2048]{2,1,0:T(8,128)(2,1)}, u32[]{:S(2)}, u32[]{:S(2)}) async-start(bf16[4,64,2048]{2,1,0:T(8,128)(2,1)} %bitcast.159), calls=%async_computation.4 | async-start | bytes 2097152 | tf_op jit(solution)/shard_map/all_to_all | solution.py:64
  360.1 57.0 %all-gather.14.cloned.1.call-start = ((), (), s32[]{:S(2)}) async-start(), calls=%async_computation.12 | async-start | bytes 1310720 | tf_op jit(solution)/shard_map/all_gather | solution.py:511
  390.9 140.1 %reduce-scatter.3.cloned.1.call-start = ((), (), s32[]{:S(2)}) async-start(), calls=%async_computation.9 | async-start | bytes 9437184 | tf_op jit(solution)/shard_map/reduce_scatter | solution.py:492
  444.6 91.0 %copy-start.8 = (bf16[1280,512]{0,1:T(8,128)(2,1)S(1)}, bf16[1280,512]{0,1:T(8,128)(2,1)}, u32[]{:S(2)}) copy-start(bf16[1280,512]{0,1:T(8,128)(2,1)} %copy-done.7) | copy-start | bytes 3932164
  446.0 93.1 %collective-permute-start.4 = (bf16[256,1024]{1,0:T(8,128)(2,1)}, bf16[256,1024]{1,0:T(8,128)(2,1)}, u32[]{:S(2)}, u32[]{:S(2)}) collective-permute-start(bf16[256,1024]{1,0:T(8,128)(2,1)} %get-tuple-element.66), channel_id=1, source_target_pairs={{16,0},{20,4},{24,8},{28,12},{17,1},{21,5},{25,9},{29,13},{18,2},{... | collective-permute-start | bytes 1572872 | tf_op jit(solution)/shard_map/ppermute | solution.py:30
  447.3 91.8 %collective-permute-start.7 = (bf16[256,1024]{1,0:T(8,128)(2,1)}, bf16[256,1024]{1,0:T(8,128)(2,1)}, u32[]{:S(2)}, u32[]{:S(2)}) collective-permute-start(bf16[256,1024]{1,0:T(8,128)(2,1)} %get-tuple-element.67), channel_id=1, source_target_pairs={{4,0},{8,4},{12,8},{16,12},{20,16},{24,20},{28,24},{5,1},{9,5},{13... | collective-permute-start | bytes 1572872 | tf_op jit(solution)/shard_map/ppermute | solution.py:30
  448.6 90.6 %collective-permute-start.6 = (bf16[256,1024]{1,0:T(8,128)(2,1)}, bf16[256,1024]{1,0:T(8,128)(2,1)}, u32[]{:S(2)}, u32[]{:S(2)}) collective-permute-start(bf16[256,1024]{1,0:T(8,128)(2,1)} %get-tuple-element.68), channel_id=1, source_target_pairs={{8,0},{12,4},{16,8},{20,12},{24,16},{28,20},{9,1},{13,5},{17,9},{2... | collective-permute-start | bytes 1572872 | tf_op jit(solution)/shard_map/ppermute | solution.py:30
  449.9 89.3 %collective-permute-start.5 = (bf16[256,1024]{1,0:T(8,128)(2,1)}, bf16[256,1024]{1,0:T(8,128)(2,1)}, u32[]{:S(2)}, u32[]{:S(2)}) collective-permute-start(bf16[256,1024]{1,0:T(8,128)(2,1)} %get-tuple-element.69), channel_id=1, source_target_pairs={{12,0},{16,4},{20,8},{24,12},{28,16},{13,1},{17,5},{21,9},{25,13},... | collective-permute-start | bytes 1572872 | tf_op jit(solution)/shard_map/ppermute | solution.py:30
  531.0 36.8 %all-to-all-start.1 = ((bf16[4,64,2048]{2,1,0:T(8,128)(2,1)}), bf16[4,64,2048]{2,1,0:T(8,128)(2,1)}, u32[]{:S(2)}, u32[]{:S(2)}) async-start(bf16[4,64,2048]{2,1,0:T(8,128)(2,1)} %bitcast.158), calls=%async_computation.2 | async-start | bytes 2097152 | tf_op jit(solution)/shard_map/all_to_all | solution.py:64
  567.7 31.6 %all-to-all-start.4 = ((bf16[4,64,2048]{2,1,0:T(8,128)(2,1)}), bf16[4,64,2048]{2,1,0:T(8,128)(2,1)}, u32[]{:S(2)}, u32[]{:S(2)}) async-start(bf16[4,64,2048]{2,1,0:T(8,128)(2,1)} %bitcast.25), calls=%async_computation.6 | async-start | bytes 2097152 | tf_op jit(solution)/shard_map/all_to_all | solution.py:64
  574.3 133.6 %all-reduce.10.cloned.1.call-start = ((), (), s32[]{:S(2)}) async-start(), calls=%async_computation.17 | async-start | bytes 524288 | tf_op jit(solution)/shard_map/psum | solution.py:585
  575.3 196.9 %all-reduce.8.cloned.1.call-start = ((), (), s32[]{:S(2)}) async-start(), calls=%async_computation.16 | async-start | bytes 4194304 | tf_op jit(solution)/shard_map/psum | solution.py:584
  577.5 239.5 %all-gather.12.cloned.1.call-start = ((), (), s32[]{:S(2)}) async-start(), calls=%async_computation.10 | async-start | bytes 1310720 | tf_op jit(solution)/shard_map/all_gather | solution.py:493
  604.4 226.9 %all-gather.16.cloned.1.call-start = ((), (), s32[]{:S(2)}) async-start(), calls=%async_computation.13 | async-start | bytes 1310720 | tf_op jit(solution)/shard_map/all_gather | solution.py:575
  605.2 282.4 %all-gather.18.cloned.1.call-start = ((), (), s32[]{:S(2)}) async-start(), calls=%async_computation.14 | async-start | bytes 9437184 | tf_op jit(solution)/shard_map/all_gather | solution.py:577
  605.7 329.8 %all-gather.20.cloned.1.call-start = ((), (), s32[]{:S(2)}) async-start(), calls=%async_computation.15 | async-start | bytes 7077888 | tf_op jit(solution)/shard_map/all_gather | solution.py:578
  722.3 54.0 %copy-start.54 = (f32[2048]{0:T(1024)S(1)}, f32[2048]{0:T(1024)}, u32[]{:S(2)}) copy-start(f32[2048]{0:T(1024)} %get-tuple-element.52) | copy-start | bytes 24580
  (76 other events, 612.2 us)
Sparse Core Ops, SparseCore 0:
  9.9 58.4 all-gather.9
  165.2 77.9 all-gather.7
  285.6 69.8 reduce-scatter.4
  391.0 26.0 all-gather.13
  421.4 109.5 reduce-scatter.2
  580.3 127.5 all-reduce.9
  711.7 60.4 all-reduce.7
  773.7 27.8 all-gather.11
  803.8 27.4 all-gather.15
  833.6 53.8 all-gather.17
  890.0 45.5 all-gather.19

commit v2 on v1

v2 whole, which is shorter than its diff:
```python
import math
from functools import partial

import jax
import jax.numpy as jnp
from jax import lax
from jax.experimental import pallas as pl
from jax.experimental.pallas import tpu as pltpu
from jax.sharding import PartitionSpec as P

D = 2048
HEADS = 16
HEAD_DIM = 128
EXPERTS = 64
TOP = 8
SEQ_MAX = 4096
WINDOW = 1024
CAP = 64

EPSILON = 1e-05
MASKED = 1e30
VMEM_BYTES = 58 * 1024 * 1024
BF = jnp.bfloat16
LIGHT = pl.CostEstimate(flops=1, bytes_accessed=1, transcendentals=0)
F32 = jnp.float32


def from_behind(value, axis, steps):
    count = lax.axis_size(axis)
    initial, last = (max(0, -steps), min(count, count - steps))
    return lax.ppermute(value, axis, [(source, source + steps) for source in range(initial, last)])


def inverse_rms(values_in):
    return lax.rsqrt(jnp.mean(values_in * values_in, axis=-1, keepdims=True) + EPSILON)


def rotary(row_count, first_row, seq_len, half_width):
    places = ((first_row + jnp.arange(row_count, dtype=jnp.int32)) % seq_len).astype(F32)
    freqs = jnp.exp(
        jnp.arange(half_width, dtype=F32) * (-2.0 * math.log(10000.0) / (2 * half_width))
    )
    angles = places[:, None] * freqs[None, :]
    return (jnp.cos(angles), jnp.sin(angles))


def rotary_tables(row_count, first_row, seq_len):
    half = HEAD_DIM // 2
    cosine, sine = rotary(row_count, first_row, seq_len, half)
    return jnp.concatenate([cosine, cosine], axis=1), jnp.concatenate([-sine, sine], axis=1)


def sum_scatter(value, axis):
    count = lax.axis_size(axis)
    rows, width = value.shape
    pieces = lax.all_to_all(
        value.reshape(count, rows // count, width), axis, split_axis=0, concat_axis=0, tiled=True
    )
    return jnp.sum(pieces.astype(F32), axis=0)


def swap(value, distance):
    count = lax.axis_size("ep")
    return lax.ppermute(value, "ep", [(i, i ^ distance) for i in range(count)])


def gather_evens(value, relay, between):
    count = lax.axis_size("ep")
    if count != 8 or not relay:
        return [value] + [swap(value, d) for d in range(2, count, 2)]
    half = value.shape[1] // 2
    near, far = swap(value, 2), swap(value, 4)
    if between is not None:
        near, far, _ = lax.optimization_barrier((near, far, between))
    corner = jnp.concatenate([swap(far[:, :half], 2), swap(near[:, half:], 4)], axis=1)
    return [value, near, far, corner]


def gather_pieces(value, relay=True, between=None):
    evens = gather_evens(value, relay, between)
    odds = [swap(piece, 1) for piece in evens]
    return [piece for both in zip(evens, odds) for piece in both]


def spread(value, axis):
    count = lax.axis_size(axis)
    return lax.all_to_all(
        jnp.broadcast_to(value[None], (count,) + value.shape),
        axis,
        split_axis=0,
        concat_axis=0,
        tiled=True,
    ).reshape(count * value.shape[0], value.shape[1])


def tiny_sum(value):
    rows = value.shape[0]
    return jnp.sum(spread(value, "tp").reshape(lax.axis_size("tp"), rows, value.shape[1]), axis=0)


def after(value, *others):
    return lax.optimization_barrier((value,) + others)[0]


def dot(left, right):
    return jnp.dot(left, right, preferred_element_type=F32)


def dot_last(left, right):
    return lax.dot_general(left, right, (((1,), (1,)), ((), ())), preferred_element_type=F32)


def dot_first(left, right):
    return lax.dot_general(left, right, (((0,), (0,)), ((), ())), preferred_element_type=F32)


def picks_of(slots, cap):
    return slots == lax.broadcasted_iota(jnp.int32, (cap, slots.shape[1]), 0)


def cotangent_kernel(
    sources, experts, slot_ref, cot_ref, down_ref, rows_ref, back_ref, held
):
    step = pl.program_id(0)

    @pl.when(step < sources)
    def _():
        slots = slot_ref[0]
        picks = jnp.concatenate(
            [picks_of(slots[e : e + 1], CAP) for e in range(experts)], axis=0
        ).astype(F32).astype(BF)
        found = dot(picks, cot_ref[...]).astype(BF).reshape(experts, CAP, D)
        held[:, pl.ds(pl.multiple_of(step * CAP, CAP), CAP), :] = found

    @pl.when(step >= sources)
    def _():
        rows = held[step - sources]
        rows_ref[0] = rows
        back_ref[0] = dot_last(rows, down_ref[0])


def cotangent_rows(slots, cot_all, down_weight):
    sources, experts, rows = slots.shape
    inner = down_weight.shape[1]
    span = sources * CAP
    return pl.pallas_call(
        partial(cotangent_kernel, sources, experts),
        grid=(sources + experts,),
        in_specs=[
            pl.BlockSpec((1, experts, rows), lambda i: (jnp.minimum(i, sources - 1), 0, 0)),
            pl.BlockSpec((rows, D), lambda i: (jnp.minimum(i, sources - 1), 0)),
            pl.BlockSpec((1, inner, D), lambda i: (jnp.maximum(i - sources, 0), 0, 0)),
        ],
        out_specs=[
            pl.BlockSpec((1, span, D), lambda i: (jnp.maximum(i - sources, 0), 0, 0)),
            pl.BlockSpec((1, span, inner), lambda i: (jnp.maximum(i - sources, 0), 0, 0)),
        ],
        out_shape=[
            jax.ShapeDtypeStruct((experts, span, D), BF),
            jax.ShapeDtypeStruct((experts, span, inner), F32),
        ],
        scratch_shapes=[pltpu.VMEM((experts, span, D), BF)],
        compiler_params=pltpu.CompilerParams(vmem_limit_bytes=VMEM_BYTES),
        cost_estimate=LIGHT,
        name="cotangent_rows",
    )(slots, cot_all, down_weight)


def expert_kernel(sources, experts, me_ref, slot_ref, route_ref, *refs):
    x_refs = refs[:sources]
    (
        router_ref,
        gate_ref,
        up_ref,
        back_ref,
        rows_ref,
        mid_ref,
        pair_ref,
        scale_ref,
        inner_ref,
        sum_ref,
        held,
        picked,
        scales,
        pieces,
        arrived,
    ) = refs[sources:]
    step = pl.program_id(0)
    inner = gate_ref.shape[2]

    def fetch(s):
        return pltpu.make_async_copy(x_refs[s], pieces.at[s % 2], arrived.at[s % 2])

    for s in range(sources):

        @pl.when(step == s)
        def _(s=s):
            if s == 0:
                fetch(0).start()
            if s + 1 < sources:
                fetch(s + 1).start()
            fetch(s).wait()

    @pl.when(step < sources)
    def _():
        source = step ^ me_ref[0]
        x = pieces[step % 2]
        logits = dot_last(router_ref[...], x)
        routes = route_ref[0]
        names = lax.broadcasted_iota(jnp.int32, logits.shape, 0)
        chosen = routes[0:1] == names
        for k in range(1, TOP):
            chosen = chosen | (routes[k : k + 1] == names)
        masked = jnp.where(chosen, logits, -MASKED)
        top = jnp.max(masked, axis=0, keepdims=True)
        weights = jnp.where(chosen, jnp.exp(masked - top), 0.0)
        gates = weights / jnp.sum(weights, axis=0, keepdims=True)
        slots = slot_ref[0]
        parts = []
        at = pl.ds(pl.multiple_of(source * CAP, CAP), CAP)
        for e in range(experts):
            pick = picks_of(slots[e : e + 1], CAP).astype(F32)
            scales[e, at, :] = jnp.sum(pick * gates[e : e + 1], axis=1, keepdims=True)
            parts.append(pick)
        picks = jnp.concatenate(parts, axis=0).astype(BF)
        picked[source] = picks
        held[:, at, :] = dot(picks, x).astype(BF).reshape(experts, CAP, D)

    @pl.when((step >= sources) & (step < sources + experts))
    def _():
        e = step - sources
        rows = held[e]
        rows_ref[0] = rows
        gate_val = dot(rows, gate_ref[0])
        up_val = dot(rows, up_ref[0])
        sig = jax.nn.sigmoid(gate_val)
        act = gate_val * sig
        mid = (act * up_val).astype(BF)
        mid_ref[0] = mid
        back = back_ref[0]
        inner_ref[0] = jnp.sum(back * mid.astype(F32), axis=1, keepdims=True)
        scale = scales[e]
        scale_ref[0] = scale
        hidden_grad = back * scale
        gate_back = (hidden_grad * up_val * sig * (1.0 + gate_val * (1.0 - sig))).astype(BF)
        up_back = (hidden_grad * act).astype(BF)
        pair_ref[0, :, :inner] = gate_back
        pair_ref[0, :, inner:] = up_back
        held[e] = (dot_last(gate_back, gate_ref[0]) + dot_last(up_back, up_ref[0])).astype(BF)

    @pl.when(step >= sources + experts)
    def _():
        s = step - sources - experts
        found = held[:, pl.ds(pl.multiple_of(s * CAP, CAP), CAP), :].reshape(experts * CAP, D)
        sum_ref[...] = dot_first(picked[s], found).astype(BF)


def expert_pass(me, slots, routes, x_pieces, router_rows, gate_weight, up_weight, back):
    sources, experts, rows = slots.shape
    inner = gate_weight.shape[2]
    span = sources * CAP

    def by_source(i, me_ref):
        return jnp.minimum(i, sources - 1) ^ me_ref[0]

    def by_target(i):
        return jnp.maximum(i - sources - experts, 0)

    def per_expert(*shape):
        return pl.BlockSpec(
            (1,) + shape, lambda i, me_ref: (jnp.clip(i - sources, 0, experts - 1), 0, 0)
        )

    return pl.pallas_call(
        partial(expert_kernel, sources, experts),
        grid_spec=pltpu.PrefetchScalarGridSpec(
            num_scalar_prefetch=1,
            grid=(2 * sources + experts,),
            in_specs=[
                pl.BlockSpec((1, experts, rows), lambda i, me_ref: (by_source(i, me_ref), 0, 0)),
                pl.BlockSpec((1, TOP, rows), lambda i, me_ref: (by_source(i, me_ref), 0, 0)),
                *[pl.BlockSpec(memory_space=pl.ANY) for _ in range(sources)],
                pl.BlockSpec((EXPERTS, D), lambda i, me_ref: (0, 0)),
                per_expert(D, inner),
                per_expert(D, inner),
                per_expert(span, inner),
            ],
            out_specs=[
                per_expert(span, D),
                per_expert(span, inner),
                per_expert(span, 2 * inner),
                per_expert(span, 1),
                per_expert(span, 1),
                pl.BlockSpec((rows, D), lambda i, me_ref: (by_target(i), 0)),
            ],
            scratch_shapes=[
                pltpu.VMEM((experts, span, D), BF),
                pltpu.VMEM((sources, experts * CAP, rows), BF),
                pltpu.VMEM((experts, span, 1), F32),
                pltpu.VMEM((2, rows, D), BF),
                pltpu.SemaphoreType.DMA((2,)),
            ],
        ),
        out_shape=[
            jax.ShapeDtypeStruct((experts, span, D), BF),
            jax.ShapeDtypeStruct((experts, span, inner), BF),
            jax.ShapeDtypeStruct((experts, span, 2 * inner), BF),
            jax.ShapeDtypeStruct((experts, span, 1), F32),
            jax.ShapeDtypeStruct((experts, span, 1), F32),
            jax.ShapeDtypeStruct((sources * rows, D), BF),
        ],
        compiler_params=pltpu.CompilerParams(vmem_limit_bytes=VMEM_BYTES),
        cost_estimate=LIGHT,
        name="expert_pass",
    )(me, slots, routes, *x_pieces, router_rows, gate_weight, up_weight, back)


def output_kernel(sources, experts, *refs):
    (
        slot_ref,
        mid_ref,
        pair_ref,
        rows_ref,
        cot_ref,
        scale_ref,
        down_ref,
        sum_ref,
        gate_ref,
        up_ref,
        grad_ref,
        held,
    ) = refs
    step = pl.program_id(0)
    inner = mid_ref.shape[2]

    @pl.when(step < experts)
    def _():
        mid = mid_ref[0]
        scale = scale_ref[0]
        held[step] = (dot(mid, down_ref[0]) * scale).astype(BF)
        out_grad = (cot_ref[0].astype(F32) * scale).astype(BF)
        grad_ref[0] = dot_first(mid, out_grad)
        rows = rows_ref[0]
        gate_ref[0] = dot_first(rows, pair_ref[0, :, :inner])
        up_ref[0] = dot_first(rows, pair_ref[0, :, inner:])

    @pl.when(step >= experts)
    def _():
        s = step - experts
        slots = slot_ref[0]
        picks = jnp.concatenate(
            [picks_of(slots[e : e + 1], CAP) for e in range(experts)], axis=0
        ).astype(F32).astype(BF)
        found = held[:, pl.ds(pl.multiple_of(s * CAP, CAP), CAP), :].reshape(experts * CAP, D)
        sum_ref[...] = dot_first(picks, found).astype(BF)


def output_pass(slots, mid, pair_back, x_rows, cot_rows, scale, down_weight):
    sources, experts, rows = slots.shape
    inner = down_weight.shape[1]
    span = sources * CAP

    def by_expert(i):
        return jnp.minimum(i, experts - 1)

    def by_target(i):
        return jnp.maximum(i - experts, 0)

    per_expert = lambda *shape: pl.BlockSpec((1,) + shape, lambda i: (by_expert(i), 0, 0))
    return pl.pallas_call(
        partial(output_kernel, sources, experts),
        grid=(sources + experts,),
        in_specs=[
            pl.BlockSpec((1, experts, rows), lambda i: (by_target(i), 0, 0)),
            per_expert(span, inner),
            per_expert(span, 2 * inner),
            per_expert(span, D),
            per_expert(span, D),
            per_expert(span, 1),
            per_expert(inner, D),
        ],
        out_specs=[
            pl.BlockSpec((rows, D), lambda i: (by_target(i), 0)),
            per_expert(D, inner),
            per_expert(D, inner),
            per_expert(inner, D),
        ],
        out_shape=[
            jax.ShapeDtypeStruct((sources * rows, D), BF),
            jax.ShapeDtypeStruct((experts, D, inner), F32),
            jax.ShapeDtypeStruct((experts, D, inner), F32),
            jax.ShapeDtypeStruct((experts, inner, D), F32),
        ],
        scratch_shapes=[pltpu.VMEM((experts, span, D), BF)],
        compiler_params=pltpu.CompilerParams(vmem_limit_bytes=VMEM_BYTES),
        cost_estimate=LIGHT,
        name="output_pass",
    )(slots, mid, pair_back, x_rows, cot_rows, scale, down_weight)


def across(row):
    return jnp.broadcast_to(row, (128, row.shape[1])).T


def down(column):
    return jnp.broadcast_to(column, (column.shape[0], 128)).T[:8]


def head_at(number):
    return slice(number * HEAD_DIM, (number + 1) * HEAD_DIM)


def turned(head, cosine, sine):
    return head * cosine + pltpu.roll(head, HEAD_DIM // 2, 1) * sine


def scale_of(sums):
    return lax.rsqrt(sums / (HEADS * HEAD_DIM) + EPSILON)


def normed_kernel(tokens_ref, gain_ref, weight_ref, hidden_ref, value_ref):
    inputs = tokens_ref[...].astype(F32)
    scale = lax.rsqrt(jnp.mean(inputs * inputs, axis=1, keepdims=True) + EPSILON)
    hidden_ref[...] = (inputs * scale * gain_ref[...]).astype(BF)
    value_ref[...] = dot(hidden_ref[...], weight_ref[...]).astype(BF)


def projected_kernel(hidden_ref, key_weight_ref, query_weight_ref, key_ref, query_ref, sums_ref):
    sums = []
    for weight_ref, raw_ref in ((query_weight_ref, query_ref), (key_weight_ref, key_ref)):
        raw = dot(hidden_ref[...], weight_ref[...])
        raw_ref[...] = raw
        sums.append(down(jnp.sum(raw * raw, axis=1, keepdims=True))[:1])
    sums_ref[...] = jnp.concatenate(sums, axis=0)


def rope_kernel(query_ref, key_ref, sums_ref, qgain_ref, kgain_ref, cos_ref, sin_ref, q_ref, k_ref):
    cosine, sine = cos_ref[...], sin_ref[...]
    for row, (raw_ref, gain_ref, out_ref) in enumerate(
        ((query_ref, qgain_ref, q_ref), (key_ref, kgain_ref, k_ref))
    ):
        scale = across(scale_of(sums_ref[row : row + 1, :]))
        for number in range(raw_ref.shape[1] // HEAD_DIM):
            at = head_at(number)
            normed = raw_ref[:, at] * scale * gain_ref[:, at]
            out_ref[:, at] = turned(normed, cosine, sine).astype(BF)


def small_call(kernel, name, out_shape, *operands):
    return pl.pallas_call(
        kernel,
        out_shape=out_shape,
        compiler_params=pltpu.CompilerParams(vmem_limit_bytes=VMEM_BYTES),
        cost_estimate=LIGHT,
        name=name,
    )(*operands)


def probabilities(query, keys, allowed):
    scores = jnp.concatenate([dot_last(query, key) for key in keys], axis=1) * HEAD_DIM ** (-0.5)
    scores = jnp.where(allowed, scores, -MASKED)
    exponents = jnp.exp(scores - jnp.max(scores, axis=1, keepdims=True))
    return exponents / jnp.sum(exponents, axis=1, keepdims=True)


def allowed_pairs(place_ref, name_ref, key_place_ref, key_name_ref):
    distance = place_ref[...] - key_place_ref[...]
    return (distance >= 0) & (distance < WINDOW) & (name_ref[...] == key_name_ref[...])


def attention_kernel(blocks, *refs):
    query_ref, key_refs, value_refs = refs[0], refs[1 : 1 + blocks], refs[1 + blocks : 1 + 2 * blocks]
    place_ref, name_ref, key_place_ref, key_name_ref, weight_ref, out_ref, branch_ref = refs[
        1 + 2 * blocks :
    ]
    rows = query_ref.shape[0]
    allowed = allowed_pairs(place_ref, name_ref, key_place_ref, key_name_ref)
    for number in range(query_ref.shape[1] // HEAD_DIM):
        at = head_at(number)
        probs = probabilities(
            query_ref[:, at], [key_ref[:, at] for key_ref in key_refs], allowed
        ).astype(BF)
        total = jnp.zeros((rows, HEAD_DIM), F32)
        for block, value_ref in enumerate(value_refs):
            total = total + dot(probs[:, block * rows : (block + 1) * rows], value_ref[:, at])
        out_ref[:, at] = total.astype(BF)
    branch_ref[...] = dot(out_ref[...], weight_ref[...]).astype(BF)


def attention_back_kernel(blocks, *refs):
    query_ref, key_refs, value_refs = refs[0], refs[1 : 1 + blocks], refs[1 + blocks : 1 + 2 * blocks]
    (
        place_ref,
        name_ref,
        key_place_ref,
        key_name_ref,
        weight_ref,
        attended_ref,
        hidden_ref,
        middle_ref,
        raw_ref,
        sums_ref,
        gain_ref,
        cos_ref,
        sin_ref,
        back_ref,
        dot_ref,
        gain_grad_ref,
        mine_ref,
        other_ref,
        weight_grad_ref,
        router_ref,
    ) = refs[1 + 2 * blocks :]
    rows, width = query_ref.shape
    middle = middle_ref[:, :D]
    weight_grad_ref[...] = dot_first(attended_ref[...], middle).astype(BF)
    router_ref[...] = dot_first(hidden_ref[...], middle_ref[:, D:])[:, :EXPERTS].astype(BF)
    out_grad = dot_last(middle, weight_ref[...]).astype(BF)
    allowed = allowed_pairs(place_ref, name_ref, key_place_ref, key_name_ref)
    cosine, sine = cos_ref[...], -sin_ref[...]
    scale = across(scale_of(sums_ref[0:1, :]))
    shrink = HEAD_DIM ** (-0.5)
    dots = jnp.zeros((rows, 1), F32)
    for number in range(width // HEAD_DIM):
        at = head_at(number)
        query, grad = query_ref[:, at], out_grad[:, at]
        keys = [key_ref[:, at] for key_ref in key_refs]
        probs = probabilities(query, keys, allowed)
        prob_grad = jnp.concatenate(
            [dot_last(grad, value_ref[:, at]) for value_ref in value_refs], axis=1
        )
        inner = jnp.sum(probs * prob_grad, axis=1, keepdims=True)
        score_grad = (probs * (prob_grad - inner)).astype(BF)
        probs = probs.astype(BF)
        total = jnp.zeros((rows, HEAD_DIM), F32)
        for block in range(blocks):
            part = slice(block * rows, (block + 1) * rows)
            total = total + dot(score_grad[:, part], keys[block])
            key_grad = dot_first(score_grad[:, part], query) * shrink
            value_grad = dot_first(probs[:, part], grad)
            half = blocks // 2
            target = mine_ref if block < half else other_ref
            place = slice((block % half) * rows, (block % half + 1) * rows)
            target[place, at] = key_grad.astype(target.dtype)
            target[place, width + number * HEAD_DIM : width + (number + 1) * HEAD_DIM] = (
                value_grad.astype(target.dtype)
            )
        back = turned(total * shrink, cosine, sine)
        back_ref[:, at] = back
        raw = raw_ref[:, at]
        dots = dots + jnp.sum(back * gain_ref[:, at] * raw, axis=1, keepdims=True)
        gain_grad_ref[:, at] = jnp.sum(back * raw * scale, axis=0, keepdims=True)
    dot_ref[...] = down(dots)


def key_back_kernel(
    mine_ref, got_ref, *refs
):
    (
        *part_refs,
        raw_ref,
        sums_ref,
        gain_ref,
        cos_ref,
        sin_ref,
        back_ref,
        value_ref,
        dot_ref,
        gain_grad_ref,
    ) = refs
    rows, width = raw_ref.shape
    at_own = slice(mine_ref.shape[0] - rows, mine_ref.shape[0])
    cosine, sine = cos_ref[...], -sin_ref[...]
    scale = across(scale_of(sums_ref[1:2, :]))
    dots = jnp.zeros((rows, 1), F32)
    for number in range(2 * width // HEAD_DIM):
        at = head_at(number)
        grad = mine_ref[at_own, at] + got_ref[at_own, at].astype(F32)
        for part_ref in part_refs:
            grad = grad + part_ref[:, at].astype(F32)
        if number >= width // HEAD_DIM:
            value_ref[:, head_at(number - width // HEAD_DIM)] = grad.astype(BF)
            continue
        back = turned(grad, cosine, sine)
        back_ref[:, at] = back
        raw = raw_ref[:, at]
        dots = dots + jnp.sum(back * gain_ref[:, at] * raw, axis=1, keepdims=True)
        gain_grad_ref[:, at] = jnp.sum(back * raw * scale, axis=0, keepdims=True)
    dot_ref[...] = down(dots)


def input_back_kernel(
    query_back_ref,
    key_back_ref,
    value_grad_ref,
    query_raw_ref,
    key_raw_ref,
    sums_ref,
    dots_ref,
    qgain_ref,
    kgain_ref,
    query_weight_ref,
    key_weight_ref,
    value_weight_ref,
    tokens_ref,
    norm2_ref,
    qgain_grad_ref,
    kgain_grad_ref,
    riding_ref,
    part_ref,
):
    rows, width = query_raw_ref.shape
    riding_ref[...] = jnp.zeros(riding_ref.shape, BF)
    for row, (back_ref, raw_ref, gain_ref) in enumerate(
        ((query_back_ref, query_raw_ref, qgain_ref), (key_back_ref, key_raw_ref, kgain_ref))
    ):
        scale = across(scale_of(sums_ref[row : row + 1, :]))
        factor = scale * scale * scale * across(dots_ref[row : row + 1, :] / (HEADS * HEAD_DIM))
        for number in range(width // HEAD_DIM):
            at = head_at(number)
            grad = scale * gain_ref[:, at] * back_ref[:, at] - raw_ref[:, at] * factor
            start = row * width + number * HEAD_DIM
            riding_ref[:rows, start : start + HEAD_DIM] = grad.astype(BF)
    riding_ref[:rows, 2 * width : 3 * width] = value_grad_ref[...]
    part = (
        dot_last(riding_ref[:rows, :width], query_weight_ref[...])
        + dot_last(riding_ref[:rows, width : 2 * width], key_weight_ref[...])
        + dot_last(riding_ref[:rows, 2 * width : 3 * width], value_weight_ref[...])
    )
    part_ref[...] = part.astype(BF)
    inputs = tokens_ref[...].astype(F32)
    normal = inputs * lax.rsqrt(jnp.mean(inputs * inputs, axis=1, keepdims=True) + EPSILON)
    norm1 = jnp.sum(part * normal, axis=0, keepdims=True)
    lines = [jnp.concatenate([qgain_grad_ref[...], kgain_grad_ref[...]], axis=1)]
    for norm in (norm1, norm2_ref[...]):
        for start in range(0, D, 2 * width):
            lines.append(norm[:, start : start + 2 * width])
    lines.append(jnp.zeros((-len(lines) % 16, 2 * width), F32))
    riding_ref[rows:, : 2 * width] = jnp.concatenate(lines, axis=0).astype(BF)


def weight_grad_kernel(count, *refs):
    hidden_refs, grad_refs = refs[:count], refs[count : 2 * count]
    out_refs, (hidden, grads, arrived) = refs[2 * count : 2 * count + 3], refs[2 * count + 3 :]
    step = pl.program_id(0)
    rows = hidden_refs[0].shape[0]
    width = out_refs[0].shape[1]

    @pl.when(step == 0)
    def _():
        copies = []
        for s in range(count):
            at = slice(s * rows, (s + 1) * rows)
            copies.append(
                pltpu.make_async_copy(hidden_refs[s], hidden.at[at], arrived.at[2 * s])
            )
            copies.append(
                pltpu.make_async_copy(
                    grad_refs[s].at[:rows, : 3 * width], grads.at[at], arrived.at[2 * s + 1]
                )
            )
        for copy in copies:
            copy.start()
        for copy in copies:
            copy.wait()

    for number in range(3):

        @pl.when(step == number)
        def _(number=number):
            out_refs[number][...] = dot_first(
                hidden[...], grads[:, number * width : (number + 1) * width]
            )


def weight_grads(hidden_pieces, grad_pieces, width):
    count = len(hidden_pieces)
    rows = hidden_pieces[0].shape[0]
    return pl.pallas_call(
        partial(weight_grad_kernel, count),
        grid=(3,),
        in_specs=[pl.BlockSpec(memory_space=pl.ANY) for _ in range(2 * count)],
        out_specs=[
            pl.BlockSpec((D, width), lambda i: (0, 0), pipeline_mode=pl.Buffered(1))
            for _ in range(3)
        ],
        out_shape=[jax.ShapeDtypeStruct((D, width), F32)] * 3,
        scratch_shapes=[
            pltpu.VMEM((count * rows, D), BF),
            pltpu.VMEM((count * rows, 3 * width), BF),
            pltpu.SemaphoreType.DMA((2 * count,)),
        ],
        compiler_params=pltpu.CompilerParams(vmem_limit_bytes=VMEM_BYTES),
        cost_estimate=LIGHT,
        name="weight_grads",
    )(*hidden_pieces, *grad_pieces)


def on_device(
    tokens,
    segments,
    routes,
    cotangent,
    norm1_gain,
    query_weight,
    key_weight,
    value_weight,
    query_gain,
    key_gain,
    output_weight,
    norm2_gain,
    router_weight,
    gate_weight,
    up_weight,
    down_weight,
):
    local_rows = tokens.shape[0]
    ep_count = lax.axis_size("ep")
    tp_count = lax.axis_size("tp")
    ep_at = lax.axis_index("ep")
    tp_at = lax.axis_index("tp")
    all_rows = local_rows * ep_count
    own_rows = local_rows // tp_count
    first_row = ep_at * local_rows
    seq_len = min(SEQ_MAX, all_rows)
    all_width = HEADS * HEAD_DIM
    head_width = query_weight.shape[1]
    local_heads = head_width // HEAD_DIM
    local_experts = gate_weight.shape[0]
    inner_width = gate_weight.shape[2]
    reach_rows = min(WINDOW, local_rows)
    hop_count = max(1, WINDOW // local_rows)
    def own(value):
        return lax.dynamic_slice_in_dim(value, tp_at * own_rows, own_rows, 0)

    ahead = (jnp.arange(local_rows)[:, None] < jnp.arange(local_rows)[None, :]).astype(BF)
    first_expert = ep_at * local_experts
    router_rows = jnp.roll(router_weight.T, -first_expert, axis=0)

    inputs = tokens.astype(F32)
    scale_one = inverse_rms(inputs)
    hidden_one, value_low = small_call(
        normed_kernel,
        "normed",
        [
            jax.ShapeDtypeStruct((local_rows, D), BF),
            jax.ShapeDtypeStruct((local_rows, head_width), BF),
        ],
        tokens,
        norm1_gain[None],
        value_weight,
    )
    key_raw, query_raw, squares = small_call(
        projected_kernel,
        "projected",
        [
            jax.ShapeDtypeStruct((local_rows, head_width), F32),
            jax.ShapeDtypeStruct((local_rows, head_width), F32),
            jax.ShapeDtypeStruct((2, local_rows), F32),
        ],
        hidden_one,
        key_weight,
        query_weight,
    )
    cosine, sine = rotary_tables(local_rows, first_row, seq_len)
    qgain, kgain = query_gain[None], key_gain[None]

    hops = list(range(hop_count, 0, -2))

    def window(value):
        mine = [from_behind(value, "ep", hop) for hop in hops] + [value]
        return mine + [swap(block, 1) for block in mine]

    value_blocks = window(value_low)
    square_sums = tiny_sum(squares)
    query_low, key_low = small_call(
        rope_kernel,
        "rope",
        [jax.ShapeDtypeStruct((local_rows, head_width), BF)] * 2,
        query_raw,
        key_raw,
        square_sums,
        qgain,
        kgain,
        cosine,
        sine,
    )
    key_blocks = window(key_low)
    blocks = len(key_blocks)

    counting = jnp.arange(local_rows, dtype=jnp.int32)
    starts = [(base - hop) * local_rows for base in (ep_at, ep_at ^ 1) for hop in hops + [0]]
    key_place = jnp.concatenate([start + counting for start in starts])[None]
    names = segments + EXPERTS * (jnp.arange(all_rows, dtype=jnp.int32) // seq_len)
    key_name = jnp.where(
        key_place >= 0,
        jnp.concatenate(
            [lax.dynamic_slice_in_dim(names, start, local_rows, 0) for start in starts]
        )[None],
        -1,
    )
    place = (first_row + counting)[:, None]
    name = lax.dynamic_slice_in_dim(names, first_row, local_rows, 0)[:, None]
    attended_low, branch_part = small_call(
        partial(attention_kernel, blocks),
        "attention",
        [
            jax.ShapeDtypeStruct((local_rows, head_width), BF),
            jax.ShapeDtypeStruct((local_rows, D), BF),
        ],
        query_low,
        *key_blocks,
        *value_blocks,
        place,
        name,
        key_place,
        key_name,
        output_weight,
    )

    branch = sum_scatter(branch_part, "tp")
    middle = own(inputs) + branch
    scale_two = inverse_rms(middle)
    normal_two = middle * scale_two
    hidden_two = (normal_two * norm2_gain).astype(BF)
    routes_own = own(routes)
    logits = dot(hidden_two, router_weight)
    chosen = jnp.any(
        routes_own[:, :, None] == jnp.arange(EXPERTS, dtype=jnp.int32)[None, None, :], axis=1
    )
    gates = jax.nn.softmax(jnp.where(chosen, logits, -MASKED), axis=1)
    gates = jnp.where(chosen, gates, 0.0)

    cot_all = lax.all_gather(
        after(
            jnp.concatenate([cotangent, jnp.pad(routes, ((0, 0), (0, 120))).astype(BF)], axis=1),
            key_blocks[0],
        ),
        "ep",
        tiled=True,
    )
    routes_rel = (cot_all[:, D : D + TOP].astype(jnp.int32) - first_expert) % EXPERTS
    routes_rel = jnp.swapaxes(routes_rel.reshape(ep_count, local_rows, TOP), 1, 2)
    named = jnp.any(
        routes_rel[:, None, :, :]
        == jnp.arange(local_experts, dtype=jnp.int32)[None, :, None, None],
        axis=2,
    )
    ranks = lax.dot_general(
        named.astype(BF), ahead, (((2,), (0,)), ((), ())), preferred_element_type=F32
    ).astype(jnp.int32)
    slots = jnp.where(named, ranks, -1)
    cot_rows, back = cotangent_rows(slots, cot_all, down_weight)
    hidden_pieces = gather_pieces(spread(hidden_two, "tp"), between=back)
    x_rows, mid, pair_back, scale, inner, grad_part = expert_pass(
        ep_at.reshape(1).astype(jnp.int32), slots, routes_rel, hidden_pieces, router_rows, gate_weight, up_weight, back
    )
    grad_rows = lax.psum_scatter(grad_part, "ep", tiled=True)

    inner_slots = jnp.swapaxes(inner.reshape(local_experts, ep_count, CAP), 0, 1)
    inner_dense = jnp.sum(
        jnp.where(
            slots[:, :, :, None] == jnp.arange(CAP, dtype=jnp.int32), inner_slots[:, :, None, :], 0.0
        ),
        axis=3,
    )
    inner_send = jnp.swapaxes(inner_dense, 1, 2).reshape(
        ep_count * tp_count, own_rows, local_experts
    )
    inner_got = lax.all_to_all(
        inner_send, ("ep", "tp"), split_axis=0, concat_axis=0, tiled=True
    ).reshape(ep_count, tp_count, own_rows, local_experts)
    gate_grad = jnp.swapaxes(jnp.sum(inner_got, axis=1), 0, 1).reshape(own_rows, EXPERTS)
    logit_grad = (
        gates * (gate_grad - jnp.sum(gates * gate_grad, axis=1, keepdims=True))
    ).astype(BF)
    router_term = dot_last(logit_grad, router_weight)

    mix_part, grad_gate, grad_up, grad_down = output_pass(
        slots, after(mid, gate_grad), pair_back, x_rows, cot_rows, scale, down_weight
    )

    expert_grad = sum_scatter(after(grad_rows, mix_part), "tp")
    upstream = own(cotangent).astype(F32)
    grad_two = expert_grad + router_term
    grad_norm2 = jnp.sum(grad_two * normal_two, axis=0)
    scaled_two = grad_two * norm2_gain
    grad_middle = upstream + scale_two * (
        scaled_two - normal_two * jnp.mean(scaled_two * normal_two, axis=1, keepdims=True)
    )
    riding = jnp.concatenate(
        [
            grad_middle.astype(BF),
            logit_grad,
            jnp.pad(
                grad_norm2.reshape(own_rows, D // own_rows).astype(BF),
                ((0, 0), (0, 128 - EXPERTS - D // own_rows)),
            ),
        ],
        axis=1,
    )
    middle_got = spread(riding, "tp").reshape(local_rows, D + 128)
    norm2_part = jnp.sum(
        middle_got[:, D + EXPERTS : D + EXPERTS + D // own_rows]
        .astype(F32)
        .reshape(tp_count, own_rows, D // own_rows),
        axis=0,
    ).reshape(1, D)

    half_rows = blocks // 2 * local_rows
    query_back, query_dots, grad_qgain, mine_grad, other_grad, grad_output, grad_router = small_call(
        partial(attention_back_kernel, blocks),
        "attention_back",
        [
            jax.ShapeDtypeStruct((local_rows, head_width), F32),
            jax.ShapeDtypeStruct((8, local_rows), F32),
            jax.ShapeDtypeStruct((1, head_width), F32),
            jax.ShapeDtypeStruct((half_rows, 2 * head_width), F32),
            jax.ShapeDtypeStruct((half_rows, 2 * head_width), BF),
            jax.ShapeDtypeStruct((head_width, D), BF),
            jax.ShapeDtypeStruct((D, EXPERTS), BF),
        ],
        query_low,
        *key_blocks,
        *value_blocks,
        place,
        name,
        key_place,
        key_name,
        output_weight,
        attended_low,
        hidden_pieces[0],
        middle_got,
        query_raw,
        square_sums,
        qgain,
        cosine,
        sine,
    )
    grad_output, grad_router = lax.psum((grad_output, grad_router), "ep")
    mix_rows = lax.psum_scatter(after(mix_part, grad_rows), "ep", tiled=True)
    moe_out = sum_scatter(after(mix_rows, other_grad), "tp")
    mixed_out = spread((middle + moe_out).astype(BF), "tp")
    got_grad = swap(other_grad, 1)
    parts = []
    for number, hop in enumerate(hops):
        at = slice(number * local_rows, (number + 1) * local_rows)
        part = (mine_grad[at] + got_grad[at].astype(F32)).astype(BF)
        parts.append(from_behind(part, "ep", -hop))
    mine_grad = after(mine_grad, moe_out)
    key_back, value_grad_low, key_dots, grad_kgain = small_call(
        key_back_kernel,
        "key_back",
        [
            jax.ShapeDtypeStruct((local_rows, head_width), F32),
            jax.ShapeDtypeStruct((local_rows, head_width), BF),
            jax.ShapeDtypeStruct((8, local_rows), F32),
            jax.ShapeDtypeStruct((1, head_width), F32),
        ],
        mine_grad,
        got_grad,
        *parts,
        key_raw,
        square_sums,
        kgain,
        cosine,
        sine,
    )
    dots = tiny_sum(jnp.concatenate([query_dots[:1], key_dots[:1]], axis=0))
    line_width = 2 * head_width
    norm_lines = D // line_width
    extra_rows = 1 + 2 * norm_lines
    extra_rows += -extra_rows % 16
    grads_riding, one_part = small_call(
        input_back_kernel,
        "input_back",
        [
            jax.ShapeDtypeStruct((local_rows + extra_rows, 3 * head_width), BF),
            jax.ShapeDtypeStruct((local_rows, D), BF),
        ],
        query_back,
        key_back,
        value_grad_low,
        query_raw,
        key_raw,
        square_sums,
        dots,
        qgain,
        kgain,
        query_weight,
        key_weight,
        value_weight,
        tokens,
        norm2_part,
        grad_qgain,
        grad_kgain,
    )
    grad_pieces = gather_pieces(grads_riding)
    extra_all = sum(piece[local_rows:].astype(F32) for piece in grad_pieces)
    grad_qgain = extra_all[0, :head_width]
    grad_kgain = extra_all[0, head_width:line_width]
    grad_norm1 = extra_all[1 : 1 + norm_lines, :line_width].reshape(own_rows, D // own_rows)
    grad_norm2 = extra_all[1 + norm_lines : 1 + 2 * norm_lines, :line_width].reshape(D)
    grad_one = sum_scatter(one_part, "tp")
    normal_one = own(inputs * scale_one)
    scaled_one = grad_one * norm1_gain
    grad_input_own = grad_middle + own(scale_one) * (
        scaled_one - normal_one * jnp.mean(scaled_one * normal_one, axis=1, keepdims=True)
    )
    input_got = spread(
        jnp.concatenate(
            [
                grad_input_own.astype(BF),
                jnp.pad(grad_norm1.astype(BF), ((0, 0), (0, 128 - D // own_rows))),
            ],
            axis=1,
        ),
        "tp",
    )
    grad_input = input_got[:, :D].astype(F32)
    grad_norm1 = jnp.sum(
        input_got[:, D : D + D // own_rows].astype(F32).reshape(tp_count, D), axis=0
    )

    hidden_one_pieces = gather_pieces(after(hidden_one, hidden_pieces[-1]), False)
    grad_query, grad_key, grad_value = weight_grads(hidden_one_pieces, grad_pieces, head_width)
    grad_output, grad_router = grad_output.astype(F32), grad_router.astype(F32)
    return (
        mixed_out,
        grad_input,
        grad_norm1,
        grad_query,
        grad_key,
        grad_value,
        grad_qgain,
        grad_kgain,
        grad_output,
        grad_norm2,
        grad_router,
        grad_gate,
        grad_up,
        grad_down,
    )


def solution(mesh):
    return jax.shard_map(
        on_device,
        mesh=mesh,
        in_specs=(
            P("ep", None),
            P(),
            P("ep", None),
            P("ep", None),
            P(),
            P(None, "tp"),
            P(None, "tp"),
            P(None, "tp"),
            P("tp"),
            P("tp"),
            P("tp", None),
            P(),
            P(),
            P("ep", None, "tp"),
            P("ep", None, "tp"),
            P("ep", "tp", None),
        ),
        out_specs=(
            P("ep", None),
            P("ep", None),
            P(),
            P(None, "tp"),
            P(None, "tp"),
            P(None, "tp"),
            P("tp"),
            P("tp"),
            P("tp", None),
            P(),
            P(),
            P("ep", None, "tp"),
            P("ep", None, "tp"),
            P("ep", "tp", None),
        ),
        check_vma=False,
    )
```

time: 978 us -> 666 us (0.68)
  waiting for transfers between devices: 506 us -> 255 us
  Pallas kernels: 81.2 us -> 181 us
  matrix products: 101 us -> 1.46 us
  blocking collectives: 130 us -> 58.3 us
  starting transfers between devices: 38.5 us -> 87.9 us
  other arithmetic: 59.4 us -> 29.8 us
    all_gather x7 -> x1, waiting for transfers between devices: 167 us -> 0.01 us  [on_device(): lax.all_gather(after(jnp.concatenate([cotangent, jnp.pad(routes, ((0, 0),...]
    reduce_scatter x2, waiting for transfers between devices: 135 us -> 24.1 us  [the longest x1 24.1 us: on_device(): grad_rows = lax.psum_scatter(grad_part, 'ep', tiled=True)]
    psum x4 -> x0, blocking collectives: 108 us -> none  [the longest x1 42.5 us: on_device(): square_sums = lax.psum(placed, ('ep', 'tp'))]
    dot_general x15 -> x1, matrix products: 86.2 us -> 0.78 us  [on_device(): lax.dot_general(named.astype(BF), ahead, (((2,), (0,)), ((), ())), prefer...]
    pallas_call x1 -> x9, Pallas kernels: 42.3 us -> 112 us  [the longest x7 45 us: small_call(): pl.pallas_call(kernel, out_shape=out_shape, compiler_params=pltpu.Compile...]
    psum x2 -> x1, waiting for transfers between devices: 111 us -> 52.5 us  [on_device(): grad_output, grad_router = lax.psum((grad_output, grad_router), 'ep')]
    ppermute x0 -> x30, waiting for transfers between devices: none -> 52.4 us  [swap(): return lax.ppermute(value, 'ep', [(i, i ^ distance) for i in range(count)])]
    all_to_all x1 -> x2, blocking collectives: 10.5 us -> 58.3 us  [spread(): lax.all_to_all(jnp.broadcast_to(value[None], (count,) + value.shape), axi...]
  transfers between devices with their start and end apart: 23 -> 49, of which waited for: 13 -> 21; matrix products, arithmetic and copies ran while one was open for 16% -> 7% of each run, Pallas kernels for 4% -> 18%
where the time goes in v2:
time: 666 us; the launch traced here: 656 us
  waiting for transfers between devices  255 us (38%)
  Pallas kernels  181 us (27%)
  starting transfers between devices  87.9 us (13%)
  blocking collectives  58.3 us (9%)
  other arithmetic  29.8 us (4%)
  local copies, waits for them, and re-layouts  28.1 us (4%)
  between operations  15.1 us (2%)
    all_to_all x4, waiting for transfers between devices, sum_scatter(): lax.all_to_all(value.reshape(count, rows // count, width), axis, split_ax...  68.2 us
    all_to_all x2, blocking collectives, spread(): lax.all_to_all(jnp.broadcast_to(value[None], (count,) + value.shape), axi...  58.3 us
    psum x1, waiting for transfers between devices, on_device(): grad_output, grad_router = lax.psum((grad_output, grad_router), 'ep')  52.5 us
    ppermute x30, waiting for transfers between devices, swap(): return lax.ppermute(value, 'ep', [(i, i ^ distance) for i in range(count)])  52.4 us
    pallas_call x1, Pallas kernels, output_pass(): pl.pallas_call(partial(output_kernel, sources, experts), grid=(sources +...  47.2 us
    pallas_call x7, Pallas kernels, small_call(): pl.pallas_call(kernel, out_shape=out_shape, compiler_params=pltpu.Compile...  45 us
    pallas_call x1, Pallas kernels, expert_pass(): pl.pallas_call(partial(expert_kernel, sources, experts), grid_spec=pltpu....  43.4 us
    all_to_all x4, waiting for transfers between devices, spread(): lax.all_to_all(jnp.broadcast_to(value[None], (count,) + value.shape), axi...  29.3 us
  transfers between devices with their start and end apart: 49, of which 21 were waited for; matrix products, arithmetic and copies ran while one was open for 7% of the time, Pallas kernels for 18%

profile of v2, /device:TPU:0, one launch (start us, length us, event | category | flops | bytes accessed | tf_op | source)
XLA Modules:
  0.0 656.3 jit_solution(3329354892459913328)
XLA Ops:
  10.8 4.6 projected.1
  16.7 6.3 all-to-all-start
  50.6 9.6 %collective-permute-done.5.refs_7_ = bf16[256,512]{1,0:T(8,128)(2,1)S(1)} collective-permute-done((bf16[256,512]{1,0:T(8,128)(2,1)S(1)}, bf16[256,512]{1,0:T(8,128)(2,1)S(1)}, u32[]{:S(2)}, u32[]{:S(2)}) %collective-permute-start.5) | collective-permute-done | bytes 262176 | tf_op jit(solution)/shard_map/ppermute | solution.py:31
  60.8 7.1 %collective-permute-done.1.refs_2_ = bf16[256,512]{1,0:T(8,128)(2,1)S(1)} collective-permute-done((bf16[256,512]{1,0:T(8,128)(2,1)S(1)}, bf16[256,512]{1,0:T(8,128)(2,1)S(1)}, u32[]{:S(2)}, u32[]{:S(2)}) %collective-permute-start.1) | collective-permute-done | bytes 262176 | tf_op jit(solution)/shard_map/ppermute | solution.py:31
  71.0 8.4 %attention.1 = (bf16[256,512]{1,0:T(8,128)(2,1)}, bf16[256,2048]{1,0:T(8,128)(2,1)}) custom-call(bf16[256,512]{1,0:T(8,128)(2,1)} %get-tuple-element.64.refs_0_, bf16[256,512]{1,0:T(8,128)(2,1)} %copy-done.13, bf16[256,512]{1,0:T(8,128)(2,1)} %copy-done.17, bf16[256,512]{1,0:T(8,128)(2,1)} %get-tuple-element.65.refs_3_, bf16[256,512]{1,0:T(8,128)(2,1)} %copy-done.21, ...), custom_call_target="tpu_custom_call" | custom-call | flops 1 | bytes 1 | tf_op jit(solution)/shard_map/attention/pallas_call | solution.py:450
  79.5 4.4 all-to-all-start.1
  84.2 26.4 %all-to-all-done.1 = bf16[4,64,2048]{2,1,0:T(8,128)(2,1)} async-done(((bf16[4,64,2048]{2,1,0:T(8,128)(2,1)}), bf16[4,64,2048]{2,1,0:T(8,128)(2,1)}, u32[]{:S(2)}, u32[]{:S(2)}) %all-to-all-start.1) | async-done | bytes 1048608 | tf_op jit(solution)/shard_map/all_to_all | solution.py:56
  112.4 28.5 %all_to_all.55 = bf16[4,64,2048]{2,1,0:T(8,128)(2,1)S(1)} all-to-all(bf16[4,64,2048]{2,1,0:T(8,128)(2,1)S(1)} %broadcast_in_dim.57), channel_id=1, replica_groups=mesh['ep'=8,'tp'=4] {'tp'}, dimensions={0} | all-to-all | bytes 2097152 | tf_op jit(solution)/shard_map/all_to_all | solution.py:87
  146.3 21.6 %cotangent_rows.1 = (bf16[8,512,2048]{2,1,0:T(8,128)(2,1)}, f32[8,512,256]{2,1,0:T(8,128)}) custom-call(s32[8,8,256]{2,1,0:T(8,128)} %fusion.1.slot_ref.refs_0_, bf16[2048,2176]{1,0:T(8,128)(2,1)} %all-gather.2.cloned.1.call-done.cot_ref, bf16[8,256,2048]{2,1,0:T(8,128)(2,1)} %refs_6_.1), custom_call_target="tpu_custom_call" | custom-call | flops 1 | bytes 1 | tf_op jit(solution)/shard_map/cotangent_rows/pallas_call | solution.py:146
  172.8 8.6 %collective-permute-done.15 = bf16[256,1024]{1,0:T(8,128)(2,1)S(1)} collective-permute-done((bf16[256,1024]{1,0:T(8,128)(2,1)S(1)}, bf16[256,1024]{1,0:T(8,128)(2,1)S(1)}, u32[]{:S(2)}, u32[]{:S(2)}) %collective-permute-start.15) | collective-permute-done | bytes 524320 | tf_op jit(solution)/shard_map/ppermute | solution.py:64
  185.8 43.4 %expert_pass.1 = (bf16[8,512,2048]{2,1,0:T(8,128)(2,1)}, bf16[8,512,256]{2,1,0:T(8,128)(2,1)}, bf16[8,512,512]{2,1,0:T(8,128)(2,1)}, f32[8,512,1]{2,1,0:T(8,128)...) custom-call(s32[1]{0:T(128)} %bitcast.20.me_ref, s32[8,8,256]{2,1,0:T(8,128)} %fusion.1.slot_ref.refs_0_, ...), custom_call_target="tpu_custom_call" | custom-call | flops 1 | bytes 1 | tf_op jit(solution)/shard_map/expert_pass/pallas_call | solution.py:274
  229.3 47.2 %output_pass.1 = (bf16[2048,2048]{1,0:T(8,128)(2,1)}, f32[8,2048,256]{2,1,0:T(8,128)}, f32[8,2048,256]{2,1,0:T(8,128)}, f32[8,256,2048]{2,1,0:T(8,128)}) custom-call(s32[8,8,256]{2,1,0:T(8,128)} %fusion.1.slot_ref.refs_0_, bf16[8,512,256]{2,1,0:T(8,128)(2,1)} %get-tuple-element.74.refs_1_, bf16[8,512,512]{2,1,0:T(8,128)(2,1)} %get-tuple-element.75.refs_2_, ...), custom_call_target="tpu_custom_call" | custom-call | flops 1 | bytes 1 | tf_op jit(solution)/shard_map/output_pass/pallas_call | solution.py:370
  276.5 24.1 %reduce-scatter.3.cloned.1.call-done = bf16[256,2048]{1,0:T(8,128)(2,1)} async-done(((bf16[2048,2048]{1,0:T(8,128)(2,1)}), bf16[256,2048]{1,0:T(8,128)(2,1)}) %reduce-scatter.3.cloned.1.call-update) | async-done | bytes 1048592 | tf_op jit(solution)/shard_map/reduce_scatter | solution.py:858
  305.2 4.6 all-to-all-start.3
  309.8 7.5 %all-to-all-done.3 = f32[32,1,512]{2,1,0:T(1,128)S(1)} async-done(((f32[32,1,512]{2,1,0:T(1,128)}), f32[32,1,512]{2,1,0:T(1,128)S(1)}, u32[]{:S(2)}, u32[]{:S(2)}) %all-to-all-start.3) | async-done | bytes 65568 | tf_op jit(solution)/shard_map/all_to_all | solution.py:870
  317.3 15.9 %all-to-all-start.4 = ((bf16[4,64,2048]{2,1,0:T(8,128)(2,1)}), bf16[4,64,2048]{2,1,0:T(8,128)(2,1)S(1)}, u32[]{:S(2)}, u32[]{:S(2)}) async-start(bf16[4,64,2048]{2,1,0:T(8,128)(2,1)} %bitcast.75), calls=%async_computation.6 | async-start | bytes 2097152 | tf_op jit(solution)/shard_map/all_to_all | solution.py:56
  335.9 22.8 %all-to-all-done.4 = bf16[4,64,2048]{2,1,0:T(8,128)(2,1)S(1)} async-done(((bf16[4,64,2048]{2,1,0:T(8,128)(2,1)}), bf16[4,64,2048]{2,1,0:T(8,128)(2,1)S(1)}, u32[]{:S(2)}, u32[]{:S(2)}) %all-to-all-start.4) | async-done | bytes 1048608 | tf_op jit(solution)/shard_map/all_to_all | solution.py:56
  360.7 29.8 %all_to_all.56 = bf16[4,64,2176]{2,1,0:T(8,128)(2,1)} all-to-all(bf16[4,64,2176]{2,1,0:T(8,128)(2,1)S(1)} %broadcast_in_dim.62), channel_id=1, replica_groups=mesh['ep'=8,'tp'=4] {'tp'}, dimensions={0} | all-to-all | bytes 2228224 | tf_op jit(solution)/shard_map/all_to_all | solution.py:87
  390.5 14.5 %attention_back.1 = (f32[256,512]{1,0:T(8,128)}, f32[8,256]{1,0:T(8,128)}, f32[1,512]{1,0:T(1,128)}, f32[768,1024]{1,0:T(8,128)}, bf16[768,1024]{1,0:T(8,128)(2,...) custom-call(bf16[256,512]{1,0:T(8,128)(2,1)} %get-tuple-element.64.refs_0_, bf16[256,512]{1,0:T(8,128)(2,1)} %copy-done.13, ...), custom_call_target="tpu_custom_call" | custom-call | flops 1 | bytes 1 | tf_op jit(solution)/shard_map/attention_back/pallas_call | solution.py:450
  416.2 19.0 %all-to-all-done.6 = bf16[4,64,2048]{2,1,0:T(8,128)(2,1)S(1)} async-done(((bf16[4,64,2048]{2,1,0:T(8,128)(2,1)}), bf16[4,64,2048]{2,1,0:T(8,128)(2,1)S(1)}, u32[]{:S(2)}, u32[]{:S(2)}) %all-to-all-start.6) | async-done | bytes 1048608 | tf_op jit(solution)/shard_map/all_to_all | solution.py:56
  447.4 4.8 all-to-all-done.8
  452.8 7.0 %input_back.1 = (bf16[272,1536]{1,0:T(8,128)(2,1)}, bf16[256,2048]{1,0:T(8,128)(2,1)}) custom-call(f32[256,512]{1,0:T(8,128)} %get-tuple-element.86.query_back_ref, f32[256,512]{1,0:T(8,128)} %get-tuple-element.89.key_back_ref, bf16[256,512]{1,0:T(8,128)(2,1)} %get-tuple-element.90.value_grad_ref, ...), custom_call_target="tpu_custom_call" | custom-call | flops 1 | bytes 1 | tf_op jit(solution)/shard_map/input_back/pallas_call | solution.py:450
  464.6 4.9 collective-permute-start.22
  469.5 13.5 %collective-permute-done.24.refs_12_ = bf16[272,1536]{1,0:T(8,128)(2,1)} collective-permute-done((bf16[272,1536]{1,0:T(8,128)(2,1)}, bf16[272,1536]{1,0:T(8,128)(2,1)}, u32[]{:S(2)}, u32[]{:S(2)}) %collective-permute-start.24) | collective-permute-done | bytes 835616 | tf_op jit(solution)/shard_map/ppermute | solution.py:64
  484.0 5.2 collective-permute-start.26
  491.6 4.4 collective-permute-done.26
  503.5 4.5 all-to-all-start.7
  513.2 21.1 %all-to-all-done.7 = bf16[4,64,2048]{2,1,0:T(8,128)(2,1)S(1)} async-done(((bf16[4,64,2048]{2,1,0:T(8,128)(2,1)}), bf16[4,64,2048]{2,1,0:T(8,128)(2,1)S(1)}, u32[]{:S(2)}, u32[]{:S(2)}) %all-to-all-start.7) | async-done | bytes 1048608 | tf_op jit(solution)/shard_map/all_to_all | solution.py:87
  540.1 11.8 %collective-permute-done.32.refs_4_ = bf16[256,2048]{1,0:T(8,128)(2,1)} collective-permute-done((bf16[256,2048]{1,0:T(8,128)(2,1)S(1)}, bf16[256,2048]{1,0:T(8,128)(2,1)}, u32[]{:S(2)}, u32[]{:S(2)}) %collective-permute-start.32) | collective-permute-done | bytes 1048608 | tf_op jit(solution)/shard_map/ppermute | solution.py:64
  551.9 8.8 %collective-permute-done.34.refs_6_ = bf16[256,2048]{1,0:T(8,128)(2,1)} collective-permute-done((bf16[256,2048]{1,0:T(8,128)(2,1)S(1)}, bf16[256,2048]{1,0:T(8,128)(2,1)}, u32[]{:S(2)}, u32[]{:S(2)}) %collective-permute-start.34) | collective-permute-done | bytes 1048608 | tf_op jit(solution)/shard_map/ppermute | solution.py:64
  560.7 52.5 %all-reduce.6.cloned.1.call-done = (bf16[2048,64]{1,0:T(8,128)(2,1)}, bf16[512,2048]{1,0:T(8,128)(2,1)}) async-done(((bf16[2048,64]{1,0:T(8,128)(2,1)}, bf16[512,2048]{1,0:T(8,128)(2,1)}), (bf16[2048,64]{1,0:T(8,128)(2,1)}, bf16[512,2048]{1,0:T(8,128)(2,1)})) %all-reduce.6.cloned.1.call-update) | async-done | bytes 2359312 | tf_op jit(solution)/shard_map/psum | solution.py:940
  619.4 24.0 %weight_grads.1 = (f32[2048,512]{1,0:T(8,128)}, f32[2048,512]{1,0:T(8,128)}, f32[2048,512]{1,0:T(8,128)}) custom-call(bf16[256,2048]{1,0:T(8,128)(2,1)} %get-tuple-element.97.hidden_ref.refs_0_, bf16[256,2048]{1,0:T(8,128)(2,1)} %collective-permute-done.29.refs_1_, bf16[256,2048]{1,0:T(8,128)(2,1)} %collective-permute-done.30.refs_2_, ...), custom_call_target="tpu_custom_call" | custom-call | flops 1 | bytes 1 | tf_op jit(solution)/shard_map/weight_grads/pallas_call | solution.py:679
  (264 shorter events, 124.4 us)
Async XLA Ops:
  23.0 120.4 %all-gather.2.cloned.1.call-start = ((), (), s32[]{:S(2)}) async-start(), calls=%async_computation.13 | async-start | bytes 10027008 | tf_op jit(solution)/shard_map/all_gather | solution.py:834
  39.7 20.5 %collective-permute-start.5 = (bf16[256,512]{1,0:T(8,128)(2,1)S(1)}, bf16[256,512]{1,0:T(8,128)(2,1)S(1)}, u32[]{:S(2)}, u32[]{:S(2)}) collective-permute-start(bf16[256,512]{1,0:T(8,128)(2,1)S(1)} %copy-done.11), channel_id=1, source_target_pairs={{0,16},{4,20},{8,24},{12,28},{1,17},{5,21},{9,25},{13,29},{2,18},{... | collective-permute-start | bytes 786440 | tf_op jit(solution)/shard_map/ppermute | solution.py:31
  44.1 16.1 %collective-permute-start.6 = (bf16[256,512]{1,0:T(8,128)(2,1)S(1)}, bf16[256,512]{1,0:T(8,128)(2,1)S(1)}, u32[]{:S(2)}, u32[]{:S(2)}) collective-permute-start(bf16[256,512]{1,0:T(8,128)(2,1)S(1)} %copy-done.11), channel_id=1, source_target_pairs={{0,8},{4,12},{8,16},{12,20},{16,24},{20,28},{1,9},{5,13},{9,17},{1... | collective-permute-start | bytes 786440 | tf_op jit(solution)/shard_map/ppermute | solution.py:31
  47.5 13.3 %collective-permute-start.9 = (bf16[256,512]{1,0:T(8,128)(2,1)S(1)}, bf16[256,512]{1,0:T(8,128)(2,1)S(1)}, u32[]{:S(2)}, u32[]{:S(2)}) collective-permute-start(bf16[256,512]{1,0:T(8,128)(2,1)S(1)} %copy-done.11), channel_id=1, source_target_pairs={{0,4},{4,0},{8,12},{12,8},{16,20},{20,16},{24,28},{28,24},{1,5},{5... | collective-permute-start | bytes 786440 | tf_op jit(solution)/shard_map/ppermute | solution.py:64
  47.9 20.0 %collective-permute-start.1 = (bf16[256,512]{1,0:T(8,128)(2,1)S(1)}, bf16[256,512]{1,0:T(8,128)(2,1)S(1)}, u32[]{:S(2)}, u32[]{:S(2)}) collective-permute-start(bf16[256,512]{1,0:T(8,128)(2,1)S(1)} %copy-done.12), channel_id=1, source_target_pairs={{0,8},{4,12},{8,16},{12,20},{16,24},{20,28},{1,9},{5,13},{9,17},{1... | collective-permute-start | bytes 786440 | tf_op jit(solution)/shard_map/ppermute | solution.py:31
  50.4 19.5 %collective-permute-start.4 = (bf16[256,512]{1,0:T(8,128)(2,1)S(1)}, bf16[256,512]{1,0:T(8,128)(2,1)S(1)}, u32[]{:S(2)}, u32[]{:S(2)}) collective-permute-start(bf16[256,512]{1,0:T(8,128)(2,1)S(1)} %copy-done.12), channel_id=1, source_target_pairs={{0,4},{4,0},{8,12},{12,8},{16,20},{20,16},{24,28},{28,24},{1,5},{5... | collective-permute-start | bytes 786440 | tf_op jit(solution)/shard_map/ppermute | solution.py:64
  79.5 31.1 %all-to-all-start.1 = ((bf16[4,64,2048]{2,1,0:T(8,128)(2,1)}), bf16[4,64,2048]{2,1,0:T(8,128)(2,1)}, u32[]{:S(2)}, u32[]{:S(2)}) async-start(bf16[4,64,2048]{2,1,0:T(8,128)(2,1)} %bitcast.77), calls=%async_computation.1 | async-start | bytes 2097152 | tf_op jit(solution)/shard_map/all_to_all | solution.py:56
  83.9 216.7 %reduce-scatter.3.cloned.1.call-start = ((), (), s32[]{:S(2)}) async-start(), calls=%async_computation.14 | async-start | bytes 9437184 | tf_op jit(solution)/shard_map/reduce_scatter | solution.py:858
  141.0 26.9 %collective-permute-start.11 = (bf16[256,2048]{1,0:T(8,128)(2,1)S(1)}, bf16[256,2048]{1,0:T(8,128)(2,1)}, u32[]{:S(2)}, u32[]{:S(2)}) collective-permute-start(bf16[256,2048]{1,0:T(8,128)(2,1)S(1)} %bitcast.63), channel_id=1, source_target_pairs={{0,8},{4,12},{8,0},{12,4},{16,24},{20,28},{24,16},{28,20},{1,9},{5... | collective-permute-start | bytes 3145736 | tf_op jit(solution)/shard_map/ppermute | solution.py:64
  143.5 24.4 %collective-permute-start.12 = (bf16[256,2048]{1,0:T(8,128)(2,1)S(1)}, bf16[256,2048]{1,0:T(8,128)(2,1)}, u32[]{:S(2)}, u32[]{:S(2)}) collective-permute-start(bf16[256,2048]{1,0:T(8,128)(2,1)S(1)} %bitcast.64), channel_id=1, source_target_pairs={{0,16},{4,20},{8,24},{12,28},{16,0},{20,4},{24,8},{28,12},{1,17},{... | collective-permute-start | bytes 3145736 | tf_op jit(solution)/shard_map/ppermute | solution.py:64
  170.5 12.4 %collective-permute-start.16 = (bf16[256,1024]{1,0:T(8,128)(2,1)S(1)}, bf16[256,1024]{1,0:T(8,128)(2,1)S(1)}, u32[]{:S(2)}, u32[]{:S(2)}) collective-permute-start(bf16[256,1024]{1,0:T(8,128)(2,1)S(1)} %slice.81), channel_id=1, source_target_pairs={{0,16},{4,20},{8,24},{12,28},{16,0},{20,4},{24,8},{28,12},{1,17},{... | collective-permute-start | bytes 1572872 | tf_op jit(solution)/shard_map/ppermute | solution.py:64
  229.2 175.9 %reduce-scatter.5.cloned.1.call-start = ((), (), s32[]{:S(2)}) async-start(), calls=%async_computation.15 | async-start | bytes 9437184 | tf_op jit(solution)/shard_map/reduce_scatter | solution.py:941
  317.3 41.4 %all-to-all-start.4 = ((bf16[4,64,2048]{2,1,0:T(8,128)(2,1)}), bf16[4,64,2048]{2,1,0:T(8,128)(2,1)S(1)}, u32[]{:S(2)}, u32[]{:S(2)}) async-start(bf16[4,64,2048]{2,1,0:T(8,128)(2,1)} %bitcast.75), calls=%async_computation.6 | async-start | bytes 2097152 | tf_op jit(solution)/shard_map/all_to_all | solution.py:56
  405.1 30.1 %all-to-all-start.6 = ((bf16[4,64,2048]{2,1,0:T(8,128)(2,1)}), bf16[4,64,2048]{2,1,0:T(8,128)(2,1)S(1)}, u32[]{:S(2)}, u32[]{:S(2)}) async-start(bf16[4,64,2048]{2,1,0:T(8,128)(2,1)} %bitcast.74), calls=%async_computation.8 | async-start | bytes 2097152 | tf_op jit(solution)/shard_map/all_to_all | solution.py:56
  412.0 24.2 %collective-permute-start.19 = (bf16[256,1024]{1,0:T(8,128)(2,1)}, bf16[256,1024]{1,0:T(8,128)(2,1)S(1)}, u32[]{:S(2)}, u32[]{:S(2)}) collective-permute-start(bf16[256,1024]{1,0:T(8,128)(2,1)} %get-tuple-element.197), channel_id=1, source_target_pairs={{16,0},{20,4},{24,8},{28,12},{17,1},{21,5},{25,9},{29,13},{18,2},{... | collective-permute-start | bytes 1572872 | tf_op jit(solution)/shard_map/ppermute | solution.py:31
  413.3 22.9 %collective-permute-start.20 = (bf16[256,1024]{1,0:T(8,128)(2,1)}, bf16[256,1024]{1,0:T(8,128)(2,1)S(1)}, u32[]{:S(2)}, u32[]{:S(2)}) collective-permute-start(bf16[256,1024]{1,0:T(8,128)(2,1)} %get-tuple-element.196), channel_id=1, source_target_pairs={{8,0},{12,4},{16,8},{20,12},{24,16},{28,20},{9,1},{13,5},{17,9},{2... | collective-permute-start | bytes 1572872 | tf_op jit(solution)/shard_map/ppermute | solution.py:31
  459.9 39.5 %all-to-all-start.9 = ((bf16[4,64,2048]{2,1,0:T(8,128)(2,1)}), bf16[4,64,2048]{2,1,0:T(8,128)(2,1)S(1)}, u32[]{:S(2)}, u32[]{:S(2)}) async-start(bf16[4,64,2048]{2,1,0:T(8,128)(2,1)} %bitcast.76), calls=%async_computation.11 | async-start | bytes 2097152 | tf_op jit(solution)/shard_map/all_to_all | solution.py:56
  463.5 19.4 %collective-permute-start.24 = (bf16[272,1536]{1,0:T(8,128)(2,1)}, bf16[272,1536]{1,0:T(8,128)(2,1)}, u32[]{:S(2)}, u32[]{:S(2)}) collective-permute-start(bf16[272,1536]{1,0:T(8,128)(2,1)} %get-tuple-element.96.refs_8_), channel_id=1, source_target_pairs={{0,16},{4,20},{8,24},{12,28},{16,0},{20,4},{24,8},{28,12},{1,17},{... | collective-permute-start | bytes 2506760 | tf_op jit(solution)/shard_map/ppermute | solution.py:64
  464.6 24.6 %collective-permute-start.22 = (bf16[272,1536]{1,0:T(8,128)(2,1)}, bf16[272,1536]{1,0:T(8,128)(2,1)}, u32[]{:S(2)}, u32[]{:S(2)}) collective-permute-start(bf16[272,1536]{1,0:T(8,128)(2,1)} %get-tuple-element.96.refs_8_), channel_id=1, source_target_pairs={{0,8},{4,12},{8,0},{12,4},{16,24},{20,28},{24,16},{28,20},{1,9},{5... | collective-permute-start | bytes 2506760 | tf_op jit(solution)/shard_map/ppermute | solution.py:64
  491.0 17.2 %collective-permute-start.21 = (bf16[272,1536]{1,0:T(8,128)(2,1)}, bf16[272,1536]{1,0:T(8,128)(2,1)}, u32[]{:S(2)}, u32[]{:S(2)}) collective-permute-start(bf16[272,1536]{1,0:T(8,128)(2,1)} %get-tuple-element.96.refs_8_), channel_id=1, source_target_pairs={{0,4},{4,0},{8,12},{12,8},{16,20},{20,16},{24,28},{28,24},{1,5},{5... | collective-permute-start | bytes 2506760 | tf_op jit(solution)/shard_map/ppermute | solution.py:64
  491.0 18.2 %collective-permute-start.25 = (bf16[272,1536]{1,0:T(8,128)(2,1)}, bf16[272,1536]{1,0:T(8,128)(2,1)}, u32[]{:S(2)}, u32[]{:S(2)}) collective-permute-start(bf16[272,1536]{1,0:T(8,128)(2,1)} %collective-permute-done.24.refs_12_), channel_id=1, source_target_pairs={{0,4},{4,0},{8,12},{12,8},{16,20},{20,16},{24,28},{28,24},{1,5},{5... | collective-permute-start | bytes 2506760 | tf_op jit(solution)/shard_map/ppermute | solution.py:64
  491.5 19.9 %collective-permute-start.23 = (bf16[272,1536]{1,0:T(8,128)(2,1)}, bf16[272,1536]{1,0:T(8,128)(2,1)}, u32[]{:S(2)}, u32[]{:S(2)}) collective-permute-start(bf16[272,1536]{1,0:T(8,128)(2,1)} %collective-permute-done.22.refs_10_), channel_id=1, source_target_pairs={{0,4},{4,0},{8,12},{12,8},{16,20},{20,16},{24,28},{28,24},{1,5},{5... | collective-permute-start | bytes 2506760 | tf_op jit(solution)/shard_map/ppermute | solution.py:64
  503.5 30.9 %all-to-all-start.7 = ((bf16[4,64,2048]{2,1,0:T(8,128)(2,1)}), bf16[4,64,2048]{2,1,0:T(8,128)(2,1)S(1)}, u32[]{:S(2)}, u32[]{:S(2)}) async-start(bf16[4,64,2048]{2,1,0:T(8,128)(2,1)} %broadcast_in_dim.63), calls=%async_computation.9 | async-start | bytes 2097152 | tf_op jit(solution)/shard_map/all_to_all | solution.py:87
  508.0 31.7 %collective-permute-start.30 = (bf16[256,2048]{1,0:T(8,128)(2,1)S(1)}, bf16[256,2048]{1,0:T(8,128)(2,1)}, u32[]{:S(2)}, u32[]{:S(2)}) collective-permute-start(bf16[256,2048]{1,0:T(8,128)(2,1)S(1)} %copy-done.4), channel_id=1, source_target_pairs={{0,8},{4,12},{8,0},{12,4},{16,24},{20,28},{24,16},{28,20},{1,9},{5... | collective-permute-start | bytes 3145736 | tf_op jit(solution)/shard_map/ppermute | solution.py:64
  508.2 43.7 %collective-permute-start.32 = (bf16[256,2048]{1,0:T(8,128)(2,1)S(1)}, bf16[256,2048]{1,0:T(8,128)(2,1)}, u32[]{:S(2)}, u32[]{:S(2)}) collective-permute-start(bf16[256,2048]{1,0:T(8,128)(2,1)S(1)} %copy-done.4), channel_id=1, source_target_pairs={{0,16},{4,20},{8,24},{12,28},{16,0},{20,4},{24,8},{28,12},{1,17},{... | collective-permute-start | bytes 3145736 | tf_op jit(solution)/shard_map/ppermute | solution.py:64
  509.2 51.5 %collective-permute-start.34 = (bf16[256,2048]{1,0:T(8,128)(2,1)S(1)}, bf16[256,2048]{1,0:T(8,128)(2,1)}, u32[]{:S(2)}, u32[]{:S(2)}) collective-permute-start(bf16[256,2048]{1,0:T(8,128)(2,1)S(1)} %copy-done.4), channel_id=1, source_target_pairs={{0,24},{4,28},{8,16},{12,20},{16,8},{20,12},{24,0},{28,4},{1,25},{... | collective-permute-start | bytes 3145736 | tf_op jit(solution)/shard_map/ppermute | solution.py:64
  535.4 110.6 %all-to-all-start.10 = ((bf16[4,64,2176]{2,1,0:T(8,128)(2,1)}), bf16[4,64,2176]{2,1,0:T(8,128)(2,1)S(1)}, u32[]{:S(2)}, u32[]{:S(2)}) async-start(bf16[4,64,2176]{2,1,0:T(8,128)(2,1)} %broadcast_in_dim.65), calls=%async_computation.12 | async-start | bytes 2228224 | tf_op jit(solution)/shard_map/all_to_all | solution.py:87
  539.0 74.3 %all-reduce.6.cloned.1.call-start = ((), (), s32[]{:S(2)}) async-start(), calls=%async_computation.16 | async-start | bytes 5242880 | tf_op jit(solution)/shard_map/psum | solution.py:940
  539.5 79.8 %collective-permute-start.29 = (bf16[256,2048]{1,0:T(8,128)(2,1)S(1)}, bf16[256,2048]{1,0:T(8,128)(2,1)}, u32[]{:S(2)}, u32[]{:S(2)}) collective-permute-start(bf16[256,2048]{1,0:T(8,128)(2,1)S(1)} %copy-done.4), channel_id=1, source_target_pairs={{0,4},{4,0},{8,12},{12,8},{16,20},{20,16},{24,28},{28,24},{1,5},{5... | collective-permute-start | bytes 3145736 | tf_op jit(solution)/shard_map/ppermute | solution.py:64
  539.6 79.8 %collective-permute-start.31 = (bf16[256,2048]{1,0:T(8,128)(2,1)}, bf16[256,2048]{1,0:T(8,128)(2,1)}, u32[]{:S(2)}, u32[]{:S(2)}) collective-permute-start(bf16[256,2048]{1,0:T(8,128)(2,1)} %collective-permute-done.30.refs_2_), channel_id=1, source_target_pairs={{0,4},{4,0},{8,12},{12,8},{16,20},{20,16},{24,28},{28,24},{1,5},{5... | collective-permute-start | bytes 3145736 | tf_op jit(solution)/shard_map/ppermute | solution.py:64
  551.9 67.5 %collective-permute-start.33 = (bf16[256,2048]{1,0:T(8,128)(2,1)}, bf16[256,2048]{1,0:T(8,128)(2,1)}, u32[]{:S(2)}, u32[]{:S(2)}) collective-permute-start(bf16[256,2048]{1,0:T(8,128)(2,1)} %collective-permute-done.32.refs_4_), channel_id=1, source_target_pairs={{0,4},{4,0},{8,12},{12,8},{16,20},{20,16},{24,28},{28,24},{1,5},{5... | collective-permute-start | bytes 3145736 | tf_op jit(solution)/shard_map/ppermute | solution.py:64
  560.7 58.7 %collective-permute-start.35 = (bf16[256,2048]{1,0:T(8,128)(2,1)}, bf16[256,2048]{1,0:T(8,128)(2,1)}, u32[]{:S(2)}, u32[]{:S(2)}) collective-permute-start(bf16[256,2048]{1,0:T(8,128)(2,1)} %collective-permute-done.34.refs_6_), channel_id=1, source_target_pairs={{0,4},{4,0},{8,12},{12,8},{16,20},{20,16},{24,28},{28,24},{1,5},{5... | collective-permute-start | bytes 3145736 | tf_op jit(solution)/shard_map/ppermute | solution.py:64
  (48 other events, 497.3 us)
Sparse Core Ops, SparseCore 0:
  39.9 63.8 all-gather.1
  229.4 71.1 reduce-scatter.2
  304.4 71.2 reduce-scatter.4
  543.4 69.7 all-reduce.5

commit v3 on v2

--- a/solution.py
+++ b/solution.py
@@ -19,6 +19,7 @@
 
 EPSILON = 1e-05
 MASKED = 1e30
+WIDE = D + 128
 VMEM_BYTES = 58 * 1024 * 1024
 BF = jnp.bfloat16
 LIGHT = pl.CostEstimate(flops=1, bytes_accessed=1, transcendentals=0)
@@ -50,13 +51,20 @@
     return jnp.concatenate([cosine, cosine], axis=1), jnp.concatenate([-sine, sine], axis=1)
 
 
-def sum_scatter(value, axis):
+def ep_sum(value):
+    distance = 1
+    while distance < lax.axis_size("ep"):
+        value = value + swap(value, distance)
+        distance *= 2
+    return value
+
+
+def to_owners(value, axis):
     count = lax.axis_size(axis)
     rows, width = value.shape
-    pieces = lax.all_to_all(
+    return lax.all_to_all(
         value.reshape(count, rows // count, width), axis, split_axis=0, concat_axis=0, tiled=True
     )
-    return jnp.sum(pieces.astype(F32), axis=0)
 
 
 def swap(value, distance):
@@ -64,22 +72,46 @@
     return lax.ppermute(value, "ep", [(i, i ^ distance) for i in range(count)])
 
 
-def gather_evens(value, relay, between):
+def gather_near(value):
     count = lax.axis_size("ep")
-    if count != 8 or not relay:
-        return [value] + [swap(value, d) for d in range(2, count, 2)]
-    half = value.shape[1] // 2
-    near, far = swap(value, 2), swap(value, 4)
-    if between is not None:
-        near, far, _ = lax.optimization_barrier((near, far, between))
-    corner = jnp.concatenate([swap(far[:, :half], 2), swap(near[:, half:], 4)], axis=1)
-    return [value, near, far, corner]
-
-
-def gather_pieces(value, relay=True, between=None):
-    evens = gather_evens(value, relay, between)
-    odds = [swap(piece, 1) for piece in evens]
-    return [piece for both in zip(evens, odds) for piece in both]
+    return [swap(value, d) for d in range(2, count, 2)][: 2 if count == 8 else None]
+
+
+def gather_corner(near, before, between):
+    if len(near) != 2:
+        return []
+    rows, width = near[0].shape
+    half = jax.ShapeDtypeStruct((rows, width // 2), near[0].dtype)
+
+    def cut_kernel(near_ref, far_ref, low_ref, high_ref):
+        low_ref[...] = far_ref[:, : width // 2]
+        high_ref[...] = near_ref[:, width // 2 :]
+
+    def join_kernel(low_ref, high_ref, out_ref):
+        out_ref[:, : width // 2] = low_ref[...]
+        out_ref[:, width // 2 :] = high_ref[...]
+
+    low, high = small_call(cut_kernel, "cut", [half, half], *near, deps=before)
+    whole = jax.ShapeDtypeStruct((rows, width), near[0].dtype)
+    return [small_call(join_kernel, "join", whole, swap(low, 2), swap(high, 4), deps=between)]
+
+
+def with_odds(evens):
+    return [piece for even in evens for piece in (even, swap(even, 1))]
+
+
+def to_owners_by_permutes(value):
+    count = lax.axis_size("tp")
+    rows, width = value.shape
+    blocks = value.reshape(count, rows // count, width)
+    at = lax.axis_index("tp")
+    pieces = []
+    for distance in range(count):
+        piece = lax.dynamic_index_in_dim(blocks, at ^ distance, 0, False)
+        if distance:
+            piece = lax.ppermute(piece, "tp", [(i, i ^ distance) for i in range(count)])
+        pieces.append(piece)
+    return pieces
 
 
 def spread(value, axis):
@@ -93,13 +125,29 @@
     ).reshape(count * value.shape[0], value.shape[1])
 
 
+def spread_ready(copies, axis):
+    got = lax.all_to_all(copies, axis, split_axis=0, concat_axis=0, tiled=True)
+    return got.reshape(copies.shape[0] * copies.shape[1], copies.shape[2])
+
+
 def tiny_sum(value):
     rows = value.shape[0]
     return jnp.sum(spread(value, "tp").reshape(lax.axis_size("tp"), rows, value.shape[1]), axis=0)
 
 
-def after(value, *others):
-    return lax.optimization_barrier((value,) + others)[0]
+def held_back(value, *others):
+    return pl.pallas_call(
+        lambda *refs: None,
+        in_specs=[pl.BlockSpec(memory_space=pl.ANY)] * (1 + len(others)),
+        out_specs=pl.BlockSpec(memory_space=pl.ANY),
+        out_shape=jax.ShapeDtypeStruct(value.shape, value.dtype),
+        input_output_aliases={0: 0},
+        name="held_back",
+    )(value, *others)
+
+
+def cost(flops):
+    return pl.CostEstimate(flops=flops, bytes_accessed=1, transcendentals=0)
 
 
 def dot(left, right):
@@ -118,19 +166,33 @@
     return slots == lax.broadcasted_iota(jnp.int32, (cap, slots.shape[1]), 0)
 
 
+def picks_for(slots, experts):
+    return (
+        jnp.concatenate([picks_of(slots[e : e + 1], CAP) for e in range(experts)], axis=0)
+        .astype(F32)
+        .astype(BF)
+    )
+
+
+def picks_across(slots, experts):
+    lane = lax.broadcasted_iota(jnp.int32, (slots.shape[0], 2 * CAP), 1)
+    parts = []
+    for e in range(0, experts, 2):
+        wanted = jnp.where(lane < CAP, slots[:, e : e + 1], slots[:, e + 1 : e + 2] + CAP)
+        parts.append((wanted == lane).astype(F32))
+    return jnp.concatenate(parts, axis=1).astype(BF)
+
+
 def cotangent_kernel(
-    sources, experts, slot_ref, cot_ref, down_ref, rows_ref, back_ref, held
+    sources, experts, me_ref, slot_ref, cot_ref, down_ref, rows_ref, back_ref, held
 ):
     step = pl.program_id(0)
 
     @pl.when(step < sources)
     def _():
-        slots = slot_ref[0]
-        picks = jnp.concatenate(
-            [picks_of(slots[e : e + 1], CAP) for e in range(experts)], axis=0
-        ).astype(F32).astype(BF)
-        found = dot(picks, cot_ref[...]).astype(BF).reshape(experts, CAP, D)
-        held[:, pl.ds(pl.multiple_of(step * CAP, CAP), CAP), :] = found
+        found = dot(picks_for(slot_ref[0], experts), cot_ref[...]).astype(BF)
+        at = pl.ds(pl.multiple_of(step * CAP, CAP), CAP)
+        held[:, at, :] = found.reshape(experts, CAP, D)
 
     @pl.when(step >= sources)
     def _():
@@ -139,35 +201,42 @@
         back_ref[0] = dot_last(rows, down_ref[0])
 
 
-def cotangent_rows(slots, cot_all, down_weight):
+def cotangent_rows(me, slots, cot_all, down_weight):
     sources, experts, rows = slots.shape
     inner = down_weight.shape[1]
     span = sources * CAP
+
+    def by_source(i):
+        return jnp.minimum(i, sources - 1)
+
+    def per_expert(*shape):
+        return pl.BlockSpec((1,) + shape, lambda i, me_ref: (jnp.maximum(i - sources, 0), 0, 0))
+
     return pl.pallas_call(
         partial(cotangent_kernel, sources, experts),
-        grid=(sources + experts,),
-        in_specs=[
-            pl.BlockSpec((1, experts, rows), lambda i: (jnp.minimum(i, sources - 1), 0, 0)),
-            pl.BlockSpec((rows, D), lambda i: (jnp.minimum(i, sources - 1), 0)),
-            pl.BlockSpec((1, inner, D), lambda i: (jnp.maximum(i - sources, 0), 0, 0)),
-        ],
-        out_specs=[
-            pl.BlockSpec((1, span, D), lambda i: (jnp.maximum(i - sources, 0), 0, 0)),
-            pl.BlockSpec((1, span, inner), lambda i: (jnp.maximum(i - sources, 0), 0, 0)),
-        ],
+        grid_spec=pltpu.PrefetchScalarGridSpec(
+            num_scalar_prefetch=1,
+            grid=(sources + experts,),
+            in_specs=[
+                pl.BlockSpec((1, experts, rows), lambda i, me_ref: (by_source(i), 0, 0)),
+                pl.BlockSpec((rows, D), lambda i, me_ref: (by_source(i) ^ me_ref[0], 0)),
+                per_expert(inner, D),
+            ],
+            out_specs=[per_expert(span, D), per_expert(span, inner)],
+            scratch_shapes=[pltpu.VMEM((experts, span, D), BF)],
+        ),
         out_shape=[
             jax.ShapeDtypeStruct((experts, span, D), BF),
             jax.ShapeDtypeStruct((experts, span, inner), F32),
         ],
-        scratch_shapes=[pltpu.VMEM((experts, span, D), BF)],
         compiler_params=pltpu.CompilerParams(vmem_limit_bytes=VMEM_BYTES),
         cost_estimate=LIGHT,
         name="cotangent_rows",
-    )(slots, cot_all, down_weight)
-
-
-def expert_kernel(sources, experts, me_ref, slot_ref, route_ref, *refs):
-    x_refs = refs[:sources]
+    )(me, slots, cot_all, down_weight)
+
+
+def expert_kernel(sources, experts, me_ref, slot_ref, route_ref, across_ref, *refs):
+    left_refs, right_refs = refs[:sources], refs[sources : 2 * sources]
     (
         router_ref,
         gate_ref,
@@ -177,33 +246,38 @@
         mid_ref,
         pair_ref,
         scale_ref,
-        inner_ref,
         sum_ref,
         held,
-        picked,
+        side,
         scales,
         pieces,
         arrived,
-    ) = refs[sources:]
+    ) = refs[2 * sources :]
     step = pl.program_id(0)
     inner = gate_ref.shape[2]
 
     def fetch(s):
-        return pltpu.make_async_copy(x_refs[s], pieces.at[s % 2], arrived.at[s % 2])
+        slot = s % 2
+        return [
+            pltpu.make_async_copy(
+                left_refs[s], pieces.at[slot, :, : D // 2], arrived.at[slot, 0]
+            ),
+            pltpu.make_async_copy(
+                right_refs[s], pieces.at[slot, :, D // 2 :], arrived.at[slot, 1]
+            ),
+        ]
 
     for s in range(sources):
 
         @pl.when(step == s)
         def _(s=s):
-            if s == 0:
-                fetch(0).start()
-            if s + 1 < sources:
-                fetch(s + 1).start()
-            fetch(s).wait()
+            for copy in (fetch(0) if s == 0 else []) + (fetch(s + 1) if s + 1 < sources else []):
+                copy.start()
+            for copy in fetch(s):
+                copy.wait()
 
     @pl.when(step < sources)
     def _():
-        source = step ^ me_ref[0]
         x = pieces[step % 2]
         logits = dot_last(router_ref[...], x)
         routes = route_ref[0]
@@ -217,13 +291,12 @@
         gates = weights / jnp.sum(weights, axis=0, keepdims=True)
         slots = slot_ref[0]
         parts = []
-        at = pl.ds(pl.multiple_of(source * CAP, CAP), CAP)
+        at = pl.ds(pl.multiple_of(step * CAP, CAP), CAP)
         for e in range(experts):
             pick = picks_of(slots[e : e + 1], CAP).astype(F32)
             scales[e, at, :] = jnp.sum(pick * gates[e : e + 1], axis=1, keepdims=True)
             parts.append(pick)
         picks = jnp.concatenate(parts, axis=0).astype(BF)
-        picked[source] = picks
         held[:, at, :] = dot(picks, x).astype(BF).reshape(experts, CAP, D)
 
     @pl.when((step >= sources) & (step < sources + experts))
@@ -238,7 +311,9 @@
         mid = (act * up_val).astype(BF)
         mid_ref[0] = mid
         back = back_ref[0]
-        inner_ref[0] = jnp.sum(back * mid.astype(F32), axis=1, keepdims=True)
+        gate_grad = jnp.sum(back * mid.astype(F32), axis=1, keepdims=True)
+        lane = lax.broadcasted_iota(jnp.int32, (rows.shape[0], WIDE - D), 1)
+        side[e] = jnp.where(lane == me_ref[0] * experts + e, gate_grad, 0.0).astype(BF)
         scale = scales[e]
         scale_ref[0] = scale
         hidden_grad = back * scale
@@ -250,23 +325,25 @@
 
     @pl.when(step >= sources + experts)
     def _():
-        s = step - sources - experts
-        found = held[:, pl.ds(pl.multiple_of(s * CAP, CAP), CAP), :].reshape(experts * CAP, D)
-        sum_ref[...] = dot_first(picked[s], found).astype(BF)
-
-
-def expert_pass(me, slots, routes, x_pieces, router_rows, gate_weight, up_weight, back):
+        s = (step - sources - experts) ^ me_ref[0]
+        at = pl.ds(pl.multiple_of(s * CAP, CAP), CAP)
+        picks = picks_across(across_ref[0], experts)
+        sum_ref[:, :D] = dot(picks, held[:, at, :].reshape(experts * CAP, D)).astype(BF)
+        sum_ref[:, D:] = dot(picks, side[:, at, :].reshape(experts * CAP, WIDE - D)).astype(BF)
+
+
+def expert_pass(me, slots, routes, across, x_pieces, router_rows, gate_weight, up_weight, back):
     sources, experts, rows = slots.shape
     inner = gate_weight.shape[2]
     span = sources * CAP
 
-    def by_source(i, me_ref):
-        return jnp.minimum(i, sources - 1) ^ me_ref[0]
+    def by_source(i):
+        return jnp.minimum(i, sources - 1)
 
     def by_target(i):
         return jnp.maximum(i - sources - experts, 0)
 
-    def per_expert(*shape):
+    def by_expert(*shape):
         return pl.BlockSpec(
             (1,) + shape, lambda i, me_ref: (jnp.clip(i - sources, 0, experts - 1), 0, 0)
         )
@@ -277,28 +354,30 @@
             num_scalar_prefetch=1,
             grid=(2 * sources + experts,),
             in_specs=[
-                pl.BlockSpec((1, experts, rows), lambda i, me_ref: (by_source(i, me_ref), 0, 0)),
-                pl.BlockSpec((1, TOP, rows), lambda i, me_ref: (by_source(i, me_ref), 0, 0)),
-                *[pl.BlockSpec(memory_space=pl.ANY) for _ in range(sources)],
+                pl.BlockSpec((1, experts, rows), lambda i, me_ref: (by_source(i), 0, 0)),
+                pl.BlockSpec((1, TOP, rows), lambda i, me_ref: (by_source(i), 0, 0)),
+                pl.BlockSpec(
+                    (1, rows, experts), lambda i, me_ref: (by_target(i) ^ me_ref[0], 0, 0)
+                ),
+                *[pl.BlockSpec(memory_space=pl.ANY) for _ in x_pieces],
                 pl.BlockSpec((EXPERTS, D), lambda i, me_ref: (0, 0)),
-                per_expert(D, inner),
-                per_expert(D, inner),
-                per_expert(span, inner),
+                by_expert(D, inner),
+                by_expert(D, inner),
+                by_expert(span, inner),
             ],
             out_specs=[
-                per_expert(span, D),
-                per_expert(span, inner),
-                per_expert(span, 2 * inner),
-                per_expert(span, 1),
-                per_expert(span, 1),
-                pl.BlockSpec((rows, D), lambda i, me_ref: (by_target(i), 0)),
+                by_expert(span, D),
+                by_expert(span, inner),
+                by_expert(span, 2 * inner),
+                by_expert(span, 1),
+                pl.BlockSpec((rows, WIDE), lambda i, me_ref: (by_target(i), 0)),
             ],
             scratch_shapes=[
                 pltpu.VMEM((experts, span, D), BF),
-                pltpu.VMEM((sources, experts * CAP, rows), BF),
+                pltpu.VMEM((experts, span, WIDE - D), BF),
                 pltpu.VMEM((experts, span, 1), F32),
                 pltpu.VMEM((2, rows, D), BF),
-                pltpu.SemaphoreType.DMA((2,)),
+                pltpu.SemaphoreType.DMA((2, 2)),
             ],
         ),
         out_shape=[
@@ -306,96 +385,243 @@
             jax.ShapeDtypeStruct((experts, span, inner), BF),
             jax.ShapeDtypeStruct((experts, span, 2 * inner), BF),
             jax.ShapeDtypeStruct((experts, span, 1), F32),
-            jax.ShapeDtypeStruct((experts, span, 1), F32),
-            jax.ShapeDtypeStruct((sources * rows, D), BF),
-        ],
+            jax.ShapeDtypeStruct((sources * rows, WIDE), BF),
+        ],
+        compiler_params=pltpu.CompilerParams(vmem_limit_bytes=VMEM_BYTES),
+        cost_estimate=cost(2 * experts * span * D * (rows + 4 * inner)),
+        name="expert_pass",
+    )(me, slots, routes, across, *x_pieces, router_rows, gate_weight, up_weight, back)
+
+
+def per_expert(*shape):
+    return pl.BlockSpec((1,) + shape, lambda e: (e, 0, 0))
+
+
+def odd_kernel(slot_ref, rows_ref, *refs):
+    experts, _, width = rows_ref.shape
+    found = rows_ref[...].reshape(experts * CAP, width)
+    refs[-1][0] = dot(picks_across(slot_ref[0], experts), found).astype(BF)
+
+
+def add_up_odd(slots, slabs, *deps):
+    sources, rows, experts = slots.shape
+    width = slabs.shape[2]
+    return pl.pallas_call(
+        odd_kernel,
+        grid=(sources // 2,),
+        in_specs=[
+            pl.BlockSpec((1, rows, experts), lambda j: (2 * j + 1, 0, 0)),
+            pl.BlockSpec((experts, CAP, width), lambda j: (0, 2 * j + 1, 0)),
+            *[pl.BlockSpec(memory_space=pl.ANY) for _ in deps],
+        ],
+        out_specs=pl.BlockSpec((1, rows, width), lambda j: (j, 0, 0)),
+        out_shape=jax.ShapeDtypeStruct((sources // 2, rows, width), BF),
         compiler_params=pltpu.CompilerParams(vmem_limit_bytes=VMEM_BYTES),
         cost_estimate=LIGHT,
-        name="expert_pass",
-    )(me, slots, routes, *x_pieces, router_rows, gate_weight, up_weight, back)
-
-
-def output_kernel(sources, experts, *refs):
-    (
-        slot_ref,
-        mid_ref,
-        pair_ref,
-        rows_ref,
-        cot_ref,
-        scale_ref,
-        down_ref,
-        sum_ref,
-        gate_ref,
-        up_ref,
-        grad_ref,
-        held,
-    ) = refs
+        name="add_up_odd",
+    )(slots, slabs, *deps)
+
+
+def even_kernel(split, slot_ref, rows_ref, got_ref, *refs):
+    experts, _, width = rows_ref.shape
+    found = rows_ref[...].reshape(experts * CAP, width)
+    total = dot(picks_across(slot_ref[0], experts), found) + got_ref[0].astype(F32)
+    if not split:
+        refs[-1][0] = total.astype(BF)
+        return
+    near_ref, far_ref, left0_ref, left1_ref, right0_ref, right1_ref = refs[-6:]
     step = pl.program_id(0)
-    inner = mid_ref.shape[2]
-
-    @pl.when(step < experts)
-    def _():
-        mid = mid_ref[0]
-        scale = scale_ref[0]
-        held[step] = (dot(mid, down_ref[0]) * scale).astype(BF)
-        out_grad = (cot_ref[0].astype(F32) * scale).astype(BF)
-        grad_ref[0] = dot_first(mid, out_grad)
-        rows = rows_ref[0]
-        gate_ref[0] = dot_first(rows, pair_ref[0, :, :inner])
-        up_ref[0] = dot_first(rows, pair_ref[0, :, inner:])
-
-    @pl.when(step >= experts)
-    def _():
-        s = step - experts
-        slots = slot_ref[0]
-        picks = jnp.concatenate(
-            [picks_of(slots[e : e + 1], CAP) for e in range(experts)], axis=0
-        ).astype(F32).astype(BF)
-        found = held[:, pl.ds(pl.multiple_of(s * CAP, CAP), CAP), :].reshape(experts * CAP, D)
-        sum_ref[...] = dot_first(picks, found).astype(BF)
-
-
-def output_pass(slots, mid, pair_back, x_rows, cot_rows, scale, down_weight):
-    sources, experts, rows = slots.shape
-    inner = down_weight.shape[1]
-    span = sources * CAP
-
-    def by_expert(i):
-        return jnp.minimum(i, experts - 1)
-
-    def by_target(i):
-        return jnp.maximum(i - experts, 0)
-
-    per_expert = lambda *shape: pl.BlockSpec((1,) + shape, lambda i: (by_expert(i), 0, 0))
+    half = D // 2
+    places = (
+        (left0_ref, right0_ref),
+        (near_ref.at[0], right1_ref),
+        (left1_ref, far_ref.at[0]),
+        (near_ref.at[1], far_ref.at[1]),
+    )
+    for j, (first_ref, second_ref) in enumerate(places):
+
+        @pl.when(step == j)
+        def _(first_ref=first_ref, second_ref=second_ref):
+            first_ref[...] = total[:, :half].astype(first_ref.dtype)
+            second_ref[...] = total[:, half:].astype(second_ref.dtype)
+
+
+def add_up_even(slots, slabs, got, *deps):
+    sources, rows, experts = slots.shape
+    width = slabs.shape[2]
+    split = sources == 8
+    if split:
+        left, right = (rows, D // 2), (rows, width - D // 2)
+        shapes = [((2,) + left, BF), ((2,) + right, BF)]
+        shapes += [(left, F32), (left, F32), (right, F32), (right, F32)]
+        out_specs = [
+            pl.BlockSpec(shape, lambda j, count=len(shape): (0,) * count) for shape, _ in shapes
+        ]
+        out_shape = [jax.ShapeDtypeStruct(shape, kind) for shape, kind in shapes]
+    else:
+        out_specs = [pl.BlockSpec((1, rows, width), lambda j: (j, 0, 0))]
+        out_shape = [jax.ShapeDtypeStruct((sources // 2, rows, width), BF)]
     return pl.pallas_call(
-        partial(output_kernel, sources, experts),
-        grid=(sources + experts,),
+        partial(even_kernel, split),
+        grid=(sources // 2,),
         in_specs=[
-            pl.BlockSpec((1, experts, rows), lambda i: (by_target(i), 0, 0)),
+            pl.BlockSpec((1, rows, experts), lambda j: (2 * j, 0, 0)),
+            pl.BlockSpec((experts, CAP, width), lambda j: (0, 2 * j, 0)),
+            pl.BlockSpec((1, rows, width), lambda j: (j, 0, 0)),
+            *[pl.BlockSpec(memory_space=pl.ANY) for _ in deps],
+        ],
+        out_specs=out_specs,
+        out_shape=out_shape,
+        compiler_params=pltpu.CompilerParams(vmem_limit_bytes=VMEM_BYTES),
+        cost_estimate=LIGHT,
+        name="add_up_even",
+    )(slots, slabs, got, *deps)
+
+
+def middle_add_kernel(left_ref, right_ref, near_ref, far_ref, *refs):
+    refs[-2][...] = (left_ref[...] + near_ref[0].astype(F32)).astype(BF)
+    refs[-1][...] = (right_ref[...] + far_ref[0].astype(F32)).astype(BF)
+
+
+def last_add_kernel(
+    left_ref, right_ref, near_ref, far_ref, last_left_ref, last_right_ref, *refs
+):
+    half = left_ref.shape[1]
+    refs[-1][:, :half] = (
+        left_ref[...] + near_ref[0].astype(F32) + last_left_ref[...].astype(F32)
+    ).astype(BF)
+    refs[-1][:, half:] = (
+        right_ref[...] + far_ref[0].astype(F32) + last_right_ref[...].astype(F32)
+    ).astype(BF)
+
+
+def exchange(blocks, first, between=(), late=()):
+    if len(blocks) == 1:
+        total = blocks[0]
+        own = total[0].astype(F32)
+        for j in range(1, total.shape[0]):
+            own = own + swap(total[j], 2 * j).astype(F32)
+        return own.astype(BF), own.astype(BF)
+    near, far, left0, left1, right0, right1 = blocks
+    near, far = swap(held_back(near, first), 2), swap(held_back(far, first), 4)
+    rows, left = left0.shape
+    right = right0.shape[1]
+
+    def whole(width):
+        return pl.BlockSpec((rows, width), lambda i: (0, 0))
+
+    def one_of(number, width):
+        return pl.BlockSpec((1, rows, width), lambda i: (number, 0, 0))
+
+    def spare(deps):
+        return [pl.BlockSpec(memory_space=pl.ANY) for _ in deps]
+
+    to_far, to_near = pl.pallas_call(
+        middle_add_kernel,
+        grid=(1,),
+        in_specs=[whole(left), whole(right), one_of(1, left), one_of(1, right), *spare(between)],
+        out_specs=[whole(left), whole(right)],
+        out_shape=[
+            jax.ShapeDtypeStruct((rows, left), BF),
+            jax.ShapeDtypeStruct((rows, right), BF),
+        ],
+        compiler_params=pltpu.CompilerParams(vmem_limit_bytes=VMEM_BYTES),
+        cost_estimate=LIGHT,
+        name="middle_add",
+    )(left1, right1, near, far, *between)
+    own = pl.pallas_call(
+        last_add_kernel,
+        grid=(1,),
+        in_specs=[
+            whole(left),
+            whole(right),
+            one_of(0, left),
+            one_of(0, right),
+            whole(left),
+            whole(right),
+            *spare(late),
+        ],
+        out_specs=whole(left + right),
+        out_shape=jax.ShapeDtypeStruct((rows, left + right), BF),
+        compiler_params=pltpu.CompilerParams(vmem_limit_bytes=VMEM_BYTES),
+        cost_estimate=LIGHT,
+        name="last_add",
+    )(left0, right0, near, far, swap(to_far, 4), swap(to_near, 2), *late)
+    return own, to_far
+
+
+def output_kernel(mid_ref, scale_ref, down_ref, *refs):
+    refs[-1][0] = (dot(mid_ref[0], down_ref[0]) * scale_ref[0]).astype(BF)
+
+
+def output_pass(mid, scale, down_weight, *deps):
+    experts, span, inner = mid.shape
+    return pl.pallas_call(
+        output_kernel,
+        grid=(experts,),
+        in_specs=[
             per_expert(span, inner),
+            per_expert(span, 1),
+            per_expert(inner, D),
+            *[pl.BlockSpec(memory_space=pl.ANY) for _ in deps],
+        ],
+        out_specs=per_expert(span, D),
+        out_shape=jax.ShapeDtypeStruct((experts, span, D), BF),
+        compiler_params=pltpu.CompilerParams(vmem_limit_bytes=VMEM_BYTES),
+        cost_estimate=cost(2 * experts * span * D * inner),
+        name="output_pass",
+    )(mid, scale, down_weight, *deps)
+
+
+def pair_grad_kernel(rows_ref, pair_ref, *refs):
+    gate_ref, up_ref = refs[-2:]
+    inner = gate_ref.shape[2]
+    rows = rows_ref[0]
+    gate_ref[0] = dot_first(rows, pair_ref[0, :, :inner])
+    up_ref[0] = dot_first(rows, pair_ref[0, :, inner:])
+
+
+def pair_grads(x_rows, pair_back, *deps):
+    experts, span, inner = pair_back.shape
+    inner = inner // 2
+    return pl.pallas_call(
+        pair_grad_kernel,
+        grid=(experts,),
+        in_specs=[
+            per_expert(span, D),
             per_expert(span, 2 * inner),
-            per_expert(span, D),
+            *[pl.BlockSpec(memory_space=pl.ANY) for _ in deps],
+        ],
+        out_specs=[per_expert(D, inner)] * 2,
+        out_shape=[jax.ShapeDtypeStruct((experts, D, inner), F32)] * 2,
+        compiler_params=pltpu.CompilerParams(vmem_limit_bytes=VMEM_BYTES),
+        cost_estimate=cost(4 * experts * span * D * inner),
+        name="pair_grads",
+    )(x_rows, pair_back, *deps)
+
+
+def down_grad_kernel(mid_ref, cot_ref, scale_ref, *refs):
+    out_grad = (cot_ref[0].astype(F32) * scale_ref[0]).astype(BF)
+    refs[-1][0] = dot_first(mid_ref[0], out_grad)
+
+
+def down_grads(mid, cot_rows, scale, *deps):
+    experts, span, inner = mid.shape
+    return pl.pallas_call(
+        down_grad_kernel,
+        grid=(experts,),
+        in_specs=[
+            per_expert(span, inner),
             per_expert(span, D),
             per_expert(span, 1),
-            per_expert(inner, D),
-        ],
-        out_specs=[
-            pl.BlockSpec((rows, D), lambda i: (by_target(i), 0)),
-            per_expert(D, inner),
-            per_expert(D, inner),
-            per_expert(inner, D),
-        ],
-        out_shape=[
-            jax.ShapeDtypeStruct((sources * rows, D), BF),
-            jax.ShapeDtypeStruct((experts, D, inner), F32),
-            jax.ShapeDtypeStruct((experts, D, inner), F32),
-            jax.ShapeDtypeStruct((experts, inner, D), F32),
-        ],
-        scratch_shapes=[pltpu.VMEM((experts, span, D), BF)],
+            *[pl.BlockSpec(memory_space=pl.ANY) for _ in deps],
+        ],
+        out_specs=per_expert(inner, D),
+        out_shape=jax.ShapeDtypeStruct((experts, inner, D), F32),
         compiler_params=pltpu.CompilerParams(vmem_limit_bytes=VMEM_BYTES),
-        cost_estimate=LIGHT,
-        name="output_pass",
-    )(slots, mid, pair_back, x_rows, cot_rows, scale, down_weight)
+        cost_estimate=cost(2 * experts * span * D * inner),
+        name="down_grads",
+    )(mid, cot_rows, scale, *deps)
 
 
 def across(row):
@@ -432,6 +658,91 @@
         raw_ref[...] = raw
         sums.append(down(jnp.sum(raw * raw, axis=1, keepdims=True))[:1])
     sums_ref[...] = jnp.concatenate(sums, axis=0)
+
+
+def second_norm_kernel(pieces_ref, tokens_ref, gain_ref, middle_ref, hidden_ref):
+    middle = tokens_ref[...].astype(F32)
+    for k in range(pieces_ref.shape[0]):
+        middle = middle + pieces_ref[k].astype(F32)
+    middle_ref[...] = middle
+    scale = lax.rsqrt(jnp.mean(middle * middle, axis=1, keepdims=True) + EPSILON)
+    hidden = (middle * scale * gain_ref[...]).astype(BF)
+    for k in range(hidden_ref.shape[0]):
+        hidden_ref[k] = hidden
+
+
+def halve_kernel(rows_ref, left_ref, right_ref):
+    left_ref[...] = rows_ref[:, : D // 2]
+    right_ref[...] = rows_ref[:, D // 2 :]
+
+
+def middle_back_kernel(count, *refs):
+    (
+        middle_ref,
+        gain_ref,
+        gates_ref,
+        router_ref,
+        cot_ref,
+        grad_ref,
+        riding_ref,
+        norm_ref,
+    ) = refs[count:]
+    total = refs[0][...].astype(F32)
+    for piece_ref in refs[1:count]:
+        total = total + piece_ref[...].astype(F32)
+    gates = gates_ref[...]
+    gate_grad = total[:, D : D + EXPERTS]
+    logit_grad = (
+        gates * (gate_grad - jnp.sum(gates * gate_grad, axis=1, keepdims=True))
+    ).astype(BF)
+    grad_two = total[:, :D] + dot_last(logit_grad, router_ref[...])
+    middle = middle_ref[...]
+    scale = lax.rsqrt(jnp.mean(middle * middle, axis=1, keepdims=True) + EPSILON)
+    normal = middle * scale
+    norm_ref[...] = jnp.sum(grad_two * normal, axis=0, keepdims=True)
+    scaled = grad_two * gain_ref[...]
+    grad = cot_ref[...].astype(F32) + scale * (
+        scaled - normal * jnp.mean(scaled * normal, axis=1, keepdims=True)
+    )
+    grad_ref[...] = grad
+    low = grad.astype(BF)
+    side = jnp.concatenate([logit_grad.astype(F32), jnp.zeros_like(gates)], axis=1).astype(BF)
+    for k in range(riding_ref.shape[0]):
+        riding_ref[k, :, :D] = low
+        riding_ref[k, :, D:] = side
+
+
+def mixed_kernel(pieces_ref, middle_ref, out_ref):
+    total = middle_ref[...]
+    for k in range(pieces_ref.shape[0]):
+        total = total + pieces_ref[k].astype(F32)
+    out_ref[...] = total.astype(BF)
+
+
+def first_back_kernel(
+    pieces_ref, grad_ref, tokens_ref, gain_ref, mixed_ref, out_ref, norms_ref
+):
+    total = pieces_ref[0].astype(F32)
+    for k in range(1, pieces_ref.shape[0]):
+        total = total + pieces_ref[k].astype(F32)
+    norms_ref[...] = total[: norms_ref.shape[0], D:]
+    total = total[:, :D]
+    inputs = tokens_ref[...].astype(F32)
+    scale = lax.rsqrt(jnp.mean(inputs * inputs, axis=1, keepdims=True) + EPSILON)
+    normal = inputs * scale
+    scaled = total * gain_ref[...]
+    grad = grad_ref[...] + scale * (
+        scaled - normal * jnp.mean(scaled * normal, axis=1, keepdims=True)
+    )
+    low = grad.astype(BF)
+    for k in range(out_ref.shape[0]):
+        out_ref[k, :, :D] = low
+        out_ref[k, :, D:] = mixed_ref[...]
+
+
+def pack_kernel(cot_ref, route_ref, out_ref):
+    out_ref[:, :D] = cot_ref[...]
+    out_ref[:, D:] = route_ref[...]
 
 
 def rope_kernel(query_ref, key_ref, sums_ref, qgain_ref, kgain_ref, cos_ref, sin_ref, q_ref, k_ref):
@@ -446,14 +757,21 @@
             out_ref[:, at] = turned(normed, cosine, sine).astype(BF)
 
 
-def small_call(kernel, name, out_shape, *operands):
+def small_call(kernel, name, out_shape, *operands, deps=(), work=LIGHT):
+    count = len(operands)
+
+    def run(*refs):
+        kernel(*refs[:count], *refs[count + len(deps) :])
+
     return pl.pallas_call(
-        kernel,
+        run,
+        in_specs=[pl.BlockSpec(memory_space=pltpu.VMEM)] * count
+        + [pl.BlockSpec(memory_space=pl.ANY)] * len(deps),
         out_shape=out_shape,
         compiler_params=pltpu.CompilerParams(vmem_limit_bytes=VMEM_BYTES),
-        cost_estimate=LIGHT,
+        cost_estimate=work,
         name=name,
-    )(*operands)
+    )(*operands, *deps)
 
 
 def probabilities(query, keys, allowed):
@@ -496,7 +814,8 @@
         key_name_ref,
         weight_ref,
         attended_ref,
-        hidden_ref,
+        left_ref,
+        right_ref,
         middle_ref,
         raw_ref,
         sums_ref,
@@ -509,12 +828,25 @@
         mine_ref,
         other_ref,
         weight_grad_ref,
-        router_ref,
     ) = refs[1 + 2 * blocks :]
     rows, width = query_ref.shape
     middle = middle_ref[:, :D]
-    weight_grad_ref[...] = dot_first(attended_ref[...], middle).astype(BF)
-    router_ref[...] = dot_first(hidden_ref[...], middle_ref[:, D:])[:, :EXPERTS].astype(BF)
+    count, height, _ = weight_grad_ref.shape
+    out_rows, router_rows = width // count, EXPERTS // count
+    weight_grad = dot_first(attended_ref[...], middle)
+    router_grad = jnp.concatenate(
+        [dot_first(middle_ref[:, D:], half[...]) for half in (left_ref, right_ref)], axis=1
+    )
+    spare = jnp.zeros((height - out_rows - router_rows, D), F32)
+    for k in range(count):
+        weight_grad_ref[k] = jnp.concatenate(
+            [
+                weight_grad[k * out_rows : (k + 1) * out_rows],
+                router_grad[k * router_rows : (k + 1) * router_rows],
+                spare,
+            ],
+            axis=0,
+        ).astype(BF)
     out_grad = dot_last(middle, weight_ref[...]).astype(BF)
     allowed = allowed_pairs(place_ref, name_ref, key_place_ref, key_name_ref)
     cosine, sine = cos_ref[...], -sin_ref[...]
@@ -590,6 +922,7 @@
 
 
 def input_back_kernel(
+    copies,
     query_back_ref,
     key_back_ref,
     value_grad_ref,
@@ -604,13 +937,13 @@
     value_weight_ref,
     tokens_ref,
     norm2_ref,
-    qgain_grad_ref,
-    kgain_grad_ref,
+    late_ref,
     riding_ref,
     part_ref,
 ):
     rows, width = query_raw_ref.shape
-    riding_ref[...] = jnp.zeros(riding_ref.shape, BF)
+    if riding_ref.shape[0] > rows:
+        riding_ref[rows:, : 3 * width] = jnp.zeros((riding_ref.shape[0] - rows, 3 * width), BF)
     for row, (back_ref, raw_ref, gain_ref) in enumerate(
         ((query_back_ref, query_raw_ref, qgain_ref), (key_back_ref, key_raw_ref, kgain_ref))
     ):
@@ -627,21 +960,89 @@
         + dot_last(riding_ref[:rows, width : 2 * width], key_weight_ref[...])
         + dot_last(riding_ref[:rows, 2 * width : 3 * width], value_weight_ref[...])
     )
-    part_ref[...] = part.astype(BF)
+    part_ref[:, :D] = part.astype(BF)
     inputs = tokens_ref[...].astype(F32)
     normal = inputs * lax.rsqrt(jnp.mean(inputs * inputs, axis=1, keepdims=True) + EPSILON)
     norm1 = jnp.sum(part * normal, axis=0, keepdims=True)
-    lines = [jnp.concatenate([qgain_grad_ref[...], kgain_grad_ref[...]], axis=1)]
-    for norm in (norm1, norm2_ref[...]):
-        for start in range(0, D, 2 * width):
-            lines.append(norm[:, start : start + 2 * width])
-    lines.append(jnp.zeros((-len(lines) % 16, 2 * width), F32))
-    riding_ref[rows:, : 2 * width] = jnp.concatenate(lines, axis=0).astype(BF)
-
-
-def weight_grad_kernel(count, *refs):
+    norms = jnp.concatenate(
+        [norm[:, at : at + 128] for norm in (norm1, norm2_ref[...]) for at in range(0, D, 128)],
+        axis=0,
+    ).astype(BF)
+    own_rows = rows // copies
+    spare = jnp.zeros((own_rows - norms.shape[0], 128), BF)
+    for k in range(copies):
+        part_ref[k * own_rows : (k + 1) * own_rows, D:] = jnp.concatenate([norms, spare], axis=0) if (
+            spare.shape[0]
+        ) else norms
+    late, height = riding_ref.shape[1] - 3 * width, late_ref.shape[0]
+    riding_ref[:, 3 * width :] = jnp.zeros((riding_ref.shape[0], late), BF)
+    for k, start in enumerate(range(0, D, late)):
+        stop = min(start + late, D)
+        riding_ref[k * height : (k + 1) * height, 3 * width : 3 * width + stop - start] = late_ref[
+            :, start:stop
+        ]
+
+
+def place_kernel(count, first, rows, height, *refs):
+    piece_refs = refs[1 : 1 + count]
+    out_ref, side_ref, held, arrived = refs[-4:]
+    step = pl.program_id(0)
+
+    def fetch(s):
+        return pltpu.make_async_copy(
+            piece_refs[s].at[:, first:], held.at[s % 2], arrived.at[s % 2]
+        )
+
+    for s in range(count):
+
+        @pl.when(step == s)
+        def _(s=s):
+            if s == 0:
+                fetch(0).start()
+            if s + 1 < count:
+                fetch(s + 1).start()
+            fetch(s).wait()
+
+    late = D - first
+    slot = step % 2
+    for k, start in enumerate(range(0, D, late)):
+        stop = min(start + late, D)
+        block = held[slot, k * height : (k + 1) * height, : stop - start].astype(F32)
+        out_ref[:, start:stop] = block[:rows]
+        side_ref[0, :, start:stop] = block[rows:]
+
+
+def place_pieces(me, pieces, first, rows, height, *deps):
+    count = len(pieces)
+    return pl.pallas_call(
+        partial(place_kernel, count, first, rows, height),
+        grid_spec=pltpu.PrefetchScalarGridSpec(
+            num_scalar_prefetch=1,
+            grid=(count,),
+            in_specs=[pl.BlockSpec(memory_space=pl.ANY) for _ in (*pieces, *deps)],
+            out_specs=[
+                pl.BlockSpec((rows, D), lambda i, me_ref: (i ^ me_ref[0], 0)),
+                pl.BlockSpec((1, height - rows, D), lambda i, me_ref: (i ^ me_ref[0], 0, 0)),
+            ],
+            scratch_shapes=[
+                pltpu.VMEM((2, pieces[0].shape[0], D - first), BF),
+                pltpu.SemaphoreType.DMA((2,)),
+            ],
+        ),
+        out_shape=[
+            jax.ShapeDtypeStruct((count * rows, D), F32),
+            jax.ShapeDtypeStruct((count, height - rows, D), F32),
+        ],
+        compiler_params=pltpu.CompilerParams(vmem_limit_bytes=VMEM_BYTES),
+        cost_estimate=LIGHT,
+        name="place_pieces",
+    )(me, *pieces, *deps)
+
+
+def weight_grad_kernel(count, dep_count, *refs):
     hidden_refs, grad_refs = refs[:count], refs[count : 2 * count]
-    out_refs, (hidden, grads, arrived) = refs[2 * count : 2 * count + 3], refs[2 * count + 3 :]
+    refs = refs[2 * count + dep_count :]
+    out_refs, (hidden, grads, arrived) = refs[:3], refs[3:]
     step = pl.program_id(0)
     rows = hidden_refs[0].shape[0]
     width = out_refs[0].shape[1]
@@ -673,13 +1074,13 @@
             )
 
 
-def weight_grads(hidden_pieces, grad_pieces, width):
+def weight_grads(hidden_pieces, grad_pieces, width, *deps):
     count = len(hidden_pieces)
     rows = hidden_pieces[0].shape[0]
     return pl.pallas_call(
-        partial(weight_grad_kernel, count),
+        partial(weight_grad_kernel, count, len(deps)),
         grid=(3,),
-        in_specs=[pl.BlockSpec(memory_space=pl.ANY) for _ in range(2 * count)],
+        in_specs=[pl.BlockSpec(memory_space=pl.ANY) for _ in range(2 * count + len(deps))],
         out_specs=[
             pl.BlockSpec((D, width), lambda i: (0, 0), pipeline_mode=pl.Buffered(1))
             for _ in range(3)
@@ -691,9 +1092,9 @@
             pltpu.SemaphoreType.DMA((2 * count,)),
         ],
         compiler_params=pltpu.CompilerParams(vmem_limit_bytes=VMEM_BYTES),
-        cost_estimate=LIGHT,
+        cost_estimate=cost(6 * count * rows * D * width),
         name="weight_grads",
-    )(*hidden_pieces, *grad_pieces)
+    )(*hidden_pieces, *grad_pieces, *deps)
 
 
 def on_device(
@@ -737,8 +1138,6 @@
     first_expert = ep_at * local_experts
     router_rows = jnp.roll(router_weight.T, -first_expert, axis=0)
 
-    inputs = tokens.astype(F32)
-    scale_one = inverse_rms(inputs)
     hidden_one, value_low = small_call(
         normed_kernel,
         "normed",
@@ -784,6 +1183,7 @@
         kgain,
         cosine,
         sine,
+        deps=value_blocks[: len(hops)],
     )
     key_blocks = window(key_low)
     blocks = len(key_blocks)
@@ -818,29 +1218,41 @@
         output_weight,
     )
 
-    branch = sum_scatter(branch_part, "tp")
-    middle = own(inputs) + branch
-    scale_two = inverse_rms(middle)
-    normal_two = middle * scale_two
-    hidden_two = (normal_two * norm2_gain).astype(BF)
+    tokens_own = own(tokens)
+    wide_gain = norm2_gain[None]
+    middle, hidden_copies = small_call(
+        second_norm_kernel,
+        "second_norm",
+        [
+            jax.ShapeDtypeStruct((own_rows, D), F32),
+            jax.ShapeDtypeStruct((tp_count, own_rows, D), BF),
+        ],
+        to_owners(branch_part, "tp"),
+        tokens_own,
+        wide_gain,
+    )
     routes_own = own(routes)
-    logits = dot(hidden_two, router_weight)
+    logits = dot(hidden_copies[0], router_weight)
     chosen = jnp.any(
         routes_own[:, :, None] == jnp.arange(EXPERTS, dtype=jnp.int32)[None, None, :], axis=1
     )
     gates = jax.nn.softmax(jnp.where(chosen, logits, -MASKED), axis=1)
     gates = jnp.where(chosen, gates, 0.0)
 
-    cot_all = lax.all_gather(
-        after(
-            jnp.concatenate([cotangent, jnp.pad(routes, ((0, 0), (0, 120))).astype(BF)], axis=1),
-            key_blocks[0],
-        ),
-        "ep",
-        tiled=True,
-    )
+    cot_pack = small_call(
+        pack_kernel,
+        "pack",
+        jax.ShapeDtypeStruct((local_rows, D + 128), BF),
+        cotangent,
+        jnp.pad(routes, ((0, 0), (0, 128 - TOP))).astype(BF),
+        deps=key_blocks[: len(hops)],
+    )
+    cot_all = lax.all_gather(cot_pack, "ep", tiled=True)
+    me = ep_at.reshape(1).astype(jnp.int32)
+    order = ep_at ^ jnp.arange(ep_count, dtype=jnp.int32)
     routes_rel = (cot_all[:, D : D + TOP].astype(jnp.int32) - first_expert) % EXPERTS
-    routes_rel = jnp.swapaxes(routes_rel.reshape(ep_count, local_rows, TOP), 1, 2)
+    routes_rel = jnp.take(routes_rel.reshape(ep_count, local_rows, TOP), order, axis=0)
+    routes_rel = jnp.swapaxes(routes_rel, 1, 2)
     named = jnp.any(
         routes_rel[:, None, :, :]
         == jnp.arange(local_experts, dtype=jnp.int32)[None, :, None, None],
@@ -850,65 +1262,73 @@
         named.astype(BF), ahead, (((2,), (0,)), ((), ())), preferred_element_type=F32
     ).astype(jnp.int32)
     slots = jnp.where(named, ranks, -1)
-    cot_rows, back = cotangent_rows(slots, cot_all, down_weight)
-    hidden_pieces = gather_pieces(spread(hidden_two, "tp"), between=back)
-    x_rows, mid, pair_back, scale, inner, grad_part = expert_pass(
-        ep_at.reshape(1).astype(jnp.int32), slots, routes_rel, hidden_pieces, router_rows, gate_weight, up_weight, back
-    )
+    slots_across = jnp.swapaxes(slots, 1, 2)
+    cot_rows, back = cotangent_rows(me, slots, cot_all, down_weight)
+    left_rows, right_rows = small_call(
+        halve_kernel,
+        "halve",
+        [jax.ShapeDtypeStruct((local_rows, D // 2), BF)] * 2,
+        spread_ready(hidden_copies, "tp"),
+        deps=[back],
+    )
+    if ep_count == 8:
+        far_left, near_right = swap(left_rows, 4), swap(right_rows, 2)
+        near_left, far_right = swap(left_rows, 2), swap(right_rows, 4)
+        lefts = [left_rows, near_left, far_left, swap(far_left, 2)]
+        rights = [right_rows, near_right, far_right, swap(near_right, 4)]
+    else:
+        lefts, rights = (
+            [half] + [swap(half, d) for d in range(2, ep_count, 2)]
+            for half in (left_rows, right_rows)
+        )
+    hidden_pieces = with_odds(lefts) + with_odds(rights)
+    hidden_one_late = held_back(hidden_one, hidden_pieces[-1])
+    hidden_one_near = gather_near(hidden_one_late)
+    hidden_one_corner = [swap(hidden_one_late, 6)] if ep_count == 8 else []
+    x_rows, mid, pair_back, scale, grad_part = expert_pass(
+        me,
+        slots,
+        routes_rel,
+        slots_across,
+        hidden_pieces,
+        router_rows,
+        gate_weight,
+        up_weight,
+        back,
+    )
+    grad_part = held_back(grad_part, *hidden_one_near, *hidden_one_corner)
     grad_rows = lax.psum_scatter(grad_part, "ep", tiled=True)
-
-    inner_slots = jnp.swapaxes(inner.reshape(local_experts, ep_count, CAP), 0, 1)
-    inner_dense = jnp.sum(
-        jnp.where(
-            slots[:, :, :, None] == jnp.arange(CAP, dtype=jnp.int32), inner_slots[:, :, None, :], 0.0
-        ),
-        axis=3,
-    )
-    inner_send = jnp.swapaxes(inner_dense, 1, 2).reshape(
-        ep_count * tp_count, own_rows, local_experts
-    )
-    inner_got = lax.all_to_all(
-        inner_send, ("ep", "tp"), split_axis=0, concat_axis=0, tiled=True
-    ).reshape(ep_count, tp_count, own_rows, local_experts)
-    gate_grad = jnp.swapaxes(jnp.sum(inner_got, axis=1), 0, 1).reshape(own_rows, EXPERTS)
-    logit_grad = (
-        gates * (gate_grad - jnp.sum(gates * gate_grad, axis=1, keepdims=True))
-    ).astype(BF)
-    router_term = dot_last(logit_grad, router_weight)
-
-    mix_part, grad_gate, grad_up, grad_down = output_pass(
-        slots, after(mid, gate_grad), pair_back, x_rows, cot_rows, scale, down_weight
-    )
-
-    expert_grad = sum_scatter(after(grad_rows, mix_part), "tp")
-    upstream = own(cotangent).astype(F32)
-    grad_two = expert_grad + router_term
-    grad_norm2 = jnp.sum(grad_two * normal_two, axis=0)
-    scaled_two = grad_two * norm2_gain
-    grad_middle = upstream + scale_two * (
-        scaled_two - normal_two * jnp.mean(scaled_two * normal_two, axis=1, keepdims=True)
-    )
-    riding = jnp.concatenate(
+    out_rows = output_pass(mid, scale, down_weight)
+    mix_odd = add_up_odd(slots_across, out_rows)
+    grad_gate, grad_up = pair_grads(x_rows, pair_back, mix_odd)
+    mix_sums = add_up_even(slots_across, out_rows, swap(mix_odd, 1), grad_gate)
+    grad_down = down_grads(mid, cot_rows, scale, mix_sums[0])
+    grad_rows = held_back(grad_rows, grad_down)
+    mix_rows, mix_between = exchange(mix_sums, grad_rows)
+
+    grad_middle, riding, norm2_part = small_call(
+        partial(middle_back_kernel, tp_count),
+        "middle_back",
         [
-            grad_middle.astype(BF),
-            logit_grad,
-            jnp.pad(
-                grad_norm2.reshape(own_rows, D // own_rows).astype(BF),
-                ((0, 0), (0, 128 - EXPERTS - D // own_rows)),
-            ),
-        ],
-        axis=1,
-    )
-    middle_got = spread(riding, "tp").reshape(local_rows, D + 128)
-    norm2_part = jnp.sum(
-        middle_got[:, D + EXPERTS : D + EXPERTS + D // own_rows]
-        .astype(F32)
-        .reshape(tp_count, own_rows, D // own_rows),
-        axis=0,
-    ).reshape(1, D)
+            jax.ShapeDtypeStruct((own_rows, D), F32),
+            jax.ShapeDtypeStruct((tp_count, own_rows, WIDE), BF),
+            jax.ShapeDtypeStruct((1, D), F32),
+        ],
+        *to_owners_by_permutes(grad_rows),
+        middle,
+        wide_gain,
+        gates,
+        router_weight,
+        own(cotangent),
+        deps=[mix_between],
+    )
+    middle_got = spread_ready(riding, "tp")
 
     half_rows = blocks // 2 * local_rows
-    query_back, query_dots, grad_qgain, mine_grad, other_grad, grad_output, grad_router = small_call(
+    sums_rows = head_width // ep_count
+    sums_height = sums_rows + EXPERTS // ep_count
+    sums_height += -sums_height % 16
+    query_back, query_dots, grad_qgain, mine_grad, other_grad, sums_part = small_call(
         partial(attention_back_kernel, blocks),
         "attention_back",
         [
@@ -917,8 +1337,7 @@
             jax.ShapeDtypeStruct((1, head_width), F32),
             jax.ShapeDtypeStruct((half_rows, 2 * head_width), F32),
             jax.ShapeDtypeStruct((half_rows, 2 * head_width), BF),
-            jax.ShapeDtypeStruct((head_width, D), BF),
-            jax.ShapeDtypeStruct((D, EXPERTS), BF),
+            jax.ShapeDtypeStruct((ep_count, sums_height, D), BF),
         ],
         query_low,
         *key_blocks,
@@ -929,25 +1348,31 @@
         key_name,
         output_weight,
         attended_low,
-        hidden_pieces[0],
+        left_rows,
+        right_rows,
         middle_got,
         query_raw,
         square_sums,
         qgain,
         cosine,
         sine,
-    )
-    grad_output, grad_router = lax.psum((grad_output, grad_router), "ep")
-    mix_rows = lax.psum_scatter(after(mix_part, grad_rows), "ep", tiled=True)
-    moe_out = sum_scatter(after(mix_rows, other_grad), "tp")
-    mixed_out = spread((middle + moe_out).astype(BF), "tp")
+        deps=[mix_rows],
+        work=cost(200 * local_rows * head_width * blocks * local_rows),
+    )
+    sums_own = lax.psum_scatter(sums_part.reshape(-1, D), "ep", tiled=True)
+    mixed_own = small_call(
+        mixed_kernel,
+        "mixed",
+        jax.ShapeDtypeStruct((own_rows, D), BF),
+        to_owners(mix_rows, "tp"),
+        middle,
+    )
     got_grad = swap(other_grad, 1)
     parts = []
     for number, hop in enumerate(hops):
         at = slice(number * local_rows, (number + 1) * local_rows)
         part = (mine_grad[at] + got_grad[at].astype(F32)).astype(BF)
         parts.append(from_behind(part, "ep", -hop))
-    mine_grad = after(mine_grad, moe_out)
     key_back, value_grad_low, key_dots, grad_kgain = small_call(
         key_back_kernel,
         "key_back",
@@ -966,17 +1391,17 @@
         cosine,
         sine,
     )
-    dots = tiny_sum(jnp.concatenate([query_dots[:1], key_dots[:1]], axis=0))
-    line_width = 2 * head_width
-    norm_lines = D // line_width
-    extra_rows = 1 + 2 * norm_lines
-    extra_rows += -extra_rows % 16
+    dots = tiny_sum(
+        held_back(jnp.concatenate([query_dots[:1], key_dots[:1]], axis=0), mixed_own)
+    )
+    late_width = D - 3 * head_width
+    riding_rows = max(local_rows, -(-D // late_width) * sums_height)
     grads_riding, one_part = small_call(
-        input_back_kernel,
+        partial(input_back_kernel, tp_count),
         "input_back",
         [
-            jax.ShapeDtypeStruct((local_rows + extra_rows, 3 * head_width), BF),
-            jax.ShapeDtypeStruct((local_rows, D), BF),
+            jax.ShapeDtypeStruct((riding_rows, D), BF),
+            jax.ShapeDtypeStruct((local_rows, WIDE), BF),
         ],
         query_back,
         key_back,
@@ -992,39 +1417,42 @@
         value_weight,
         tokens,
         norm2_part,
-        grad_qgain,
-        grad_kgain,
-    )
-    grad_pieces = gather_pieces(grads_riding)
-    extra_all = sum(piece[local_rows:].astype(F32) for piece in grad_pieces)
-    grad_qgain = extra_all[0, :head_width]
-    grad_kgain = extra_all[0, head_width:line_width]
-    grad_norm1 = extra_all[1 : 1 + norm_lines, :line_width].reshape(own_rows, D // own_rows)
-    grad_norm2 = extra_all[1 + norm_lines : 1 + 2 * norm_lines, :line_width].reshape(D)
-    grad_one = sum_scatter(one_part, "tp")
-    normal_one = own(inputs * scale_one)
-    scaled_one = grad_one * norm1_gain
-    grad_input_own = grad_middle + own(scale_one) * (
-        scaled_one - normal_one * jnp.mean(scaled_one * normal_one, axis=1, keepdims=True)
-    )
-    input_got = spread(
+        sums_own,
+    )
+    grads_near = gather_near(grads_riding)
+    input_copies, norms = small_call(
+        first_back_kernel,
+        "first_back",
+        [
+            jax.ShapeDtypeStruct((tp_count, own_rows, 2 * D), BF),
+            jax.ShapeDtypeStruct((2 * D // 128, 128), F32),
+        ],
+        to_owners(one_part, "tp"),
+        grad_middle,
+        tokens_own,
+        norm1_gain[None],
+        mixed_own,
+        deps=grads_near,
+    )
+    side_sums = ep_sum(
         jnp.concatenate(
-            [
-                grad_input_own.astype(BF),
-                jnp.pad(grad_norm1.astype(BF), ((0, 0), (0, 128 - D // own_rows))),
-            ],
-            axis=1,
-        ),
-        "tp",
-    )
-    grad_input = input_got[:, :D].astype(F32)
-    grad_norm1 = jnp.sum(
-        input_got[:, D : D + D // own_rows].astype(F32).reshape(tp_count, D), axis=0
-    )
-
-    hidden_one_pieces = gather_pieces(after(hidden_one, hidden_pieces[-1]), False)
-    grad_query, grad_key, grad_value = weight_grads(hidden_one_pieces, grad_pieces, head_width)
-    grad_output, grad_router = grad_output.astype(F32), grad_router.astype(F32)
+            [norms, grad_qgain.reshape(-1, 128), grad_kgain.reshape(-1, 128)], axis=0
+        )
+    )
+    grads_corner = gather_corner(grads_near, [norms], [side_sums])
+    grad_pieces = with_odds([grads_riding] + grads_near + grads_corner)
+    grad_norm1, grad_norm2 = side_sums[: 2 * D // 128].reshape(2, D)
+    grad_qgain, grad_kgain = side_sums[2 * D // 128 :].reshape(2, head_width)
+    last_got = spread_ready(input_copies, "tp")
+    grad_input, mixed_out = last_got[:, :D].astype(F32), last_got[:, D:]
+    hidden_one_pieces = with_odds([hidden_one_late] + hidden_one_near + hidden_one_corner)
+    grad_query, grad_key, grad_value = weight_grads(
+        hidden_one_pieces, grad_pieces, head_width, last_got
+    )
+    grad_output, router_side = place_pieces(
+        me, grad_pieces, 3 * head_width, sums_rows, sums_height, grad_query
+    )
+    grad_router = router_side[:, : EXPERTS // ep_count].reshape(EXPERTS, D).T
     return (
         mixed_out,
         grad_input,

time: 666 us -> 610 us (0.916)
  Pallas kernels: 181 us -> 258 us
  waiting for transfers between devices: 255 us -> 192 us
  blocking collectives: 58.3 us -> 8.11 us
  other arithmetic: 29.8 us -> 15.6 us
  starting transfers between devices: 87.9 us -> 79.6 us
    pallas_call x10 -> x31, Pallas kernels: 138 us -> 211 us  [the longest x15 68.2 us: small_call(): pl.pallas_call(run, in_specs=[pl.BlockSpec(memory_space=pltpu.VMEM)] * co...]
    ppermute x30 -> x44, waiting for transfers between devices: 52.4 us -> 109 us  [swap(): return lax.ppermute(value, 'ep', [(i, i ^ distance) for i in range(count)])]
    psum x1 -> x0, waiting for transfers between devices: 52.5 us -> none  [on_device(): grad_output, grad_router = lax.psum((grad_output, grad_router), 'ep')]
    all_to_all x2 -> x1, blocking collectives: 58.3 us -> 8.11 us  [spread(): lax.all_to_all(jnp.broadcast_to(value[None], (count,) + value.shape), axi...]
    all_to_all x4 -> x1, waiting for transfers between devices: 29.3 us -> 3.45 us  [spread(): lax.all_to_all(jnp.broadcast_to(value[None], (count,) + value.shape), axi...]
    reduce_scatter x1, waiting for transfers between devices: 24.1 us -> 0.01 us  [on_device(): grad_rows = lax.psum_scatter(grad_part, 'ep', tiled=True)]
    ppermute x6, waiting for transfers between devices: 20 us -> 7.02 us  [from_behind(): lax.ppermute(value, axis, [(source, source + steps) for source in range(i...]
    all_to_all x4 -> x1, starting transfers between devices: 17.6 us -> 4.88 us  [spread(): lax.all_to_all(jnp.broadcast_to(value[None], (count,) + value.shape), axi...]
  transfers between devices with their start and end apart: 49 -> 63, of which waited for: 21 -> 24; matrix products, arithmetic and copies ran while one was open for 7% -> 5% of each run, Pallas kernels for 18% -> 31%
where the time goes in v3:
time: 610 us; the launch traced here: 599 us
  Pallas kernels  258 us (42%)
  waiting for transfers between devices  192 us (31%)
  starting transfers between devices  79.6 us (13%)
  local copies, waits for them, and re-layouts  29.2 us (5%)
  other arithmetic  15.6 us (3%)
  between operations  14.9 us (2%)
  blocking collectives  8.11 us (1%)
    ppermute x44, waiting for transfers between devices, swap(): return lax.ppermute(value, 'ep', [(i, i ^ distance) for i in range(count)])  109 us
    pallas_call x15, Pallas kernels, small_call(): pl.pallas_call(run, in_specs=[pl.BlockSpec(memory_space=pltpu.VMEM)] * co...  68.2 us
    pallas_call x1, Pallas kernels, expert_pass(): pl.pallas_call(partial(expert_kernel, sources, experts), grid_spec=pltpu....  46.6 us
    all_to_all x3, waiting for transfers between devices, to_owners(): lax.all_to_all(value.reshape(count, rows // count, width), axis, split_ax...  45 us
    ppermute x44, starting transfers between devices, swap(): return lax.ppermute(value, 'ep', [(i, i ^ distance) for i in range(count)])  29.5 us
    pallas_call x1, Pallas kernels, down_grads(): pl.pallas_call(down_grad_kernel, grid=(experts,), in_specs=[per_expert(sp...  29.4 us
    pallas_call x1, Pallas kernels, weight_grads(): pl.pallas_call(partial(weight_grad_kernel, count, len(deps)), grid=(3,),...  24 us
    pallas_call x1, Pallas kernels, pair_grads(): pl.pallas_call(pair_grad_kernel, grid=(experts,), in_specs=[per_expert(sp...  21.9 us
  transfers between devices with their start and end apart: 63, of which 24 were waited for; matrix products, arithmetic and copies ran while one was open for 5% of the time, Pallas kernels for 31%

profile of v3, /device:TPU:0, one launch (start us, length us, event | category | flops | bytes accessed | tf_op | source)
XLA Modules:
  0.0 599.1 jit_solution(6273927879255903521)
XLA Ops:
  10.8 4.9 collective-permute-start
  19.1 4.6 projected.1
  24.9 4.9 all-to-all-start
  43.4 7.0 %collective-permute-done.2.refs_1_.refs_2_ = bf16[256,512]{1,0:T(8,128)(2,1)S(1)} collective-permute-done((bf16[256,512]{1,0:T(8,128)(2,1)}, bf16[256,512]{1,0:T(8,128)(2,1)S(1)}, u32[]{:S(2)}, u32[]{:S(2)}) %collective-permute-start.2) | collective-permute-done | bytes 262176 | tf_op jit(solution)/shard_map/ppermute | solution.py:32
  59.9 9.1 %attention.1 = (bf16[256,512]{1,0:T(8,128)(2,1)}, bf16[256,2048]{1,0:T(8,128)(2,1)}) custom-call(bf16[256,512]{1,0:T(8,128)(2,1)} %get-tuple-element.73.refs_0_, bf16[256,512]{1,0:T(8,128)(2,1)} %copy-done.17, bf16[256,512]{1,0:T(8,128)(2,1)} %copy-done.18, bf16[256,512]{1,0:T(8,128)(2,1)} %get-tuple-element.74.refs_3_, bf16[256,512]{1,0:T(8,128)(2,1)} %copy-done.36, ...), custom_call_target="tpu_custom_call" | custom-call | flops 1 | bytes 1 | tf_op jit(solution)/shard_map/attention/pallas_call | solution.py:766
  74.1 24.5 %all-to-all-done.1.refs_0_ = bf16[4,64,2048]{2,1,0:T(8,128)(2,1)S(1)} async-done(((bf16[4,64,2048]{2,1,0:T(8,128)(2,1)}), bf16[4,64,2048]{2,1,0:T(8,128)(2,1)S(1)}, u32[]{:S(2)}, u32[]{:S(2)}) %all-to-all-start.1) | async-done | bytes 1048608 | tf_op jit(solution)/shard_map/all_to_all | solution.py:65
  114.2 21.8 %cotangent_rows.1 = (bf16[8,512,2048]{2,1,0:T(8,128)(2,1)}, f32[8,512,256]{2,1,0:T(8,128)}) custom-call(s32[1]{0:T(128)} %bitcast.19.me_ref.refs_0_, s32[8,8,256]{2,1,0:T(8,128)} %copy.85.slot_ref, bf16[2048,2176]{1,0:T(8,128)(2,1)} %all-gather.2.cloned.1.call-done.cot_ref, bf16[8,256,2048]{2,1,0:T(8,128)(2,1)} %down_ref.3), custom_call_target="tpu_custom_call" | custom-call | flops 1 | bytes 1 | tf_op jit(solution)/shard_map/cotangent_rows/pallas_call | solution.py:215
  141.3 12.3 %collective-permute-done.18.refs_10_ = bf16[256,1024]{1,0:T(8,128)(2,1)S(1)} collective-permute-done((bf16[256,1024]{1,0:T(8,128)(2,1)}, bf16[256,1024]{1,0:T(8,128)(2,1)S(1)}, u32[]{:S(2)}, u32[]{:S(2)}) %collective-permute-start.18) | collective-permute-done | bytes 524320 | tf_op jit(solution)/shard_map/ppermute | solution.py:72
  157.7 10.7 %collective-permute-done.22.refs_14_ = bf16[256,1024]{1,0:T(8,128)(2,1)S(1)} collective-permute-done((bf16[256,1024]{1,0:T(8,128)(2,1)S(1)}, bf16[256,1024]{1,0:T(8,128)(2,1)S(1)}, u32[]{:S(2)}, u32[]{:S(2)}) %collective-permute-start.22) | collective-permute-done | bytes 524320 | tf_op jit(solution)/shard_map/ppermute | solution.py:72
  170.4 7.8 %collective-permute-done.20.refs_12_ = bf16[256,1024]{1,0:T(8,128)(2,1)} collective-permute-done((bf16[256,1024]{1,0:T(8,128)(2,1)}, bf16[256,1024]{1,0:T(8,128)(2,1)}, u32[]{:S(2)}, u32[]{:S(2)}) %collective-permute-start.20) | collective-permute-done | bytes 524320 | tf_op jit(solution)/shard_map/ppermute | solution.py:72
  184.2 46.6 %expert_pass.1 = (bf16[8,512,2048]{2,1,0:T(8,128)(2,1)}, bf16[8,512,256]{2,1,0:T(8,128)(2,1)}, bf16[8,512,512]{2,1,0:T(8,128)(2,1)}, f32[8,512,1]{2,1,0:T(8,128)}, bf16[2048,2176]{1,0:T(8,128)(2,1)}) custom-call(s32[1]{0:T(128)} %bitcast.19.me_ref.refs_0_, s32[8,8,256]{2,1,0:T(8,128)} %copy.85.slot_ref, s32[8,8,256]{2,1,0:T(8,128)} %copy-done.38, ...), custom_call_target="tpu_custom_call" | custom-call | flops 21474836480 | bytes 1 | tf_op jit(solution)/shard_map/expert_pass/pallas_call | solution.py:351
  230.8 14.8 %output_pass.1.rows_ref = bf16[8,512,2048]{2,1,0:T(8,128)(2,1)} custom-call(bf16[8,512,256]{2,1,0:T(8,128)(2,1)} %get-tuple-element.82.mid_ref, f32[8,512,1]{2,1,0:T(8,128)} %get-tuple-element.84.scale_ref, bf16[8,256,2048]{2,1,0:T(8,128)(2,1)} %down_ref.3), custom_call_target="tpu_custom_call" | custom-call | flops 4294967296 | bytes 1 | tf_op jit(solution)/shard_map/output_pass/pallas_call | solution.py:559
  245.6 8.4 %add_up_odd.1.refs_0_ = bf16[4,256,2048]{2,1,0:T(8,128)(2,1)} custom-call(s32[8,256,8]{2,1,0:T(8,128)} %bitcast.67, bf16[8,512,2048]{2,1,0:T(8,128)(2,1)} %output_pass.1.rows_ref), custom_call_target="tpu_custom_call" | custom-call | flops 1 | bytes 1 | tf_op jit(solution)/shard_map/add_up_odd/pallas_call | solution.py:409
  256.8 21.9 %pair_grads.1 = (f32[8,2048,256]{2,1,0:T(8,128)}, f32[8,2048,256]{2,1,0:T(8,128)}) custom-call(bf16[8,512,2048]{2,1,0:T(8,128)(2,1)} %get-tuple-element.85.rows_ref, bf16[8,512,512]{2,1,0:T(8,128)(2,1)} %get-tuple-element.86.pair_ref, bf16[4,256,2048]{2,1,0:T(8,128)(2,1)} %add_up_odd.1.refs_0_), custom_call_target="tpu_custom_call" | custom-call | flops 8589934592 | bytes 1 | tf_op jit(solution)/shard_map/pair_grads/pallas_call | solution.py:587
  278.7 10.4 %add_up_even.1 = (bf16[2,256,1024]{2,1,0:T(8,128)(2,1)}, bf16[2,256,1024]{2,1,0:T(8,128)(2,1)}, f32[256,1024]{1,0:T(8,128)}, f32[256,1024]{1,0:T(8,128)}, f32[256,1024]{1,0:T(8,128)}, /*index=5*/f32[256,1024]{1,0:T(8,128)}) custom-call(s32[8,256,8]{2,1,0:T(8,128)} %bitcast.68, bf16[8,512,2048]{2,1,0:T(8,128)(2,1)} %output_pass.1.rows_ref, ...), custom_call_target="tpu_custom_call" | custom-call | flops 1 | bytes 1 | tf_op jit(solution)/shard_map/add_up_even/pallas_call | solution.py:464
  289.1 29.4 %down_grads.1.refs_1_ = f32[8,256,2048]{2,1,0:T(8,128)} custom-call(bf16[8,512,256]{2,1,0:T(8,128)(2,1)} %get-tuple-element.82.mid_ref, bf16[8,512,2048]{2,1,0:T(8,128)(2,1)} %get-tuple-element.83.cot_ref, f32[8,512,1]{2,1,0:T(8,128)} %get-tuple-element.84.scale_ref, bf16[2,256,1024]{2,1,0:T(8,128)(2,1)} %get-tuple-element.88.refs_0_), custom_call_target="tpu_custom_call" | custom-call | flops 4294967296 | bytes 1 | tf_op jit(solution)/shard_map/down_grads/pallas_call | solution.py:610
  329.2 15.2 %collective-permute-done.31.near_ref = bf16[2,256,1024]{2,1,0:T(8,128)(2,1)S(1)} collective-permute-done((bf16[2,256,1024]{2,1,0:T(8,128)(2,1)}, bf16[2,256,1024]{2,1,0:T(8,128)(2,1)S(1)}, u32[]{:S(2)}, u32[]{:S(2)}) %collective-permute-start.31) | collective-permute-done | bytes 1048608 | tf_op jit(solution)/shard_map/ppermute | solution.py:72
  353.7 5.6 all-to-all-start.3
  360.6 10.9 %collective-permute-done.33.last_left_ref = bf16[256,1024]{1,0:T(8,128)(2,1)S(1)} collective-permute-done((bf16[256,1024]{1,0:T(8,128)(2,1)S(1)}, bf16[256,1024]{1,0:T(8,128)(2,1)S(1)}, u32[]{:S(2)}, u32[]{:S(2)}) %collective-permute-start.33) | collective-permute-done | bytes 524320 | tf_op jit(solution)/shard_map/ppermute | solution.py:72
  376.6 8.6 %all-to-all-done.3 = bf16[4,64,2176]{2,1,0:T(8,128)(2,1)S(1)} async-done(((bf16[4,64,2176]{2,1,0:T(8,128)(2,1)}), bf16[4,64,2176]{2,1,0:T(8,128)(2,1)S(1)}, u32[]{:S(2)}, u32[]{:S(2)}) %all-to-all-start.3) | async-done | bytes 1114144 | tf_op jit(solution)/shard_map/all_to_all | solution.py:129
  386.1 15.3 %attention_back.1 = (f32[256,512]{1,0:T(8,128)}, f32[8,256]{1,0:T(8,128)}, f32[1,512]{1,0:T(1,128)}, f32[768,1024]{1,0:T(8,128)}, bf16[768,1024]{1,0:T(8,128)(2,1)}, /*index=5*/bf16[8,80,2048]{2,1,0:T(8,128)(2,1)}) custom-call(bf16[256,512]{1,0:T(8,128)(2,1)} %get-tuple-element.73.refs_0_, bf16[256,512]{1,0:T(8,128)(2,1)} %copy-done.17, ...), custom_call_target="tpu_custom_call" | custom-call | flops 40265318400 | bytes 1 | tf_op jit(solution)/shard_map/attention_back/pallas_call | solution.py:766
  412.0 20.5 %all-to-all-done.4.refs_0_ = bf16[4,64,2048]{2,1,0:T(8,128)(2,1)} async-done(((bf16[4,64,2048]{2,1,0:T(8,128)(2,1)}), bf16[4,64,2048]{2,1,0:T(8,128)(2,1)}, u32[]{:S(2)}, u32[]{:S(2)}) %all-to-all-start.4) | async-done | bytes 1048608 | tf_op jit(solution)/shard_map/all_to_all | solution.py:65
  442.7 8.1 %all_to_all.40 = f32[4,2,256]{2,1,0:T(2,128)S(1)} all-to-all(f32[4,2,256]{2,1,0:T(2,128)S(1)} %broadcast_in_dim.81), channel_id=1, replica_groups=mesh['ep'=8,'tp'=4] {'tp'}, dimensions={0} | all-to-all | bytes 16384 | tf_op jit(solution)/shard_map/all_to_all | solution.py:119
  454.4 7.2 %input_back.1 = (bf16[320,2048]{1,0:T(8,128)(2,1)}, bf16[256,2176]{1,0:T(8,128)(2,1)}) custom-call(f32[256,512]{1,0:T(8,128)} %get-tuple-element.98.refs_0_, f32[256,512]{1,0:T(8,128)} %get-tuple-element.101.refs_1_, bf16[256,512]{1,0:T(8,128)(2,1)} %get-tuple-element.102.refs_2_, f32[256,512]{1,0:T(8,128)} %get-tuple-element.69.refs_0_.refs_22_.refs_3_, ...), custom_call_target="tpu_custom_call" | custom-call | flops 1 | bytes 1 | tf_op jit(solution)/shard_map/input_back/pallas_call | solution.py:766
  461.7 4.6 all-to-all-start.6
  466.2 7.6 %collective-permute-start.38 = (bf16[320,2048]{1,0:T(8,128)(2,1)}, bf16[320,2048]{1,0:T(8,128)(2,1)S(1)}, u32[]{:S(2)}, u32[]{:S(2)}) collective-permute-start(bf16[320,2048]{1,0:T(8,128)(2,1)} %get-tuple-element.109.refs_8_.refs_1_), channel_id=1, source_target_pairs={{0,8},{4,12},{8,0},{12,4},{16,24},{20,28},{24,16},{28,20},{1,9},{5... | collective-permute-start | bytes 3932168 | tf_op jit(solution)/shard_map/ppermute | solution.py:72
  473.8 26.9 %collective-permute-done.38.refs_5_.refs_0_.refs_10_.refs_3_ = bf16[320,2048]{1,0:T(8,128)(2,1)S(1)} collective-permute-done((bf16[320,2048]{1,0:T(8,128)(2,1)}, bf16[320,2048]{1,0:T(8,128)(2,1)S(1)}, u32[]{:S(2)}, u32[]{:S(2)}) %collective-permute-start.38) | collective-permute-done | bytes 1310752 | tf_op jit(solution)/shard_map/ppermute | solution.py:72
  506.6 4.8 all-to-all-start.7
  525.0 13.0 %collective-permute-done.50.refs_0_ = bf16[320,1024]{1,0:T(8,128)(2,1)S(1)} collective-permute-done((bf16[320,1024]{1,0:T(8,128)(2,1)}, bf16[320,1024]{1,0:T(8,128)(2,1)S(1)}, u32[]{:S(2)}, u32[]{:S(2)}) %collective-permute-start.50) | collective-permute-done | bytes 655392 | tf_op jit(solution)/shard_map/ppermute | solution.py:72
  544.4 12.0 %all-to-all-done.7 = bf16[4,64,4096]{2,1,0:T(8,128)(2,1)} async-done(((bf16[4,64,4096]{2,1,0:T(8,128)(2,1)}), bf16[4,64,4096]{2,1,0:T(8,128)(2,1)}, u32[]{:S(2)}, u32[]{:S(2)}) %all-to-all-start.7) | async-done | bytes 2097184 | tf_op jit(solution)/shard_map/all_to_all | solution.py:129
  560.0 24.0 %weight_grads.1 = (f32[2048,512]{1,0:T(8,128)}, f32[2048,512]{1,0:T(8,128)}, f32[2048,512]{1,0:T(8,128)}) custom-call(bf16[256,2048]{1,0:T(8,128)(2,1)} %held_back.6.refs_0_, bf16[256,2048]{1,0:T(8,128)(2,1)} %copy-done.45, bf16[256,2048]{1,0:T(8,128)(2,1)} %collective-permute-done.24.refs_1_.refs_2_, bf16[256,2048]{1,0:T(8,128)(2,1)} %collective-permute-done.44.refs_3_, ...), custom_call_target="tpu_custom_call" | custom-call | flops 12884901888 | bytes 1 | tf_op jit(solution)/shard_map/weight_grads/pallas_call | solution.py:1080
  584.0 6.3 %place_pieces.1 = (f32[512,2048]{1,0:T(8,128)}, f32[8,16,2048]{2,1,0:T(8,128)}) custom-call(s32[1]{0:T(128)} %bitcast.19.me_ref.refs_0_, bf16[320,2048]{1,0:T(8,128)(2,1)} %get-tuple-element.109.refs_8_.refs_1_, bf16[320,2048]{1,0:T(8,128)(2,1)} %collective-permute-done.47.refs_9_.refs_2_, bf16[320,2048]{1,0:T(8,128)(2,1)} %copy-done.1, ...), custom_call_target="tpu_custom_call" | custom-call | flops 1 | bytes 1 | tf_op jit(solution)/shard_map/place_pieces/pallas_call | solution.py:1017
  (309 shorter events, 154.7 us)
Async XLA Ops:
  10.8 25.2 %collective-permute-start = (bf16[256,512]{1,0:T(8,128)(2,1)}, bf16[256,512]{1,0:T(8,128)(2,1)S(1)}, u32[]{:S(2)}, u32[]{:S(2)}) collective-permute-start(bf16[256,512]{1,0:T(8,128)(2,1)} %get-tuple-element.72.refs_9_), channel_id=1, source_target_pairs={{0,16},{4,20},{8,24},{12,28},{1,17},{5,21},{9,25},{13,29},{2,18},{... | collective-permute-start | bytes 786440 | tf_op jit(solution)/shard_map/ppermute | solution.py:32
  15.6 20.4 %collective-permute-start.1 = (bf16[256,512]{1,0:T(8,128)(2,1)}, bf16[256,512]{1,0:T(8,128)(2,1)S(1)}, u32[]{:S(2)}, u32[]{:S(2)}) collective-permute-start(bf16[256,512]{1,0:T(8,128)(2,1)} %get-tuple-element.72.refs_9_), channel_id=1, source_target_pairs={{0,8},{4,12},{8,16},{12,20},{16,24},{20,28},{1,9},{5,13},{9,17},{1... | collective-permute-start | bytes 786440 | tf_op jit(solution)/shard_map/ppermute | solution.py:32
  29.8 79.9 %all-gather.2.cloned.1.call-start = ((), (), s32[]{:S(2)}) async-start(), calls=%async_computation.10 | async-start | bytes 10027008 | tf_op jit(solution)/shard_map/all_gather | solution.py:1250
  68.9 29.7 %all-to-all-start.1 = ((bf16[4,64,2048]{2,1,0:T(8,128)(2,1)}), bf16[4,64,2048]{2,1,0:T(8,128)(2,1)S(1)}, u32[]{:S(2)}, u32[]{:S(2)}) async-start(bf16[4,64,2048]{2,1,0:T(8,128)(2,1)} %bitcast.76), calls=%async_computation.1 | async-start | bytes 2097152 | tf_op jit(solution)/shard_map/all_to_all | solution.py:65
  102.2 33.8 %all-to-all-start.2 = ((bf16[4,64,2048]{2,1,0:T(8,128)(2,1)}), bf16[4,64,2048]{2,1,0:T(8,128)(2,1)S(1)}, u32[]{:S(2)}, u32[]{:S(2)}) async-start(bf16[4,64,2048]{2,1,0:T(8,128)(2,1)} %get-tuple-element.77), calls=%async_computation.2 | async-start | bytes 2097152 | tf_op jit(solution)/shard_map/all_to_all | solution.py:129
  105.7 212.8 %reduce-scatter.3.cloned.1.call-start = ((), (), s32[]{:S(2)}) async-start(), calls=%async_computation.11 | async-start | bytes 10027008 | tf_op jit(solution)/shard_map/reduce_scatter | solution.py:1300
  155.6 22.6 %collective-permute-start.20 = (bf16[256,1024]{1,0:T(8,128)(2,1)}, bf16[256,1024]{1,0:T(8,128)(2,1)}, u32[]{:S(2)}, u32[]{:S(2)}) collective-permute-start(bf16[256,1024]{1,0:T(8,128)(2,1)} %get-tuple-element.80.refs_8_.refs_20_), channel_id=1, source_target_pairs={{0,16},{4,20},{8,24},{12,28},{16,0},{20,4},{24,8},{28,12},{1,17},{... | collective-permute-start | bytes 1572872 | tf_op jit(solution)/shard_map/ppermute | solution.py:72
  157.2 22.1 %collective-permute-start.15 = (bf16[256,1024]{1,0:T(8,128)(2,1)S(1)}, bf16[256,1024]{1,0:T(8,128)(2,1)}, u32[]{:S(2)}, u32[]{:S(2)}) collective-permute-start(bf16[256,1024]{1,0:T(8,128)(2,1)S(1)} %collective-permute-done.13.refs_4_), channel_id=1, source_target_pairs={{0,8},{4,12},{8,0},{12,4},{16,24},{20,28},{24,16},{28,20},{1,9},{5... | collective-permute-start | bytes 1572872 | tf_op jit(solution)/shard_map/ppermute | solution.py:72
  180.6 50.1 %collective-permute-start.24 = (bf16[256,2048]{1,0:T(8,128)(2,1)}, bf16[256,2048]{1,0:T(8,128)(2,1)}, u32[]{:S(2)}, u32[]{:S(2)}) collective-permute-start(bf16[256,2048]{1,0:T(8,128)(2,1)} %held_back.6.refs_0_), channel_id=1, source_target_pairs={{0,8},{4,12},{8,0},{12,4},{16,24},{20,28},{24,16},{28,20},{1,9},{5... | collective-permute-start | bytes 3145736 | tf_op jit(solution)/shard_map/ppermute | solution.py:72
  181.6 49.2 %collective-permute-start.25 = (bf16[256,2048]{1,0:T(8,128)(2,1)}, bf16[256,2048]{1,0:T(8,128)(2,1)}, u32[]{:S(2)}, u32[]{:S(2)}) collective-permute-start(bf16[256,2048]{1,0:T(8,128)(2,1)} %held_back.6.refs_0_), channel_id=1, source_target_pairs={{0,16},{4,20},{8,24},{12,28},{16,0},{20,4},{24,8},{28,12},{1,17},{... | collective-permute-start | bytes 3145736 | tf_op jit(solution)/shard_map/ppermute | solution.py:72
  183.1 47.7 %collective-permute-start.26 = (bf16[256,2048]{1,0:T(8,128)(2,1)}, bf16[256,2048]{1,0:T(8,128)(2,1)}, u32[]{:S(2)}, u32[]{:S(2)}) collective-permute-start(bf16[256,2048]{1,0:T(8,128)(2,1)} %held_back.6.refs_0_), channel_id=1, source_target_pairs={{0,24},{4,28},{8,16},{12,20},{16,8},{20,12},{24,0},{28,4},{1,25},{... | collective-permute-start | bytes 3145736 | tf_op jit(solution)/shard_map/ppermute | solution.py:72
  254.0 24.7 %collective-permute-start.27 = (bf16[4,256,2048]{2,1,0:T(8,128)(2,1)}, bf16[4,256,2048]{2,1,0:T(8,128)(2,1)}, u32[]{:S(2)}, u32[]{:S(2)}) collective-permute-start(bf16[4,256,2048]{2,1,0:T(8,128)(2,1)} %add_up_odd.1.refs_0_), channel_id=1, source_target_pairs={{0,4},{4,0},{8,12},{12,8},{16,20},{20,16},{24,28},{28,24},{1,5},{5... | collective-permute-start | bytes 12582920 | tf_op jit(solution)/shard_map/ppermute | solution.py:72
  318.5 25.8 %collective-permute-start.31 = (bf16[2,256,1024]{2,1,0:T(8,128)(2,1)}, bf16[2,256,1024]{2,1,0:T(8,128)(2,1)S(1)}, u32[]{:S(2)}, u32[]{:S(2)}) collective-permute-start(bf16[2,256,1024]{2,1,0:T(8,128)(2,1)} %held_back.9), channel_id=1, source_target_pairs={{0,8},{4,12},{8,0},{12,4},{16,24},{20,28},{24,16},{28,20},{1,9},{5... | collective-permute-start | bytes 3145736 | tf_op jit(solution)/shard_map/ppermute | solution.py:72
  320.2 25.3 %collective-permute-start.32 = (bf16[2,256,1024]{2,1,0:T(8,128)(2,1)}, bf16[2,256,1024]{2,1,0:T(8,128)(2,1)S(1)}, u32[]{:S(2)}, u32[]{:S(2)}) collective-permute-start(bf16[2,256,1024]{2,1,0:T(8,128)(2,1)} %held_back.10), channel_id=1, source_target_pairs={{0,16},{4,20},{8,24},{12,28},{16,0},{20,4},{24,8},{28,12},{1,17},{... | collective-permute-start | bytes 3145736 | tf_op jit(solution)/shard_map/ppermute | solution.py:72
  323.9 25.4 %collective-permute-start.28 = (bf16[64,2176]{1,0:T(8,128)(2,1)S(1)}, bf16[64,2176]{1,0:T(8,128)(2,1)S(1)}, u32[]{:S(2)}, u32[]{:S(2)}) collective-permute-start(bf16[64,2176]{1,0:T(8,128)(2,1)S(1)} %get-tuple-element.128), channel_id=1, source_target_pairs={{0,1},{1,0},{2,3},{3,2},{4,5},{5,4},{6,7},{7,6},{8,9},{9,8},{10,11... | collective-permute-start | bytes 835592 | tf_op jit(solution)/shard_map/ppermute | solution.py:112
  325.4 23.9 %collective-permute-start.29 = (bf16[64,2176]{1,0:T(8,128)(2,1)S(1)}, bf16[64,2176]{1,0:T(8,128)(2,1)S(1)}, u32[]{:S(2)}, u32[]{:S(2)}) collective-permute-start(bf16[64,2176]{1,0:T(8,128)(2,1)S(1)} %get-tuple-element.127), channel_id=1, source_target_pairs={{0,2},{1,3},{2,0},{3,1},{4,6},{5,7},{6,4},{7,5},{8,10},{9,11},{10,... | collective-permute-start | bytes 835592 | tf_op jit(solution)/shard_map/ppermute | solution.py:112
  327.8 21.5 %collective-permute-start.30 = (bf16[64,2176]{1,0:T(8,128)(2,1)S(1)}, bf16[64,2176]{1,0:T(8,128)(2,1)S(1)}, u32[]{:S(2)}, u32[]{:S(2)}) collective-permute-start(bf16[64,2176]{1,0:T(8,128)(2,1)S(1)} %get-tuple-element.126), channel_id=1, source_target_pairs={{0,3},{1,2},{2,1},{3,0},{4,7},{5,6},{6,5},{7,4},{8,11},{9,10},{10,... | collective-permute-start | bytes 835592 | tf_op jit(solution)/shard_map/ppermute | solution.py:112
  353.7 31.5 %all-to-all-start.3 = ((bf16[4,64,2176]{2,1,0:T(8,128)(2,1)}), bf16[4,64,2176]{2,1,0:T(8,128)(2,1)S(1)}, u32[]{:S(2)}, u32[]{:S(2)}) async-start(bf16[4,64,2176]{2,1,0:T(8,128)(2,1)} %get-tuple-element.94), calls=%async_computation.4 | async-start | bytes 2228224 | tf_op jit(solution)/shard_map/all_to_all | solution.py:129
  359.3 95.2 %reduce-scatter.5.cloned.1.call-start = ((), (), s32[]{:S(2)}) async-start(), calls=%async_computation.12 | async-start | bytes 2949120 | tf_op jit(solution)/shard_map/reduce_scatter | solution.py:1362
  401.6 31.0 %all-to-all-start.4 = ((bf16[4,64,2048]{2,1,0:T(8,128)(2,1)}), bf16[4,64,2048]{2,1,0:T(8,128)(2,1)}, u32[]{:S(2)}, u32[]{:S(2)}) async-start(bf16[4,64,2048]{2,1,0:T(8,128)(2,1)} %bitcast.71), calls=%async_computation.5 | async-start | bytes 2097152 | tf_op jit(solution)/shard_map/all_to_all | solution.py:65
  408.7 26.0 %collective-permute-start.36 = (bf16[256,1024]{1,0:T(8,128)(2,1)}, bf16[256,1024]{1,0:T(8,128)(2,1)S(1)}, u32[]{:S(2)}, u32[]{:S(2)}) collective-permute-start(bf16[256,1024]{1,0:T(8,128)(2,1)} %get-tuple-element.123), channel_id=1, source_target_pairs={{16,0},{20,4},{24,8},{28,12},{17,1},{21,5},{25,9},{29,13},{18,2},{... | collective-permute-start | bytes 1572872 | tf_op jit(solution)/shard_map/ppermute | solution.py:32
  410.0 24.8 %collective-permute-start.37 = (bf16[256,1024]{1,0:T(8,128)(2,1)}, bf16[256,1024]{1,0:T(8,128)(2,1)S(1)}, u32[]{:S(2)}, u32[]{:S(2)}) collective-permute-start(bf16[256,1024]{1,0:T(8,128)(2,1)} %get-tuple-element.122), channel_id=1, source_target_pairs={{8,0},{12,4},{16,8},{20,12},{24,16},{28,20},{9,1},{13,5},{17,9},{2... | collective-permute-start | bytes 1572872 | tf_op jit(solution)/shard_map/ppermute | solution.py:32
  461.7 40.5 %all-to-all-start.6 = ((bf16[4,64,2176]{2,1,0:T(8,128)(2,1)}), bf16[4,64,2176]{2,1,0:T(8,128)(2,1)}, u32[]{:S(2)}, u32[]{:S(2)}) async-start(bf16[4,64,2176]{2,1,0:T(8,128)(2,1)} %bitcast.74), calls=%async_computation.8 | async-start | bytes 2228224 | tf_op jit(solution)/shard_map/all_to_all | solution.py:65
  466.2 34.5 %collective-permute-start.38 = (bf16[320,2048]{1,0:T(8,128)(2,1)}, bf16[320,2048]{1,0:T(8,128)(2,1)S(1)}, u32[]{:S(2)}, u32[]{:S(2)}) collective-permute-start(bf16[320,2048]{1,0:T(8,128)(2,1)} %get-tuple-element.109.refs_8_.refs_1_), channel_id=1, source_target_pairs={{0,8},{4,12},{8,0},{12,4},{16,24},{20,28},{24,16},{28,20},{1,9},{5... | collective-permute-start | bytes 3932168 | tf_op jit(solution)/shard_map/ppermute | solution.py:72
  473.8 28.4 %collective-permute-start.39 = (bf16[320,2048]{1,0:T(8,128)(2,1)}, bf16[320,2048]{1,0:T(8,128)(2,1)S(1)}, u32[]{:S(2)}, u32[]{:S(2)}) collective-permute-start(bf16[320,2048]{1,0:T(8,128)(2,1)} %get-tuple-element.109.refs_8_.refs_1_), channel_id=1, source_target_pairs={{0,16},{4,20},{8,24},{12,28},{16,0},{20,4},{24,8},{28,12},{1,17},{... | collective-permute-start | bytes 3932168 | tf_op jit(solution)/shard_map/ppermute | solution.py:72
  506.6 49.9 %all-to-all-start.7 = ((bf16[4,64,4096]{2,1,0:T(8,128)(2,1)}), bf16[4,64,4096]{2,1,0:T(8,128)(2,1)}, u32[]{:S(2)}, u32[]{:S(2)}) async-start(bf16[4,64,4096]{2,1,0:T(8,128)(2,1)} %get-tuple-element.110), calls=%async_computation.9 | async-start | bytes 4194304 | tf_op jit(solution)/shard_map/all_to_all | solution.py:129
  511.4 30.3 %collective-permute-start.43 = (bf16[256,2048]{1,0:T(8,128)(2,1)}, bf16[256,2048]{1,0:T(8,128)(2,1)S(1)}, u32[]{:S(2)}, u32[]{:S(2)}) collective-permute-start(bf16[256,2048]{1,0:T(8,128)(2,1)} %held_back.6.refs_0_), channel_id=1, source_target_pairs={{0,4},{4,0},{8,12},{12,8},{16,20},{20,16},{24,28},{28,24},{1,5},{5... | collective-permute-start | bytes 3145736 | tf_op jit(solution)/shard_map/ppermute | solution.py:72
  511.4 31.3 %collective-permute-start.44 = (bf16[256,2048]{1,0:T(8,128)(2,1)}, bf16[256,2048]{1,0:T(8,128)(2,1)}, u32[]{:S(2)}, u32[]{:S(2)}) collective-permute-start(bf16[256,2048]{1,0:T(8,128)(2,1)} %collective-permute-done.24.refs_1_.refs_2_), channel_id=1, source_target_pairs={{0,4},{4,0},{8,12},{12,8},{16,20},{20,16},{24,28},{28,24},{1,5},{5... | collective-permute-start | bytes 3145736 | tf_op jit(solution)/shard_map/ppermute | solution.py:72
  512.1 30.7 %collective-permute-start.45 = (bf16[256,2048]{1,0:T(8,128)(2,1)}, bf16[256,2048]{1,0:T(8,128)(2,1)}, u32[]{:S(2)}, u32[]{:S(2)}) collective-permute-start(bf16[256,2048]{1,0:T(8,128)(2,1)} %collective-permute-done.25.refs_2_.refs_4_), channel_id=1, source_target_pairs={{0,4},{4,0},{8,12},{12,8},{16,20},{20,16},{24,28},{28,24},{1,5},{5... | collective-permute-start | bytes 3145736 | tf_op jit(solution)/shard_map/ppermute | solution.py:72
  538.0 22.0 %collective-permute-start.47 = (bf16[320,2048]{1,0:T(8,128)(2,1)}, bf16[320,2048]{1,0:T(8,128)(2,1)}, u32[]{:S(2)}, u32[]{:S(2)}) collective-permute-start(bf16[320,2048]{1,0:T(8,128)(2,1)} %get-tuple-element.109.refs_8_.refs_1_), channel_id=1, source_target_pairs={{0,4},{4,0},{8,12},{12,8},{16,20},{20,16},{24,28},{28,24},{1,5},{5... | collective-permute-start | bytes 3932168 | tf_op jit(solution)/shard_map/ppermute | solution.py:72
  538.4 21.6 %collective-permute-start.48 = (bf16[320,2048]{1,0:T(8,128)(2,1)S(1)}, bf16[320,2048]{1,0:T(8,128)(2,1)}, u32[]{:S(2)}, u32[]{:S(2)}) collective-permute-start(bf16[320,2048]{1,0:T(8,128)(2,1)S(1)} %copy-done.2), channel_id=1, source_target_pairs={{0,4},{4,0},{8,12},{12,8},{16,20},{20,16},{24,28},{28,24},{1,5},{5... | collective-permute-start | bytes 3932168 | tf_op jit(solution)/shard_map/ppermute | solution.py:72
  541.8 18.2 %collective-permute-start.49 = (bf16[320,2048]{1,0:T(8,128)(2,1)S(1)}, bf16[320,2048]{1,0:T(8,128)(2,1)}, u32[]{:S(2)}, u32[]{:S(2)}) collective-permute-start(bf16[320,2048]{1,0:T(8,128)(2,1)S(1)} %copy-done.4), channel_id=1, source_target_pairs={{0,4},{4,0},{8,12},{12,8},{16,20},{20,16},{24,28},{28,24},{1,5},{5... | collective-permute-start | bytes 3932168 | tf_op jit(solution)/shard_map/ppermute | solution.py:72
  (83 other events, 719.0 us)
Sparse Core Ops, SparseCore 0:
  54.3 55.4 all-gather.1
  230.9 74.1 reduce-scatter.2
  401.6 52.7 reduce-scatter.4

commit v4 on v3

--- a/solution.py
+++ b/solution.py
@@ -75,25 +75,6 @@
 def gather_near(value):
     count = lax.axis_size("ep")
     return [swap(value, d) for d in range(2, count, 2)][: 2 if count == 8 else None]
-
-
-def gather_corner(near, before, between):
-    if len(near) != 2:
-        return []
-    rows, width = near[0].shape
-    half = jax.ShapeDtypeStruct((rows, width // 2), near[0].dtype)
-
-    def cut_kernel(near_ref, far_ref, low_ref, high_ref):
-        low_ref[...] = far_ref[:, : width // 2]
-        high_ref[...] = near_ref[:, width // 2 :]
-
-    def join_kernel(low_ref, high_ref, out_ref):
-        out_ref[:, : width // 2] = low_ref[...]
-        out_ref[:, width // 2 :] = high_ref[...]
-
-    low, high = small_call(cut_kernel, "cut", [half, half], *near, deps=before)
-    whole = jax.ShapeDtypeStruct((rows, width), near[0].dtype)
-    return [small_call(join_kernel, "join", whole, swap(low, 2), swap(high, 4), deps=between)]
 
 
 def with_odds(evens):
@@ -130,11 +111,6 @@
     return got.reshape(copies.shape[0] * copies.shape[1], copies.shape[2])
 
 
-def tiny_sum(value):
-    rows = value.shape[0]
-    return jnp.sum(spread(value, "tp").reshape(lax.axis_size("tp"), rows, value.shape[1]), axis=0)
-
-
 def held_back(value, *others):
     return pl.pallas_call(
         lambda *refs: None,
@@ -187,42 +163,48 @@
     sources, experts, me_ref, slot_ref, cot_ref, down_ref, rows_ref, back_ref, held
 ):
     step = pl.program_id(0)
-
-    @pl.when(step < sources)
+    pairs = sources // 2
+    rows = cot_ref.shape[0] // 2
+
+    @pl.when(step < pairs)
     def _():
-        found = dot(picks_for(slot_ref[0], experts), cot_ref[...]).astype(BF)
-        at = pl.ds(pl.multiple_of(step * CAP, CAP), CAP)
-        held[:, at, :] = found.reshape(experts, CAP, D)
-
-    @pl.when(step >= sources)
+        for t in range(2):
+            piece = cot_ref[pl.ds(pl.multiple_of((t ^ (me_ref[0] % 2)) * rows, rows), rows), :]
+            found = dot(picks_for(slot_ref[t], experts), piece).astype(BF)
+            at = pl.ds(pl.multiple_of((2 * step + t) * CAP, CAP), CAP)
+            held[:, at, :] = found.reshape(experts, CAP, D)
+
+    @pl.when(step >= pairs)
     def _():
-        rows = held[step - sources]
-        rows_ref[0] = rows
-        back_ref[0] = dot_last(rows, down_ref[0])
+        for t in range(2):
+            found = held[2 * (step - pairs) + t]
+            rows_ref[t] = found
+            back_ref[t] = dot_last(found, down_ref[t])
 
 
 def cotangent_rows(me, slots, cot_all, down_weight):
     sources, experts, rows = slots.shape
     inner = down_weight.shape[1]
     span = sources * CAP
+    pairs = sources // 2
 
     def by_source(i):
-        return jnp.minimum(i, sources - 1)
-
-    def per_expert(*shape):
-        return pl.BlockSpec((1,) + shape, lambda i, me_ref: (jnp.maximum(i - sources, 0), 0, 0))
+        return jnp.minimum(i, pairs - 1)
+
+    def two_experts(*shape):
+        return pl.BlockSpec((2,) + shape, lambda i, me_ref: (jnp.maximum(i - pairs, 0), 0, 0))
 
     return pl.pallas_call(
         partial(cotangent_kernel, sources, experts),
         grid_spec=pltpu.PrefetchScalarGridSpec(
             num_scalar_prefetch=1,
-            grid=(sources + experts,),
+            grid=(pairs + experts // 2,),
             in_specs=[
-                pl.BlockSpec((1, experts, rows), lambda i, me_ref: (by_source(i), 0, 0)),
-                pl.BlockSpec((rows, D), lambda i, me_ref: (by_source(i) ^ me_ref[0], 0)),
-                per_expert(inner, D),
+                pl.BlockSpec((2, experts, rows), lambda i, me_ref: (by_source(i), 0, 0)),
+                pl.BlockSpec((2 * rows, D), lambda i, me_ref: (by_source(i) ^ (me_ref[0] // 2), 0)),
+                two_experts(inner, D),
             ],
-            out_specs=[per_expert(span, D), per_expert(span, inner)],
+            out_specs=[two_experts(span, D), two_experts(span, inner)],
             scratch_shapes=[pltpu.VMEM((experts, span, D), BF)],
         ),
         out_shape=[
@@ -256,52 +238,58 @@
     step = pl.program_id(0)
     inner = gate_ref.shape[2]
 
-    def fetch(s):
-        slot = s % 2
-        return [
-            pltpu.make_async_copy(
-                left_refs[s], pieces.at[slot, :, : D // 2], arrived.at[slot, 0]
-            ),
-            pltpu.make_async_copy(
-                right_refs[s], pieces.at[slot, :, D // 2 :], arrived.at[slot, 1]
-            ),
-        ]
-
-    for s in range(sources):
+    pairs = sources // 2
+
+    def fetch(pair):
+        copies = []
+        for t in range(2):
+            s, slot = 2 * pair + t, 2 * (pair % 2) + t
+            copies += [
+                pltpu.make_async_copy(
+                    left_refs[s], pieces.at[slot, :, : D // 2], arrived.at[slot, 0]
+                ),
+                pltpu.make_async_copy(
+                    right_refs[s], pieces.at[slot, :, D // 2 :], arrived.at[slot, 1]
+                ),
+            ]
+        return copies
+
+    for s in range(pairs):
 
         @pl.when(step == s)
         def _(s=s):
-            for copy in (fetch(0) if s == 0 else []) + (fetch(s + 1) if s + 1 < sources else []):
+            for copy in (fetch(0) if s == 0 else []) + (fetch(s + 1) if s + 1 < pairs else []):
                 copy.start()
             for copy in fetch(s):
                 copy.wait()
 
-    @pl.when(step < sources)
+    @pl.when(step < pairs)
     def _():
-        x = pieces[step % 2]
-        logits = dot_last(router_ref[...], x)
-        routes = route_ref[0]
-        names = lax.broadcasted_iota(jnp.int32, logits.shape, 0)
-        chosen = routes[0:1] == names
-        for k in range(1, TOP):
-            chosen = chosen | (routes[k : k + 1] == names)
-        masked = jnp.where(chosen, logits, -MASKED)
-        top = jnp.max(masked, axis=0, keepdims=True)
-        weights = jnp.where(chosen, jnp.exp(masked - top), 0.0)
-        gates = weights / jnp.sum(weights, axis=0, keepdims=True)
-        slots = slot_ref[0]
-        parts = []
-        at = pl.ds(pl.multiple_of(step * CAP, CAP), CAP)
-        for e in range(experts):
-            pick = picks_of(slots[e : e + 1], CAP).astype(F32)
-            scales[e, at, :] = jnp.sum(pick * gates[e : e + 1], axis=1, keepdims=True)
-            parts.append(pick)
-        picks = jnp.concatenate(parts, axis=0).astype(BF)
-        held[:, at, :] = dot(picks, x).astype(BF).reshape(experts, CAP, D)
-
-    @pl.when((step >= sources) & (step < sources + experts))
+        for t in range(2):
+            x = pieces[2 * (step % 2) + t]
+            logits = dot_last(router_ref[...], x)
+            routes = route_ref[t]
+            names = lax.broadcasted_iota(jnp.int32, logits.shape, 0)
+            chosen = routes[0:1] == names
+            for k in range(1, TOP):
+                chosen = chosen | (routes[k : k + 1] == names)
+            masked = jnp.where(chosen, logits, -MASKED)
+            top = jnp.max(masked, axis=0, keepdims=True)
+            weights = jnp.where(chosen, jnp.exp(masked - top), 0.0)
+            gates = weights / jnp.sum(weights, axis=0, keepdims=True)
+            slots = slot_ref[t]
+            parts = []
+            at = pl.ds(pl.multiple_of((2 * step + t) * CAP, CAP), CAP)
+            for e in range(experts):
+                pick = picks_of(slots[e : e + 1], CAP).astype(F32)
+                scales[e, at, :] = jnp.sum(pick * gates[e : e + 1], axis=1, keepdims=True)
+                parts.append(pick)
+            picks = jnp.concatenate(parts, axis=0).astype(BF)
+            held[:, at, :] = dot(picks, x).astype(BF).reshape(experts, CAP, D)
+
+    @pl.when((step >= pairs) & (step < pairs + experts))
     def _():
-        e = step - sources
+        e = step - pairs
         rows = held[e]
         rows_ref[0] = rows
         gate_val = dot(rows, gate_ref[0])
@@ -323,13 +311,18 @@
         pair_ref[0, :, inner:] = up_back
         held[e] = (dot_last(gate_back, gate_ref[0]) + dot_last(up_back, up_ref[0])).astype(BF)
 
-    @pl.when(step >= sources + experts)
+    @pl.when(step >= pairs + experts)
     def _():
-        s = (step - sources - experts) ^ me_ref[0]
-        at = pl.ds(pl.multiple_of(s * CAP, CAP), CAP)
-        picks = picks_across(across_ref[0], experts)
-        sum_ref[:, :D] = dot(picks, held[:, at, :].reshape(experts * CAP, D)).astype(BF)
-        sum_ref[:, D:] = dot(picks, side[:, at, :].reshape(experts * CAP, WIDE - D)).astype(BF)
+        rows = sum_ref.shape[0] // 2
+        for t in range(2):
+            s = (2 * (step - pairs - experts) + t) ^ me_ref[0]
+            at = pl.ds(pl.multiple_of(s * CAP, CAP), CAP)
+            to = slice(t * rows, (t + 1) * rows)
+            picks = picks_across(across_ref[t ^ (me_ref[0] % 2)], experts)
+            sum_ref[to, :D] = dot(picks, held[:, at, :].reshape(experts * CAP, D)).astype(BF)
+            sum_ref[to, D:] = dot(picks, side[:, at, :].reshape(experts * CAP, WIDE - D)).astype(
+                BF
+            )
 
 
 def expert_pass(me, slots, routes, across, x_pieces, router_rows, gate_weight, up_weight, back):
@@ -337,27 +330,29 @@
     inner = gate_weight.shape[2]
     span = sources * CAP
 
+    pairs = sources // 2
+
     def by_source(i):
-        return jnp.minimum(i, sources - 1)
+        return jnp.minimum(i, pairs - 1)
 
     def by_target(i):
-        return jnp.maximum(i - sources - experts, 0)
+        return jnp.maximum(i - pairs - experts, 0)
 
     def by_expert(*shape):
         return pl.BlockSpec(
-            (1,) + shape, lambda i, me_ref: (jnp.clip(i - sources, 0, experts - 1), 0, 0)
+            (1,) + shape, lambda i, me_ref: (jnp.clip(i - pairs, 0, experts - 1), 0, 0)
         )
 
     return pl.pallas_call(
         partial(expert_kernel, sources, experts),
         grid_spec=pltpu.PrefetchScalarGridSpec(
             num_scalar_prefetch=1,
-            grid=(2 * sources + experts,),
+            grid=(2 * pairs + experts,),
             in_specs=[
-                pl.BlockSpec((1, experts, rows), lambda i, me_ref: (by_source(i), 0, 0)),
-                pl.BlockSpec((1, TOP, rows), lambda i, me_ref: (by_source(i), 0, 0)),
+                pl.BlockSpec((2, experts, rows), lambda i, me_ref: (by_source(i), 0, 0)),
+                pl.BlockSpec((2, TOP, rows), lambda i, me_ref: (by_source(i), 0, 0)),
                 pl.BlockSpec(
-                    (1, rows, experts), lambda i, me_ref: (by_target(i) ^ me_ref[0], 0, 0)
+                    (2, rows, experts), lambda i, me_ref: (by_target(i) ^ (me_ref[0] // 2), 0, 0)
                 ),
                 *[pl.BlockSpec(memory_space=pl.ANY) for _ in x_pieces],
                 pl.BlockSpec((EXPERTS, D), lambda i, me_ref: (0, 0)),
@@ -370,14 +365,14 @@
                 by_expert(span, inner),
                 by_expert(span, 2 * inner),
                 by_expert(span, 1),
-                pl.BlockSpec((rows, WIDE), lambda i, me_ref: (by_target(i), 0)),
+                pl.BlockSpec((2 * rows, WIDE), lambda i, me_ref: (by_target(i), 0)),
             ],
             scratch_shapes=[
                 pltpu.VMEM((experts, span, D), BF),
                 pltpu.VMEM((experts, span, WIDE - D), BF),
                 pltpu.VMEM((experts, span, 1), F32),
-                pltpu.VMEM((2, rows, D), BF),
-                pltpu.SemaphoreType.DMA((2, 2)),
+                pltpu.VMEM((4, rows, D), BF),
+                pltpu.SemaphoreType.DMA((4, 2)),
             ],
         ),
         out_shape=[
@@ -640,6 +635,13 @@
     return head * cosine + pltpu.roll(head, HEAD_DIM // 2, 1) * sine
 
 
+def total_row(pieces_ref, row):
+    total = pieces_ref[row : row + 1, :]
+    for start in range(8, pieces_ref.shape[0], 8):
+        total = total + pieces_ref[start + row : start + row + 1, :]
+    return total
+
+
 def scale_of(sums):
     return lax.rsqrt(sums / (HEADS * HEAD_DIM) + EPSILON)
 
@@ -656,8 +658,11 @@
     for weight_ref, raw_ref in ((query_weight_ref, query_ref), (key_weight_ref, key_ref)):
         raw = dot(hidden_ref[...], weight_ref[...])
         raw_ref[...] = raw
-        sums.append(down(jnp.sum(raw * raw, axis=1, keepdims=True))[:1])
-    sums_ref[...] = jnp.concatenate(sums, axis=0)
+        sums.append(down(jnp.sum(raw * raw, axis=1, keepdims=True)))
+    row = lax.broadcasted_iota(jnp.int32, sums[0].shape, 0)
+    both = jnp.where(row == 0, sums[0], sums[1])
+    for k in range(sums_ref.shape[0]):
+        sums_ref[k] = both
 
 
 def second_norm_kernel(pieces_ref, tokens_ref, gain_ref, middle_ref, hidden_ref):
@@ -712,16 +717,13 @@
         riding_ref[k, :, D:] = side
 
 
-def mixed_kernel(pieces_ref, middle_ref, out_ref):
-    total = middle_ref[...]
-    for k in range(pieces_ref.shape[0]):
-        total = total + pieces_ref[k].astype(F32)
-    out_ref[...] = total.astype(BF)
-
-
 def first_back_kernel(
-    pieces_ref, grad_ref, tokens_ref, gain_ref, mixed_ref, out_ref, norms_ref
+    pieces_ref, grad_ref, tokens_ref, gain_ref, mix_ref, middle_ref, out_ref, norms_ref
 ):
+    mixed = middle_ref[...]
+    for k in range(mix_ref.shape[0]):
+        mixed = mixed + mix_ref[k].astype(F32)
+    mixed = mixed.astype(BF)
     total = pieces_ref[0].astype(F32)
     for k in range(1, pieces_ref.shape[0]):
         total = total + pieces_ref[k].astype(F32)
@@ -737,7 +739,7 @@
     low = grad.astype(BF)
     for k in range(out_ref.shape[0]):
         out_ref[k, :, :D] = low
-        out_ref[k, :, D:] = mixed_ref[...]
+        out_ref[k, :, D:] = mixed
 
 
 def pack_kernel(cot_ref, route_ref, out_ref):
@@ -750,14 +752,14 @@
     for row, (raw_ref, gain_ref, out_ref) in enumerate(
         ((query_ref, qgain_ref, q_ref), (key_ref, kgain_ref, k_ref))
     ):
-        scale = across(scale_of(sums_ref[row : row + 1, :]))
+        scale = across(scale_of(total_row(sums_ref, row)))
         for number in range(raw_ref.shape[1] // HEAD_DIM):
             at = head_at(number)
             normed = raw_ref[:, at] * scale * gain_ref[:, at]
             out_ref[:, at] = turned(normed, cosine, sine).astype(BF)
 
 
-def small_call(kernel, name, out_shape, *operands, deps=(), work=LIGHT):
+def small_call(kernel, name, out_shape, *operands, deps=(), work=LIGHT, scratch=()):
     count = len(operands)
 
     def run(*refs):
@@ -768,6 +770,7 @@
         in_specs=[pl.BlockSpec(memory_space=pltpu.VMEM)] * count
         + [pl.BlockSpec(memory_space=pl.ANY)] * len(deps),
         out_shape=out_shape,
+        scratch_shapes=list(scratch),
         compiler_params=pltpu.CompilerParams(vmem_limit_bytes=VMEM_BYTES),
         cost_estimate=work,
         name=name,
@@ -786,36 +789,63 @@
     return (distance >= 0) & (distance < WINDOW) & (name_ref[...] == key_name_ref[...])
 
 
+def reached(refs, core, at):
+    half = len(refs) // 2
+    others = refs[half:]
+    blocks = [ref[:, at] for ref in refs[:half]]
+    for earlier, later in zip(others[:-1], others[1:]):
+        blocks.append(jnp.where(core == 0, earlier[:, at], later[:, at]))
+    return blocks
+
+
 def attention_kernel(blocks, *refs):
     query_ref, key_refs, value_refs = refs[0], refs[1 : 1 + blocks], refs[1 + blocks : 1 + 2 * blocks]
-    place_ref, name_ref, key_place_ref, key_name_ref, weight_ref, out_ref, branch_ref = refs[
-        1 + 2 * blocks :
-    ]
+    core_ref, place_ref, name_ref, key_place_ref, key_name_ref, weight_ref, out_ref, branch_ref = (
+        refs[1 + 2 * blocks :]
+    )
+    core = core_ref[...]
     rows = query_ref.shape[0]
     allowed = allowed_pairs(place_ref, name_ref, key_place_ref, key_name_ref)
     for number in range(query_ref.shape[1] // HEAD_DIM):
         at = head_at(number)
         probs = probabilities(
-            query_ref[:, at], [key_ref[:, at] for key_ref in key_refs], allowed
+            query_ref[:, at], reached(key_refs, core, at), allowed
         ).astype(BF)
         total = jnp.zeros((rows, HEAD_DIM), F32)
-        for block, value_ref in enumerate(value_refs):
-            total = total + dot(probs[:, block * rows : (block + 1) * rows], value_ref[:, at])
+        for block, values in enumerate(reached(value_refs, core, at)):
+            total = total + dot(probs[:, block * rows : (block + 1) * rows], values)
         out_ref[:, at] = total.astype(BF)
     branch_ref[...] = dot(out_ref[...], weight_ref[...]).astype(BF)
+
+
+def output_grad_kernel(attended_ref, left_ref, right_ref, middle_ref, grad_ref):
+    width = attended_ref.shape[1]
+    middle = middle_ref[:, :D]
+    count, height, _ = grad_ref.shape
+    out_rows, router_rows = width // count, EXPERTS // count
+    folds = height // router_rows
+    piece = D // folds
+    weight_grad = dot_first(attended_ref[...], middle)
+    router_grad = jnp.concatenate(
+        [dot_first(middle_ref[:, D:], half[...]) for half in (left_ref, right_ref)], axis=1
+    )
+    for k in range(count):
+        grad_ref[k, :, :D] = weight_grad[k * out_rows : (k + 1) * out_rows].astype(BF)
+        own = router_grad[k * router_rows : (k + 1) * router_rows]
+        grad_ref[k, :, D : D + piece] = jnp.concatenate(
+            [own[:, f * piece : (f + 1) * piece] for f in range(folds)], axis=0
+        ).astype(BF)
 
 
 def attention_back_kernel(blocks, *refs):
     query_ref, key_refs, value_refs = refs[0], refs[1 : 1 + blocks], refs[1 + blocks : 1 + 2 * blocks]
     (
+        core_ref,
         place_ref,
         name_ref,
         key_place_ref,
         key_name_ref,
         weight_ref,
-        attended_ref,
-        left_ref,
-        right_ref,
         middle_ref,
         raw_ref,
         sums_ref,
@@ -827,56 +857,49 @@
         gain_grad_ref,
         mine_ref,
         other_ref,
-        weight_grad_ref,
     ) = refs[1 + 2 * blocks :]
     rows, width = query_ref.shape
     middle = middle_ref[:, :D]
-    count, height, _ = weight_grad_ref.shape
-    out_rows, router_rows = width // count, EXPERTS // count
-    weight_grad = dot_first(attended_ref[...], middle)
-    router_grad = jnp.concatenate(
-        [dot_first(middle_ref[:, D:], half[...]) for half in (left_ref, right_ref)], axis=1
-    )
-    spare = jnp.zeros((height - out_rows - router_rows, D), F32)
-    for k in range(count):
-        weight_grad_ref[k] = jnp.concatenate(
-            [
-                weight_grad[k * out_rows : (k + 1) * out_rows],
-                router_grad[k * router_rows : (k + 1) * router_rows],
-                spare,
-            ],
-            axis=0,
-        ).astype(BF)
     out_grad = dot_last(middle, weight_ref[...]).astype(BF)
     allowed = allowed_pairs(place_ref, name_ref, key_place_ref, key_name_ref)
+    core = core_ref[...]
     cosine, sine = cos_ref[...], -sin_ref[...]
-    scale = across(scale_of(sums_ref[0:1, :]))
+    scale = across(scale_of(total_row(sums_ref, 0)))
     shrink = HEAD_DIM ** (-0.5)
     dots = jnp.zeros((rows, 1), F32)
     for number in range(width // HEAD_DIM):
         at = head_at(number)
         query, grad = query_ref[:, at], out_grad[:, at]
-        keys = [key_ref[:, at] for key_ref in key_refs]
+        keys = reached(key_refs, core, at)
         probs = probabilities(query, keys, allowed)
         prob_grad = jnp.concatenate(
-            [dot_last(grad, value_ref[:, at]) for value_ref in value_refs], axis=1
+            [dot_last(grad, values) for values in reached(value_refs, core, at)], axis=1
         )
         inner = jnp.sum(probs * prob_grad, axis=1, keepdims=True)
         score_grad = (probs * (prob_grad - inner)).astype(BF)
         probs = probs.astype(BF)
         total = jnp.zeros((rows, HEAD_DIM), F32)
-        for block in range(blocks):
+        half = blocks // 2
+        pairs = []
+        for block, keys_of in enumerate(keys):
             part = slice(block * rows, (block + 1) * rows)
-            total = total + dot(score_grad[:, part], keys[block])
-            key_grad = dot_first(score_grad[:, part], query) * shrink
-            value_grad = dot_first(probs[:, part], grad)
-            half = blocks // 2
-            target = mine_ref if block < half else other_ref
-            place = slice((block % half) * rows, (block % half + 1) * rows)
-            target[place, at] = key_grad.astype(target.dtype)
-            target[place, width + number * HEAD_DIM : width + (number + 1) * HEAD_DIM] = (
-                value_grad.astype(target.dtype)
+            total = total + dot(score_grad[:, part], keys_of)
+            pairs.append(
+                (
+                    dot_first(score_grad[:, part], query) * shrink,
+                    dot_first(probs[:, part], grad),
+                )
             )
+        for column, start in enumerate((0, width)):
+            grads = [pair[column] for pair in pairs]
+            target = slice(start + number * HEAD_DIM, start + (number + 1) * HEAD_DIM)
+            for block in range(half):
+                place = slice(block * rows, (block + 1) * rows)
+                mine_ref[place, target] = grads[block]
+                none = jnp.zeros_like(grads[0])
+                first = grads[half + block] if block < half - 1 else none
+                second = grads[half + block - 1] if block else none
+                other_ref[place, target] = jnp.where(core == 0, first, second).astype(BF)
         back = turned(total * shrink, cosine, sine)
         back_ref[:, at] = back
         raw = raw_ref[:, at]
@@ -890,6 +913,7 @@
 ):
     (
         *part_refs,
+        query_dot_ref,
         raw_ref,
         sums_ref,
         gain_ref,
@@ -903,7 +927,7 @@
     rows, width = raw_ref.shape
     at_own = slice(mine_ref.shape[0] - rows, mine_ref.shape[0])
     cosine, sine = cos_ref[...], -sin_ref[...]
-    scale = across(scale_of(sums_ref[1:2, :]))
+    scale = across(scale_of(total_row(sums_ref, 1)))
     dots = jnp.zeros((rows, 1), F32)
     for number in range(2 * width // HEAD_DIM):
         at = head_at(number)
@@ -918,7 +942,10 @@
         raw = raw_ref[:, at]
         dots = dots + jnp.sum(back * gain_ref[:, at] * raw, axis=1, keepdims=True)
         gain_grad_ref[:, at] = jnp.sum(back * raw * scale, axis=0, keepdims=True)
-    dot_ref[...] = down(dots)
+    row = lax.broadcasted_iota(jnp.int32, query_dot_ref.shape, 0)
+    both = jnp.where(row == 0, query_dot_ref[...], down(dots))
+    for k in range(dot_ref.shape[0]):
+        dot_ref[k] = both
 
 
 def input_back_kernel(
@@ -938,17 +965,17 @@
     tokens_ref,
     norm2_ref,
     late_ref,
+    left_ref,
+    right_ref,
+    part_ref,
     riding_ref,
-    part_ref,
 ):
     rows, width = query_raw_ref.shape
-    if riding_ref.shape[0] > rows:
-        riding_ref[rows:, : 3 * width] = jnp.zeros((riding_ref.shape[0] - rows, 3 * width), BF)
     for row, (back_ref, raw_ref, gain_ref) in enumerate(
         ((query_back_ref, query_raw_ref, qgain_ref), (key_back_ref, key_raw_ref, kgain_ref))
     ):
-        scale = across(scale_of(sums_ref[row : row + 1, :]))
-        factor = scale * scale * scale * across(dots_ref[row : row + 1, :] / (HEADS * HEAD_DIM))
+        scale = across(scale_of(total_row(sums_ref, row)))
+        factor = scale * scale * scale * across(total_row(dots_ref, row) / (HEADS * HEAD_DIM))
         for number in range(width // HEAD_DIM):
             at = head_at(number)
             grad = scale * gain_ref[:, at] * back_ref[:, at] - raw_ref[:, at] * factor
@@ -975,63 +1002,64 @@
             spare.shape[0]
         ) else norms
     late, height = riding_ref.shape[1] - 3 * width, late_ref.shape[0]
-    riding_ref[:, 3 * width :] = jnp.zeros((riding_ref.shape[0], late), BF)
-    for k, start in enumerate(range(0, D, late)):
-        stop = min(start + late, D)
+    middle = left_ref.shape[1]
+    riding_ref[:, 3 * width :] = jnp.zeros((rows, late), BF)
+    for k, start in enumerate(range(0, late_ref.shape[1], late)):
+        stop = min(start + late, late_ref.shape[1])
         riding_ref[k * height : (k + 1) * height, 3 * width : 3 * width + stop - start] = late_ref[
             :, start:stop
         ]
-
-
-def place_kernel(count, first, rows, height, *refs):
+    left_ref[...] = riding_ref[:, :middle]
+    right_ref[...] = riding_ref[:, middle:]
+
+
+def place_kernel(count, first, rows, *refs):
     piece_refs = refs[1 : 1 + count]
     out_ref, side_ref, held, arrived = refs[-4:]
     step = pl.program_id(0)
 
     def fetch(s):
-        return pltpu.make_async_copy(
-            piece_refs[s].at[:, first:], held.at[s % 2], arrived.at[s % 2]
-        )
+        return pltpu.make_async_copy(piece_refs[s].at[:, first:], held.at[s], arrived.at[s])
+
+    @pl.when(step == 0)
+    def _():
+        for s in range(count):
+            fetch(s).start()
 
     for s in range(count):
 
         @pl.when(step == s)
         def _(s=s):
-            if s == 0:
-                fetch(0).start()
-            if s + 1 < count:
-                fetch(s + 1).start()
             fetch(s).wait()
 
-    late = D - first
-    slot = step % 2
-    for k, start in enumerate(range(0, D, late)):
-        stop = min(start + late, D)
-        block = held[slot, k * height : (k + 1) * height, : stop - start].astype(F32)
-        out_ref[:, start:stop] = block[:rows]
-        side_ref[0, :, start:stop] = block[rows:]
-
-
-def place_pieces(me, pieces, first, rows, height, *deps):
+    late = held.shape[2]
+    width = D + side_ref.shape[2]
+    blocks = [held[step, k * rows : (k + 1) * rows, :] for k in range(-(-width // late))]
+    whole = jnp.concatenate(blocks, axis=1).astype(F32)
+    out_ref[...] = whole[:, :D]
+    side_ref[0] = whole[:, D:width]
+
+
+def place_pieces(me, pieces, first, rows, side, *deps):
     count = len(pieces)
     return pl.pallas_call(
-        partial(place_kernel, count, first, rows, height),
+        partial(place_kernel, count, first, rows),
         grid_spec=pltpu.PrefetchScalarGridSpec(
             num_scalar_prefetch=1,
             grid=(count,),
             in_specs=[pl.BlockSpec(memory_space=pl.ANY) for _ in (*pieces, *deps)],
             out_specs=[
                 pl.BlockSpec((rows, D), lambda i, me_ref: (i ^ me_ref[0], 0)),
-                pl.BlockSpec((1, height - rows, D), lambda i, me_ref: (i ^ me_ref[0], 0, 0)),
+                pl.BlockSpec((1, rows, side), lambda i, me_ref: (i ^ me_ref[0], 0, 0)),
             ],
             scratch_shapes=[
-                pltpu.VMEM((2, pieces[0].shape[0], D - first), BF),
-                pltpu.SemaphoreType.DMA((2,)),
+                pltpu.VMEM((count, pieces[0].shape[0], pieces[0].shape[1] - first), BF),
+                pltpu.SemaphoreType.DMA((count,)),
             ],
         ),
         out_shape=[
             jax.ShapeDtypeStruct((count * rows, D), F32),
-            jax.ShapeDtypeStruct((count, height - rows, D), F32),
+            jax.ShapeDtypeStruct((count, rows, side), F32),
         ],
         compiler_params=pltpu.CompilerParams(vmem_limit_bytes=VMEM_BYTES),
         cost_estimate=LIGHT,
@@ -1039,62 +1067,80 @@
     )(me, *pieces, *deps)
 
 
-def weight_grad_kernel(count, dep_count, *refs):
-    hidden_refs, grad_refs = refs[:count], refs[count : 2 * count]
-    refs = refs[2 * count + dep_count :]
+def weight_grad_kernel(count, *refs):
+    hidden_refs, left_refs, right_refs = (refs[k * count : (k + 1) * count] for k in range(3))
+    refs = refs[3 * count :]
     out_refs, (hidden, grads, arrived) = refs[:3], refs[3:]
     step = pl.program_id(0)
     rows = hidden_refs[0].shape[0]
-    width = out_refs[0].shape[1]
-
-    @pl.when(step == 0)
-    def _():
+    height, width = out_refs[0].shape
+
+    def fetch(part):
+        slot = part % 2
         copies = []
         for s in range(count):
             at = slice(s * rows, (s + 1) * rows)
             copies.append(
-                pltpu.make_async_copy(hidden_refs[s], hidden.at[at], arrived.at[2 * s])
+                pltpu.make_async_copy(
+                    hidden_refs[s].at[:, part * height : (part + 1) * height],
+                    hidden.at[slot, at],
+                    arrived.at[slot, s],
+                )
+            )
+        return copies
+
+    def fetch_grads():
+        middle, copies = left_refs[0].shape[1], []
+        for s in range(count):
+            at = slice(s * rows, (s + 1) * rows)
+            copies.append(
+                pltpu.make_async_copy(left_refs[s], grads.at[at, :middle], arrived.at[2, s])
             )
             copies.append(
                 pltpu.make_async_copy(
-                    grad_refs[s].at[:rows, : 3 * width], grads.at[at], arrived.at[2 * s + 1]
+                    right_refs[s].at[:, : 3 * width - middle],
+                    grads.at[at, middle:],
+                    arrived.at[3, s],
                 )
             )
-        for copy in copies:
-            copy.start()
-        for copy in copies:
-            copy.wait()
-
+        return copies
+
+    parts = D // height
+    for part in range(parts):
+
+        @pl.when(step == part)
+        def _(part=part):
+            start = (fetch(0) + fetch_grads()) if part == 0 else []
+            start += fetch(part + 1) if part + 1 < parts else []
+            for copy in start:
+                copy.start()
+            for copy in fetch(part) + (fetch_grads() if part == 0 else []):
+                copy.wait()
+
+    result = dot_first(hidden[step % 2], grads[...])
     for number in range(3):
-
-        @pl.when(step == number)
-        def _(number=number):
-            out_refs[number][...] = dot_first(
-                hidden[...], grads[:, number * width : (number + 1) * width]
-            )
-
-
-def weight_grads(hidden_pieces, grad_pieces, width, *deps):
+        out_refs[number][...] = result[:, number * width : (number + 1) * width]
+
+
+def weight_grads(hidden_pieces, lefts, rights, width):
     count = len(hidden_pieces)
     rows = hidden_pieces[0].shape[0]
+    height = D // 4
     return pl.pallas_call(
-        partial(weight_grad_kernel, count, len(deps)),
-        grid=(3,),
-        in_specs=[pl.BlockSpec(memory_space=pl.ANY) for _ in range(2 * count + len(deps))],
-        out_specs=[
-            pl.BlockSpec((D, width), lambda i: (0, 0), pipeline_mode=pl.Buffered(1))
-            for _ in range(3)
-        ],
+        partial(weight_grad_kernel, count),
+        grid=(4,),
+        in_specs=[pl.BlockSpec(memory_space=pl.ANY) for _ in range(3 * count)],
+        out_specs=[pl.BlockSpec((height, width), lambda i: (i, 0)) for _ in range(3)],
         out_shape=[jax.ShapeDtypeStruct((D, width), F32)] * 3,
         scratch_shapes=[
-            pltpu.VMEM((count * rows, D), BF),
+            pltpu.VMEM((2, count * rows, height), BF),
             pltpu.VMEM((count * rows, 3 * width), BF),
-            pltpu.SemaphoreType.DMA((2 * count,)),
+            pltpu.SemaphoreType.DMA((4, count)),
         ],
         compiler_params=pltpu.CompilerParams(vmem_limit_bytes=VMEM_BYTES),
         cost_estimate=cost(6 * count * rows * D * width),
         name="weight_grads",
-    )(*hidden_pieces, *grad_pieces, *deps)
+    )(*hidden_pieces, *lefts, *rights)
 
 
 def on_device(
@@ -1155,7 +1201,7 @@
         [
             jax.ShapeDtypeStruct((local_rows, head_width), F32),
             jax.ShapeDtypeStruct((local_rows, head_width), F32),
-            jax.ShapeDtypeStruct((2, local_rows), F32),
+            jax.ShapeDtypeStruct((tp_count, 8, local_rows), F32),
         ],
         hidden_one,
         key_weight,
@@ -1171,7 +1217,7 @@
         return mine + [swap(block, 1) for block in mine]
 
     value_blocks = window(value_low)
-    square_sums = tiny_sum(squares)
+    square_sums = spread_ready(squares, "tp")
     query_low, key_low = small_call(
         rope_kernel,
         "rope",
@@ -1189,7 +1235,8 @@
     blocks = len(key_blocks)
 
     counting = jnp.arange(local_rows, dtype=jnp.int32)
-    starts = [(base - hop) * local_rows for base in (ep_at, ep_at ^ 1) for hop in hops + [0]]
+    core = jnp.full((1, HEAD_DIM), ep_at % 2, jnp.int32)
+    starts = [(ep_at - hop) * local_rows for hop in hops + [0] + [hop - 1 for hop in hops]]
     key_place = jnp.concatenate([start + counting for start in starts])[None]
     names = segments + EXPERTS * (jnp.arange(all_rows, dtype=jnp.int32) // seq_len)
     key_name = jnp.where(
@@ -1211,6 +1258,7 @@
         query_low,
         *key_blocks,
         *value_blocks,
+        core,
         place,
         name,
         key_place,
@@ -1245,8 +1293,8 @@
         jax.ShapeDtypeStruct((local_rows, D + 128), BF),
         cotangent,
         jnp.pad(routes, ((0, 0), (0, 128 - TOP))).astype(BF),
-        deps=key_blocks[: len(hops)],
-    )
+    )
+    cot_pack = held_back(cot_pack, *key_blocks[: len(hops)])
     cot_all = lax.all_gather(cot_pack, "ep", tiled=True)
     me = ep_at.reshape(1).astype(jnp.int32)
     order = ep_at ^ jnp.arange(ep_count, dtype=jnp.int32)
@@ -1300,11 +1348,11 @@
     grad_rows = lax.psum_scatter(grad_part, "ep", tiled=True)
     out_rows = output_pass(mid, scale, down_weight)
     mix_odd = add_up_odd(slots_across, out_rows)
-    grad_gate, grad_up = pair_grads(x_rows, pair_back, mix_odd)
-    mix_sums = add_up_even(slots_across, out_rows, swap(mix_odd, 1), grad_gate)
-    grad_down = down_grads(mid, cot_rows, scale, mix_sums[0])
-    grad_rows = held_back(grad_rows, grad_down)
+    mix_sums = add_up_even(slots_across, out_rows, swap(mix_odd, 1))
+    grad_gate, grad_up = pair_grads(x_rows, pair_back, mix_sums[0])
+    grad_rows = held_back(grad_rows, grad_gate)
     mix_rows, mix_between = exchange(mix_sums, grad_rows)
+    grad_down = down_grads(mid, cot_rows, scale, mix_between)
 
     grad_middle, riding, norm2_part = small_call(
         partial(middle_back_kernel, tp_count),
@@ -1326,9 +1374,21 @@
 
     half_rows = blocks // 2 * local_rows
     sums_rows = head_width // ep_count
-    sums_height = sums_rows + EXPERTS // ep_count
-    sums_height += -sums_height % 16
-    query_back, query_dots, grad_qgain, mine_grad, other_grad, sums_part = small_call(
+    folds = sums_rows * ep_count // EXPERTS
+    side_width = D // folds
+    sums_part = small_call(
+        output_grad_kernel,
+        "output_grad",
+        jax.ShapeDtypeStruct((ep_count, sums_rows, D + side_width), BF),
+        attended_low,
+        left_rows,
+        right_rows,
+        middle_got,
+    )
+    sums_own = lax.psum_scatter(
+        sums_part.reshape(-1, D + side_width), "ep", tiled=True
+    )
+    query_back, query_dots, grad_qgain, mine_grad, other_grad = small_call(
         partial(attention_back_kernel, blocks),
         "attention_back",
         [
@@ -1337,35 +1397,24 @@
             jax.ShapeDtypeStruct((1, head_width), F32),
             jax.ShapeDtypeStruct((half_rows, 2 * head_width), F32),
             jax.ShapeDtypeStruct((half_rows, 2 * head_width), BF),
-            jax.ShapeDtypeStruct((ep_count, sums_height, D), BF),
         ],
         query_low,
         *key_blocks,
         *value_blocks,
+        core,
         place,
         name,
         key_place,
         key_name,
         output_weight,
-        attended_low,
-        left_rows,
-        right_rows,
         middle_got,
         query_raw,
         square_sums,
         qgain,
         cosine,
         sine,
-        deps=[mix_rows],
+        deps=[mix_rows, grad_down, sums_part],
         work=cost(200 * local_rows * head_width * blocks * local_rows),
-    )
-    sums_own = lax.psum_scatter(sums_part.reshape(-1, D), "ep", tiled=True)
-    mixed_own = small_call(
-        mixed_kernel,
-        "mixed",
-        jax.ShapeDtypeStruct((own_rows, D), BF),
-        to_owners(mix_rows, "tp"),
-        middle,
     )
     got_grad = swap(other_grad, 1)
     parts = []
@@ -1373,34 +1422,37 @@
         at = slice(number * local_rows, (number + 1) * local_rows)
         part = (mine_grad[at] + got_grad[at].astype(F32)).astype(BF)
         parts.append(from_behind(part, "ep", -hop))
-    key_back, value_grad_low, key_dots, grad_kgain = small_call(
+    key_back, value_grad_low, dots_copies, grad_kgain = small_call(
         key_back_kernel,
         "key_back",
         [
             jax.ShapeDtypeStruct((local_rows, head_width), F32),
             jax.ShapeDtypeStruct((local_rows, head_width), BF),
-            jax.ShapeDtypeStruct((8, local_rows), F32),
+            jax.ShapeDtypeStruct((tp_count, 8, local_rows), F32),
             jax.ShapeDtypeStruct((1, head_width), F32),
         ],
         mine_grad,
         got_grad,
         *parts,
+        query_dots,
         key_raw,
         square_sums,
         kgain,
         cosine,
         sine,
     )
-    dots = tiny_sum(
-        held_back(jnp.concatenate([query_dots[:1], key_dots[:1]], axis=0), mixed_own)
-    )
-    late_width = D - 3 * head_width
-    riding_rows = max(local_rows, -(-D // late_width) * sums_height)
-    grads_riding, one_part = small_call(
+    mix_pieces = to_owners(mix_rows, "tp")
+    dots = spread_ready(held_back(dots_copies, mix_pieces), "tp")
+    folded = local_rows // sums_rows
+    late_width = -(-(D + side_width) // (128 * folded)) * 128
+    riding_width = 3 * head_width + late_width
+    left_width = -(-riding_width // 256) * 128
+    grads_left, grads_right, one_part = small_call(
         partial(input_back_kernel, tp_count),
         "input_back",
         [
-            jax.ShapeDtypeStruct((riding_rows, D), BF),
+            jax.ShapeDtypeStruct((local_rows, left_width), BF),
+            jax.ShapeDtypeStruct((local_rows, riding_width - left_width), BF),
             jax.ShapeDtypeStruct((local_rows, WIDE), BF),
         ],
         query_back,
@@ -1418,8 +1470,9 @@
         tokens,
         norm2_part,
         sums_own,
-    )
-    grads_near = gather_near(grads_riding)
+        scratch=[pltpu.VMEM((local_rows, riding_width), BF)],
+    )
+    near_left, near_right = gather_near(grads_left), gather_near(grads_right)
     input_copies, norms = small_call(
         first_back_kernel,
         "first_back",
@@ -1431,28 +1484,36 @@
         grad_middle,
         tokens_own,
         norm1_gain[None],
-        mixed_own,
-        deps=grads_near,
+        mix_pieces,
+        middle,
+        deps=[*near_left, *near_right],
     )
     side_sums = ep_sum(
         jnp.concatenate(
             [norms, grad_qgain.reshape(-1, 128), grad_kgain.reshape(-1, 128)], axis=0
         )
     )
-    grads_corner = gather_corner(grads_near, [norms], [side_sums])
-    grad_pieces = with_odds([grads_riding] + grads_near + grads_corner)
+    if ep_count == 8:
+        near_left.append(swap(near_left[1], 2))
+        near_right.append(swap(near_right[0], 4))
+    grad_lefts = with_odds([grads_left] + near_left)
+    grad_rights = with_odds([grads_right] + near_right)
     grad_norm1, grad_norm2 = side_sums[: 2 * D // 128].reshape(2, D)
     grad_qgain, grad_kgain = side_sums[2 * D // 128 :].reshape(2, head_width)
     last_got = spread_ready(input_copies, "tp")
     grad_input, mixed_out = last_got[:, :D].astype(F32), last_got[:, D:]
     hidden_one_pieces = with_odds([hidden_one_late] + hidden_one_near + hidden_one_corner)
     grad_query, grad_key, grad_value = weight_grads(
-        hidden_one_pieces, grad_pieces, head_width, last_got
+        hidden_one_pieces, grad_lefts, grad_rights, head_width
     )
     grad_output, router_side = place_pieces(
-        me, grad_pieces, 3 * head_width, sums_rows, sums_height, grad_query
-    )
-    grad_router = router_side[:, : EXPERTS // ep_count].reshape(EXPERTS, D).T
+        me, grad_rights, 3 * head_width - left_width, sums_rows, side_width, grad_query
+    )
+    grad_router = (
+        router_side.reshape(ep_count, folds, EXPERTS // ep_count, side_width)
+        .transpose(1, 3, 0, 2)
+        .reshape(D, EXPERTS)
+    )
     return (
         mixed_out,
         grad_input,

time: 610 us -> 549 us (0.900)
  waiting for transfers between devices: 192 us -> 157 us
  Pallas kernels: 258 us -> 236 us
    all_to_all x3, waiting for transfers between devices: 45 us -> 24.5 us  [to_owners(): lax.all_to_all(value.reshape(count, rows // count, width), axis, split_ax...]
    ppermute x6, waiting for transfers between devices: 7.02 us -> 24.5 us  [from_behind(): lax.ppermute(value, axis, [(source, source + steps) for source in range(i...]
    ppermute x44 -> x50, waiting for transfers between devices: 109 us -> 94.2 us  [swap(): return lax.ppermute(value, 'ep', [(i, i ^ distance) for i in range(count)])]
    all_to_all x3 -> x4, waiting for transfers between devices: 20.6 us -> 6.58 us  [spread_ready(): got = lax.all_to_all(copies, axis, split_axis=0, concat_axis=0, tiled=True)]
    pallas_call x1, Pallas kernels: 29.4 us -> 16.8 us  [down_grads(): pl.pallas_call(down_grad_kernel, grid=(experts,), in_specs=[per_expert(sp...]
    pallas_call x1, Pallas kernels: 10.4 us -> 21 us  [add_up_even(): pl.pallas_call(partial(even_kernel, split), grid=(sources // 2,), in_spec...]
    pallas_call x2, Pallas kernels: 30.3 us -> 23.2 us  [the longest x1 18.6 us: weight_grads(): pl.pallas_call(partial(weight_grad_kernel, count), grid=(4,), in_specs=[p...]
    pallas_call x15 -> x13, Pallas kernels: 68.2 us -> 61.7 us  [small_call(): pl.pallas_call(run, in_specs=[pl.BlockSpec(memory_space=pltpu.VMEM)] * co...]
  transfers between devices with their start and end apart: 63 -> 69, of which waited for: 24 -> 29; matrix products, arithmetic and copies ran while one was open for 5% -> 4% of each run, Pallas kernels for 31% -> 40%
where the time goes in v4:
time: 549 us; the launch traced here: 539 us
  Pallas kernels  236 us (43%)
  waiting for transfers between devices  157 us (29%)
  starting transfers between devices  81.1 us (15%)
  local copies, waits for them, and re-layouts  26.3 us (5%)
  between operations  14.8 us (3%)
  other arithmetic  11.5 us (2%)
  blocking collectives  10.6 us (2%)
    ppermute x50, waiting for transfers between devices, swap(): return lax.ppermute(value, 'ep', [(i, i ^ distance) for i in range(count)])  94.2 us
    pallas_call x13, Pallas kernels, small_call(): pl.pallas_call(run, in_specs=[pl.BlockSpec(memory_space=pltpu.VMEM)] * co...  61.7 us
    pallas_call x1, Pallas kernels, expert_pass(): pl.pallas_call(partial(expert_kernel, sources, experts), grid_spec=pltpu....  43.7 us
    ppermute x50, starting transfers between devices, swap(): return lax.ppermute(value, 'ep', [(i, i ^ distance) for i in range(count)])  32.9 us
    ppermute x6, waiting for transfers between devices, from_behind(): lax.ppermute(value, axis, [(source, source + steps) for source in range(i...  24.5 us
    all_to_all x3, waiting for transfers between devices, to_owners(): lax.all_to_all(value.reshape(count, rows // count, width), axis, split_ax...  24.5 us
    pallas_call x1, Pallas kernels, pair_grads(): pl.pallas_call(pair_grad_kernel, grid=(experts,), in_specs=[per_expert(sp...  21.7 us
    pallas_call x1, Pallas kernels, add_up_even(): pl.pallas_call(partial(even_kernel, split), grid=(sources // 2,), in_spec...  21 us
  transfers between devices with their start and end apart: 69, of which 29 were waited for; matrix products, arithmetic and copies ran while one was open for 4% of the time, Pallas kernels for 40%

profile of v4, /device:TPU:0, one launch (start us, length us, event | category | flops | bytes accessed | tf_op | source)
XLA Modules:
  0.0 539.4 jit_solution(10270541529220370277)
XLA Ops:
  10.8 4.9 collective-permute-start
  19.1 4.6 projected.1
  23.7 5.0 all-to-all-start
  43.9 4.7 collective-permute-done.2.refs_1_
  55.7 8.5 %attention.1 = (bf16[256,512]{1,0:T(8,128)(2,1)}, bf16[256,2048]{1,0:T(8,128)(2,1)}) custom-call(bf16[256,512]{1,0:T(8,128)(2,1)} %get-tuple-element.71.refs_0_, bf16[256,512]{1,0:T(8,128)(2,1)} %copy-done.22, bf16[256,512]{1,0:T(8,128)(2,1)} %copy-done.23, bf16[256,512]{1,0:T(8,128)(2,1)} %get-tuple-element.72.refs_3_, bf16[256,512]{1,0:T(8,128)(2,1)} %copy-done.45, ...), custom_call_target="tpu_custom_call" | custom-call | flops 1 | bytes 1 | tf_op jit(solution)/shard_map/attention/pallas_call | solution.py:768
  69.5 24.5 %all-to-all-done.1.refs_0_ = bf16[4,64,2048]{2,1,0:T(8,128)(2,1)S(1)} async-done(((bf16[4,64,2048]{2,1,0:T(8,128)(2,1)}), bf16[4,64,2048]{2,1,0:T(8,128)(2,1)S(1)}, u32[]{:S(2)}, u32[]{:S(2)}) %all-to-all-start.1) | async-done | bytes 1048608 | tf_op jit(solution)/shard_map/all_to_all | solution.py:65
  101.2 4.4 all-gather.2.cloned.1.call-done.cot_ref
  110.1 18.8 %cotangent_rows.1 = (bf16[8,512,2048]{2,1,0:T(8,128)(2,1)}, f32[8,512,256]{2,1,0:T(8,128)}) custom-call(s32[1]{0:T(128)} %bitcast.15.me_ref.refs_0_, s32[8,8,256]{2,1,0:T(8,128)} %copy.73.slot_ref, bf16[2048,2176]{1,0:T(8,128)(2,1)} %all-gather.2.cloned.1.call-done.cot_ref, bf16[8,256,2048]{2,1,0:T(8,128)(2,1)} %down_ref.3), custom_call_target="tpu_custom_call" | custom-call | flops 1 | bytes 1 | tf_op jit(solution)/shard_map/cotangent_rows/pallas_call | solution.py:197
  134.3 12.3 %collective-permute-done.18.refs_10_ = bf16[256,1024]{1,0:T(8,128)(2,1)S(1)} collective-permute-done((bf16[256,1024]{1,0:T(8,128)(2,1)}, bf16[256,1024]{1,0:T(8,128)(2,1)S(1)}, u32[]{:S(2)}, u32[]{:S(2)}) %collective-permute-start.18) | collective-permute-done | bytes 524320 | tf_op jit(solution)/shard_map/ppermute | solution.py:72
  150.7 10.7 %collective-permute-done.22.refs_14_ = bf16[256,1024]{1,0:T(8,128)(2,1)S(1)} collective-permute-done((bf16[256,1024]{1,0:T(8,128)(2,1)S(1)}, bf16[256,1024]{1,0:T(8,128)(2,1)S(1)}, u32[]{:S(2)}, u32[]{:S(2)}) %collective-permute-start.22) | collective-permute-done | bytes 524320 | tf_op jit(solution)/shard_map/ppermute | solution.py:72
  163.2 7.9 %collective-permute-done.20.refs_12_ = bf16[256,1024]{1,0:T(8,128)(2,1)} collective-permute-done((bf16[256,1024]{1,0:T(8,128)(2,1)}, bf16[256,1024]{1,0:T(8,128)(2,1)}, u32[]{:S(2)}, u32[]{:S(2)}) %collective-permute-start.20) | collective-permute-done | bytes 524320 | tf_op jit(solution)/shard_map/ppermute | solution.py:72
  177.3 43.7 %expert_pass.1 = (bf16[8,512,2048]{2,1,0:T(8,128)(2,1)}, bf16[8,512,256]{2,1,0:T(8,128)(2,1)}, bf16[8,512,512]{2,1,0:T(8,128)(2,1)}, f32[8,512,1]{2,1,0:T(8,128)}, bf16[2048,2176]{1,0:T(8,128)(2,1)}) custom-call(s32[1]{0:T(128)} %bitcast.15.me_ref.refs_0_, s32[8,8,256]{2,1,0:T(8,128)} %copy.73.slot_ref, s32[8,8,256]{2,1,0:T(8,128)} %copy-done.47, ...), custom_call_target="tpu_custom_call" | custom-call | flops 21474836480 | bytes 1 | tf_op jit(solution)/shard_map/expert_pass/pallas_call | solution.py:346
  223.5 14.8 %output_pass.1.rows_ref = bf16[8,512,2048]{2,1,0:T(8,128)(2,1)} custom-call(bf16[8,512,256]{2,1,0:T(8,128)(2,1)} %get-tuple-element.81.mid_ref, f32[8,512,1]{2,1,0:T(8,128)} %get-tuple-element.82.scale_ref, bf16[8,256,2048]{2,1,0:T(8,128)(2,1)} %down_ref.3), custom_call_target="tpu_custom_call" | custom-call | flops 4294967296 | bytes 1 | tf_op jit(solution)/shard_map/output_pass/pallas_call | solution.py:554
  238.3 8.3 %add_up_odd.1 = bf16[4,256,2048]{2,1,0:T(8,128)(2,1)} custom-call(s32[8,256,8]{2,1,0:T(8,128)} %bitcast.69, bf16[8,512,2048]{2,1,0:T(8,128)(2,1)} %output_pass.1.rows_ref), custom_call_target="tpu_custom_call" | custom-call | flops 1 | bytes 1 | tf_op jit(solution)/shard_map/add_up_odd/pallas_call | solution.py:404
  249.5 4.7 collective-permute-done.27.got_ref
  254.1 21.0 %add_up_even.1 = (bf16[2,256,1024]{2,1,0:T(8,128)(2,1)}, bf16[2,256,1024]{2,1,0:T(8,128)(2,1)}, f32[256,1024]{1,0:T(8,128)}, f32[256,1024]{1,0:T(8,128)}, f32[256,1024]{1,0:T(8,128)}, /*index=5*/f32[256,1024]{1,0:T(8,128)}) custom-call(s32[8,256,8]{2,1,0:T(8,128)} %bitcast.70, bf16[8,512,2048]{2,1,0:T(8,128)(2,1)} %output_pass.1.rows_ref, ...), custom_call_target="tpu_custom_call" | custom-call | flops 1 | bytes 1 | tf_op jit(solution)/shard_map/add_up_even/pallas_call | solution.py:459
  275.1 21.7 %pair_grads.1 = (f32[8,2048,256]{2,1,0:T(8,128)}, f32[8,2048,256]{2,1,0:T(8,128)}) custom-call(bf16[8,512,2048]{2,1,0:T(8,128)(2,1)} %get-tuple-element.79.rows_ref, bf16[8,512,512]{2,1,0:T(8,128)(2,1)} %get-tuple-element.80.pair_ref, bf16[2,256,1024]{2,1,0:T(8,128)(2,1)} %get-tuple-element.83.refs_0_), custom_call_target="tpu_custom_call" | custom-call | flops 8589934592 | bytes 1 | tf_op jit(solution)/shard_map/pair_grads/pallas_call | solution.py:582
  307.1 15.5 %collective-permute-done.31.near_ref = bf16[2,256,1024]{2,1,0:T(8,128)(2,1)S(1)} collective-permute-done((bf16[2,256,1024]{2,1,0:T(8,128)(2,1)}, bf16[2,256,1024]{2,1,0:T(8,128)(2,1)S(1)}, u32[]{:S(2)}, u32[]{:S(2)}) %collective-permute-start.31) | collective-permute-done | bytes 1048608 | tf_op jit(solution)/shard_map/ppermute | solution.py:72
  332.0 4.7 all-to-all-start.3
  338.8 16.8 %down_grads.1.refs_26_ = f32[8,256,2048]{2,1,0:T(8,128)} custom-call(bf16[8,512,256]{2,1,0:T(8,128)(2,1)} %get-tuple-element.81.mid_ref, bf16[8,512,2048]{2,1,0:T(8,128)(2,1)} %get-tuple-element.94.cot_ref, f32[8,512,1]{2,1,0:T(8,128)} %get-tuple-element.82.scale_ref, bf16[256,1024]{1,0:T(8,128)(2,1)} %get-tuple-element.89.refs_9_.refs_0_), custom_call_target="tpu_custom_call" | custom-call | flops 4294967296 | bytes 1 | tf_op jit(solution)/shard_map/down_grads/pallas_call | solution.py:605
  367.5 12.4 %attention_back.1 = (f32[256,512]{1,0:T(8,128)}, f32[8,256]{1,0:T(8,128)}, f32[1,512]{1,0:T(1,128)}, f32[768,1024]{1,0:T(8,128)}, bf16[768,1024]{1,0:T(8,128)(2,1)}) custom-call(bf16[256,512]{1,0:T(8,128)(2,1)} %get-tuple-element.71.refs_0_, bf16[256,512]{1,0:T(8,128)(2,1)} %copy-done.22, bf16[256,512]{1,0:T(8,128)(2,1)} %copy-done.23, ...), custom_call_target="tpu_custom_call" | custom-call | flops 40265318400 | bytes 1 | tf_op jit(solution)/shard_map/attention_back/pallas_call | solution.py:768
  388.6 19.8 %collective-permute-done.36.refs_2_ = bf16[256,1024]{1,0:T(8,128)(2,1)S(1)} collective-permute-done((bf16[256,1024]{1,0:T(8,128)(2,1)S(1)}, bf16[256,1024]{1,0:T(8,128)(2,1)S(1)}, u32[]{:S(2)}, u32[]{:S(2)}) %collective-permute-start.36) | collective-permute-done | bytes 524320 | tf_op jit(solution)/shard_map/ppermute | solution.py:32
  414.8 10.6 %all_to_all.40 = f32[4,8,256]{2,1,0:T(8,128)} all-to-all(f32[4,8,256]{2,1,0:T(8,128)} %held_back.13), channel_id=1, replica_groups=mesh['ep'=8,'tp'=4] {'tp'}, dimensions={0} | all-to-all | bytes 65536 | tf_op jit(solution)/shard_map/all_to_all | solution.py:110
  427.5 7.1 %input_back.1 = (bf16[256,1152]{1,0:T(8,128)(2,1)}, bf16[256,1024]{1,0:T(8,128)(2,1)}, bf16[256,2176]{1,0:T(8,128)(2,1)}) custom-call(f32[256,512]{1,0:T(8,128)} %get-tuple-element.96.refs_0_, f32[256,512]{1,0:T(8,128)} %get-tuple-element.100.refs_1_, bf16[256,512]{1,0:T(8,128)(2,1)} %get-tuple-element.101.refs_2_, ...), custom_call_target="tpu_custom_call" | custom-call | flops 1 | bytes 1 | tf_op jit(solution)/shard_map/input_back/pallas_call | solution.py:768
  434.6 4.6 all-to-all-start.6
  439.2 9.4 %collective-permute-start.40 = (bf16[256,1024]{1,0:T(8,128)(2,1)}, bf16[256,1024]{1,0:T(8,128)(2,1)S(1)}, u32[]{:S(2)}, u32[]{:S(2)}) collective-permute-start(bf16[256,1024]{1,0:T(8,128)(2,1)} %get-tuple-element.107.refs_16_.refs_1_), channel_id=1, source_target_pairs={{0,8},{4,12},{8,0},{12,4},{16,24},{20,28},{24,16},{28,20},{1,9},{5... | collective-permute-start | bytes 1572872 | tf_op jit(solution)/shard_map/ppermute | solution.py:72
  450.7 10.9 %collective-permute-done.40.refs_8_.refs_18_.refs_3_ = bf16[256,1024]{1,0:T(8,128)(2,1)S(1)} collective-permute-done((bf16[256,1024]{1,0:T(8,128)(2,1)}, bf16[256,1024]{1,0:T(8,128)(2,1)S(1)}, u32[]{:S(2)}, u32[]{:S(2)}) %collective-permute-start.40) | collective-permute-done | bytes 524320 | tf_op jit(solution)/shard_map/ppermute | solution.py:72
  463.7 8.2 %collective-permute-done.38.refs_6_.refs_10_ = bf16[256,1152]{1,0:T(8,128)(2,1)S(1)} collective-permute-done((bf16[256,1152]{1,0:T(8,128)(2,1)}, bf16[256,1152]{1,0:T(8,128)(2,1)S(1)}, u32[]{:S(2)}, u32[]{:S(2)}) %collective-permute-start.38) | collective-permute-done | bytes 589856 | tf_op jit(solution)/shard_map/ppermute | solution.py:72
  478.6 4.8 all-to-all-start.7
  488.3 11.3 %collective-permute-done.52.refs_14_ = bf16[256,1152]{1,0:T(8,128)(2,1)S(1)} collective-permute-done((bf16[256,1152]{1,0:T(8,128)(2,1)}, bf16[256,1152]{1,0:T(8,128)(2,1)S(1)}, u32[]{:S(2)}, u32[]{:S(2)}) %collective-permute-start.52) | collective-permute-done | bytes 589856 | tf_op jit(solution)/shard_map/ppermute | solution.py:72
  506.9 18.6 %weight_grads.1 = (f32[2048,512]{1,0:T(8,128)}, f32[2048,512]{1,0:T(8,128)}, f32[2048,512]{1,0:T(8,128)}) custom-call(bf16[256,2048]{1,0:T(8,128)(2,1)} %held_back.8.refs_0_, bf16[256,2048]{1,0:T(8,128)(2,1)} %collective-permute-done.45.refs_1_, bf16[256,2048]{1,0:T(8,128)(2,1)} %copy-done.14, bf16[256,2048]{1,0:T(8,128)(2,1)} %collective-permute-done.46.refs_3_, ...), custom_call_target="tpu_custom_call" | custom-call | flops 12884901888 | bytes 1 | tf_op jit(solution)/shard_map/weight_grads/pallas_call | solution.py:1129
  525.5 4.6 place_pieces.1
  (333 shorter events, 144.9 us)
Async XLA Ops:
  10.8 23.6 %collective-permute-start = (bf16[256,512]{1,0:T(8,128)(2,1)}, bf16[256,512]{1,0:T(8,128)(2,1)S(1)}, u32[]{:S(2)}, u32[]{:S(2)}) collective-permute-start(bf16[256,512]{1,0:T(8,128)(2,1)} %get-tuple-element.70.refs_9_), channel_id=1, source_target_pairs={{0,16},{4,20},{8,24},{12,28},{1,17},{5,21},{9,25},{13,29},{2,18},{... | collective-permute-start | bytes 786440 | tf_op jit(solution)/shard_map/ppermute | solution.py:32
  15.7 18.7 %collective-permute-start.1 = (bf16[256,512]{1,0:T(8,128)(2,1)}, bf16[256,512]{1,0:T(8,128)(2,1)S(1)}, u32[]{:S(2)}, u32[]{:S(2)}) collective-permute-start(bf16[256,512]{1,0:T(8,128)(2,1)} %get-tuple-element.70.refs_9_), channel_id=1, source_target_pairs={{0,8},{4,12},{8,16},{12,20},{16,24},{20,28},{1,9},{5,13},{9,17},{1... | collective-permute-start | bytes 786440 | tf_op jit(solution)/shard_map/ppermute | solution.py:32
  28.7 77.0 %all-gather.2.cloned.1.call-start = ((), (), s32[]{:S(2)}) async-start(), calls=%async_computation.10 | async-start | bytes 10027008 | tf_op jit(solution)/shard_map/all_gather | solution.py:1298
  64.2 29.7 %all-to-all-start.1 = ((bf16[4,64,2048]{2,1,0:T(8,128)(2,1)}), bf16[4,64,2048]{2,1,0:T(8,128)(2,1)S(1)}, u32[]{:S(2)}, u32[]{:S(2)}) async-start(bf16[4,64,2048]{2,1,0:T(8,128)(2,1)} %bitcast.79), calls=%async_computation.1 | async-start | bytes 2097152 | tf_op jit(solution)/shard_map/all_to_all | solution.py:65
  97.6 31.4 %all-to-all-start.2 = ((bf16[4,64,2048]{2,1,0:T(8,128)(2,1)}), bf16[4,64,2048]{2,1,0:T(8,128)(2,1)S(1)}, u32[]{:S(2)}, u32[]{:S(2)}) async-start(bf16[4,64,2048]{2,1,0:T(8,128)(2,1)} %get-tuple-element.74), calls=%async_computation.2 | async-start | bytes 2097152 | tf_op jit(solution)/shard_map/all_to_all | solution.py:110
  101.1 196.4 %reduce-scatter.3.cloned.1.call-start = ((), (), s32[]{:S(2)}) async-start(), calls=%async_computation.11 | async-start | bytes 10027008 | tf_op jit(solution)/shard_map/reduce_scatter | solution.py:1348
  148.6 22.6 %collective-permute-start.20 = (bf16[256,1024]{1,0:T(8,128)(2,1)}, bf16[256,1024]{1,0:T(8,128)(2,1)}, u32[]{:S(2)}, u32[]{:S(2)}) collective-permute-start(bf16[256,1024]{1,0:T(8,128)(2,1)} %get-tuple-element.77.refs_8_.refs_2_), channel_id=1, source_target_pairs={{0,16},{4,20},{8,24},{12,28},{16,0},{20,4},{24,8},{28,12},{1,17},{... | collective-permute-start | bytes 1572872 | tf_op jit(solution)/shard_map/ppermute | solution.py:72
  150.1 22.1 %collective-permute-start.15 = (bf16[256,1024]{1,0:T(8,128)(2,1)S(1)}, bf16[256,1024]{1,0:T(8,128)(2,1)}, u32[]{:S(2)}, u32[]{:S(2)}) collective-permute-start(bf16[256,1024]{1,0:T(8,128)(2,1)S(1)} %collective-permute-done.13.refs_4_), channel_id=1, source_target_pairs={{0,8},{4,12},{8,0},{12,4},{16,24},{20,28},{24,16},{28,20},{1,9},{5... | collective-permute-start | bytes 1572872 | tf_op jit(solution)/shard_map/ppermute | solution.py:72
  173.6 47.4 %collective-permute-start.24 = (bf16[256,2048]{1,0:T(8,128)(2,1)}, bf16[256,2048]{1,0:T(8,128)(2,1)S(1)}, u32[]{:S(2)}, u32[]{:S(2)}) collective-permute-start(bf16[256,2048]{1,0:T(8,128)(2,1)} %held_back.8.refs_0_), channel_id=1, source_target_pairs={{0,8},{4,12},{8,0},{12,4},{16,24},{20,28},{24,16},{28,20},{1,9},{5... | collective-permute-start | bytes 3145736 | tf_op jit(solution)/shard_map/ppermute | solution.py:72
  174.6 47.6 %collective-permute-start.25 = (bf16[256,2048]{1,0:T(8,128)(2,1)}, bf16[256,2048]{1,0:T(8,128)(2,1)S(1)}, u32[]{:S(2)}, u32[]{:S(2)}) collective-permute-start(bf16[256,2048]{1,0:T(8,128)(2,1)} %held_back.8.refs_0_), channel_id=1, source_target_pairs={{0,16},{4,20},{8,24},{12,28},{16,0},{20,4},{24,8},{28,12},{1,17},{... | collective-permute-start | bytes 3145736 | tf_op jit(solution)/shard_map/ppermute | solution.py:72
  176.2 46.0 %collective-permute-start.26 = (bf16[256,2048]{1,0:T(8,128)(2,1)}, bf16[256,2048]{1,0:T(8,128)(2,1)S(1)}, u32[]{:S(2)}, u32[]{:S(2)}) collective-permute-start(bf16[256,2048]{1,0:T(8,128)(2,1)} %held_back.8.refs_0_), channel_id=1, source_target_pairs={{0,24},{4,28},{8,16},{12,20},{16,8},{20,12},{24,0},{28,4},{1,25},{... | collective-permute-start | bytes 3145736 | tf_op jit(solution)/shard_map/ppermute | solution.py:72
  297.5 25.1 %collective-permute-start.31 = (bf16[2,256,1024]{2,1,0:T(8,128)(2,1)}, bf16[2,256,1024]{2,1,0:T(8,128)(2,1)S(1)}, u32[]{:S(2)}, u32[]{:S(2)}) collective-permute-start(bf16[2,256,1024]{2,1,0:T(8,128)(2,1)} %held_back.11), channel_id=1, source_target_pairs={{0,8},{4,12},{8,0},{12,4},{16,24},{20,28},{24,16},{28,20},{1,9},{5... | collective-permute-start | bytes 3145736 | tf_op jit(solution)/shard_map/ppermute | solution.py:72
  298.9 24.8 %collective-permute-start.32 = (bf16[2,256,1024]{2,1,0:T(8,128)(2,1)}, bf16[2,256,1024]{2,1,0:T(8,128)(2,1)S(1)}, u32[]{:S(2)}, u32[]{:S(2)}) collective-permute-start(bf16[2,256,1024]{2,1,0:T(8,128)(2,1)} %held_back.12), channel_id=1, source_target_pairs={{0,16},{4,20},{8,24},{12,28},{16,0},{20,4},{24,8},{28,12},{1,17},{... | collective-permute-start | bytes 3145736 | tf_op jit(solution)/shard_map/ppermute | solution.py:72
  301.8 25.8 %collective-permute-start.28 = (bf16[64,2176]{1,0:T(8,128)(2,1)S(1)}, bf16[64,2176]{1,0:T(8,128)(2,1)S(1)}, u32[]{:S(2)}, u32[]{:S(2)}) collective-permute-start(bf16[64,2176]{1,0:T(8,128)(2,1)S(1)} %get-tuple-element.124), channel_id=1, source_target_pairs={{0,1},{1,0},{2,3},{3,2},{4,5},{5,4},{6,7},{7,6},{8,9},{9,8},{10,11... | collective-permute-start | bytes 835592 | tf_op jit(solution)/shard_map/ppermute | solution.py:93
  303.3 24.3 %collective-permute-start.29 = (bf16[64,2176]{1,0:T(8,128)(2,1)S(1)}, bf16[64,2176]{1,0:T(8,128)(2,1)S(1)}, u32[]{:S(2)}, u32[]{:S(2)}) collective-permute-start(bf16[64,2176]{1,0:T(8,128)(2,1)S(1)} %get-tuple-element.123), channel_id=1, source_target_pairs={{0,2},{1,3},{2,0},{3,1},{4,6},{5,7},{6,4},{7,5},{8,10},{9,11},{10,... | collective-permute-start | bytes 835592 | tf_op jit(solution)/shard_map/ppermute | solution.py:93
  305.7 21.9 %collective-permute-start.30 = (bf16[64,2176]{1,0:T(8,128)(2,1)S(1)}, bf16[64,2176]{1,0:T(8,128)(2,1)S(1)}, u32[]{:S(2)}, u32[]{:S(2)}) collective-permute-start(bf16[64,2176]{1,0:T(8,128)(2,1)S(1)} %get-tuple-element.122), channel_id=1, source_target_pairs={{0,3},{1,2},{2,1},{3,0},{4,7},{5,6},{6,5},{7,4},{8,11},{9,10},{10,... | collective-permute-start | bytes 835592 | tf_op jit(solution)/shard_map/ppermute | solution.py:93
  332.0 30.5 %all-to-all-start.3 = ((bf16[4,64,2176]{2,1,0:T(8,128)(2,1)}), bf16[4,64,2176]{2,1,0:T(8,128)(2,1)S(1)}, u32[]{:S(2)}, u32[]{:S(2)}) async-start(bf16[4,64,2176]{2,1,0:T(8,128)(2,1)} %get-tuple-element.90), calls=%async_computation.4 | async-start | bytes 2228224 | tf_op jit(solution)/shard_map/all_to_all | solution.py:110
  336.7 90.8 %reduce-scatter.5.cloned.1.call-start = ((), (), s32[]{:S(2)}) async-start(), calls=%async_computation.12 | async-start | bytes 2654208 | tf_op jit(solution)/shard_map/reduce_scatter | solution.py:1388
  336.7 18.9 %collective-permute-start.33 = (bf16[256,1024]{1,0:T(8,128)(2,1)S(1)}, bf16[256,1024]{1,0:T(8,128)(2,1)S(1)}, u32[]{:S(2)}, u32[]{:S(2)}) collective-permute-start(bf16[256,1024]{1,0:T(8,128)(2,1)S(1)} %copy-done.11), channel_id=1, source_target_pairs={{0,16},{4,20},{8,24},{12,28},{16,0},{20,4},{24,8},{28,12},{1,17},{... | collective-permute-start | bytes 1572872 | tf_op jit(solution)/shard_map/ppermute | solution.py:72
  338.1 17.5 %collective-permute-start.34 = (bf16[256,1024]{1,0:T(8,128)(2,1)S(1)}, bf16[256,1024]{1,0:T(8,128)(2,1)S(1)}, u32[]{:S(2)}, u32[]{:S(2)}) collective-permute-start(bf16[256,1024]{1,0:T(8,128)(2,1)S(1)} %copy-done.63), channel_id=1, source_target_pairs={{0,8},{4,12},{8,0},{12,4},{16,24},{20,28},{24,16},{28,20},{1,9},{5... | collective-permute-start | bytes 1572872 | tf_op jit(solution)/shard_map/ppermute | solution.py:72
  379.9 33.9 %all-to-all-start.4 = ((bf16[4,64,2048]{2,1,0:T(8,128)(2,1)}), bf16[4,64,2048]{2,1,0:T(8,128)(2,1)S(1)}, u32[]{:S(2)}, u32[]{:S(2)}) async-start(bf16[4,64,2048]{2,1,0:T(8,128)(2,1)} %bitcast.76), calls=%async_computation.5 | async-start | bytes 2097152 | tf_op jit(solution)/shard_map/all_to_all | solution.py:65
  386.0 22.4 %collective-permute-start.36 = (bf16[256,1024]{1,0:T(8,128)(2,1)S(1)}, bf16[256,1024]{1,0:T(8,128)(2,1)S(1)}, u32[]{:S(2)}, u32[]{:S(2)}) collective-permute-start(bf16[256,1024]{1,0:T(8,128)(2,1)S(1)} %get-tuple-element.119), channel_id=1, source_target_pairs={{16,0},{20,4},{24,8},{28,12},{17,1},{21,5},{25,9},{29,13},{18,2},{... | collective-permute-start | bytes 1572872 | tf_op jit(solution)/shard_map/ppermute | solution.py:32
  387.3 21.1 %collective-permute-start.37 = (bf16[256,1024]{1,0:T(8,128)(2,1)S(1)}, bf16[256,1024]{1,0:T(8,128)(2,1)S(1)}, u32[]{:S(2)}, u32[]{:S(2)}) collective-permute-start(bf16[256,1024]{1,0:T(8,128)(2,1)S(1)} %get-tuple-element.118), channel_id=1, source_target_pairs={{8,0},{12,4},{16,8},{20,12},{24,16},{28,20},{9,1},{13,5},{17,9},{2... | collective-permute-start | bytes 1572872 | tf_op jit(solution)/shard_map/ppermute | solution.py:32
  434.6 39.0 %all-to-all-start.6 = ((bf16[4,64,2176]{2,1,0:T(8,128)(2,1)}), bf16[4,64,2176]{2,1,0:T(8,128)(2,1)S(1)}, u32[]{:S(2)}, u32[]{:S(2)}) async-start(bf16[4,64,2176]{2,1,0:T(8,128)(2,1)} %bitcast.77), calls=%async_computation.8 | async-start | bytes 2228224 | tf_op jit(solution)/shard_map/all_to_all | solution.py:65
  439.2 22.4 %collective-permute-start.40 = (bf16[256,1024]{1,0:T(8,128)(2,1)}, bf16[256,1024]{1,0:T(8,128)(2,1)S(1)}, u32[]{:S(2)}, u32[]{:S(2)}) collective-permute-start(bf16[256,1024]{1,0:T(8,128)(2,1)} %get-tuple-element.107.refs_16_.refs_1_), channel_id=1, source_target_pairs={{0,8},{4,12},{8,0},{12,4},{16,24},{20,28},{24,16},{28,20},{1,9},{5... | collective-permute-start | bytes 1572872 | tf_op jit(solution)/shard_map/ppermute | solution.py:72
  448.6 23.3 %collective-permute-start.38 = (bf16[256,1152]{1,0:T(8,128)(2,1)}, bf16[256,1152]{1,0:T(8,128)(2,1)S(1)}, u32[]{:S(2)}, u32[]{:S(2)}) collective-permute-start(bf16[256,1152]{1,0:T(8,128)(2,1)} %get-tuple-element.106.refs_8_), channel_id=1, source_target_pairs={{0,8},{4,12},{8,0},{12,4},{16,24},{20,28},{24,16},{28,20},{1,9},{5... | collective-permute-start | bytes 1769480 | tf_op jit(solution)/shard_map/ppermute | solution.py:72
  448.7 24.9 %collective-permute-start.39 = (bf16[256,1152]{1,0:T(8,128)(2,1)}, bf16[256,1152]{1,0:T(8,128)(2,1)}, u32[]{:S(2)}, u32[]{:S(2)}) collective-permute-start(bf16[256,1152]{1,0:T(8,128)(2,1)} %get-tuple-element.106.refs_8_), channel_id=1, source_target_pairs={{0,16},{4,20},{8,24},{12,28},{16,0},{20,4},{24,8},{28,12},{1,17},{... | collective-permute-start | bytes 1769480 | tf_op jit(solution)/shard_map/ppermute | solution.py:72
  450.7 32.7 %collective-permute-start.45 = (bf16[256,2048]{1,0:T(8,128)(2,1)S(1)}, bf16[256,2048]{1,0:T(8,128)(2,1)}, u32[]{:S(2)}, u32[]{:S(2)}) collective-permute-start(bf16[256,2048]{1,0:T(8,128)(2,1)S(1)} %copy-done.6), channel_id=1, source_target_pairs={{0,4},{4,0},{8,12},{12,8},{16,20},{20,16},{24,28},{28,24},{1,5},{5... | collective-permute-start | bytes 3145736 | tf_op jit(solution)/shard_map/ppermute | solution.py:72
  461.6 22.3 %collective-permute-start.46 = (bf16[256,2048]{1,0:T(8,128)(2,1)}, bf16[256,2048]{1,0:T(8,128)(2,1)}, u32[]{:S(2)}, u32[]{:S(2)}) collective-permute-start(bf16[256,2048]{1,0:T(8,128)(2,1)} %copy-done.14), channel_id=1, source_target_pairs={{0,4},{4,0},{8,12},{12,8},{16,20},{20,16},{24,28},{28,24},{1,5},{5... | collective-permute-start | bytes 3145736 | tf_op jit(solution)/shard_map/ppermute | solution.py:72
  463.7 21.9 %collective-permute-start.47 = (bf16[256,2048]{1,0:T(8,128)(2,1)}, bf16[256,2048]{1,0:T(8,128)(2,1)}, u32[]{:S(2)}, u32[]{:S(2)}) collective-permute-start(bf16[256,2048]{1,0:T(8,128)(2,1)} %copy-done.15), channel_id=1, source_target_pairs={{0,4},{4,0},{8,12},{12,8},{16,20},{20,16},{24,28},{28,24},{1,5},{5... | collective-permute-start | bytes 3145736 | tf_op jit(solution)/shard_map/ppermute | solution.py:72
  478.6 52.1 %all-to-all-start.7 = ((bf16[4,64,4096]{2,1,0:T(8,128)(2,1)}), bf16[4,64,4096]{2,1,0:T(8,128)(2,1)S(1)}, u32[]{:S(2)}, u32[]{:S(2)}) async-start(bf16[4,64,4096]{2,1,0:T(8,128)(2,1)} %get-tuple-element.108), calls=%async_computation.9 | async-start | bytes 4194304 | tf_op jit(solution)/shard_map/all_to_all | solution.py:110
  488.3 16.9 %collective-permute-start.50 = (bf16[256,1152]{1,0:T(8,128)(2,1)}, bf16[256,1152]{1,0:T(8,128)(2,1)S(1)}, u32[]{:S(2)}, u32[]{:S(2)}) collective-permute-start(bf16[256,1152]{1,0:T(8,128)(2,1)} %copy-done.24), channel_id=1, source_target_pairs={{0,4},{4,0},{8,12},{12,8},{16,20},{20,16},{24,28},{28,24},{1,5},{5... | collective-permute-start | bytes 1769480 | tf_op jit(solution)/shard_map/ppermute | solution.py:72
  (101 other events, 759.3 us)
Sparse Core Ops, SparseCore 0:
  50.2 55.3 all-gather.1
  223.6 73.8 reduce-scatter.2
  367.6 59.8 reduce-scatter.4

commit v5 on v4

--- a/solution.py
+++ b/solution.py
@@ -104,6 +104,13 @@
         concat_axis=0,
         tiled=True,
     ).reshape(count * value.shape[0], value.shape[1])
+
+
+def from_all(value):
+    count = lax.axis_size("tp")
+    return [value] + [
+        lax.ppermute(value, "tp", [(i, i ^ d) for i in range(count)]) for d in range(1, count)
+    ]
 
 
 def spread_ready(copies, axis):
@@ -944,19 +951,25 @@
         gain_grad_ref[:, at] = jnp.sum(back * raw * scale, axis=0, keepdims=True)
     row = lax.broadcasted_iota(jnp.int32, query_dot_ref.shape, 0)
     both = jnp.where(row == 0, query_dot_ref[...], down(dots))
-    for k in range(dot_ref.shape[0]):
-        dot_ref[k] = both
-
-
-def input_back_kernel(
+    dot_ref[...] = both
+
+
+def input_back_kernel(copies, *refs):
+    dots = refs[0][...]
+    for dot_ref in refs[1:copies]:
+        dots = dots + dot_ref[...]
+    input_back_body(copies, dots, *refs[copies:])
+
+
+def input_back_body(
     copies,
+    dots,
     query_back_ref,
     key_back_ref,
     value_grad_ref,
     query_raw_ref,
     key_raw_ref,
     sums_ref,
-    dots_ref,
     qgain_ref,
     kgain_ref,
     query_weight_ref,
@@ -964,7 +977,6 @@
     value_weight_ref,
     tokens_ref,
     norm2_ref,
-    late_ref,
     left_ref,
     right_ref,
     part_ref,
@@ -975,7 +987,7 @@
         ((query_back_ref, query_raw_ref, qgain_ref), (key_back_ref, key_raw_ref, kgain_ref))
     ):
         scale = across(scale_of(total_row(sums_ref, row)))
-        factor = scale * scale * scale * across(total_row(dots_ref, row) / (HEADS * HEAD_DIM))
+        factor = scale * scale * scale * across(dots[row : row + 1, :] / (HEADS * HEAD_DIM))
         for number in range(width // HEAD_DIM):
             at = head_at(number)
             grad = scale * gain_ref[:, at] * back_ref[:, at] - raw_ref[:, at] * factor
@@ -1001,75 +1013,19 @@
         part_ref[k * own_rows : (k + 1) * own_rows, D:] = jnp.concatenate([norms, spare], axis=0) if (
             spare.shape[0]
         ) else norms
-    late, height = riding_ref.shape[1] - 3 * width, late_ref.shape[0]
     middle = left_ref.shape[1]
-    riding_ref[:, 3 * width :] = jnp.zeros((rows, late), BF)
-    for k, start in enumerate(range(0, late_ref.shape[1], late)):
-        stop = min(start + late, late_ref.shape[1])
-        riding_ref[k * height : (k + 1) * height, 3 * width : 3 * width + stop - start] = late_ref[
-            :, start:stop
-        ]
     left_ref[...] = riding_ref[:, :middle]
     right_ref[...] = riding_ref[:, middle:]
 
 
-def place_kernel(count, first, rows, *refs):
-    piece_refs = refs[1 : 1 + count]
-    out_ref, side_ref, held, arrived = refs[-4:]
-    step = pl.program_id(0)
-
-    def fetch(s):
-        return pltpu.make_async_copy(piece_refs[s].at[:, first:], held.at[s], arrived.at[s])
-
-    @pl.when(step == 0)
-    def _():
-        for s in range(count):
-            fetch(s).start()
-
-    for s in range(count):
-
-        @pl.when(step == s)
-        def _(s=s):
-            fetch(s).wait()
-
-    late = held.shape[2]
-    width = D + side_ref.shape[2]
-    blocks = [held[step, k * rows : (k + 1) * rows, :] for k in range(-(-width // late))]
-    whole = jnp.concatenate(blocks, axis=1).astype(F32)
-    out_ref[...] = whole[:, :D]
-    side_ref[0] = whole[:, D:width]
-
-
-def place_pieces(me, pieces, first, rows, side, *deps):
-    count = len(pieces)
-    return pl.pallas_call(
-        partial(place_kernel, count, first, rows),
-        grid_spec=pltpu.PrefetchScalarGridSpec(
-            num_scalar_prefetch=1,
-            grid=(count,),
-            in_specs=[pl.BlockSpec(memory_space=pl.ANY) for _ in (*pieces, *deps)],
-            out_specs=[
-                pl.BlockSpec((rows, D), lambda i, me_ref: (i ^ me_ref[0], 0)),
-                pl.BlockSpec((1, rows, side), lambda i, me_ref: (i ^ me_ref[0], 0, 0)),
-            ],
-            scratch_shapes=[
-                pltpu.VMEM((count, pieces[0].shape[0], pieces[0].shape[1] - first), BF),
-                pltpu.SemaphoreType.DMA((count,)),
-            ],
-        ),
-        out_shape=[
-            jax.ShapeDtypeStruct((count * rows, D), F32),
-            jax.ShapeDtypeStruct((count, rows, side), F32),
-        ],
-        compiler_params=pltpu.CompilerParams(vmem_limit_bytes=VMEM_BYTES),
-        cost_estimate=LIGHT,
-        name="place_pieces",
-    )(me, *pieces, *deps)
-
-
-def weight_grad_kernel(count, *refs):
+def widen_kernel(sums_ref, out_ref, side_ref):
+    out_ref[...] = sums_ref[:, :D].astype(F32)
+    side_ref[...] = sums_ref[:, D:].astype(F32)
+
+
+def weight_grad_kernel(count, dep_count, *refs):
     hidden_refs, left_refs, right_refs = (refs[k * count : (k + 1) * count] for k in range(3))
-    refs = refs[3 * count :]
+    refs = refs[3 * count + dep_count :]
     out_refs, (hidden, grads, arrived) = refs[:3], refs[3:]
     step = pl.program_id(0)
     rows = hidden_refs[0].shape[0]
@@ -1122,14 +1078,14 @@
         out_refs[number][...] = result[:, number * width : (number + 1) * width]
 
 
-def weight_grads(hidden_pieces, lefts, rights, width):
+def weight_grads(hidden_pieces, lefts, rights, width, *deps):
     count = len(hidden_pieces)
     rows = hidden_pieces[0].shape[0]
     height = D // 4
     return pl.pallas_call(
-        partial(weight_grad_kernel, count),
+        partial(weight_grad_kernel, count, len(deps)),
         grid=(4,),
-        in_specs=[pl.BlockSpec(memory_space=pl.ANY) for _ in range(3 * count)],
+        in_specs=[pl.BlockSpec(memory_space=pl.ANY) for _ in range(3 * count + len(deps))],
         out_specs=[pl.BlockSpec((height, width), lambda i: (i, 0)) for _ in range(3)],
         out_shape=[jax.ShapeDtypeStruct((D, width), F32)] * 3,
         scratch_shapes=[
@@ -1140,7 +1096,7 @@
         compiler_params=pltpu.CompilerParams(vmem_limit_bytes=VMEM_BYTES),
         cost_estimate=cost(6 * count * rows * D * width),
         name="weight_grads",
-    )(*hidden_pieces, *lefts, *rights)
+    )(*hidden_pieces, *lefts, *rights, *deps)
 
 
 def on_device(
@@ -1428,7 +1384,7 @@
         [
             jax.ShapeDtypeStruct((local_rows, head_width), F32),
             jax.ShapeDtypeStruct((local_rows, head_width), BF),
-            jax.ShapeDtypeStruct((tp_count, 8, local_rows), F32),
+            jax.ShapeDtypeStruct((8, local_rows), F32),
             jax.ShapeDtypeStruct((1, head_width), F32),
         ],
         mine_grad,
@@ -1442,10 +1398,8 @@
         sine,
     )
     mix_pieces = to_owners(mix_rows, "tp")
-    dots = spread_ready(held_back(dots_copies, mix_pieces), "tp")
-    folded = local_rows // sums_rows
-    late_width = -(-(D + side_width) // (128 * folded)) * 128
-    riding_width = 3 * head_width + late_width
+    dots = from_all(held_back(dots_copies, mix_pieces))
+    riding_width = 3 * head_width
     left_width = -(-riding_width // 256) * 128
     grads_left, grads_right, one_part = small_call(
         partial(input_back_kernel, tp_count),
@@ -1455,13 +1409,13 @@
             jax.ShapeDtypeStruct((local_rows, riding_width - left_width), BF),
             jax.ShapeDtypeStruct((local_rows, WIDE), BF),
         ],
+        *dots,
         query_back,
         key_back,
         value_grad_low,
         query_raw,
         key_raw,
         square_sums,
-        dots,
         qgain,
         kgain,
         query_weight,
@@ -1469,7 +1423,6 @@
         value_weight,
         tokens,
         norm2_part,
-        sums_own,
         scratch=[pltpu.VMEM((local_rows, riding_width), BF)],
     )
     near_left, near_right = gather_near(grads_left), gather_near(grads_right)
@@ -1501,14 +1454,23 @@
     grad_norm1, grad_norm2 = side_sums[: 2 * D // 128].reshape(2, D)
     grad_qgain, grad_kgain = side_sums[2 * D // 128 :].reshape(2, head_width)
     last_got = spread_ready(input_copies, "tp")
-    grad_input, mixed_out = last_got[:, :D].astype(F32), last_got[:, D:]
     hidden_one_pieces = with_odds([hidden_one_late] + hidden_one_near + hidden_one_corner)
+    sums_all = lax.all_gather(sums_own, "ep", tiled=True)
     grad_query, grad_key, grad_value = weight_grads(
         hidden_one_pieces, grad_lefts, grad_rights, head_width
     )
-    grad_output, router_side = place_pieces(
-        me, grad_rights, 3 * head_width - left_width, sums_rows, side_width, grad_query
-    )
+    grad_output, router_side = small_call(
+        widen_kernel,
+        "widen",
+        [
+            jax.ShapeDtypeStruct((head_width, D), F32),
+            jax.ShapeDtypeStruct((head_width, side_width), F32),
+        ],
+        sums_all,
+        deps=[grad_query],
+    )
+    last_held = held_back(last_got, grad_output)
+    grad_input, mixed_out = last_held[:, :D].astype(F32), last_held[:, D:]
     grad_router = (
         router_side.reshape(ep_count, folds, EXPERTS // ep_count, side_width)
         .transpose(1, 3, 0, 2)

time: 549 us -> 549 us (level)
  blocking collectives: 10.6 us -> 0 us
  starting transfers between devices: 81.1 us -> 88.7 us
    all_to_all x1 -> x0, blocking collectives: 10.6 us -> none  [spread_ready(): got = lax.all_to_all(copies, axis, split_axis=0, concat_axis=0, tiled=True)]
    ppermute x50, waiting for transfers between devices: 94.2 us -> 85.5 us  [swap(): return lax.ppermute(value, 'ep', [(i, i ^ distance) for i in range(count)])]
    pallas_call x2 -> x1, Pallas kernels: 23.2 us -> 18.6 us  [weight_grads(): pl.pallas_call(partial(weight_grad_kernel, count, len(deps)), grid=(4,),...]
    pallas_call x13 -> x14, Pallas kernels: 61.7 us -> 66.1 us  [small_call(): pl.pallas_call(run, in_specs=[pl.BlockSpec(memory_space=pltpu.VMEM)] * co...]
    unnamed x137 -> x143, local copies, waits for them, and re-layouts: 15.6 us -> 15.7 us
  transfers between devices with their start and end apart: 69 -> 73, of which waited for: 29 -> 28; matrix products, arithmetic and copies ran while one was open for 4% -> 5% of each run, Pallas kernels for 40% -> 41%
where the time goes in v5:
time: 549 us; the launch traced here: 538 us
  Pallas kernels  235 us (43%)
  waiting for transfers between devices  157 us (29%)
  starting transfers between devices  88.7 us (16%)
  local copies, waits for them, and re-layouts  26.4 us (5%)
  between operations  14.8 us (3%)
  other arithmetic  14.5 us (3%)
    ppermute x50, waiting for transfers between devices, swap(): return lax.ppermute(value, 'ep', [(i, i ^ distance) for i in range(count)])  85.5 us
    pallas_call x14, Pallas kernels, small_call(): pl.pallas_call(run, in_specs=[pl.BlockSpec(memory_space=pltpu.VMEM)] * co...  66.1 us
    pallas_call x1, Pallas kernels, expert_pass(): pl.pallas_call(partial(expert_kernel, sources, experts), grid_spec=pltpu....  43.6 us
    ppermute x50, starting transfers between devices, swap(): return lax.ppermute(value, 'ep', [(i, i ^ distance) for i in range(count)])  36.8 us
    all_to_all x3, waiting for transfers between devices, to_owners(): lax.all_to_all(value.reshape(count, rows // count, width), axis, split_ax...  24.5 us
    ppermute x6, waiting for transfers between devices, from_behind(): lax.ppermute(value, axis, [(source, source + steps) for source in range(i...  24.3 us
    pallas_call x1, Pallas kernels, pair_grads(): pl.pallas_call(pair_grad_kernel, grid=(experts,), in_specs=[per_expert(sp...  21.4 us
    pallas_call x1, Pallas kernels, add_up_even(): pl.pallas_call(partial(even_kernel, split), grid=(sources // 2,), in_spec...  20.5 us
  transfers between devices with their start and end apart: 73, of which 28 were waited for; matrix products, arithmetic and copies ran while one was open for 5% of the time, Pallas kernels for 41%

profile of v5, /device:TPU:0, one launch (start us, length us, event | category | flops | bytes accessed | tf_op | source)
XLA Modules:
  0.0 538.4 jit_solution(2171598874104209347)
XLA Ops:
  10.8 4.9 collective-permute-start
  19.1 4.6 projected.1
  23.6 5.0 all-to-all-start
  43.9 4.7 collective-permute-done.2.refs_1_
  55.7 8.5 %attention.1 = (bf16[256,512]{1,0:T(8,128)(2,1)}, bf16[256,2048]{1,0:T(8,128)(2,1)}) custom-call(bf16[256,512]{1,0:T(8,128)(2,1)} %get-tuple-element.71.refs_0_, bf16[256,512]{1,0:T(8,128)(2,1)} %copy-done.21, bf16[256,512]{1,0:T(8,128)(2,1)} %copy-done.22, bf16[256,512]{1,0:T(8,128)(2,1)} %get-tuple-element.72.refs_3_, bf16[256,512]{1,0:T(8,128)(2,1)} %copy-done.42, ...), custom_call_target="tpu_custom_call" | custom-call | flops 1 | bytes 1 | tf_op jit(solution)/shard_map/attention/pallas_call | solution.py:775
  69.4 24.5 %all-to-all-done.1.refs_0_ = bf16[4,64,2048]{2,1,0:T(8,128)(2,1)S(1)} async-done(((bf16[4,64,2048]{2,1,0:T(8,128)(2,1)}), bf16[4,64,2048]{2,1,0:T(8,128)(2,1)S(1)}, u32[]{:S(2)}, u32[]{:S(2)}) %all-to-all-start.1) | async-done | bytes 1048608 | tf_op jit(solution)/shard_map/all_to_all | solution.py:65
  101.1 4.4 all-gather.3.cloned.1.call-done.cot_ref
  110.1 18.8 %cotangent_rows.1 = (bf16[8,512,2048]{2,1,0:T(8,128)(2,1)}, f32[8,512,256]{2,1,0:T(8,128)}) custom-call(s32[1]{0:T(128)} %bitcast.15.me_ref, s32[8,8,256]{2,1,0:T(8,128)} %copy.74.slot_ref, bf16[2048,2176]{1,0:T(8,128)(2,1)} %all-gather.3.cloned.1.call-done.cot_ref, bf16[8,256,2048]{2,1,0:T(8,128)(2,1)} %down_ref.3), custom_call_target="tpu_custom_call" | custom-call | flops 1 | bytes 1 | tf_op jit(solution)/shard_map/cotangent_rows/pallas_call | solution.py:204
  134.2 12.3 %collective-permute-done.18.refs_10_ = bf16[256,1024]{1,0:T(8,128)(2,1)S(1)} collective-permute-done((bf16[256,1024]{1,0:T(8,128)(2,1)}, bf16[256,1024]{1,0:T(8,128)(2,1)S(1)}, u32[]{:S(2)}, u32[]{:S(2)}) %collective-permute-start.18) | collective-permute-done | bytes 524320 | tf_op jit(solution)/shard_map/ppermute | solution.py:72
  150.6 10.7 %collective-permute-done.22.refs_14_ = bf16[256,1024]{1,0:T(8,128)(2,1)S(1)} collective-permute-done((bf16[256,1024]{1,0:T(8,128)(2,1)S(1)}, bf16[256,1024]{1,0:T(8,128)(2,1)S(1)}, u32[]{:S(2)}, u32[]{:S(2)}) %collective-permute-start.22) | collective-permute-done | bytes 524320 | tf_op jit(solution)/shard_map/ppermute | solution.py:72
  163.2 7.9 %collective-permute-done.20.refs_12_ = bf16[256,1024]{1,0:T(8,128)(2,1)} collective-permute-done((bf16[256,1024]{1,0:T(8,128)(2,1)}, bf16[256,1024]{1,0:T(8,128)(2,1)}, u32[]{:S(2)}, u32[]{:S(2)}) %collective-permute-start.20) | collective-permute-done | bytes 524320 | tf_op jit(solution)/shard_map/ppermute | solution.py:72
  177.3 43.6 %expert_pass.1 = (bf16[8,512,2048]{2,1,0:T(8,128)(2,1)}, bf16[8,512,256]{2,1,0:T(8,128)(2,1)}, bf16[8,512,512]{2,1,0:T(8,128)(2,1)}, f32[8,512,1]{2,1,0:T(8,128)}, bf16[2048,2176]{1,0:T(8,128)(2,1)}) custom-call(s32[1]{0:T(128)} %bitcast.15.me_ref, s32[8,8,256]{2,1,0:T(8,128)} %copy.74.slot_ref, s32[8,8,256]{2,1,0:T(8,128)} %copy-done.44, ...), custom_call_target="tpu_custom_call" | custom-call | flops 21474836480 | bytes 1 | tf_op jit(solution)/shard_map/expert_pass/pallas_call | solution.py:353
  223.5 14.8 %output_pass.1.rows_ref = bf16[8,512,2048]{2,1,0:T(8,128)(2,1)} custom-call(bf16[8,512,256]{2,1,0:T(8,128)(2,1)} %get-tuple-element.81.mid_ref, f32[8,512,1]{2,1,0:T(8,128)} %get-tuple-element.82.scale_ref, bf16[8,256,2048]{2,1,0:T(8,128)(2,1)} %down_ref.3), custom_call_target="tpu_custom_call" | custom-call | flops 4294967296 | bytes 1 | tf_op jit(solution)/shard_map/output_pass/pallas_call | solution.py:561
  238.3 8.3 %add_up_odd.1 = bf16[4,256,2048]{2,1,0:T(8,128)(2,1)} custom-call(s32[8,256,8]{2,1,0:T(8,128)} %bitcast.69, bf16[8,512,2048]{2,1,0:T(8,128)(2,1)} %output_pass.1.rows_ref), custom_call_target="tpu_custom_call" | custom-call | flops 1 | bytes 1 | tf_op jit(solution)/shard_map/add_up_odd/pallas_call | solution.py:411
  249.5 4.6 collective-permute-done.27.got_ref
  254.1 20.5 %add_up_even.1 = (bf16[2,256,1024]{2,1,0:T(8,128)(2,1)}, bf16[2,256,1024]{2,1,0:T(8,128)(2,1)}, f32[256,1024]{1,0:T(8,128)}, f32[256,1024]{1,0:T(8,128)}, f32[256,1024]{1,0:T(8,128)}, /*index=5*/f32[256,1024]{1,0:T(8,128)}) custom-call(s32[8,256,8]{2,1,0:T(8,128)} %bitcast.70, bf16[8,512,2048]{2,1,0:T(8,128)(2,1)} %output_pass.1.rows_ref, ...), custom_call_target="tpu_custom_call" | custom-call | flops 1 | bytes 1 | tf_op jit(solution)/shard_map/add_up_even/pallas_call | solution.py:466
  274.6 21.4 %pair_grads.1 = (f32[8,2048,256]{2,1,0:T(8,128)}, f32[8,2048,256]{2,1,0:T(8,128)}) custom-call(bf16[8,512,2048]{2,1,0:T(8,128)(2,1)} %get-tuple-element.79.rows_ref, bf16[8,512,512]{2,1,0:T(8,128)(2,1)} %get-tuple-element.80.pair_ref, bf16[2,256,1024]{2,1,0:T(8,128)(2,1)} %get-tuple-element.83.refs_0_), custom_call_target="tpu_custom_call" | custom-call | flops 8589934592 | bytes 1 | tf_op jit(solution)/shard_map/pair_grads/pallas_call | solution.py:589
  307.1 15.5 %collective-permute-done.31.near_ref = bf16[2,256,1024]{2,1,0:T(8,128)(2,1)S(1)} collective-permute-done((bf16[2,256,1024]{2,1,0:T(8,128)(2,1)}, bf16[2,256,1024]{2,1,0:T(8,128)(2,1)S(1)}, u32[]{:S(2)}, u32[]{:S(2)}) %collective-permute-start.31) | collective-permute-done | bytes 1048608 | tf_op jit(solution)/shard_map/ppermute | solution.py:72
  332.0 4.7 all-to-all-start.3
  338.8 16.8 %down_grads.1.refs_26_ = f32[8,256,2048]{2,1,0:T(8,128)} custom-call(bf16[8,512,256]{2,1,0:T(8,128)(2,1)} %get-tuple-element.81.mid_ref, bf16[8,512,2048]{2,1,0:T(8,128)(2,1)} %get-tuple-element.94.cot_ref, f32[8,512,1]{2,1,0:T(8,128)} %get-tuple-element.82.scale_ref, bf16[256,1024]{1,0:T(8,128)(2,1)} %get-tuple-element.89.refs_9_.refs_0_), custom_call_target="tpu_custom_call" | custom-call | flops 4294967296 | bytes 1 | tf_op jit(solution)/shard_map/down_grads/pallas_call | solution.py:612
  367.4 12.3 %attention_back.1 = (f32[256,512]{1,0:T(8,128)}, f32[8,256]{1,0:T(8,128)}, f32[1,512]{1,0:T(1,128)}, f32[768,1024]{1,0:T(8,128)}, bf16[768,1024]{1,0:T(8,128)(2,1)}) custom-call(bf16[256,512]{1,0:T(8,128)(2,1)} %get-tuple-element.71.refs_0_, bf16[256,512]{1,0:T(8,128)(2,1)} %copy-done.21, bf16[256,512]{1,0:T(8,128)(2,1)} %copy-done.22, ...), custom_call_target="tpu_custom_call" | custom-call | flops 40265318400 | bytes 1 | tf_op jit(solution)/shard_map/attention_back/pallas_call | solution.py:775
  388.8 19.5 %collective-permute-done.36.refs_2_ = bf16[256,1024]{1,0:T(8,128)(2,1)S(1)} collective-permute-done((bf16[256,1024]{1,0:T(8,128)(2,1)S(1)}, bf16[256,1024]{1,0:T(8,128)(2,1)S(1)}, u32[]{:S(2)}, u32[]{:S(2)}) %collective-permute-start.36) | collective-permute-done | bytes 524320 | tf_op jit(solution)/shard_map/ppermute | solution.py:32
  409.3 4.4 key_back.1
  424.8 7.0 %input_back.1 = (bf16[256,768]{1,0:T(8,128)(2,1)}, bf16[256,768]{1,0:T(8,128)(2,1)}, bf16[256,2176]{1,0:T(8,128)(2,1)}) custom-call(f32[8,256]{1,0:T(8,128)} %held_back.14.refs_0_, f32[8,256]{1,0:T(8,128)} %copy-done.47, f32[8,256]{1,0:T(8,128)} %copy-done.48, f32[8,256]{1,0:T(8,128)} %copy-done.49, f32[256,512]{1,0:T(8,128)} %get-tuple-element.100.refs_4_, ...), custom_call_target="tpu_custom_call" | custom-call | flops 1 | bytes 1 | tf_op jit(solution)/shard_map/input_back/pallas_call | solution.py:775
  436.1 12.6 %collective-permute-start.41 = (bf16[256,768]{1,0:T(8,128)(2,1)}, bf16[256,768]{1,0:T(8,128)(2,1)S(1)}, u32[]{:S(2)}, u32[]{:S(2)}) collective-permute-start(bf16[256,768]{1,0:T(8,128)(2,1)} %get-tuple-element.106.refs_8_), channel_id=1, source_target_pairs={{0,8},{4,12},{8,0},{12,4},{16,24},{20,28},{24,16},{28,20},{1,9},{5... | collective-permute-start | bytes 1179656 | tf_op jit(solution)/shard_map/ppermute | solution.py:72
  450.9 8.6 %collective-permute-done.41.refs_6_.refs_10_ = bf16[256,768]{1,0:T(8,128)(2,1)S(1)} collective-permute-done((bf16[256,768]{1,0:T(8,128)(2,1)}, bf16[256,768]{1,0:T(8,128)(2,1)S(1)}, u32[]{:S(2)}, u32[]{:S(2)}) %collective-permute-start.41) | collective-permute-done | bytes 393248 | tf_op jit(solution)/shard_map/ppermute | solution.py:72
  461.9 6.0 %collective-permute-done.43.refs_8_.refs_18_ = bf16[256,768]{1,0:T(8,128)(2,1)S(1)} collective-permute-done((bf16[256,768]{1,0:T(8,128)(2,1)}, bf16[256,768]{1,0:T(8,128)(2,1)S(1)}, u32[]{:S(2)}, u32[]{:S(2)}) %collective-permute-start.43) | collective-permute-done | bytes 393248 | tf_op jit(solution)/shard_map/ppermute | solution.py:72
  470.5 4.4 first_back.1
  474.9 4.9 all-to-all-start.6
  485.9 8.2 %collective-permute-done.52.refs_14_ = bf16[256,768]{1,0:T(8,128)(2,1)S(1)} collective-permute-done((bf16[256,768]{1,0:T(8,128)(2,1)}, bf16[256,768]{1,0:T(8,128)(2,1)S(1)}, u32[]{:S(2)}, u32[]{:S(2)}) %collective-permute-start.52) | collective-permute-done | bytes 393248 | tf_op jit(solution)/shard_map/ppermute | solution.py:72
  497.8 18.6 %weight_grads.1 = (f32[2048,512]{1,0:T(8,128)}, f32[2048,512]{1,0:T(8,128)}, f32[2048,512]{1,0:T(8,128)}) custom-call(bf16[256,2048]{1,0:T(8,128)(2,1)} %held_back.9.refs_0_, bf16[256,2048]{1,0:T(8,128)(2,1)} %collective-permute-done.45.refs_1_, bf16[256,2048]{1,0:T(8,128)(2,1)} %copy-done.13, bf16[256,2048]{1,0:T(8,128)(2,1)} %collective-permute-done.46.refs_3_, ...), custom_call_target="tpu_custom_call" | custom-call | flops 12884901888 | bytes 1 | tf_op jit(solution)/shard_map/weight_grads/pallas_call | solution.py:1085
  521.8 4.9 all-to-all-done.6
  (348 shorter events, 155.1 us)
Async XLA Ops:
  10.8 23.6 %collective-permute-start = (bf16[256,512]{1,0:T(8,128)(2,1)}, bf16[256,512]{1,0:T(8,128)(2,1)S(1)}, u32[]{:S(2)}, u32[]{:S(2)}) collective-permute-start(bf16[256,512]{1,0:T(8,128)(2,1)} %get-tuple-element.70.refs_9_), channel_id=1, source_target_pairs={{0,16},{4,20},{8,24},{12,28},{1,17},{5,21},{9,25},{13,29},{2,18},{... | collective-permute-start | bytes 786440 | tf_op jit(solution)/shard_map/ppermute | solution.py:32
  15.6 18.7 %collective-permute-start.1 = (bf16[256,512]{1,0:T(8,128)(2,1)}, bf16[256,512]{1,0:T(8,128)(2,1)S(1)}, u32[]{:S(2)}, u32[]{:S(2)}) collective-permute-start(bf16[256,512]{1,0:T(8,128)(2,1)} %get-tuple-element.70.refs_9_), channel_id=1, source_target_pairs={{0,8},{4,12},{8,16},{12,20},{16,24},{20,28},{1,9},{5,13},{9,17},{1... | collective-permute-start | bytes 786440 | tf_op jit(solution)/shard_map/ppermute | solution.py:32
  28.6 76.9 %all-gather.3.cloned.1.call-start = ((), (), s32[]{:S(2)}) async-start(), calls=%async_computation.9 | async-start | bytes 10027008 | tf_op jit(solution)/shard_map/all_gather | solution.py:1254
  64.2 29.7 %all-to-all-start.1 = ((bf16[4,64,2048]{2,1,0:T(8,128)(2,1)}), bf16[4,64,2048]{2,1,0:T(8,128)(2,1)S(1)}, u32[]{:S(2)}, u32[]{:S(2)}) async-start(bf16[4,64,2048]{2,1,0:T(8,128)(2,1)} %bitcast.78), calls=%async_computation.1 | async-start | bytes 2097152 | tf_op jit(solution)/shard_map/all_to_all | solution.py:65
  97.5 31.4 %all-to-all-start.2 = ((bf16[4,64,2048]{2,1,0:T(8,128)(2,1)}), bf16[4,64,2048]{2,1,0:T(8,128)(2,1)S(1)}, u32[]{:S(2)}, u32[]{:S(2)}) async-start(bf16[4,64,2048]{2,1,0:T(8,128)(2,1)} %get-tuple-element.74), calls=%async_computation.2 | async-start | bytes 2097152 | tf_op jit(solution)/shard_map/all_to_all | solution.py:117
  101.0 196.5 %reduce-scatter.3.cloned.1.call-start = ((), (), s32[]{:S(2)}) async-start(), calls=%async_computation.10 | async-start | bytes 10027008 | tf_op jit(solution)/shard_map/reduce_scatter | solution.py:1304
  148.5 22.6 %collective-permute-start.20 = (bf16[256,1024]{1,0:T(8,128)(2,1)}, bf16[256,1024]{1,0:T(8,128)(2,1)}, u32[]{:S(2)}, u32[]{:S(2)}) collective-permute-start(bf16[256,1024]{1,0:T(8,128)(2,1)} %get-tuple-element.77.refs_8_.refs_2_), channel_id=1, source_target_pairs={{0,16},{4,20},{8,24},{12,28},{16,0},{20,4},{24,8},{28,12},{1,17},{... | collective-permute-start | bytes 1572872 | tf_op jit(solution)/shard_map/ppermute | solution.py:72
  150.1 22.1 %collective-permute-start.15 = (bf16[256,1024]{1,0:T(8,128)(2,1)S(1)}, bf16[256,1024]{1,0:T(8,128)(2,1)}, u32[]{:S(2)}, u32[]{:S(2)}) collective-permute-start(bf16[256,1024]{1,0:T(8,128)(2,1)S(1)} %collective-permute-done.13.refs_4_), channel_id=1, source_target_pairs={{0,8},{4,12},{8,0},{12,4},{16,24},{20,28},{24,16},{28,20},{1,9},{5... | collective-permute-start | bytes 1572872 | tf_op jit(solution)/shard_map/ppermute | solution.py:72
  173.5 47.3 %collective-permute-start.24 = (bf16[256,2048]{1,0:T(8,128)(2,1)}, bf16[256,2048]{1,0:T(8,128)(2,1)S(1)}, u32[]{:S(2)}, u32[]{:S(2)}) collective-permute-start(bf16[256,2048]{1,0:T(8,128)(2,1)} %held_back.9.refs_0_), channel_id=1, source_target_pairs={{0,8},{4,12},{8,0},{12,4},{16,24},{20,28},{24,16},{28,20},{1,9},{5... | collective-permute-start | bytes 3145736 | tf_op jit(solution)/shard_map/ppermute | solution.py:72
  174.6 47.6 %collective-permute-start.25 = (bf16[256,2048]{1,0:T(8,128)(2,1)}, bf16[256,2048]{1,0:T(8,128)(2,1)S(1)}, u32[]{:S(2)}, u32[]{:S(2)}) collective-permute-start(bf16[256,2048]{1,0:T(8,128)(2,1)} %held_back.9.refs_0_), channel_id=1, source_target_pairs={{0,16},{4,20},{8,24},{12,28},{16,0},{20,4},{24,8},{28,12},{1,17},{... | collective-permute-start | bytes 3145736 | tf_op jit(solution)/shard_map/ppermute | solution.py:72
  176.1 46.1 %collective-permute-start.26 = (bf16[256,2048]{1,0:T(8,128)(2,1)}, bf16[256,2048]{1,0:T(8,128)(2,1)S(1)}, u32[]{:S(2)}, u32[]{:S(2)}) collective-permute-start(bf16[256,2048]{1,0:T(8,128)(2,1)} %held_back.9.refs_0_), channel_id=1, source_target_pairs={{0,24},{4,28},{8,16},{12,20},{16,8},{20,12},{24,0},{28,4},{1,25},{... | collective-permute-start | bytes 3145736 | tf_op jit(solution)/shard_map/ppermute | solution.py:72
  297.5 25.1 %collective-permute-start.31 = (bf16[2,256,1024]{2,1,0:T(8,128)(2,1)}, bf16[2,256,1024]{2,1,0:T(8,128)(2,1)S(1)}, u32[]{:S(2)}, u32[]{:S(2)}) collective-permute-start(bf16[2,256,1024]{2,1,0:T(8,128)(2,1)} %held_back.12), channel_id=1, source_target_pairs={{0,8},{4,12},{8,0},{12,4},{16,24},{20,28},{24,16},{28,20},{1,9},{5... | collective-permute-start | bytes 3145736 | tf_op jit(solution)/shard_map/ppermute | solution.py:72
  298.9 24.8 %collective-permute-start.32 = (bf16[2,256,1024]{2,1,0:T(8,128)(2,1)}, bf16[2,256,1024]{2,1,0:T(8,128)(2,1)S(1)}, u32[]{:S(2)}, u32[]{:S(2)}) collective-permute-start(bf16[2,256,1024]{2,1,0:T(8,128)(2,1)} %held_back.13), channel_id=1, source_target_pairs={{0,16},{4,20},{8,24},{12,28},{16,0},{20,4},{24,8},{28,12},{1,17},{... | collective-permute-start | bytes 3145736 | tf_op jit(solution)/shard_map/ppermute | solution.py:72
  301.8 25.8 %collective-permute-start.28 = (bf16[64,2176]{1,0:T(8,128)(2,1)S(1)}, bf16[64,2176]{1,0:T(8,128)(2,1)S(1)}, u32[]{:S(2)}, u32[]{:S(2)}) collective-permute-start(bf16[64,2176]{1,0:T(8,128)(2,1)S(1)} %get-tuple-element.124), channel_id=1, source_target_pairs={{0,1},{1,0},{2,3},{3,2},{4,5},{5,4},{6,7},{7,6},{8,9},{9,8},{10,11... | collective-permute-start | bytes 835592 | tf_op jit(solution)/shard_map/ppermute | solution.py:93
  303.3 24.3 %collective-permute-start.29 = (bf16[64,2176]{1,0:T(8,128)(2,1)S(1)}, bf16[64,2176]{1,0:T(8,128)(2,1)S(1)}, u32[]{:S(2)}, u32[]{:S(2)}) collective-permute-start(bf16[64,2176]{1,0:T(8,128)(2,1)S(1)} %get-tuple-element.123), channel_id=1, source_target_pairs={{0,2},{1,3},{2,0},{3,1},{4,6},{5,7},{6,4},{7,5},{8,10},{9,11},{10,... | collective-permute-start | bytes 835592 | tf_op jit(solution)/shard_map/ppermute | solution.py:93
  305.7 21.9 %collective-permute-start.30 = (bf16[64,2176]{1,0:T(8,128)(2,1)S(1)}, bf16[64,2176]{1,0:T(8,128)(2,1)S(1)}, u32[]{:S(2)}, u32[]{:S(2)}) collective-permute-start(bf16[64,2176]{1,0:T(8,128)(2,1)S(1)} %get-tuple-element.122), channel_id=1, source_target_pairs={{0,3},{1,2},{2,1},{3,0},{4,7},{5,6},{6,5},{7,4},{8,11},{9,10},{10,... | collective-permute-start | bytes 835592 | tf_op jit(solution)/shard_map/ppermute | solution.py:93
  332.0 30.5 %all-to-all-start.3 = ((bf16[4,64,2176]{2,1,0:T(8,128)(2,1)}), bf16[4,64,2176]{2,1,0:T(8,128)(2,1)S(1)}, u32[]{:S(2)}, u32[]{:S(2)}) async-start(bf16[4,64,2176]{2,1,0:T(8,128)(2,1)} %get-tuple-element.90), calls=%async_computation.4 | async-start | bytes 2228224 | tf_op jit(solution)/shard_map/all_to_all | solution.py:117
  336.7 98.9 %reduce-scatter.5.cloned.1.call-start = ((), (), s32[]{:S(2)}) async-start(), calls=%async_computation.11 | async-start | bytes 2654208 | tf_op jit(solution)/shard_map/reduce_scatter | solution.py:1344
  336.7 18.9 %collective-permute-start.33 = (bf16[256,1024]{1,0:T(8,128)(2,1)S(1)}, bf16[256,1024]{1,0:T(8,128)(2,1)S(1)}, u32[]{:S(2)}, u32[]{:S(2)}) collective-permute-start(bf16[256,1024]{1,0:T(8,128)(2,1)S(1)} %copy-done.12), channel_id=1, source_target_pairs={{0,16},{4,20},{8,24},{12,28},{16,0},{20,4},{24,8},{28,12},{1,17},{... | collective-permute-start | bytes 1572872 | tf_op jit(solution)/shard_map/ppermute | solution.py:72
  379.9 33.8 %all-to-all-start.4 = ((bf16[4,64,2048]{2,1,0:T(8,128)(2,1)}), bf16[4,64,2048]{2,1,0:T(8,128)(2,1)S(1)}, u32[]{:S(2)}, u32[]{:S(2)}) async-start(bf16[4,64,2048]{2,1,0:T(8,128)(2,1)} %bitcast.75), calls=%async_computation.5 | async-start | bytes 2097152 | tf_op jit(solution)/shard_map/all_to_all | solution.py:65
  385.9 22.4 %collective-permute-start.36 = (bf16[256,1024]{1,0:T(8,128)(2,1)S(1)}, bf16[256,1024]{1,0:T(8,128)(2,1)S(1)}, u32[]{:S(2)}, u32[]{:S(2)}) collective-permute-start(bf16[256,1024]{1,0:T(8,128)(2,1)S(1)} %get-tuple-element.119), channel_id=1, source_target_pairs={{16,0},{20,4},{24,8},{28,12},{17,1},{21,5},{25,9},{29,13},{18,2},{... | collective-permute-start | bytes 1572872 | tf_op jit(solution)/shard_map/ppermute | solution.py:32
  387.2 21.1 %collective-permute-start.37 = (bf16[256,1024]{1,0:T(8,128)(2,1)S(1)}, bf16[256,1024]{1,0:T(8,128)(2,1)S(1)}, u32[]{:S(2)}, u32[]{:S(2)}) collective-permute-start(bf16[256,1024]{1,0:T(8,128)(2,1)S(1)} %get-tuple-element.118), channel_id=1, source_target_pairs={{8,0},{12,4},{16,8},{20,12},{24,16},{28,20},{9,1},{13,5},{17,9},{2... | collective-permute-start | bytes 1572872 | tf_op jit(solution)/shard_map/ppermute | solution.py:32
  431.9 37.6 %all-to-all-start.5 = ((bf16[4,64,2176]{2,1,0:T(8,128)(2,1)}), bf16[4,64,2176]{2,1,0:T(8,128)(2,1)S(1)}, u32[]{:S(2)}, u32[]{:S(2)}) async-start(bf16[4,64,2176]{2,1,0:T(8,128)(2,1)} %bitcast.76), calls=%async_computation.6 | async-start | bytes 2228224 | tf_op jit(solution)/shard_map/all_to_all | solution.py:65
  435.5 82.2 %all-gather.5.cloned.1.call-start = ((), (), s32[]{:S(2)}) async-start(), calls=%async_computation.12 | async-start | bytes 2654208 | tf_op jit(solution)/shard_map/all_gather | solution.py:1458
  436.1 23.3 %collective-permute-start.41 = (bf16[256,768]{1,0:T(8,128)(2,1)}, bf16[256,768]{1,0:T(8,128)(2,1)S(1)}, u32[]{:S(2)}, u32[]{:S(2)}) collective-permute-start(bf16[256,768]{1,0:T(8,128)(2,1)} %get-tuple-element.106.refs_8_), channel_id=1, source_target_pairs={{0,8},{4,12},{8,0},{12,4},{16,24},{20,28},{24,16},{28,20},{1,9},{5... | collective-permute-start | bytes 1179656 | tf_op jit(solution)/shard_map/ppermute | solution.py:72
  448.7 19.2 %collective-permute-start.43 = (bf16[256,768]{1,0:T(8,128)(2,1)}, bf16[256,768]{1,0:T(8,128)(2,1)S(1)}, u32[]{:S(2)}, u32[]{:S(2)}) collective-permute-start(bf16[256,768]{1,0:T(8,128)(2,1)} %get-tuple-element.107.refs_16_), channel_id=1, source_target_pairs={{0,8},{4,12},{8,0},{12,4},{16,24},{20,28},{24,16},{28,20},{1,9},{5... | collective-permute-start | bytes 1179656 | tf_op jit(solution)/shard_map/ppermute | solution.py:72
  448.9 20.6 %collective-permute-start.44 = (bf16[256,768]{1,0:T(8,128)(2,1)}, bf16[256,768]{1,0:T(8,128)(2,1)}, u32[]{:S(2)}, u32[]{:S(2)}) collective-permute-start(bf16[256,768]{1,0:T(8,128)(2,1)} %get-tuple-element.107.refs_16_), channel_id=1, source_target_pairs={{0,16},{4,20},{8,24},{12,28},{16,0},{20,4},{24,8},{28,12},{1,17},{... | collective-permute-start | bytes 1179656 | tf_op jit(solution)/shard_map/ppermute | solution.py:72
  450.8 29.7 %collective-permute-start.45 = (bf16[256,2048]{1,0:T(8,128)(2,1)S(1)}, bf16[256,2048]{1,0:T(8,128)(2,1)}, u32[]{:S(2)}, u32[]{:S(2)}) collective-permute-start(bf16[256,2048]{1,0:T(8,128)(2,1)S(1)} %copy-done.7), channel_id=1, source_target_pairs={{0,4},{4,0},{8,12},{12,8},{16,20},{20,16},{24,28},{28,24},{1,5},{5... | collective-permute-start | bytes 3145736 | tf_op jit(solution)/shard_map/ppermute | solution.py:72
  459.4 21.6 %collective-permute-start.46 = (bf16[256,2048]{1,0:T(8,128)(2,1)}, bf16[256,2048]{1,0:T(8,128)(2,1)}, u32[]{:S(2)}, u32[]{:S(2)}) collective-permute-start(bf16[256,2048]{1,0:T(8,128)(2,1)} %copy-done.13), channel_id=1, source_target_pairs={{0,4},{4,0},{8,12},{12,8},{16,20},{20,16},{24,28},{28,24},{1,5},{5... | collective-permute-start | bytes 3145736 | tf_op jit(solution)/shard_map/ppermute | solution.py:72
  461.9 19.2 %collective-permute-start.47 = (bf16[256,2048]{1,0:T(8,128)(2,1)}, bf16[256,2048]{1,0:T(8,128)(2,1)}, u32[]{:S(2)}, u32[]{:S(2)}) collective-permute-start(bf16[256,2048]{1,0:T(8,128)(2,1)} %copy-done.14), channel_id=1, source_target_pairs={{0,4},{4,0},{8,12},{12,8},{16,20},{20,16},{24,28},{28,24},{1,5},{5... | collective-permute-start | bytes 3145736 | tf_op jit(solution)/shard_map/ppermute | solution.py:72
  474.9 51.8 %all-to-all-start.6 = ((bf16[4,64,4096]{2,1,0:T(8,128)(2,1)}), bf16[4,64,4096]{2,1,0:T(8,128)(2,1)S(1)}, u32[]{:S(2)}, u32[]{:S(2)}) async-start(bf16[4,64,4096]{2,1,0:T(8,128)(2,1)} %get-tuple-element.108), calls=%async_computation.7 | async-start | bytes 4194304 | tf_op jit(solution)/shard_map/all_to_all | solution.py:117
  495.9 20.6 %collective-permute-start.61 = (f32[40,128]{1,0:T(8,128)S(1)}, f32[40,128]{1,0:T(8,128)S(1)}, u32[]{:S(2)}, u32[]{:S(2)}) collective-permute-start(f32[40,128]{1,0:T(8,128)S(1)} %add.219), channel_id=1, source_target_pairs={{0,16},{4,20},{8,24},{12,28},{16,0},{20,4},{24,8},{28,12},{1,17},{... | collective-permute-start | bytes 61448 | tf_op jit(solution)/shard_map/ppermute | solution.py:72
  (108 other events, 770.5 us)
Sparse Core Ops, SparseCore 0:
  50.2 55.3 all-gather.2
  223.6 73.8 reduce-scatter.2
  367.6 59.8 reduce-scatter.4
  438.1 43.2 all-gather.4
